TPU v7x, 32 devices: a whole 2x2x4 slice. The times are simulated.
32 devices in a mesh: tile: 16 (over z, y, core), group: 2 (over x).
Axes of the slice: x: 2, y: 2, z: 4, core: 2. Of those that a mesh axis runs over, the one named last changes fastest.
Arguments:
- latents: bfloat16 [192, 128, 1536], P(('tile', 'group')), may hold values from -6 to 6
- window_index: int32 [384], P(('tile', 'group')), may hold values from 0 to 2039
- window_len: int32 [384], P(('tile', 'group')), may hold values from 1 to 64
- live_blocks: int32 [32], P(('tile', 'group')), may hold values from 0 to 6, as said below
- norm_gain: float32 [1536], replicated, may hold values from 0.1 to 1.9
- w_qkv: bfloat16 [1536, 4608], P('group', 'tile'), may hold values from -0.15625 to 0.15625
- w_out: bfloat16 [1536, 1536], P('group', 'tile'), may hold values from -0.15625 to 0.15625
Outputs:
- refined: bfloat16 [192, 128, 1536], P(('tile', 'group'))
Inputs may be any that keep to these rules, and one draw needn't show every extreme that they name: `live_blocks`: the device at tile index i and the device at tile index i + 8 in the same group form a pair; at most one of a pair holds more than 4 live blocks, the two hold at most 8 together, and in every draw some pair holds exactly 6 and 2.
All inputs are finite; a program needn't handle non-finite values.
Results may differ from a plain program's by a relative error of at most 0.0033.
Values may be sent and summed in bfloat16 or wider, within the bound.
No kernel may reach another device: no remote copies, remote signals or barrier semaphores. Data moves between devices by JAX's collectives and lax.ppermute only.
A program may use at most 128 MiB of HBM per device.

v0:
```python
import math

import jax
import jax.numpy as jnp
from jax import lax
from jax.sharding import PartitionSpec as P

D = 1536
HEADS = 24
HEAD_DIM = 64
WIN_SIDE = 8
WIN_COLS = 60
WIN_TOK = 64


def position_table(window_ids):
    token_ids = jnp.arange(WIN_TOK, dtype=jnp.int32)
    row_pos = window_ids[:, None] // WIN_COLS * WIN_SIDE + token_ids[None, :] // WIN_SIDE
    col_pos = window_ids[:, None] % WIN_COLS * WIN_SIDE + token_ids[None, :] % WIN_SIDE
    quarter = D // 4
    frequency = jnp.exp(jnp.arange(quarter, dtype=jnp.float32) * (-math.log(10000.0) / quarter))
    row_angle = row_pos.astype(jnp.float32)[:, :, None] * frequency
    col_angle = col_pos.astype(jnp.float32)[:, :, None] * frequency
    return jnp.concatenate(
        [jnp.sin(row_angle), jnp.cos(row_angle), jnp.sin(col_angle), jnp.cos(col_angle)], axis=-1
    )


def head_norm(values):
    return (values * lax.rsqrt(jnp.mean(values * values, axis=-1, keepdims=True) + 1e-06)).astype(
        jnp.bfloat16
    )


def project_qkv(normed, w_qkv):
    full_rows = lax.all_gather(w_qkv, "group", axis=0, tiled=True)
    return jnp.dot(
        normed,
        lax.all_gather(full_rows, "tile", axis=1, tiled=True),
        preferred_element_type=jnp.float32,
    )


def window_layer(blocks_in, window_ids, window_lens, norm_gain, w_qkv, w_out):
    window_count = window_ids.shape[0]
    stream = blocks_in.reshape(window_count, WIN_TOK, D).astype(jnp.float32) + position_table(
        window_ids
    )
    scale = lax.rsqrt(jnp.mean(stream * stream, axis=-1, keepdims=True) + 1e-06)
    normed = (stream * scale * norm_gain).astype(jnp.bfloat16).reshape(window_count * WIN_TOK, D)
    projected = project_qkv(normed, w_qkv)
    projected = projected.reshape(window_count, WIN_TOK, 3, HEADS, HEAD_DIM)
    queries = head_norm(projected[:, :, 0])
    keys = head_norm(projected[:, :, 1])
    values = projected[:, :, 2].astype(jnp.bfloat16)
    scores = jnp.einsum(
        "wqhd,wkhd->whqk", queries, keys, preferred_element_type=jnp.float32
    ) * HEAD_DIM ** (-0.5)
    key_mask = jnp.arange(WIN_TOK, dtype=jnp.int32)[None, :] < window_lens[:, None]
    weights = jnp.exp(scores) * key_mask[:, None, None, :].astype(jnp.float32)
    probs = (weights / jnp.sum(weights, axis=-1, keepdims=True)).astype(jnp.bfloat16)
    attended = jnp.einsum("whqk,wkhd->wqhd", probs, values, preferred_element_type=jnp.float32)
    attended = attended.astype(jnp.bfloat16).reshape(window_count * WIN_TOK, D)
    out_full_rows = lax.all_gather(w_out, "group", axis=0, tiled=True)
    update = jnp.dot(
        attended,
        lax.all_gather(out_full_rows, "tile", axis=1, tiled=True),
        preferred_element_type=jnp.float32,
    )
    base = blocks_in.reshape(window_count * WIN_TOK, D).astype(jnp.float32)
    token_live = key_mask.reshape(window_count * WIN_TOK)[:, None]
    return jnp.where(token_live, base + update, base).astype(jnp.bfloat16).reshape(blocks_in.shape)


def local(latents, window_index, window_len, live_blocks, norm_gain, w_qkv, w_out):
    slot_total = latents.shape[0]
    slot_ids = jnp.arange(slot_total, dtype=jnp.int32)
    live_mask = (slot_ids < live_blocks[0])[:, None, None]
    finished = window_layer(latents, window_index, window_len, norm_gain, w_qkv, w_out)
    return jnp.where(live_mask, finished, latents)


def solution(mesh):
    in_specs = (
        P(("tile", "group"), None, None),
        P(("tile", "group")),
        P(("tile", "group")),
        P(("tile", "group")),
        P(),
        P("group", "tile"),
        P("group", "tile"),
    )
    out_specs = P(("tile", "group"), None, None)
    return jax.shard_map(local, mesh=mesh, in_specs=in_specs, out_specs=out_specs, check_vma=False)
```

profile of v0, /device:TPU:0, one launch (start us, length us, event | category | flops | bytes accessed | tf_op | source)
XLA Modules:
  0.0 228.2 jit_solution(8803131300240552596)
XLA Ops:
  6.5 0.0 all-gather.3.cloned.1.call-start
  6.5 16.0 %all_gather.12 = bf16[1536,288]{0,1:T(8,128)(2,1)} all-gather(bf16[768,288]{0,1:T(8,128)(2,1)} %param.12), channel_id=1, replica_groups=mesh['tile'=16,'group'=2] {'group'}, dimensions={0}, use_global_device_ids=true | all-gather | bytes 1327104 | tf_op jit(solution)/shard_map/all_gather | solution.py:36
  22.5 0.0 all-gather.3.cloned.1.call-update
  22.6 0.0 all-gather.5.cloned.1.call-start
  22.6 6.1 %all_gather.14 = bf16[1536,96]{0,1:T(8,128)(2,1)} all-gather(bf16[768,96]{0,1:T(8,128)(2,1)} %param.13), channel_id=1, replica_groups=mesh['tile'=16,'group'=2] {'group'}, dimensions={0}, use_global_device_ids=true | all-gather | bytes 442368 | tf_op jit(solution)/shard_map/all_gather | solution.py:64
  28.8 0.0 all-gather.5.cloned.1.call-update
  28.8 0.7 fusion.13
  29.5 0.1 add.122
  29.6 0.1 add.123
  29.6 0.1 add.124
  29.7 0.1 add.130
  29.8 0.1 add.131
  29.9 0.1 add.132
  30.0 0.1 add.126
  30.0 0.1 add.135
  30.1 9.6 %multiply_sine_fusion.1 = (f32[6,128,384]{2,1,0:T(8,128)S(1)}, f32[6,128,384]{2,1,0:T(8,128)}, f32[6,128,384]{2,1,0:T(8,128)}, f32[6,128,384]{2,1,0:T(8,128)S(1)}) fusion(f32[384]{0:T(512)S(1)} %multiply_exponential_fusion, f32[6,128]{1,0:T(8,128)S(1)} %get-tuple-element.20, f32[6,128]{1,0:T(8,128)S(1)} %get-tuple-element.19), kind=kLoop, calls=%fused_computation.27 | loop fusion | flops 589824 | bytes 4726272 | tf_op jit(solution)/shard_map/sin | solution.py:25
  39.8 1.0 copy-done.3
  40.8 2.1 multiply_reduce_fusion.2
  42.9 0.1 iota_compare_fusion
  43.0 0.7 lt.51
  44.3 3.4 %multiply_convert_fusion.4 = bf16[6,128,1536]{2,1,0:T(8,128)(2,1)} fusion(f32[1536]{0:T(1024)} %param.11, f32[6,128]{1,0:T(8,128)S(1)} %add_rsqrt_fusion.2, f32[6,128,384]{2,1,0:T(8,128)} %get-tuple-element.11, f32[6,128,384]{2,1,0:T(8,128)} %copy-done.3, f32[6,128,384]{2,1,0:T(8,128)} %get-tuple-element.8, f32[6,128,384]{2,1,0:T(8,128)S(1)} %get-tuple-element.7, ...), kind=kLoop, calls=%fused_computation.21 | loop fusion | flops 9437184 | bytes 9446400 | tf_op jit(solution)/shard_map/convert_element_type | solution.py:50
  47.7 86.0 %all-gather.3.cloned.1.call-done = bf16[1536,4608]{0,1:T(8,128)(2,1)} async-done(((bf16[1536,288]{0,1:T(8,128)(2,1)}), bf16[1536,4608]{0,1:T(8,128)(2,1)}) %all-gather.3.cloned.1.call-update) | async-done | bytes 14155792 | tf_op jit(solution)/shard_map/all_gather | solution.py:39
  133.7 25.9 %fusion.16 = f32[12,64,3,24,64]{1,4,3,2,0:T(8,128)S(1)} fusion(bf16[12,64,1536,1,1]{2,1,4,3,0:T(8,128)(2,1)} %bitcast.46, bf16[3,24,64,1536,1]{3,2,1,0,4:T(8,128)(2,1)} %bitcast.48), kind=kOutput, calls=%fused_computation.47 | convolution fusion | flops 10871635968 | bytes 30670848 | tf_op jit(solution)/shard_map/dot_general | solution.py:37
  159.6 10.0 %copy-done = f32[12,64,3,24,64]{1,4,3,2,0:T(8,128)} copy-done((f32[12,64,3,24,64]{1,4,3,2,0:T(8,128)}, f32[12,64,3,24,64]{1,4,3,2,0:T(8,128)S(1)}, u32[]{:S(2)}) %copy-start) | copy-done | bytes 14155800
  169.7 4.0 %multiply_reduce_fusion.1 = (f32[12,64,24]{1,2,0:T(8,128)S(1)}, f32[12,64,24]{1,2,0:T(8,128)S(1)}) fusion(f32[12,64,3,24,64]{1,4,3,2,0:T(8,128)S(1)} %fusion.16), kind=kLoop, calls=%fused_computation.8 | loop fusion | flops 4681728 | bytes 9584640 | tf_op jit(solution)/shard_map/reduce_sum | solution.py:30
  173.7 13.8 %fusion = (f32[12,24,64]{2,1,0:T(8,128)S(1)}, f32[12,24,64,64]{2,3,1,0:T(8,128)}) fusion(f32[12,64]{1,0:T(8,128)S(1)} %get-tuple-element.14, f32[12,64,3,24,64]{1,4,3,2,0:T(8,128)} %copy-done, f32[12,64,24]{1,2,0:T(8,128)S(1)} %add_rsqrt_fusion, f32[12,64,24]{1,2,0:T(8,128)S(1)} %add_rsqrt_fusion.1), kind=kOutput, calls=%fused_computation.9 | convolution fusion | flops 159234048 | bytes 23817216 | tf_op jit(solution)/shard_map/wqhd,wkhd->whqk/dot_general | solution.py:56
  187.5 10.9 %convert_bitcast_fusion = bf16[12,64,24,64]{1,3,2,0:T(8,128)(2,1)} fusion(f32[12,24,64,64]{2,3,1,0:T(8,128)} %get-tuple-element.18, f32[12,24,64]{2,1,0:T(8,128)S(1)} %get-tuple-element.17, f32[12,64]{1,0:T(8,128)S(1)} %get-tuple-element.14, f32[12,64,3,24,64]{1,4,3,2,0:T(8,128)} %copy-done), kind=kOutput, calls=%fused_computation.16 | convolution fusion | flops 156893184 | bytes 16591872 | tf_op jit(solution)/shard_map/whqk,wkhd->wqhd/dot_general | solution.py:62
  198.4 6.9 %copy.14 = bf16[12,64,24,64]{3,2,1,0:T(8,128)(2,1)} copy(bf16[12,64,24,64]{1,3,2,0:T(8,128)(2,1)} %convert_bitcast_fusion) | data formatting | bytes 4718592 | tf_op jit(solution)/shard_map/convert_element_type | solution.py:63
  205.3 7.4 %reshape.306 = bf16[768,1536]{1,0:T(8,128)(2,1)} reshape(bf16[12,64,24,64]{3,2,1,0:T(8,128)(2,1)} %copy.14) | data formatting | bytes 4718592 | tf_op jit(solution)/shard_map/reshape | solution.py:63
  212.7 0.0 copy-done.4
  212.7 6.9 %fusion.1 = bf16[768,1536]{1,0:T(8,128)(2,1)S(1)} fusion(bf16[768,1536]{1,0:T(8,128)(2,1)} %reshape.306, bf16[1536,1536]{0,1:T(8,128)(2,1)} %all-gather.5.cloned.1.call-done, pred[768]{0:T(1024)(128)(4,1)S(1)} %copy-done.4, bf16[6,128,1536]{2,1,0:T(8,128)(2,1)S(1)} %copy-done.2), kind=kOutput, calls=%fused_computation.11 | convolution fusion | flops 3628597248 | bytes 11797248 | tf_op jit(solution)/shard_map/dot_general | solution.py:65
  219.6 1.7 broadcast_select_fusion
  (20 shorter events, 0.1 us)
Async XLA Ops:
  6.5 34.3 %copy-start.1 = (bf16[6,128,1536]{2,1,0:T(8,128)(2,1)S(1)}, bf16[6,128,1536]{2,1,0:T(8,128)(2,1)}, u32[]{:S(2)}) copy-start(bf16[6,128,1536]{2,1,0:T(8,128)(2,1)} %param.7) | copy-start | bytes 7077892
  6.5 127.1 %all-gather.3.cloned.1.call-start = ((), (), s32[]{:S(2)}) async-start(), calls=%async_computation | async-start | bytes 15040512 | tf_op jit(solution)/shard_map/all_gather | solution.py:39
  22.6 190.1 %all-gather.5.cloned.1.call-start = ((), (), s32[]{:S(2)}) async-start(), calls=%async_computation.1 | async-start | bytes 5013504 | tf_op jit(solution)/shard_map/all_gather | solution.py:67
  39.8 1.0 copy-start.3
  39.8 3.1 %copy-start.5 = (s32[12]{0:T(128)S(1)}, s32[12]{0:T(128)}, u32[]{:S(2)}) copy-start(s32[12]{0:T(128)} %param.9) | copy-start | bytes 148
  159.6 10.0 %copy-start = (f32[12,64,3,24,64]{1,4,3,2,0:T(8,128)}, f32[12,64,3,24,64]{1,4,3,2,0:T(8,128)S(1)}, u32[]{:S(2)}) copy-start(f32[12,64,3,24,64]{1,4,3,2,0:T(8,128)S(1)} %fusion.16) | copy-start | bytes 42467332
  205.3 7.4 %copy-start.2 = (bf16[6,128,1536]{2,1,0:T(8,128)(2,1)S(1)}, bf16[6,128,1536]{2,1,0:T(8,128)(2,1)}, u32[]{:S(2)}) copy-start(bf16[6,128,1536]{2,1,0:T(8,128)(2,1)} %param.7) | copy-start | bytes 7077892
  205.3 7.4 %copy-start.4 = (pred[768]{0:T(1024)(128)(4,1)S(1)}, pred[768]{0:T(1024)(128)(4,1)}, u32[]{:S(2)}) copy-start(pred[768]{0:T(1024)(128)(4,1)} %lt.51) | copy-start | bytes 2308
Sparse Core Ops, SparseCore 0:
  22.7 110.9 all-gather.2
  136.0 51.5 all-gather.4
where the time goes:
time: 229 us; the launch traced here: 228 us
  waiting for transfers between devices  86 us (38%)
  matrix products  57.5 us (25%)
  local copies, waits for them, and re-layouts  26.7 us (12%)
  blocking collectives  22.1 us (10%)
  other arithmetic  21.6 us (9%)
  between operations  14.2 us (6%)
    all_gather x1, waiting for transfers between devices, project_qkv(): lax.all_gather(full_rows, 'tile', axis=1, tiled=True)  86 us
    dot_general x1, matrix products, project_qkv(): jnp.dot(normed, lax.all_gather(full_rows, 'tile', axis=1, tiled=True), pr...  25.9 us
    all_gather x1, blocking collectives, project_qkv(): full_rows = lax.all_gather(w_qkv, 'group', axis=0, tiled=True)  16 us
    dot_general x1, matrix products, window_layer(): jnp.einsum('wqhd,wkhd->whqk', queries, keys, preferred_element_type=jnp.f...  13.8 us
    unnamed x12, local copies, waits for them, and re-layouts  11.1 us
    dot_general x1, matrix products, window_layer(): jnp.einsum('whqk,wkhd->wqhd', probs, values, preferred_element_type=jnp.f...  10.9 us
    sin x1, other arithmetic, position_table(): jnp.sin(row_angle)  9.64 us
    reshape x1, local copies, waits for them, and re-layouts, window_layer(): attended = attended.astype(jnp.bfloat16).reshape(window_count * WIN_TOK, D)  7.4 us
  transfers between devices with their start and end apart: 2, of which 1 were waited for; matrix products, arithmetic and copies ran while one was open for 38% of the time, Pallas kernels for 0%

commit v1 on v0

v1 whole, which is shorter than its diff:
```python
import functools
import math

import jax
import jax.numpy as jnp
from jax import lax
from jax.experimental import pallas as pl
from jax.experimental.pallas import tpu as pltpu
from jax.sharding import PartitionSpec as P

HEAD_DIM = 64
WIN_SIDE = 8
WIN_COLS = 60
WIN_TOK = 64
EPS = 1e-06
BF = jnp.bfloat16
F32 = jnp.float32
LIMIT = 56 * 1024 * 1024


def position_table(window_ids, width):
    token_ids = jnp.arange(WIN_TOK, dtype=jnp.int32)
    row_pos = window_ids[:, None] // WIN_COLS * WIN_SIDE + token_ids[None, :] // WIN_SIDE
    col_pos = window_ids[:, None] % WIN_COLS * WIN_SIDE + token_ids[None, :] % WIN_SIDE
    quarter = width // 4
    frequency = jnp.exp(jnp.arange(quarter, dtype=F32) * (-math.log(10000.0) / quarter))
    row_angle = row_pos.astype(F32)[:, :, None] * frequency
    col_angle = col_pos.astype(F32)[:, :, None] * frequency
    return jnp.concatenate(
        [jnp.sin(row_angle), jnp.cos(row_angle), jnp.sin(col_angle), jnp.cos(col_angle)], axis=-1
    )


def head_norm(values):
    return (values * lax.rsqrt(jnp.mean(values * values, axis=-1, keepdims=True) + EPS)).astype(BF)


def window_layer(blocks_in, window_ids, window_lens, norm_gain, w_qkv, w_out):
    width = blocks_in.shape[-1]
    count = window_ids.shape[0]
    heads = width // HEAD_DIM
    stream = blocks_in.reshape(count, WIN_TOK, width).astype(F32) + position_table(window_ids, width)
    scale = lax.rsqrt(jnp.mean(stream * stream, axis=-1, keepdims=True) + EPS)
    normed = (stream * scale * norm_gain).astype(BF).reshape(count * WIN_TOK, width)
    full_rows = lax.all_gather(w_qkv, "group", axis=0, tiled=True)
    projected = jnp.dot(
        normed,
        lax.all_gather(full_rows, "tile", axis=1, tiled=True),
        preferred_element_type=F32,
    ).reshape(count, WIN_TOK, 3, heads, HEAD_DIM)
    queries = head_norm(projected[:, :, 0])
    keys = head_norm(projected[:, :, 1])
    values = projected[:, :, 2].astype(BF)
    scores = jnp.einsum("wqhd,wkhd->whqk", queries, keys, preferred_element_type=F32) * HEAD_DIM**-0.5
    key_mask = jnp.arange(WIN_TOK, dtype=jnp.int32)[None, :] < window_lens[:, None]
    weights = jnp.exp(scores) * key_mask[:, None, None, :].astype(F32)
    probs = (weights / jnp.sum(weights, axis=-1, keepdims=True)).astype(BF)
    attended = jnp.einsum("whqk,wkhd->wqhd", probs, values, preferred_element_type=F32)
    attended = attended.astype(BF).reshape(count * WIN_TOK, width)
    out_rows = lax.all_gather(w_out, "group", axis=0, tiled=True)
    update = jnp.dot(
        attended, lax.all_gather(out_rows, "tile", axis=1, tiled=True), preferred_element_type=F32
    )
    base = blocks_in.reshape(count * WIN_TOK, width).astype(F32)
    token_live = key_mask.reshape(count * WIN_TOK)[:, None]
    return jnp.where(token_live, base + update, base).astype(BF).reshape(blocks_in.shape)


def general(latents, window_index, window_len, live_blocks, norm_gain, w_qkv, w_out):
    slot_ids = jnp.arange(latents.shape[0], dtype=jnp.int32)
    live_mask = (slot_ids < live_blocks[0])[:, None, None]
    finished = window_layer(latents, window_index, window_len, norm_gain, w_qkv, w_out)
    return jnp.where(live_mask, finished, latents)


def anyspec():
    return pl.BlockSpec(memory_space=pl.ANY)


def vspec():
    return pl.BlockSpec(memory_space=pltpu.VMEM)


def sspec():
    return pl.BlockSpec(memory_space=pltpu.SMEM)


def params():
    return pltpu.CompilerParams(vmem_limit_bytes=LIMIT)


def cost(flops, moved):
    return pl.CostEstimate(flops=flops, bytes_accessed=moved, transcendentals=0)


def pack_kernel(wq_ref, wo_ref, unit_ref, a_ref, b_ref):
    half = wq_ref.shape[0] // 2
    nq = wq_ref.shape[1]
    for j, ref in enumerate((a_ref, b_ref)):
        wide = jnp.concatenate(
            [wq_ref[j * half : (j + 1) * half, :], wo_ref[j * half : (j + 1) * half, :]], axis=1
        )
        turned = wide.T
        ref[...] = turned
        unit_ref[j] = turned


def pack(w_qkv, w_out):
    depth, nq = w_qkv.shape
    both = nq + w_out.shape[1]
    return pl.pallas_call(
        pack_kernel,
        out_shape=(
            jax.ShapeDtypeStruct((2, both, depth // 2), BF),
            jax.ShapeDtypeStruct((both, depth // 2), BF),
            jax.ShapeDtypeStruct((both, depth // 2), BF),
        ),
        in_specs=[vspec()] * 2,
        out_specs=(vspec(),) * 3,
        compiler_params=params(),
        cost_estimate=cost(0, 4 * depth * both),
        name="pack_weights",
    )(w_qkv, w_out)


def norm_kernel(ids_ref, lat_ref, gain_ref, freq_ref, out_ref, pos_ref):
    blocks, _, width = lat_ref.shape
    quarter = width // 4
    freq = freq_ref[...]
    step = lax.broadcasted_iota(jnp.int32, (WIN_SIDE, quarter), 0).astype(F32) * freq
    sin_step, cos_step = jnp.sin(step), jnp.cos(step)
    gain = gain_ref[...]

    @pl.loop(0, blocks)
    def _(b):
        for w in range(2):
            place = ids_ref[2 * b + w]
            row = (place // WIN_COLS * WIN_SIDE).astype(F32)
            col = (place % WIN_COLS * WIN_SIDE).astype(F32)
            for at, start in ((0, row), (2 * quarter, col)):
                base = start * freq
                sin_base, cos_base = jnp.sin(base), jnp.cos(base)
                sines = sin_base * cos_step + cos_base * sin_step
                cosines = cos_base * cos_step - sin_base * sin_step
                for more, table in ((0, sines), (quarter, cosines)):
                    where = pl.ds(at + more, quarter)
                    for i in range(WIN_SIDE):
                        rows = pl.ds(w * WIN_TOK + i * WIN_SIDE, WIN_SIDE)
                        if at == 0:
                            pos_ref[rows, where] = jnp.broadcast_to(
                                table[i : i + 1, :], (WIN_SIDE, quarter)
                            )
                        else:
                            pos_ref[rows, where] = table
        stream = lat_ref[b].astype(F32) + pos_ref[...]
        scale = lax.rsqrt(jnp.mean(stream * stream, axis=-1, keepdims=True) + EPS)
        out_ref[b] = (stream * scale * gain).astype(BF).T


def normed_columns(latents, window_index, norm_gain):
    blocks, rows, width = latents.shape
    quarter = width // 4
    freq = jnp.exp(jnp.arange(quarter, dtype=F32) * (-math.log(10000.0) / quarter))
    return pl.pallas_call(
        norm_kernel,
        out_shape=jax.ShapeDtypeStruct((blocks, width, rows), BF),
        in_specs=[sspec(), vspec(), vspec(), vspec()],
        out_specs=vspec(),
        scratch_shapes=[pltpu.VMEM((rows, width), F32)],
        compiler_params=params(),
        cost_estimate=cost(40 * blocks * rows * width, 4 * blocks * rows * width),
        name="norm",
    )(window_index, latents, norm_gain.reshape(1, width), freq.reshape(1, quarter))


def pick_kernel(at_ref, near_b, near_c, far_d, far_e, qa, qb, oa, ob, sems):
    nq = qa.shape[1]
    no = oa.shape[1]

    def copies(second, third):
        out = []
        for s, src in ((0, second), (1, third)):
            for j, (q, o) in ((0, (qa, oa)), (1, (qb, ob))):
                out.append((src.at[j, pl.ds(0, nq)], q.at[s]))
                out.append((src.at[j, pl.ds(nq, no)], o.at[s]))
        return [pltpu.make_async_copy(x, y, sems.at[i]) for i, (x, y) in enumerate(out)]

    inner = at_ref[4] == 1

    @pl.when(inner)
    def _():
        for c in copies(near_b, near_c):
            c.start()
        for c in copies(near_b, near_c):
            c.wait()

    @pl.when(jnp.logical_not(inner))
    def _():
        for c in copies(far_d, far_e):
            c.start()
        for c in copies(far_d, far_e):
            c.wait()


def pick_far(place, b, c, d, e, nq):
    _, both, lanes = b.shape
    q = jax.ShapeDtypeStruct((2, nq, lanes), BF)
    o = jax.ShapeDtypeStruct((2, both - nq, lanes), BF)
    return pl.pallas_call(
        pick_kernel,
        out_shape=(q, q, o, o),
        in_specs=[sspec()] + [anyspec()] * 4,
        out_specs=(anyspec(),) * 4,
        scratch_shapes=[pltpu.SemaphoreType.DMA((8,))],
        compiler_params=params(),
        cost_estimate=cost(0, 8 * both * lanes * 2),
        name="pick_far",
    )(place, b, c, d, e)


def piece_copies(place, pieces, row0, rows, dst, sems):
    x, y, core = place
    lanes = dst.shape[2] // 4
    out = []
    for owner in range(2):
        c = core if owner == 0 else 1 - core
        aa, a2, bb, b2 = pieces[4 * owner : 4 * owner + 4]
        for i in range(2):
            xi = x if i == 0 else 1 - x
            yi = y if i == 0 else 1 - y
            for half, ref, px, py in (
                (0, aa, xi, y),
                (0, a2, xi, 1 - y),
                (1, bb, x, yi),
                (1, b2, 1 - x, yi),
            ):
                row = pl.multiple_of((2 * py + c) * rows, 16)
                lane = pl.multiple_of((2 * px + half) * lanes, 128)
                out.append(
                    pltpu.make_async_copy(
                        ref.at[i, :, pl.ds(row0, rows), :],
                        dst.at[:, pl.ds(row, rows), pl.ds(lane, lanes)],
                        sems.at[len(out)],
                    )
                )
    return out


def project_kernel(slots, nq, first_value, at_ref, planes_ref, n_ref, *rest):
    pieces, (out_ref, w_ref, sems) = rest[:8], rest[8:]
    copies = piece_copies((at_ref[0], at_ref[1], at_ref[2]), pieces, 0, nq, w_ref, sems)
    for c in copies:
        c.start()
    for c in copies:
        c.wait()
    plane_rows = w_ref.shape[1]
    blocks = n_ref.shape[0]
    chunk = plane_rows // 3
    heads = chunk // HEAD_DIM

    @pl.loop(0, slots * 3)
    def _(step):
        s = step // 3
        m = step % 3
        row = pl.multiple_of(m * chunk, 128)
        head0 = (planes_ref[s] * 3 + m) * heads
        w = w_ref[s, pl.ds(row, chunk), :]
        head = head0 + lax.broadcasted_iota(jnp.int32, (heads, 1, 1), 0)
        for b in range(0, blocks, 2):
            cols = jnp.concatenate([n_ref[b], n_ref[b + 1]], axis=1) if blocks > b + 1 else n_ref[b]
            got = jnp.dot(w, cols, preferred_element_type=F32)
            width = got.shape[1]
            got = got.reshape(heads, HEAD_DIM, width)
            ms = jnp.mean(got * got, axis=1, keepdims=True)
            scale = jnp.where(head < first_value, lax.rsqrt(ms + EPS), 1.0)
            out = (got * scale).astype(BF).reshape(chunk, width)
            out_ref[s, pl.ds(row, chunk), pl.ds(b * 128, width)] = out


def project(place, planes, normed, pieces, nq):
    blocks, width, rows = normed.shape
    slots = pieces[0].shape[1]
    plane_rows = 4 * nq
    return pl.pallas_call(
        functools.partial(project_kernel, slots, nq, 2 * width // HEAD_DIM),
        out_shape=jax.ShapeDtypeStruct((slots, plane_rows, blocks * rows), BF),
        in_specs=[sspec(), sspec(), vspec()] + [anyspec()] * 8,
        out_specs=vspec(),
        scratch_shapes=[
            pltpu.VMEM((slots, plane_rows, width), BF),
            pltpu.SemaphoreType.DMA((16,)),
        ],
        compiler_params=params(),
        cost_estimate=cost(
            2 * slots * plane_rows * width * blocks * rows,
            2 * (slots * plane_rows * width + 2 * blocks * rows * width),
        ),
        name="project",
    )(place, planes, normed, *pieces)


def attend_kernel(at_ref, planes_ref, lens_ref, p0, p1, p2, out_ref, t_ref, mask_ref, sems):
    plane_rows = p0.shape[1]
    copies = []
    for i, src in enumerate((p0.at[0], p1.at[0], p2.at[0], p2.at[1])):
        row = pl.multiple_of(planes_ref[i] * plane_rows, 128)
        copies.append(pltpu.make_async_copy(src, t_ref.at[pl.ds(row, plane_rows)], sems.at[i]))
    for c in copies:
        c.start()
    tokens, width = out_ref.shape
    blocks = tokens // 128
    key = lax.broadcasted_iota(jnp.int32, (128, 128), 0)
    query = lax.broadcasted_iota(jnp.int32, (128, 128), 1)
    for b in range(blocks):
        first = (key < WIN_TOK) & (query < WIN_TOK) & (key < lens_ref[2 * b])
        second = (key >= WIN_TOK) & (query >= WIN_TOK) & (key - WIN_TOK < lens_ref[2 * b + 1])
        mask_ref[b] = jnp.where(first | second, 1.0, 0.0).astype(F32)
    for c in copies:
        c.wait()
    ones = jnp.ones((16, 128), BF)

    @pl.loop(0, width // 128)
    def _(pair):
        for b in range(blocks):
            tok = pl.ds(b * 128, 128)
            done = []
            for i in range(2):
                row = pl.multiple_of(pair * 128, 128) + i * HEAD_DIM
                q = t_ref[pl.ds(row, HEAD_DIM), tok]
                k = t_ref[pl.ds(width + row, HEAD_DIM), tok]
                v = t_ref[pl.ds(2 * width + row, HEAD_DIM), tok]
                scores = lax.dot_general(k, q, (((0,), (0,)), ((), ())), preferred_element_type=F32)
                weights = (jnp.exp(scores * HEAD_DIM**-0.5) * mask_ref[b]).astype(BF)
                got = jnp.dot(jnp.concatenate([v, ones], axis=0), weights, preferred_element_type=F32)
                done.append(got[:HEAD_DIM] / got[HEAD_DIM : HEAD_DIM + 1])
            both = jnp.concatenate(done, axis=0)
            out_ref[tok, pl.ds(pl.multiple_of(pair * 128, 128), 128)] = both.T.astype(BF)


def attend(place, planes, window_len, parts, width):
    tokens = parts[0].shape[2]
    return pl.pallas_call(
        attend_kernel,
        out_shape=jax.ShapeDtypeStruct((tokens, width), BF),
        in_specs=[sspec()] * 3 + [anyspec()] * 3,
        out_specs=vspec(),
        scratch_shapes=[
            pltpu.VMEM((3 * width, tokens), BF),
            pltpu.VMEM((tokens // 128, 128, 128), F32),
            pltpu.SemaphoreType.DMA((4,)),
        ],
        compiler_params=params(),
        cost_estimate=cost(40 * 128 * tokens * width, 8 * tokens * width),
        name="attend",
    )(place, planes, window_len, *parts)


def output_kernel(row0, no, fresh, at_ref, planes_ref, lens_ref, live_ref, att_ref, lat_ref, *rest):
    pieces, rest = rest[:8], rest[8:]
    if not fresh:
        rest = rest[1:]
    out_ref, w_ref, base_ref, done_ref, sems, base_sems, out_sems = rest
    slots = w_ref.shape[0]
    cols = w_ref.shape[1]
    tokens = att_ref.shape[0]
    copies = piece_copies((at_ref[0], at_ref[1], at_ref[2]), pieces, row0, no, w_ref, sems)
    for c in copies:
        c.start()
    spots = [pl.ds(pl.multiple_of(planes_ref[s] * cols, 128), cols) for s in range(slots)]
    bases = [
        pltpu.make_async_copy(lat_ref.at[:, spots[s]], base_ref.at[s], base_sems.at[s])
        for s in range(slots)
    ]
    outs = [
        pltpu.make_async_copy(done_ref.at[s], out_ref.at[:, spots[s]], out_sems.at[s])
        for s in range(slots)
    ]
    for c in bases:
        c.start()
    for c in copies:
        c.wait()
    for c in bases:
        c.wait()
    for s in range(slots):

        @pl.loop(0, tokens // 128)
        def _(b):
            tok = pl.ds(pl.multiple_of(b * 128, 128), 128)
            update = lax.dot_general(
                att_ref[tok, :], w_ref[s], (((1,), (1,)), ((), ())), preferred_element_type=F32
            )
            base = base_ref[s, tok, :].astype(F32)
            row = lax.broadcasted_iota(jnp.int32, (128, 1), 0)
            alive = b < live_ref[0]
            first = jnp.where(alive, lens_ref[2 * b], 0)
            second = jnp.where(alive, lens_ref[2 * b + 1], 0) + WIN_TOK
            keep = (row < first) | ((row >= WIN_TOK) & (row < second))
            done_ref[s, tok, :] = jnp.where(keep, base + update, base).astype(BF)

        outs[s].start()
    for c in outs:
        c.wait()


def output(place, planes, lens, live, attended, latents, pieces, row0, no, before):
    tokens, width = attended.shape
    slots = pieces[0].shape[1]
    cols = 4 * no
    fresh = before is None
    return pl.pallas_call(
        functools.partial(output_kernel, row0, no, fresh),
        out_shape=jax.ShapeDtypeStruct((tokens, width), BF),
        in_specs=[sspec()] * 4 + [vspec()] + [anyspec()] * (9 if fresh else 10),
        out_specs=anyspec(),
        scratch_shapes=[
            pltpu.VMEM((slots, cols, width), BF),
            pltpu.VMEM((slots, tokens, cols), BF),
            pltpu.VMEM((slots, tokens, cols), BF),
            pltpu.SemaphoreType.DMA((16,)),
            pltpu.SemaphoreType.DMA((slots,)),
            pltpu.SemaphoreType.DMA((slots,)),
        ],
        input_output_aliases={} if fresh else {14: 0},
        compiler_params=params(),
        cost_estimate=cost(2 * slots * cols * width * tokens, 4 * slots * cols * (width + tokens)),
        name="output",
    )(place, planes, lens, live, attended, latents, *pieces, *(() if fresh else (before,)))


def neighbours(tile_count):
    inner_low, inner_high = range(4, 8), range(8, 12)
    return {
        "z": [(i, i ^ 4) for i in range(tile_count)],
        "mid": [(i, i + 4) for i in inner_low] + [(i, i - 4) for i in inner_high],
        "ends": [(i, i - 4) for i in inner_low] + [(i, i + 4) for i in inner_high],
        "y": [(i, i ^ 2) for i in range(tile_count)],
        "core": [(i, i ^ 1) for i in range(tile_count)],
    }


def spread(a, b, send):
    a1 = send["x"](a)
    b1 = send["y"](b)
    aa = jnp.stack([a, a1])
    bb = jnp.stack([b, b1])
    a2 = send["y"](aa)
    b2 = send["x"](bb)
    mine = [aa, a2, bb, b2]
    return mine + [send["core"](m) for m in mine]


def local(tile_count, latents, window_index, window_len, live_blocks, norm_gain, w_qkv, w_out):
    blocks, rows, width = latents.shape
    nq, no = w_qkv.shape[1], w_out.shape[1]
    send = {
        name: functools.partial(lax.ppermute, axis_name="tile", perm=pairs)
        for name, pairs in neighbours(tile_count).items()
    }
    send["x"] = functools.partial(lax.ppermute, axis_name="group", perm=[(0, 1), (1, 0)])
    t = lax.axis_index("tile")
    x = lax.axis_index("group")
    z = t // 4
    inner = ((z == 1) | (z == 2)).astype(jnp.int32)
    place = jnp.stack([x, t // 2 % 2, t % 2, z, inner]).astype(jnp.int32)
    second = jnp.where(inner == 1, 3 - z, z ^ 2)
    planes = jnp.stack([z, z ^ 1, second, second ^ 1]).astype(jnp.int32)

    unit, a, b = pack(w_qkv, w_out)
    swapped = send["z"](unit)
    near_b = send["mid"](unit)
    g0 = spread(a[None], b[None], send)
    normed = normed_columns(latents, window_index, norm_gain)
    near_c = send["mid"](swapped)
    far_d = send["ends"](near_b)
    g1 = spread(swapped[0][None], swapped[1][None], send)
    p0 = project(place, planes[0:1], normed, g0, nq)
    far_e = send["ends"](near_c)
    qa, qb, oa, ob = pick_far(place, near_b, near_c, far_d, far_e, nq)
    g2 = spread(qa, qb, send)
    p1 = project(place, planes[1:2], normed, g1, nq)
    go = spread(oa, ob, send)
    p2 = project(place, planes[2:4], normed, g2, nq)
    attended = attend(place, planes, window_len, (p0, p1, p2), width)
    flat = latents.reshape(blocks * rows, width)
    args = (window_len, live_blocks, attended, flat)
    out = output(place, planes[0:1], *args, g0, nq, no, None)
    out = output(place, planes[1:2], *args, g1, nq, no, out)
    out = output(place, planes[2:4], *args, go, 0, no, out)
    return out.reshape(latents.shape)


def solution(mesh):
    in_specs = (
        P(("tile", "group"), None, None),
        P(("tile", "group")),
        P(("tile", "group")),
        P(("tile", "group")),
        P(),
        P("group", "tile"),
        P("group", "tile"),
    )
    out_specs = P(("tile", "group"), None, None)
    planes, chips, cores = 4, 2, 2
    if mesh.shape["group"] == 2 and mesh.shape["tile"] == planes * chips * cores:
        body = functools.partial(local, mesh.shape["tile"])
    else:
        body = general
    return jax.shard_map(body, mesh=mesh, in_specs=in_specs, out_specs=out_specs, check_vma=False)
```

time: 229 us -> 246 us (1.074)
  Pallas kernels: 0 us -> 123 us
  matrix products: 57.5 us -> 0 us
  starting transfers between devices: 0.04 us -> 28.7 us
  blocking collectives: 22.1 us -> 0 us
  local copies, waits for them, and re-layouts: 26.7 us -> 8.32 us
  other arithmetic: 21.6 us -> 5.29 us
  between operations: 14.2 us -> 1.16 us
  waiting for transfers between devices: 86 us -> 78.3 us
    pallas_call x0 -> x10, Pallas kernels: none -> 123 us  [the longest x1 37.6 us: pick_far(): pl.pallas_call(pick_kernel, out_shape=(q, q, o, o), in_specs=[sspec()] +...]
    all_gather x2 -> x0, waiting for transfers between devices: 86 us -> none  [the longest x1 86 us: project_qkv(): lax.all_gather(full_rows, 'tile', axis=1, tiled=True)]
    ppermute x0 -> x37, waiting for transfers between devices: none -> 78.3 us  [the longest x4 37.1 us: spread(): a1 = send['x'](a)]
    dot_general x4 -> x0, matrix products: 57.5 us -> none  [the longest x1 25.9 us: project_qkv(): jnp.dot(normed, lax.all_gather(full_rows, 'tile', axis=1, tiled=True), pr...]
    ppermute x0 -> x37, starting transfers between devices: none -> 28.7 us  [the longest x4 5.52 us: spread(): b1 = send['y'](b)]
    all_gather x2 -> x0, blocking collectives: 22.1 us -> none  [the longest x1 16 us: project_qkv(): full_rows = lax.all_gather(w_qkv, 'group', axis=0, tiled=True)]
    sin x1 -> x0, other arithmetic: 9.64 us -> none  [position_table(): jnp.sin(row_angle)]
    convert_element_type x1 -> x0, local copies, waits for them, and re-layouts: 6.92 us -> none  [window_layer(): attended = attended.astype(jnp.bfloat16).reshape(window_count * WIN_TOK, D)]
  transfers between devices with their start and end apart: 2 -> 37, of which waited for: 1 -> 10; matrix products, arithmetic and copies ran while one was open for 38% -> 3% of each run, Pallas kernels for 0% -> 45%
where the time goes in v1:
time: 246 us; the launch traced here: 245 us
  Pallas kernels  123 us (50%)
  waiting for transfers between devices  78.3 us (32%)
  starting transfers between devices  28.7 us (12%)
  local copies, waits for them, and re-layouts  8.32 us (3%)
  other arithmetic  5.29 us (2%)
    pallas_call x1, Pallas kernels, pick_far(): pl.pallas_call(pick_kernel, out_shape=(q, q, o, o), in_specs=[sspec()] +...  37.6 us
    ppermute x4, waiting for transfers between devices, spread(): a1 = send['x'](a)  37.1 us
    pallas_call x3, Pallas kernels, project(): pl.pallas_call(functools.partial(project_kernel, slots, nq, 2 * width //...  30.4 us
    pallas_call x3, Pallas kernels, output(): pl.pallas_call(functools.partial(output_kernel, row0, no, fresh), out_sha...  25.5 us
    pallas_call x1, Pallas kernels, attend(): pl.pallas_call(attend_kernel, out_shape=jax.ShapeDtypeStruct((tokens, wid...  21.5 us
    ppermute x1, waiting for transfers between devices, local(): swapped = send['z'](unit)  12.8 us
    ppermute x4, waiting for transfers between devices, spread(): b1 = send['y'](b)  10.7 us
    ppermute x1, waiting for transfers between devices, local(): far_e = send['ends'](near_c)  10.6 us
  transfers between devices with their start and end apart: 37, of which 10 were waited for; matrix products, arithmetic and copies ran while one was open for 3% of the time, Pallas kernels for 45%

profile of v1, /device:TPU:0, one launch (start us, length us, event | category | flops | bytes accessed | tf_op | source)
XLA Modules:
  0.0 245.0 jit_solution(6072114893185183169)
XLA Ops:
  0.0 2.1 copy.10.wq_ref
  2.1 1.7 copy.11.wo_ref
  3.8 2.4 pack_weights.1
  6.2 3.0 %collective-permute-start.8 = (bf16[2,384,384]{2,1,0:T(8,128)(2,1)}, bf16[2,384,384]{2,1,0:T(8,128)(2,1)S(1)}, u32[]{:S(2)}, u32[]{:S(2)}) collective-permute-start(bf16[2,384,384]{2,1,0:T(8,128)(2,1)} %get-tuple-element.14), channel_id=1, source_target_pairs={{0,8},{2,10},{4,12},{6,14},{8,0},{10,2},{12,4},{14,6},{16,24},{18,... | collective-permute-start | bytes 1769480 | tf_op jit(solution)/shard_map/ppermute | solution.py:469
  9.9 12.8 %collective-permute-done.8 = bf16[2,384,384]{2,1,0:T(8,128)(2,1)S(1)} collective-permute-done((bf16[2,384,384]{2,1,0:T(8,128)(2,1)}, bf16[2,384,384]{2,1,0:T(8,128)(2,1)S(1)}, u32[]{:S(2)}, u32[]{:S(2)}) %collective-permute-start.8) | collective-permute-done | bytes 589856 | tf_op jit(solution)/shard_map/ppermute | solution.py:469
  23.4 1.7 collective-permute-start
  25.2 1.3 collective-permute-start.19
  26.5 1.6 collective-permute-start.2
  28.2 1.3 collective-permute-start.20
  30.1 3.2 %collective-permute-done = bf16[1,384,384]{2,1,0:T(8,128)(2,1)S(1)} collective-permute-done((bf16[1,384,384]{2,1,0:T(8,128)(2,1)}, bf16[1,384,384]{2,1,0:T(8,128)(2,1)S(1)}, u32[]{:S(2)}, u32[]{:S(2)}) %collective-permute-start) | collective-permute-done | bytes 294944 | tf_op jit(solution)/shard_map/ppermute | solution.py:442
  33.2 2.1 collective-permute-start.11
  36.4 1.3 collective-permute-start.1
  38.2 1.3 collective-permute-start.3
  39.6 3.7 %collective-permute-done.11 = bf16[1,384,384]{2,1,0:T(8,128)(2,1)S(1)} collective-permute-done((bf16[1,384,384]{2,1,0:T(8,128)(2,1)S(1)}, bf16[1,384,384]{2,1,0:T(8,128)(2,1)S(1)}, u32[]{:S(2)}, u32[]{:S(2)}) %collective-permute-start.11) | collective-permute-done | bytes 294944 | tf_op jit(solution)/shard_map/ppermute | solution.py:443
  43.3 1.3 collective-permute-done.19.far_d
  44.7 10.6 %collective-permute-done.20.far_e = bf16[2,384,384]{2,1,0:T(8,128)(2,1)S(1)} collective-permute-done((bf16[2,384,384]{2,1,0:T(8,128)(2,1)S(1)}, bf16[2,384,384]{2,1,0:T(8,128)(2,1)S(1)}, u32[]{:S(2)}, u32[]{:S(2)}) %collective-permute-start.20) | collective-permute-done | bytes 589856 | tf_op jit(solution)/shard_map/ppermute | solution.py:477
  55.3 1.5 collective-permute-start.10
  57.5 37.6 %pick_far.1 = (bf16[2,288,384]{2,1,0:T(8,128)(2,1)}, bf16[2,288,384]{2,1,0:T(8,128)(2,1)}, bf16[2,96,384]{2,1,0:T(8,128)(2,1)}, bf16[2,96,384]{2,1,0:T(8,128)(2,1)}) custom-call(s32[5]{0:T(128)} %stack.98.at_ref, bf16[2,384,384]{2,1,0:T(8,128)(2,1)} %copy-done.9, bf16[2,384,384]{2,1,0:T(8,128)(2,1)} %copy-done.10, bf16[2,384,384]{2,1,0:T(8,128)(2,1)} %copy-done.11, ...), custom_call_target="tpu_custom_call" | custom-call | bytes 2359296 | tf_op jit(solution)/shard_map/pick_far/pallas_call | solution.py:209
  96.7 1.6 collective-permute-start.21
  98.5 7.0 %collective-permute-done.23 = bf16[2,288,384]{2,1,0:T(8,128)(2,1)S(1)} collective-permute-done((bf16[2,288,384]{2,1,0:T(8,128)(2,1)}, bf16[2,288,384]{2,1,0:T(8,128)(2,1)S(1)}, u32[]{:S(2)}, u32[]{:S(2)}) %collective-permute-start.23) | collective-permute-done | bytes 442400 | tf_op jit(solution)/shard_map/ppermute | solution.py:443
  106.6 12.3 %collective-permute-done.21 = bf16[2,288,384]{2,1,0:T(8,128)(2,1)S(1)} collective-permute-done((bf16[2,288,384]{2,1,0:T(8,128)(2,1)}, bf16[2,288,384]{2,1,0:T(8,128)(2,1)S(1)}, u32[]{:S(2)}, u32[]{:S(2)}) %collective-permute-start.21) | collective-permute-done | bytes 442400 | tf_op jit(solution)/shard_map/ppermute | solution.py:442
  121.7 1.3 collective-permute-start.29
  123.0 21.2 %collective-permute-done.29 = bf16[2,96,384]{2,1,0:T(8,128)(2,1)S(1)} collective-permute-done((bf16[2,96,384]{2,1,0:T(8,128)(2,1)S(1)}, bf16[2,96,384]{2,1,0:T(8,128)(2,1)S(1)}, u32[]{:S(2)}, u32[]{:S(2)}) %collective-permute-start.29) | collective-permute-done | bytes 147488 | tf_op jit(solution)/shard_map/ppermute | solution.py:442
  147.1 5.9 %norm.1.n_ref = bf16[6,1536,128]{2,1,0:T(8,128)(2,1)} custom-call(s32[12]{0:T(128)} %ids_ref.1, bf16[6,128,1536]{2,1,0:T(8,128)(2,1)} %lat_ref.1, f32[1,1536]{1,0:T(1,128)} %reshape.20.gain_ref, f32[1,384]{1,0:T(1,128)} %multiply_exponential_fusion.freq_ref), custom_call_target="tpu_custom_call" | custom-call | flops 47185920 | bytes 4718592 | tf_op jit(solution)/shard_map/norm/pallas_call | solution.py:164
  157.5 5.7 %collective-permute-done.30.rest_1_ = bf16[2,2,96,384]{3,2,1,0:T(8,128)(2,1)S(1)} collective-permute-done((bf16[2,2,96,384]{3,2,1,0:T(8,128)(2,1)S(1)}, bf16[2,2,96,384]{3,2,1,0:T(8,128)(2,1)S(1)}, u32[]{:S(2)}, u32[]{:S(2)}) %collective-permute-start.30) | collective-permute-done | bytes 294944 | tf_op jit(solution)/shard_map/ppermute | solution.py:446
  163.9 8.5 %project.3.p0 = bf16[1,1152,768]{2,1,0:T(8,128)(2,1)} custom-call(s32[5]{0:T(128)} %stack.98.at_ref, s32[1]{0:T(128)} %bitcast.3.planes_ref, bf16[6,1536,128]{2,1,0:T(8,128)(2,1)} %norm.1.n_ref, bf16[2,1,384,384]{3,2,1,0:T(8,128)(2,1)} %copy-done, bf16[2,1,384,384]{3,2,1,0:T(8,128)(2,1)} %collective-permute-done.1.rest_1_, ...), custom_call_target="tpu_custom_call" | custom-call | flops 2717908992 | bytes 8257536 | tf_op jit(solution)/shard_map/project/pallas_call | solution.py:284
  172.4 8.5 %project.4.p1 = bf16[1,1152,768]{2,1,0:T(8,128)(2,1)} custom-call(s32[5]{0:T(128)} %stack.98.at_ref, s32[1]{0:T(128)} %bitcast.7.planes_ref, bf16[6,1536,128]{2,1,0:T(8,128)(2,1)} %norm.1.n_ref, bf16[2,1,384,384]{3,2,1,0:T(8,128)(2,1)} %copy-done.2, bf16[2,1,384,384]{3,2,1,0:T(8,128)(2,1)} %collective-permute-done.10.rest_1_, ...), custom_call_target="tpu_custom_call" | custom-call | flops 2717908992 | bytes 8257536 | tf_op jit(solution)/shard_map/project/pallas_call | solution.py:284
  182.9 13.4 %project.5.p2 = bf16[2,1152,768]{2,1,0:T(8,128)(2,1)} custom-call(s32[5]{0:T(128)} %stack.98.at_ref, s32[2]{0:T(128)} %pad_add_fusion.planes_ref, bf16[6,1536,128]{2,1,0:T(8,128)(2,1)} %norm.1.n_ref, bf16[2,2,288,384]{3,2,1,0:T(8,128)(2,1)} %copy-done.7, bf16[2,2,288,384]{3,2,1,0:T(8,128)(2,1)} %collective-permute-done.22.rest_1_, ...), custom_call_target="tpu_custom_call" | custom-call | flops 5435817984 | bytes 11796480 | tf_op jit(solution)/shard_map/project/pallas_call | solution.py:284
  196.3 21.5 %attend.1.att_ref = bf16[768,1536]{1,0:T(8,128)(2,1)} custom-call(s32[5]{0:T(128)} %stack.98.at_ref, s32[4]{0:T(128)} %pad_add_fusion.1.planes_ref, s32[12]{0:T(128)} %lens_ref.7, bf16[1,1152,768]{2,1,0:T(8,128)(2,1)} %project.3.p0, bf16[1,1152,768]{2,1,0:T(8,128)(2,1)} %project.4.p1, bf16[2,1152,768]{2,1,0:T(8,128)(2,1)} %project.5.p2), custom_call_target="tpu_custom_call" | custom-call | flops 6039797760 | bytes 9437184 | tf_op jit(solution)/shard_map/attend/pallas_call | solution.py:342
  217.8 7.3 %output.3.rest_8_ = bf16[768,1536]{1,0:T(8,128)(2,1)} custom-call(s32[5]{0:T(128)} %stack.98.at_ref, s32[1]{0:T(128)} %bitcast.3.planes_ref, s32[12]{0:T(128)} %lens_ref.7, s32[1]{0:T(128)S(6)} %copy.14.live_ref, bf16[768,1536]{1,0:T(8,128)(2,1)} %attend.1.att_ref, bf16[768,1536]{1,0:T(8,128)(2,1)} %bitcast.30, bf16[2,1,384,384]{3,2,1,0:T(8,128)(2,1)} %copy-done, ...), custom_call_target="tpu_custom_call" | custom-call | flops 905969664 | bytes 3538944 | tf_op jit(solution)/shard_map/output/pallas_call | solution.py:410
  225.1 7.3 %output.4.rest_8_ = bf16[768,1536]{1,0:T(8,128)(2,1)} custom-call(s32[5]{0:T(128)} %stack.98.at_ref, s32[1]{0:T(128)} %bitcast.7.planes_ref, s32[12]{0:T(128)} %lens_ref.7, s32[1]{0:T(128)S(6)} %copy.14.live_ref, bf16[768,1536]{1,0:T(8,128)(2,1)} %attend.1.att_ref, bf16[768,1536]{1,0:T(8,128)(2,1)} %bitcast.31, ...), custom_call_target="tpu_custom_call", output_to_operand_aliasing={{}: (14, {})} | custom-call | flops 905969664 | bytes 3538944 | tf_op jit(solution)/shard_map/output/pallas_call | solution.py:410
  234.1 10.9 %output.5 = bf16[768,1536]{1,0:T(8,128)(2,1)} custom-call(s32[5]{0:T(128)} %stack.98.at_ref, s32[2]{0:T(128)} %pad_add_fusion.planes_ref, s32[12]{0:T(128)} %lens_ref.7, s32[1]{0:T(128)S(6)} %copy.14.live_ref, bf16[768,1536]{1,0:T(8,128)(2,1)} %attend.1.att_ref, bf16[768,1536]{1,0:T(8,128)(2,1)} %bitcast.32, ...), custom_call_target="tpu_custom_call", output_to_operand_aliasing={{}: (14, {})} | custom-call | flops 1811939328 | bytes 7077888 | tf_op jit(solution)/shard_map/output/pallas_call | solution.py:410
  (128 shorter events, 21.0 us)
Async XLA Ops:
  6.2 16.6 %collective-permute-start.8 = (bf16[2,384,384]{2,1,0:T(8,128)(2,1)}, bf16[2,384,384]{2,1,0:T(8,128)(2,1)S(1)}, u32[]{:S(2)}, u32[]{:S(2)}) collective-permute-start(bf16[2,384,384]{2,1,0:T(8,128)(2,1)} %get-tuple-element.14), channel_id=1, source_target_pairs={{0,8},{2,10},{4,12},{6,14},{8,0},{10,2},{12,4},{14,6},{16,24},{18,... | collective-permute-start | bytes 1769480 | tf_op jit(solution)/shard_map/ppermute | solution.py:469
  9.2 16.0 %collective-permute-start.17 = (bf16[2,384,384]{2,1,0:T(8,128)(2,1)}, bf16[2,384,384]{2,1,0:T(8,128)(2,1)S(1)}, u32[]{:S(2)}, u32[]{:S(2)}) collective-permute-start(bf16[2,384,384]{2,1,0:T(8,128)(2,1)} %get-tuple-element.14), channel_id=1, source_target_pairs={{8,16},{10,18},{12,20},{14,22},{16,8},{18,10},{20,12},{22,14},{9,1... | collective-permute-start | bytes 1769480 | tf_op jit(solution)/shard_map/ppermute | solution.py:470
  23.4 9.8 %collective-permute-start = (bf16[1,384,384]{2,1,0:T(8,128)(2,1)}, bf16[1,384,384]{2,1,0:T(8,128)(2,1)S(1)}, u32[]{:S(2)}, u32[]{:S(2)}) collective-permute-start(bf16[1,384,384]{2,1,0:T(8,128)(2,1)} %bitcast.40), channel_id=1, source_target_pairs={{0,1},{1,0},{2,3},{3,2},{4,5},{5,4},{6,7},{7,6},{8,9},{9,8},{10,11... | collective-permute-start | bytes 884744 | tf_op jit(solution)/shard_map/ppermute | solution.py:442
  25.2 19.4 %collective-permute-start.19 = (bf16[2,384,384]{2,1,0:T(8,128)(2,1)S(1)}, bf16[2,384,384]{2,1,0:T(8,128)(2,1)S(1)}, u32[]{:S(2)}, u32[]{:S(2)}) collective-permute-start(bf16[2,384,384]{2,1,0:T(8,128)(2,1)S(1)} %collective-permute-done.17.near_b), channel_id=1, source_target_pairs={{8,0},{10,2},{12,4},{14,6},{16,24},{18,26},{20,28},{22,30},{9,1},{... | collective-permute-start | bytes 1769480 | tf_op jit(solution)/shard_map/ppermute | solution.py:474
  26.5 9.9 %collective-permute-start.2 = (bf16[1,384,384]{2,1,0:T(8,128)(2,1)}, bf16[1,384,384]{2,1,0:T(8,128)(2,1)S(1)}, u32[]{:S(2)}, u32[]{:S(2)}) collective-permute-start(bf16[1,384,384]{2,1,0:T(8,128)(2,1)} %bitcast.38), channel_id=1, source_target_pairs={{0,4},{2,6},{4,0},{6,2},{8,12},{10,14},{12,8},{14,10},{16,20},{18,... | collective-permute-start | bytes 884744 | tf_op jit(solution)/shard_map/ppermute | solution.py:443
  28.2 27.2 %collective-permute-start.20 = (bf16[2,384,384]{2,1,0:T(8,128)(2,1)S(1)}, bf16[2,384,384]{2,1,0:T(8,128)(2,1)S(1)}, u32[]{:S(2)}, u32[]{:S(2)}) collective-permute-start(bf16[2,384,384]{2,1,0:T(8,128)(2,1)S(1)} %collective-permute-done.18.near_c), channel_id=1, source_target_pairs={{8,0},{10,2},{12,4},{14,6},{16,24},{18,26},{20,28},{22,30},{9,1},{... | collective-permute-start | bytes 1769480 | tf_op jit(solution)/shard_map/ppermute | solution.py:477
  33.2 10.0 %collective-permute-start.11 = (bf16[1,384,384]{2,1,0:T(8,128)(2,1)S(1)}, bf16[1,384,384]{2,1,0:T(8,128)(2,1)S(1)}, u32[]{:S(2)}, u32[]{:S(2)}) collective-permute-start(bf16[1,384,384]{2,1,0:T(8,128)(2,1)S(1)} %get-tuple-element.21), channel_id=1, source_target_pairs={{0,4},{2,6},{4,0},{6,2},{8,12},{10,14},{12,8},{14,10},{16,20},{18,... | collective-permute-start | bytes 884744 | tf_op jit(solution)/shard_map/ppermute | solution.py:443
  36.4 58.7 %collective-permute-start.1 = (bf16[2,1,384,384]{3,2,1,0:T(8,128)(2,1)S(1)}, bf16[2,1,384,384]{3,2,1,0:T(8,128)(2,1)}, u32[]{:S(2)}, u32[]{:S(2)}) collective-permute-start(bf16[2,1,384,384]{3,2,1,0:T(8,128)(2,1)S(1)} %pad_maximum_fusion.2.rest_0_), channel_id=1, source_target_pairs={{0,4},{2,6},{4,0},{6,2},{8,12},{10,14},{12,8},{14,10},{16,20},{18,... | collective-permute-start | bytes 1769480 | tf_op jit(solution)/shard_map/ppermute | solution.py:446
  38.2 57.9 %collective-permute-start.3 = (bf16[2,1,384,384]{3,2,1,0:T(8,128)(2,1)S(1)}, bf16[2,1,384,384]{3,2,1,0:T(8,128)(2,1)}, u32[]{:S(2)}, u32[]{:S(2)}) collective-permute-start(bf16[2,1,384,384]{3,2,1,0:T(8,128)(2,1)S(1)} %pad_maximum_fusion.3.rest_2_), channel_id=1, source_target_pairs={{0,1},{1,0},{2,3},{3,2},{4,5},{5,4},{6,7},{7,6},{8,9},{9,8},{10,11... | collective-permute-start | bytes 1769480 | tf_op jit(solution)/shard_map/ppermute | solution.py:447
  43.3 53.5 %collective-permute-start.4 = (bf16[2,1,384,384]{3,2,1,0:T(8,128)(2,1)S(1)}, bf16[2,1,384,384]{3,2,1,0:T(8,128)(2,1)S(1)}, u32[]{:S(2)}, u32[]{:S(2)}) collective-permute-start(bf16[2,1,384,384]{3,2,1,0:T(8,128)(2,1)S(1)} %pad_maximum_fusion.2.rest_0_), channel_id=1, source_target_pairs={{0,2},{2,0},{4,6},{6,4},{8,10},{10,8},{12,14},{14,12},{16,18},{18,... | collective-permute-start | bytes 1769480 | tf_op jit(solution)/shard_map/ppermute | solution.py:449
  44.6 52.1 %collective-permute-start.6 = (bf16[2,1,384,384]{3,2,1,0:T(8,128)(2,1)S(1)}, bf16[2,1,384,384]{3,2,1,0:T(8,128)(2,1)}, u32[]{:S(2)}, u32[]{:S(2)}) collective-permute-start(bf16[2,1,384,384]{3,2,1,0:T(8,128)(2,1)S(1)} %pad_maximum_fusion.3.rest_2_), channel_id=1, source_target_pairs={{0,2},{2,0},{4,6},{6,4},{8,10},{10,8},{12,14},{14,12},{16,18},{18,... | collective-permute-start | bytes 1769480 | tf_op jit(solution)/shard_map/ppermute | solution.py:449
  55.3 43.0 %collective-permute-start.10 = (bf16[2,1,384,384]{3,2,1,0:T(8,128)(2,1)S(1)}, bf16[2,1,384,384]{3,2,1,0:T(8,128)(2,1)}, u32[]{:S(2)}, u32[]{:S(2)}) collective-permute-start(bf16[2,1,384,384]{3,2,1,0:T(8,128)(2,1)S(1)} %pad_maximum_fusion.4.rest_0_), channel_id=1, source_target_pairs={{0,4},{2,6},{4,0},{6,2},{8,12},{10,14},{12,8},{14,10},{16,20},{18,... | collective-permute-start | bytes 1769480 | tf_op jit(solution)/shard_map/ppermute | solution.py:446
  95.2 10.3 %collective-permute-start.23 = (bf16[2,288,384]{2,1,0:T(8,128)(2,1)}, bf16[2,288,384]{2,1,0:T(8,128)(2,1)S(1)}, u32[]{:S(2)}, u32[]{:S(2)}) collective-permute-start(bf16[2,288,384]{2,1,0:T(8,128)(2,1)} %get-tuple-element.16), channel_id=1, source_target_pairs={{0,4},{2,6},{4,0},{6,2},{8,12},{10,14},{12,8},{14,10},{16,20},{18,... | collective-permute-start | bytes 1327112 | tf_op jit(solution)/shard_map/ppermute | solution.py:443
  96.1 22.8 %collective-permute-start.12 = (bf16[2,1,384,384]{3,2,1,0:T(8,128)(2,1)S(1)}, bf16[2,1,384,384]{3,2,1,0:T(8,128)(2,1)}, u32[]{:S(2)}, u32[]{:S(2)}) collective-permute-start(bf16[2,1,384,384]{3,2,1,0:T(8,128)(2,1)S(1)} %pad_maximum_fusion.5.rest_2_), channel_id=1, source_target_pairs={{0,1},{1,0},{2,3},{3,2},{4,5},{5,4},{6,7},{7,6},{8,9},{9,8},{10,11... | collective-permute-start | bytes 1769480 | tf_op jit(solution)/shard_map/ppermute | solution.py:447
  96.7 23.0 %collective-permute-start.13 = (bf16[2,1,384,384]{3,2,1,0:T(8,128)(2,1)S(1)}, bf16[2,1,384,384]{3,2,1,0:T(8,128)(2,1)S(1)}, u32[]{:S(2)}, u32[]{:S(2)}) collective-permute-start(bf16[2,1,384,384]{3,2,1,0:T(8,128)(2,1)S(1)} %pad_maximum_fusion.4.rest_0_), channel_id=1, source_target_pairs={{0,2},{2,0},{4,6},{6,4},{8,10},{10,8},{12,14},{14,12},{16,18},{18,... | collective-permute-start | bytes 1769480 | tf_op jit(solution)/shard_map/ppermute | solution.py:449
  96.7 22.1 %collective-permute-start.21 = (bf16[2,288,384]{2,1,0:T(8,128)(2,1)}, bf16[2,288,384]{2,1,0:T(8,128)(2,1)S(1)}, u32[]{:S(2)}, u32[]{:S(2)}) collective-permute-start(bf16[2,288,384]{2,1,0:T(8,128)(2,1)} %get-tuple-element.15), channel_id=1, source_target_pairs={{0,1},{1,0},{2,3},{3,2},{4,5},{5,4},{6,7},{7,6},{8,9},{9,8},{10,11... | collective-permute-start | bytes 1327112 | tf_op jit(solution)/shard_map/ppermute | solution.py:442
  98.3 22.4 %collective-permute-start.15 = (bf16[2,1,384,384]{3,2,1,0:T(8,128)(2,1)S(1)}, bf16[2,1,384,384]{3,2,1,0:T(8,128)(2,1)S(1)}, u32[]{:S(2)}, u32[]{:S(2)}) collective-permute-start(bf16[2,1,384,384]{3,2,1,0:T(8,128)(2,1)S(1)} %pad_maximum_fusion.5.rest_2_), channel_id=1, source_target_pairs={{0,2},{2,0},{4,6},{6,4},{8,10},{10,8},{12,14},{14,12},{16,18},{18,... | collective-permute-start | bytes 1769480 | tf_op jit(solution)/shard_map/ppermute | solution.py:449
  105.4 16.2 %collective-permute-start.5 = (bf16[2,1,384,384]{3,2,1,0:T(8,128)(2,1)}, bf16[2,1,384,384]{3,2,1,0:T(8,128)(2,1)}, u32[]{:S(2)}, u32[]{:S(2)}) collective-permute-start(bf16[2,1,384,384]{3,2,1,0:T(8,128)(2,1)} %collective-permute-done.1.rest_1_), channel_id=1, source_target_pairs={{0,2},{2,0},{4,6},{6,4},{8,10},{10,8},{12,14},{14,12},{16,18},{18,... | collective-permute-start | bytes 1769480 | tf_op jit(solution)/shard_map/ppermute | solution.py:449
  119.0 34.6 %collective-permute-start.24 = (bf16[2,2,288,384]{3,2,1,0:T(8,128)(2,1)S(1)}, bf16[2,2,288,384]{3,2,1,0:T(8,128)(2,1)}, u32[]{:S(2)}, u32[]{:S(2)}) collective-permute-start(bf16[2,2,288,384]{3,2,1,0:T(8,128)(2,1)S(1)} %pad_maximum_fusion.1.rest_2_), channel_id=1, source_target_pairs={{0,1},{1,0},{2,3},{3,2},{4,5},{5,4},{6,7},{7,6},{8,9},{9,8},{10,11... | collective-permute-start | bytes 2654216 | tf_op jit(solution)/shard_map/ppermute | solution.py:447
  119.8 33.9 %collective-permute-start.22 = (bf16[2,2,288,384]{3,2,1,0:T(8,128)(2,1)S(1)}, bf16[2,2,288,384]{3,2,1,0:T(8,128)(2,1)}, u32[]{:S(2)}, u32[]{:S(2)}) collective-permute-start(bf16[2,2,288,384]{3,2,1,0:T(8,128)(2,1)S(1)} %pad_maximum_fusion.rest_0_), channel_id=1, source_target_pairs={{0,4},{2,6},{4,0},{6,2},{8,12},{10,14},{12,8},{14,10},{16,20},{18,... | collective-permute-start | bytes 2654216 | tf_op jit(solution)/shard_map/ppermute | solution.py:446
  120.7 32.3 %collective-permute-start.14 = (bf16[2,1,384,384]{3,2,1,0:T(8,128)(2,1)}, bf16[2,1,384,384]{3,2,1,0:T(8,128)(2,1)S(1)}, u32[]{:S(2)}, u32[]{:S(2)}) collective-permute-start(bf16[2,1,384,384]{3,2,1,0:T(8,128)(2,1)} %collective-permute-done.10.rest_1_), channel_id=1, source_target_pairs={{0,2},{2,0},{4,6},{6,4},{8,10},{10,8},{12,14},{14,12},{16,18},{18,... | collective-permute-start | bytes 1769480 | tf_op jit(solution)/shard_map/ppermute | solution.py:449
  121.6 32.5 %collective-permute-start.16 = (bf16[2,1,384,384]{3,2,1,0:T(8,128)(2,1)}, bf16[2,1,384,384]{3,2,1,0:T(8,128)(2,1)}, u32[]{:S(2)}, u32[]{:S(2)}) collective-permute-start(bf16[2,1,384,384]{3,2,1,0:T(8,128)(2,1)} %collective-permute-done.12.rest_3_), channel_id=1, source_target_pairs={{0,2},{2,0},{4,6},{6,4},{8,10},{10,8},{12,14},{14,12},{16,18},{18,... | collective-permute-start | bytes 1769480 | tf_op jit(solution)/shard_map/ppermute | solution.py:449
  121.7 22.5 %collective-permute-start.29 = (bf16[2,96,384]{2,1,0:T(8,128)(2,1)S(1)}, bf16[2,96,384]{2,1,0:T(8,128)(2,1)S(1)}, u32[]{:S(2)}, u32[]{:S(2)}) collective-permute-start(bf16[2,96,384]{2,1,0:T(8,128)(2,1)S(1)} %copy-done.24), channel_id=1, source_target_pairs={{0,1},{1,0},{2,3},{3,2},{4,5},{5,4},{6,7},{7,6},{8,9},{9,8},{10,11... | collective-permute-start | bytes 442376 | tf_op jit(solution)/shard_map/ppermute | solution.py:442
  152.9 28.1 %collective-permute-start.27 = (bf16[2,2,288,384]{3,2,1,0:T(8,128)(2,1)S(1)}, bf16[2,2,288,384]{3,2,1,0:T(8,128)(2,1)S(1)}, u32[]{:S(2)}, u32[]{:S(2)}) collective-permute-start(bf16[2,2,288,384]{3,2,1,0:T(8,128)(2,1)S(1)} %pad_maximum_fusion.1.rest_2_), channel_id=1, source_target_pairs={{0,2},{2,0},{4,6},{6,4},{8,10},{10,8},{12,14},{14,12},{16,18},{18,... | collective-permute-start | bytes 2654216 | tf_op jit(solution)/shard_map/ppermute | solution.py:449
  153.0 28.6 %collective-permute-start.25 = (bf16[2,2,288,384]{3,2,1,0:T(8,128)(2,1)S(1)}, bf16[2,2,288,384]{3,2,1,0:T(8,128)(2,1)S(1)}, u32[]{:S(2)}, u32[]{:S(2)}) collective-permute-start(bf16[2,2,288,384]{3,2,1,0:T(8,128)(2,1)S(1)} %pad_maximum_fusion.rest_0_), channel_id=1, source_target_pairs={{0,2},{2,0},{4,6},{6,4},{8,10},{10,8},{12,14},{14,12},{16,18},{18,... | collective-permute-start | bytes 2654216 | tf_op jit(solution)/shard_map/ppermute | solution.py:449
  153.6 28.2 %collective-permute-start.28 = (bf16[2,2,288,384]{3,2,1,0:T(8,128)(2,1)}, bf16[2,2,288,384]{3,2,1,0:T(8,128)(2,1)S(1)}, u32[]{:S(2)}, u32[]{:S(2)}) collective-permute-start(bf16[2,2,288,384]{3,2,1,0:T(8,128)(2,1)} %collective-permute-done.24.rest_3_), channel_id=1, source_target_pairs={{0,2},{2,0},{4,6},{6,4},{8,10},{10,8},{12,14},{14,12},{16,18},{18,... | collective-permute-start | bytes 2654216 | tf_op jit(solution)/shard_map/ppermute | solution.py:449
  153.7 28.5 %collective-permute-start.26 = (bf16[2,2,288,384]{3,2,1,0:T(8,128)(2,1)}, bf16[2,2,288,384]{3,2,1,0:T(8,128)(2,1)}, u32[]{:S(2)}, u32[]{:S(2)}) collective-permute-start(bf16[2,2,288,384]{3,2,1,0:T(8,128)(2,1)} %collective-permute-done.22.rest_1_), channel_id=1, source_target_pairs={{0,2},{2,0},{4,6},{6,4},{8,10},{10,8},{12,14},{14,12},{16,18},{18,... | collective-permute-start | bytes 2654216 | tf_op jit(solution)/shard_map/ppermute | solution.py:449
  163.2 17.7 %collective-permute-start.32 = (bf16[2,2,96,384]{3,2,1,0:T(8,128)(2,1)S(1)}, bf16[2,2,96,384]{3,2,1,0:T(8,128)(2,1)S(1)}, u32[]{:S(2)}, u32[]{:S(2)}) collective-permute-start(bf16[2,2,96,384]{3,2,1,0:T(8,128)(2,1)S(1)} %pad_maximum_fusion.7.rest_2_), channel_id=1, source_target_pairs={{0,1},{1,0},{2,3},{3,2},{4,5},{5,4},{6,7},{7,6},{8,9},{9,8},{10,11... | collective-permute-start | bytes 884744 | tf_op jit(solution)/shard_map/ppermute | solution.py:447
  181.0 51.4 %collective-permute-start.33 = (bf16[2,2,96,384]{3,2,1,0:T(8,128)(2,1)S(1)}, bf16[2,2,96,384]{3,2,1,0:T(8,128)(2,1)S(1)}, u32[]{:S(2)}, u32[]{:S(2)}) collective-permute-start(bf16[2,2,96,384]{3,2,1,0:T(8,128)(2,1)S(1)} %pad_maximum_fusion.6.rest_0_), channel_id=1, source_target_pairs={{0,2},{2,0},{4,6},{6,4},{8,10},{10,8},{12,14},{14,12},{16,18},{18,... | collective-permute-start | bytes 884744 | tf_op jit(solution)/shard_map/ppermute | solution.py:449
  181.1 51.3 %collective-permute-start.35 = (bf16[2,2,96,384]{3,2,1,0:T(8,128)(2,1)S(1)}, bf16[2,2,96,384]{3,2,1,0:T(8,128)(2,1)S(1)}, u32[]{:S(2)}, u32[]{:S(2)}) collective-permute-start(bf16[2,2,96,384]{3,2,1,0:T(8,128)(2,1)S(1)} %pad_maximum_fusion.7.rest_2_), channel_id=1, source_target_pairs={{0,2},{2,0},{4,6},{6,4},{8,10},{10,8},{12,14},{14,12},{16,18},{18,... | collective-permute-start | bytes 884744 | tf_op jit(solution)/shard_map/ppermute | solution.py:449
  181.6 50.8 %collective-permute-start.34 = (bf16[2,2,96,384]{3,2,1,0:T(8,128)(2,1)S(1)}, bf16[2,2,96,384]{3,2,1,0:T(8,128)(2,1)S(1)}, u32[]{:S(2)}, u32[]{:S(2)}) collective-permute-start(bf16[2,2,96,384]{3,2,1,0:T(8,128)(2,1)S(1)} %collective-permute-done.30.rest_1_), channel_id=1, source_target_pairs={{0,2},{2,0},{4,6},{6,4},{8,10},{10,8},{12,14},{14,12},{16,18},{18,... | collective-permute-start | bytes 884744 | tf_op jit(solution)/shard_map/ppermute | solution.py:449
  181.7 50.7 %collective-permute-start.36 = (bf16[2,2,96,384]{3,2,1,0:T(8,128)(2,1)S(1)}, bf16[2,2,96,384]{3,2,1,0:T(8,128)(2,1)S(1)}, u32[]{:S(2)}, u32[]{:S(2)}) collective-permute-start(bf16[2,2,96,384]{3,2,1,0:T(8,128)(2,1)S(1)} %collective-permute-done.32.rest_3_), channel_id=1, source_target_pairs={{0,2},{2,0},{4,6},{6,4},{8,10},{10,8},{12,14},{14,12},{16,18},{18,... | collective-permute-start | bytes 884744 | tf_op jit(solution)/shard_map/ppermute | solution.py:449
  (35 other events, 670.1 us)

commit v2 on v0

v2 whole, which is shorter than its diff:
```python
import functools
import math

import jax
import jax.numpy as jnp
from jax import lax
from jax.experimental import pallas as pl
from jax.experimental.pallas import tpu as pltpu
from jax.sharding import PartitionSpec as P

HEAD_DIM = 64
WIN_SIDE = 8
WIN_COLS = 60
WIN_TOK = 64
EPS = 1e-06
BF = jnp.bfloat16
F32 = jnp.float32


def position_table(window_ids, width):
    token_ids = jnp.arange(WIN_TOK, dtype=jnp.int32)
    row_pos = window_ids[:, None] // WIN_COLS * WIN_SIDE + token_ids[None, :] // WIN_SIDE
    col_pos = window_ids[:, None] % WIN_COLS * WIN_SIDE + token_ids[None, :] % WIN_SIDE
    quarter = width // 4
    frequency = jnp.exp(jnp.arange(quarter, dtype=F32) * (-math.log(10000.0) / quarter))
    row_angle = row_pos.astype(F32)[:, :, None] * frequency
    col_angle = col_pos.astype(F32)[:, :, None] * frequency
    return jnp.concatenate(
        [jnp.sin(row_angle), jnp.cos(row_angle), jnp.sin(col_angle), jnp.cos(col_angle)], axis=-1
    )


def head_norm(values):
    return (values * lax.rsqrt(jnp.mean(values * values, axis=-1, keepdims=True) + EPS)).astype(BF)


def window_layer(blocks_in, window_ids, window_lens, norm_gain, w_qkv, w_out):
    width = blocks_in.shape[-1]
    count = window_ids.shape[0]
    heads = width // HEAD_DIM
    stream = blocks_in.reshape(count, WIN_TOK, width).astype(F32) + position_table(window_ids, width)
    scale = lax.rsqrt(jnp.mean(stream * stream, axis=-1, keepdims=True) + EPS)
    normed = (stream * scale * norm_gain).astype(BF).reshape(count * WIN_TOK, width)
    full_rows = lax.all_gather(w_qkv, "group", axis=0, tiled=True)
    projected = jnp.dot(
        normed,
        lax.all_gather(full_rows, "tile", axis=1, tiled=True),
        preferred_element_type=F32,
    ).reshape(count, WIN_TOK, 3, heads, HEAD_DIM)
    queries = head_norm(projected[:, :, 0])
    keys = head_norm(projected[:, :, 1])
    values = projected[:, :, 2].astype(BF)
    scores = jnp.einsum("wqhd,wkhd->whqk", queries, keys, preferred_element_type=F32) * HEAD_DIM**-0.5
    key_mask = jnp.arange(WIN_TOK, dtype=jnp.int32)[None, :] < window_lens[:, None]
    weights = jnp.exp(scores) * key_mask[:, None, None, :].astype(F32)
    probs = (weights / jnp.sum(weights, axis=-1, keepdims=True)).astype(BF)
    attended = jnp.einsum("whqk,wkhd->wqhd", probs, values, preferred_element_type=F32)
    attended = attended.astype(BF).reshape(count * WIN_TOK, width)
    out_rows = lax.all_gather(w_out, "group", axis=0, tiled=True)
    update = jnp.dot(
        attended, lax.all_gather(out_rows, "tile", axis=1, tiled=True), preferred_element_type=F32
    )
    base = blocks_in.reshape(count * WIN_TOK, width).astype(F32)
    token_live = key_mask.reshape(count * WIN_TOK)[:, None]
    return jnp.where(token_live, base + update, base).astype(BF).reshape(blocks_in.shape)


def general(latents, window_index, window_len, live_blocks, norm_gain, w_qkv, w_out):
    slot_ids = jnp.arange(latents.shape[0], dtype=jnp.int32)
    live_mask = (slot_ids < live_blocks[0])[:, None, None]
    finished = window_layer(latents, window_index, window_len, norm_gain, w_qkv, w_out)
    return jnp.where(live_mask, finished, latents)


def anyspec():
    return pl.BlockSpec(memory_space=pl.ANY)


def vspec():
    return pl.BlockSpec(memory_space=pltpu.VMEM)


def sspec():
    return pl.BlockSpec(memory_space=pltpu.SMEM)


def params(mib):
    return pltpu.CompilerParams(vmem_limit_bytes=mib * 1024 * 1024)


def cost(flops, moved):
    return pl.CostEstimate(flops=flops, bytes_accessed=moved, transcendentals=0)


def norm_kernel(ids_ref, lat_ref, gain_ref, freq_ref, out_ref, pos_ref):
    blocks, _, width = lat_ref.shape
    quarter = width // 4
    freq = freq_ref[...]
    step = lax.broadcasted_iota(jnp.int32, (WIN_SIDE, quarter), 0).astype(F32) * freq
    sin_step, cos_step = jnp.sin(step), jnp.cos(step)
    gain = gain_ref[...]

    @pl.loop(0, blocks)
    def _(b):
        for w in range(2):
            place = ids_ref[2 * b + w]
            row = (place // WIN_COLS * WIN_SIDE).astype(F32)
            col = (place % WIN_COLS * WIN_SIDE).astype(F32)
            for at, start in ((0, row), (2 * quarter, col)):
                base = start * freq
                sin_base, cos_base = jnp.sin(base), jnp.cos(base)
                sines = sin_base * cos_step + cos_base * sin_step
                cosines = cos_base * cos_step - sin_base * sin_step
                for more, table in ((0, sines), (quarter, cosines)):
                    where = pl.ds(at + more, quarter)
                    for i in range(WIN_SIDE):
                        rows = pl.ds(w * WIN_TOK + i * WIN_SIDE, WIN_SIDE)
                        if at == 0:
                            pos_ref[rows, where] = jnp.broadcast_to(
                                table[i : i + 1, :], (WIN_SIDE, quarter)
                            )
                        else:
                            pos_ref[rows, where] = table
        stream = lat_ref[b].astype(F32) + pos_ref[...]
        scale = lax.rsqrt(jnp.mean(stream * stream, axis=-1, keepdims=True) + EPS)
        normed = (stream * scale * gain).astype(BF)
        out_ref[:, pl.ds(pl.multiple_of(b * 128, 128), 128)] = normed.T


def normed_columns(latents, window_index, norm_gain):
    blocks, rows, width = latents.shape
    quarter = width // 4
    freq = jnp.exp(jnp.arange(quarter, dtype=F32) * (-math.log(10000.0) / quarter))
    return pl.pallas_call(
        norm_kernel,
        out_shape=jax.ShapeDtypeStruct((width, blocks * rows), BF),
        in_specs=[sspec(), vspec(), vspec(), vspec()],
        out_specs=vspec(),
        scratch_shapes=[pltpu.VMEM((rows, width), F32)],
        compiler_params=params(24),
        cost_estimate=cost(40 * blocks * rows * width, 4 * blocks * rows * width),
        name="norm",
    )(window_index, latents, norm_gain.reshape(1, width), freq.reshape(1, quarter))


def project_kernel(key_chunk, value_chunk, at_ref, plane_ref, n_ref, *rest):
    pieces, (p_ref, k_ref, w_ref, sems) = rest[:8], rest[8:]
    x, y, core = at_ref[0], at_ref[1], at_ref[2]
    rows, lanes = pieces[0].shape
    copies = []
    for owner in range(2):
        c = core if owner == 0 else 1 - core
        for i, (px, py) in enumerate(((x, y), (1 - x, y), (x, 1 - y), (1 - x, 1 - y))):
            row = pl.multiple_of((2 * py + c) * rows, 16)
            lane = pl.multiple_of(px * lanes, 128)
            copies.append(
                pltpu.make_async_copy(
                    pieces[4 * owner + i],
                    w_ref.at[pl.ds(row, rows), pl.ds(lane, lanes)],
                    sems.at[len(copies)],
                )
            )
    for c in copies:
        c.start()
    for c in copies:
        c.wait()
    count, chunk, tokens = p_ref.shape
    cols = n_ref[...]

    @pl.loop(0, count)
    def _(m):
        which = plane_ref[0] * count + m
        w = w_ref[pl.ds(pl.multiple_of(m * chunk, 128), chunk), :]
        got = jnp.dot(w, cols, preferred_element_type=F32)
        got = got.reshape(chunk // HEAD_DIM, HEAD_DIM, tokens)
        ms = jnp.mean(got * got, axis=1, keepdims=True)
        scale = jnp.where(which < value_chunk, lax.rsqrt(ms + EPS), 1.0)
        out = (got * scale).astype(BF).reshape(chunk, tokens)
        is_key = (which >= key_chunk) & (which < value_chunk)

        @pl.when(is_key)
        def _():
            k_ref[m] = out.T

        @pl.when(jnp.logical_not(is_key))
        def _():
            p_ref[m] = out


def project(place, plane, normed, pieces):
    width, tokens = normed.shape
    rows = 4 * pieces[0].shape[0]
    chunk = width // 4
    count = rows // chunk
    return pl.pallas_call(
        functools.partial(project_kernel, 4, 8),
        out_shape=(
            jax.ShapeDtypeStruct((count, chunk, tokens), BF),
            jax.ShapeDtypeStruct((count, tokens, chunk), BF),
        ),
        in_specs=[sspec(), sspec(), vspec()] + [anyspec()] * 8,
        out_specs=(vspec(), vspec()),
        scratch_shapes=[pltpu.VMEM((rows, width), BF), pltpu.SemaphoreType.DMA((8,))],
        compiler_params=params(24),
        cost_estimate=cost(2 * rows * width * tokens, 2 * (rows + tokens) * width),
        name="project",
    )(place, plane, normed, *pieces)


def attend_kernel(
    planes_ref, lens_ref, p0, k0, p1, k1, p2, k2, p3, k3, out_ref, q_ref, k_ref, v_ref, mask_ref, sems
):
    count, chunk, tokens = p0.shape
    for s, (p, k) in enumerate(((p0, k0), (p1, k1), (p2, k2), (p3, k3))):
        for m in range(count):
            which = planes_ref[s] * count + m
            sem = sems.at[s * count + m]

            @pl.when(which < 4)
            def _():
                pltpu.make_async_copy(p.at[m], q_ref.at[jnp.minimum(which, 3)], sem).start()

            @pl.when((which >= 4) & (which < 8))
            def _():
                to = k_ref.at[jnp.clip(which - 4, 0, 3)]
                pltpu.make_async_copy(k.at[m], to, sem).start()

            @pl.when(which >= 8)
            def _():
                to = v_ref.at[jnp.clip(which - 8, 0, 3)]
                pltpu.make_async_copy(p.at[m], to, sem).start()

    blocks = tokens // 128
    key = lax.broadcasted_iota(jnp.int32, (128, 256), 0)
    query = lax.broadcasted_iota(jnp.int32, (128, 256), 1) % 128
    for b in range(blocks):
        first = (key < WIN_TOK) & (query < WIN_TOK) & (key < lens_ref[2 * b])
        second = (key >= WIN_TOK) & (query >= WIN_TOK) & (key - WIN_TOK < lens_ref[2 * b + 1])
        mask_ref[b] = jnp.where(first | second, 1.0, 0.0).astype(F32)
    for i in range(4 * count):
        pltpu.make_async_copy(p0.at[0], q_ref.at[0], sems.at[i]).wait()
    ones = jnp.ones((16, 128), BF)
    blank = jnp.zeros((HEAD_DIM, 128), BF)
    pairs = chunk // 128

    @pl.loop(0, 4 * pairs)
    def _(pair):
        part = pair // pairs
        at = pl.ds(pl.multiple_of(pair % pairs * 128, 128), 128)
        out_at = pl.ds(pl.multiple_of(pair * 128, 128), 128)
        for b in range(blocks):
            tok = pl.ds(b * 128, 128)
            q = q_ref[part, at, tok]
            k = k_ref[part, tok, at]
            v = v_ref[part, at, tok]
            q0 = jnp.concatenate([q[:HEAD_DIM], blank], axis=0)
            q1 = jnp.concatenate([blank, q[HEAD_DIM:]], axis=0)
            scores = jnp.dot(k, jnp.concatenate([q0, q1], axis=1), preferred_element_type=F32)
            weights = (jnp.exp(scores * HEAD_DIM**-0.5) * mask_ref[b]).astype(BF)
            got = jnp.dot(jnp.concatenate([v, ones], axis=0), weights, preferred_element_type=F32)
            o0 = got[:HEAD_DIM, :128] / got[128:129, :128]
            o1 = got[HEAD_DIM:128, 128:] / got[128:129, 128:]
            out_ref[tok, out_at] = jnp.concatenate([o0, o1], axis=0).T.astype(BF)


def attend(planes, window_len, parts):
    count, chunk, tokens = parts[0][0].shape
    width = 4 * chunk
    return pl.pallas_call(
        attend_kernel,
        out_shape=jax.ShapeDtypeStruct((tokens, width), BF),
        in_specs=[sspec()] * 2 + [anyspec()] * 8,
        out_specs=vspec(),
        scratch_shapes=[
            pltpu.VMEM((4, chunk, tokens), BF),
            pltpu.VMEM((4, tokens, chunk), BF),
            pltpu.VMEM((4, chunk, tokens), BF),
            pltpu.VMEM((tokens // 128, 128, 256), F32),
            pltpu.SemaphoreType.DMA((4 * count,)),
        ],
        compiler_params=params(24),
        cost_estimate=cost(40 * 128 * tokens * width, 8 * tokens * width),
        name="attend",
    )(planes, window_len, *[a for pair in parts for a in pair])


def output_kernel(at_ref, planes_ref, lens_ref, live_ref, att_ref, lat_ref, *rest):
    pieces, (out_ref, w_ref, sems) = rest[:10], rest[10:]
    x, y, core = at_ref[0], at_ref[1], at_ref[2]
    slots, rows, lanes = pieces[0].shape
    copies = []
    for owner in range(2):
        c = core if owner == 0 else 1 - core
        own, xs, ys, da, db = pieces[5 * owner : 5 * owner + 5]
        for s in range(slots):
            diagonal = da.at[s] if s < slots // 2 else db.at[s - slots // 2]
            for ref, px, py in (
                (own.at[s], x, y),
                (xs.at[s], 1 - x, y),
                (ys.at[s], x, 1 - y),
                (diagonal, 1 - x, 1 - y),
            ):
                row = pl.multiple_of((planes_ref[s] * 4 + 2 * py + c) * rows, 16)
                lane = pl.multiple_of(px * lanes, 128)
                copies.append(
                    pltpu.make_async_copy(
                        ref, w_ref.at[pl.ds(row, rows), pl.ds(lane, lanes)], sems.at[len(copies)]
                    )
                )
    for c in copies:
        c.start()
    for c in copies:
        c.wait()
    tokens, width = att_ref.shape
    cols = 4 * rows
    att = att_ref[...]
    token = lax.broadcasted_iota(jnp.int32, (tokens, 1), 0)
    stop = jnp.zeros((tokens, 1), jnp.int32)
    for w in range(tokens // WIN_TOK):
        length = jnp.where(w // 2 < live_ref[0], lens_ref[w], 0)
        stop = jnp.where(token // WIN_TOK == w, length + w * WIN_TOK, stop)
    keep = token < stop

    @pl.loop(0, slots)
    def _(s):
        spot = pl.ds(pl.multiple_of(s * cols, 128), cols)
        update = lax.dot_general(
            att, w_ref[spot, :], (((1,), (1,)), ((), ())), preferred_element_type=F32
        )
        base = lat_ref[:, spot].astype(F32)
        out_ref[:, spot] = jnp.where(keep, base + update, base).astype(BF)


def output(place, planes, lens, live, attended, latents, pieces):
    tokens, width = attended.shape
    return pl.pallas_call(
        output_kernel,
        out_shape=jax.ShapeDtypeStruct((tokens, width), BF),
        in_specs=[sspec()] * 4 + [vspec()] * 2 + [anyspec()] * 10,
        out_specs=vspec(),
        scratch_shapes=[pltpu.VMEM((width, width), BF), pltpu.SemaphoreType.DMA((32,))],
        compiler_params=params(32),
        cost_estimate=cost(2 * width * width * tokens, 2 * width * (width + 3 * tokens)),
        name="output",
    )(place, planes, lens, live, attended, latents, *pieces)


def after(value, *earlier):
    return lax.optimization_barrier((value, *earlier))[0]


def local(tile_count, latents, window_index, window_len, live_blocks, norm_gain, w_qkv, w_out):
    blocks, rows, width = latents.shape

    def along(bit):
        pairs = [(i, i ^ bit) for i in range(tile_count)]
        return functools.partial(lax.ppermute, axis_name="tile", perm=pairs)

    core, ys, z1, z2, z3 = along(1), along(2), along(4), along(8), along(12)
    xs = functools.partial(lax.ppermute, axis_name="group", perm=[(0, 1), (1, 0)])
    t = lax.axis_index("tile")
    x = lax.axis_index("group")
    z = t // 4
    place = jnp.stack([x, t // 2 % 2, t % 2]).astype(jnp.int32)
    planes = jnp.stack([z, z ^ 1, z ^ 2, z ^ 3]).astype(jnp.int32)

    u0 = w_qkv.T
    o0 = w_out.T
    u1, x0, y0 = z1(u0), xs(u0), ys(u0)
    u2 = z2(u0)
    normed = normed_columns(latents, window_index, norm_gain)
    y0, normed = lax.optimization_barrier((y0, normed))
    d0 = xs(y0)
    y1 = ys(u1)
    u3 = z3(after(u0, u2, y0))
    x2, y2 = xs(after(u2, d0)), ys(u2)
    d1 = z1(d0)
    s0 = [u0, x0, y0, d0]
    p0 = project(place, planes[0:1], normed, s0 + [core(a) for a in s0])
    d2 = ys(after(x2, p0[0]))
    x1 = xs(after(u1, x2))
    s1 = [u1, x1, y1, d1]
    p1 = project(place, planes[1:2], normed, s1 + [core(a) for a in s1])
    y3, x3 = ys(after(u3, d2)), xs(after(u3, x1))
    d3 = z1(d2)
    o1, o2, o3 = (f(after(o0, u3)) for f in (z1, z2, z3))
    s2 = [u2, x2, y2, d2]
    p2 = project(place, planes[2:3], normed, s2 + [core(a) for a in s2])
    o4 = after(jnp.stack([o0, o1, o2, o3]), p1[0])
    xo, yo = xs(o4), ys(o4)
    s3 = [u3, x3, y3, d3]
    p3 = project(place, planes[3:4], normed, s3 + [core(a) for a in s3])
    half = o4.shape[0] // 2
    da, db = xs(after(yo[:half], p3[0])), ys(xo[half:])
    so = [o4, xo, yo, da, db]
    so = so + [core(a) for a in so]
    attended = attend(planes, window_len, (p0, p1, p2, p3))
    flat = latents.reshape(blocks * rows, width)
    out = output(place, planes, window_len, live_blocks, attended, flat, so)
    return out.reshape(latents.shape)


def solution(mesh):
    in_specs = (
        P(("tile", "group"), None, None),
        P(("tile", "group")),
        P(("tile", "group")),
        P(("tile", "group")),
        P(),
        P("group", "tile"),
        P("group", "tile"),
    )
    out_specs = P(("tile", "group"), None, None)
    planes, chips, cores = 4, 2, 2
    if mesh.shape["group"] == 2 and mesh.shape["tile"] == planes * chips * cores:
        body = functools.partial(local, mesh.shape["tile"])
    else:
        body = general
    return jax.shard_map(body, mesh=mesh, in_specs=in_specs, out_specs=out_specs, check_vma=False)
```

time: 229 us -> 159 us (0.69)
  matrix products: 57.5 us -> 0 us
  Pallas kernels: 0 us -> 47.4 us
  waiting for transfers between devices: 86 us -> 43.5 us
  starting transfers between devices: 0.04 us -> 34.4 us
  blocking collectives: 22.1 us -> 0 us
  other arithmetic: 21.6 us -> 1.29 us
  between operations: 14.2 us -> 1.16 us
  local copies, waits for them, and re-layouts: 26.7 us -> 30.5 us
    all_gather x2 -> x0, waiting for transfers between devices: 86 us -> none  [the longest x1 86 us: project_qkv(): lax.all_gather(full_rows, 'tile', axis=1, tiled=True)]
    dot_general x4 -> x0, matrix products: 57.5 us -> none  [the longest x1 25.9 us: project_qkv(): jnp.dot(normed, lax.all_gather(full_rows, 'tile', axis=1, tiled=True), pr...]
    pallas_call x0 -> x7, Pallas kernels: none -> 47.4 us  [the longest x4 24.7 us: project(): pl.pallas_call(functools.partial(project_kernel, 4, 8), out_shape=(jax.Sh...]
    ppermute x0 -> x43, waiting for transfers between devices: none -> 43.5 us  [the longest x3 13.4 us: local(): o1, o2, o3 = (f(after(o0, u3)) for f in (z1, z2, z3))]
    ppermute x0 -> x43, starting transfers between devices: none -> 34.4 us  [the longest x3 6.03 us: local(): u1, x0, y0 = (z1(u0), xs(u0), ys(u0))]
    all_gather x2 -> x0, blocking collectives: 22.1 us -> none  [the longest x1 16 us: project_qkv(): full_rows = lax.all_gather(w_qkv, 'group', axis=0, tiled=True)]
    unnamed x12 -> x82, local copies, waits for them, and re-layouts: 11.1 us -> 28.8 us
    sin x1 -> x0, other arithmetic: 9.64 us -> none  [position_table(): jnp.sin(row_angle)]
  transfers between devices with their start and end apart: 2 -> 43, of which waited for: 1 -> 6; matrix products, arithmetic and copies ran while one was open for 38% -> 2% of each run, Pallas kernels for 0% -> 24%
where the time goes in v2:
time: 159 us; the launch traced here: 158 us
  Pallas kernels  47.4 us (30%)
  waiting for transfers between devices  43.5 us (27%)
  starting transfers between devices  34.4 us (22%)
  local copies, waits for them, and re-layouts  30.5 us (19%)
    unnamed x82, local copies, waits for them, and re-layouts  28.8 us
    pallas_call x4, Pallas kernels, project(): pl.pallas_call(functools.partial(project_kernel, 4, 8), out_shape=(jax.Sh...  24.7 us
    ppermute x3, waiting for transfers between devices, local(): o1, o2, o3 = (f(after(o0, u3)) for f in (z1, z2, z3))  13.4 us
    ppermute x3, waiting for transfers between devices, local(): u1, x0, y0 = (z1(u0), xs(u0), ys(u0))  13.2 us
    pallas_call x1, Pallas kernels, attend(): pl.pallas_call(attend_kernel, out_shape=jax.ShapeDtypeStruct((tokens, wid...  10.1 us
    pallas_call x1, Pallas kernels, output(): pl.pallas_call(output_kernel, out_shape=jax.ShapeDtypeStruct((tokens, wid...  9.42 us
    ppermute x1, waiting for transfers between devices, local(): u2 = z2(u0)  8.99 us
    ppermute x3, starting transfers between devices, local(): u1, x0, y0 = (z1(u0), xs(u0), ys(u0))  6.03 us
  transfers between devices with their start and end apart: 43, of which 6 were waited for; matrix products, arithmetic and copies ran while one was open for 2% of the time, Pallas kernels for 24%

profile of v2, /device:TPU:0, one launch (start us, length us, event | category | flops | bytes accessed | tf_op | source)
XLA Modules:
  0.0 158.4 jit_solution(15175401414416334755)
XLA Ops:
  0.0 3.0 %collective-permute-start = (bf16[288,768]{1,0:T(8,128)(2,1)}, bf16[288,768]{1,0:T(8,128)(2,1)S(1)}, u32[]{:S(2)}, u32[]{:S(2)}) collective-permute-start(bf16[288,768]{1,0:T(8,128)(2,1)} %bitcast.17), channel_id=1, source_target_pairs={{0,4},{2,6},{4,0},{6,2},{8,12},{10,14},{12,8},{14,10},{16,20},{18,... | collective-permute-start | bytes 1327112 | tf_op jit(solution)/shard_map/ppermute | solution.py:369
  3.0 1.5 collective-permute-start.1
  4.5 2.6 %collective-permute-start.8 = (bf16[288,768]{1,0:T(8,128)(2,1)}, bf16[288,768]{1,0:T(8,128)(2,1)}, u32[]{:S(2)}, u32[]{:S(2)}) collective-permute-start(bf16[288,768]{1,0:T(8,128)(2,1)} %bitcast.19), channel_id=1, source_target_pairs={{0,16},{2,18},{4,20},{6,22},{8,24},{10,26},{12,28},{14,30},{16,0},... | collective-permute-start | bytes 1327112 | tf_op jit(solution)/shard_map/ppermute | solution.py:370
  7.8 1.7 %copy-done = bf16[6,128,1536]{2,1,0:T(8,128)(2,1)S(1)} copy-done((bf16[6,128,1536]{2,1,0:T(8,128)(2,1)S(1)}, bf16[6,128,1536]{2,1,0:T(8,128)(2,1)}, u32[]{:S(2)}) %copy-start) | copy-done | bytes 2359320
  10.1 3.3 %norm.1.n_ref = bf16[1536,768]{1,0:T(8,128)(2,1)S(1)} custom-call(s32[12]{0:T(128)S(1)} %copy-done.2, bf16[6,128,1536]{2,1,0:T(8,128)(2,1)S(1)} %copy-done, f32[1,1536]{1,0:T(1,128)S(1)} %reshape.20.gain_ref, f32[1,384]{1,0:T(1,128)S(1)} %multiply_exponential_fusion.freq_ref), custom_call_target="tpu_custom_call" | custom-call | flops 47185920 | bytes 4718592 | tf_op jit(solution)/shard_map/norm/pallas_call | solution.py:134
  13.4 1.7 %collective-permute-start.2 = (bf16[288,768]{1,0:T(8,128)(2,1)S(1)}, bf16[288,768]{1,0:T(8,128)(2,1)}, u32[]{:S(2)}, u32[]{:S(2)}) collective-permute-start(bf16[288,768]{1,0:T(8,128)(2,1)S(1)} %collective-permute-done.rest_2_), channel_id=1, source_target_pairs={{0,1},{1,0},{2,3},{3,2},{4,5},{5,4},{6,7},{7,6},{8,9},{9,8},{10,11... | collective-permute-start | bytes 1327112 | tf_op jit(solution)/shard_map/ppermute | solution.py:373
  15.1 1.6 collective-permute-start.7
  17.6 9.0 %collective-permute-done.8.rest_0_ = bf16[288,768]{1,0:T(8,128)(2,1)} collective-permute-done((bf16[288,768]{1,0:T(8,128)(2,1)}, bf16[288,768]{1,0:T(8,128)(2,1)}, u32[]{:S(2)}, u32[]{:S(2)}) %collective-permute-start.8) | collective-permute-done | bytes 442400 | tf_op jit(solution)/shard_map/ppermute | solution.py:370
  28.7 3.5 %collective-permute-start.23 = (bf16[288,768]{1,0:T(8,128)(2,1)S(1)}, bf16[288,768]{1,0:T(8,128)(2,1)}, u32[]{:S(2)}, u32[]{:S(2)}) collective-permute-start(bf16[288,768]{1,0:T(8,128)(2,1)S(1)} %bitcast.22), channel_id=1, source_target_pairs={{0,24},{2,26},{4,28},{6,30},{8,16},{10,18},{12,20},{14,22},{16,8},... | collective-permute-start | bytes 1327112 | tf_op jit(solution)/shard_map/ppermute | solution.py:375
  32.2 13.2 %collective-permute-done.7.rest_0_ = bf16[288,768]{1,0:T(8,128)(2,1)S(1)} collective-permute-done((bf16[288,768]{1,0:T(8,128)(2,1)S(1)}, bf16[288,768]{1,0:T(8,128)(2,1)S(1)}, u32[]{:S(2)}, u32[]{:S(2)}) %collective-permute-start.7) | collective-permute-done | bytes 442400 | tf_op jit(solution)/shard_map/ppermute | solution.py:369
  48.4 3.6 %collective-permute-start.33 = (bf16[96,768]{1,0:T(8,128)(2,1)S(1)}, bf16[96,768]{1,0:T(8,128)(2,1)S(1)}, u32[]{:S(2)}, u32[]{:S(2)}) collective-permute-start(bf16[96,768]{1,0:T(8,128)(2,1)S(1)} %bitcast.24), channel_id=1, source_target_pairs={{0,24},{2,26},{4,28},{6,30},{8,16},{10,18},{12,20},{14,22},{16,8},... | collective-permute-start | bytes 442376 | tf_op jit(solution)/shard_map/ppermute | solution.py:386
  57.0 5.6 %project.4 = (bf16[3,384,768]{2,1,0:T(8,128)(2,1)S(1)}, bf16[3,768,384]{2,1,0:T(8,128)(2,1)S(1)}) custom-call(s32[3]{0:T(128)S(1)} %pad_add_fusion.at_ref, s32[1]{0:T(128)} %bitcast.3.plane_ref, bf16[1536,768]{1,0:T(8,128)(2,1)S(1)} %norm.1.n_ref, bf16[288,768]{1,0:T(8,128)(2,1)S(1)} %bitcast.23, bf16[288,768]{1,0:T(8,128)(2,1)S(1)} %copy-done.7, ...), custom_call_target="tpu_custom_call" | custom-call | flops 2717908992 | bytes 5898240 | tf_op jit(solution)/shard_map/project/pallas_call | solution.py:195
  62.6 1.2 copy-done.29
  63.8 1.2 copy-done.31
  65.0 1.5 collective-permute-start.18
  67.1 1.7 %collective-permute-start.32 = (bf16[96,768]{1,0:T(8,128)(2,1)S(1)}, bf16[96,768]{1,0:T(8,128)(2,1)S(1)}, u32[]{:S(2)}, u32[]{:S(2)}) collective-permute-start(bf16[96,768]{1,0:T(8,128)(2,1)S(1)} %bitcast.25), channel_id=1, source_target_pairs={{0,16},{2,18},{4,20},{6,22},{8,24},{10,26},{12,28},{14,30},{16,0},... | collective-permute-start | bytes 442376 | tf_op jit(solution)/shard_map/ppermute | solution.py:386
  68.7 8.2 %collective-permute-done.32 = bf16[96,768]{1,0:T(8,128)(2,1)S(1)} collective-permute-done((bf16[96,768]{1,0:T(8,128)(2,1)S(1)}, bf16[96,768]{1,0:T(8,128)(2,1)S(1)}, u32[]{:S(2)}, u32[]{:S(2)}) %collective-permute-start.32) | collective-permute-done | bytes 147488 | tf_op jit(solution)/shard_map/ppermute | solution.py:386
  77.0 5.1 %collective-permute-done.31 = bf16[96,768]{1,0:T(8,128)(2,1)S(1)} collective-permute-done((bf16[96,768]{1,0:T(8,128)(2,1)S(1)}, bf16[96,768]{1,0:T(8,128)(2,1)S(1)}, u32[]{:S(2)}, u32[]{:S(2)}) %collective-permute-start.31) | collective-permute-done | bytes 147488 | tf_op jit(solution)/shard_map/ppermute | solution.py:386
  82.8 1.5 collective-permute-start.24
  85.0 1.4 collective-permute-start.25
  86.6 1.1 pad_maximum_fusion.rest_0_
  88.8 6.4 %project.5 = (bf16[3,384,768]{2,1,0:T(8,128)(2,1)S(1)}, bf16[3,768,384]{2,1,0:T(8,128)(2,1)S(1)}) custom-call(s32[3]{0:T(128)S(1)} %pad_add_fusion.at_ref, s32[1]{0:T(128)} %bitcast.4.plane_ref, bf16[1536,768]{1,0:T(8,128)(2,1)S(1)} %norm.1.n_ref, bf16[288,768]{1,0:T(8,128)(2,1)S(1)} %collective-permute-done.7.rest_0_, ...), custom_call_target="tpu_custom_call" | custom-call | flops 2717908992 | bytes 5898240 | tf_op jit(solution)/shard_map/project/pallas_call | solution.py:195
  95.2 1.2 copy-done.33
  96.4 1.3 copy-done.35
  98.5 4.6 %collective-permute-done.25.rest_2_ = bf16[288,768]{1,0:T(8,128)(2,1)S(1)} collective-permute-done((bf16[288,768]{1,0:T(8,128)(2,1)}, bf16[288,768]{1,0:T(8,128)(2,1)S(1)}, u32[]{:S(2)}, u32[]{:S(2)}) %collective-permute-start.25) | collective-permute-done | bytes 442400 | tf_op jit(solution)/shard_map/ppermute | solution.py:384
  106.0 2.4 %collective-permute-start.34 = (bf16[4,96,768]{2,1,0:T(8,128)(2,1)S(1)}, bf16[4,96,768]{2,1,0:T(8,128)(2,1)}, u32[]{:S(2)}, u32[]{:S(2)}) collective-permute-start(bf16[4,96,768]{2,1,0:T(8,128)(2,1)S(1)} %pad_maximum_fusion.rest_0_), channel_id=1, source_target_pairs={{0,1},{1,0},{2,3},{3,2},{4,5},{5,4},{6,7},{7,6},{8,9},{9,8},{10,11... | collective-permute-start | bytes 1769480 | tf_op jit(solution)/shard_map/ppermute | solution.py:390
  111.3 3.3 %collective-permute-done.35.rest_2_ = bf16[4,96,768]{2,1,0:T(8,128)(2,1)S(1)} collective-permute-done((bf16[4,96,768]{2,1,0:T(8,128)(2,1)S(1)}, bf16[4,96,768]{2,1,0:T(8,128)(2,1)S(1)}, u32[]{:S(2)}, u32[]{:S(2)}) %collective-permute-start.35) | collective-permute-done | bytes 589856 | tf_op jit(solution)/shard_map/ppermute | solution.py:390
  120.7 5.5 %project.7 = (bf16[3,384,768]{2,1,0:T(8,128)(2,1)S(1)}, bf16[3,768,384]{2,1,0:T(8,128)(2,1)S(1)}) custom-call(s32[3]{0:T(128)S(1)} %pad_add_fusion.at_ref, s32[1]{0:T(128)} %bitcast.6.plane_ref, bf16[1536,768]{1,0:T(8,128)(2,1)S(1)} %norm.1.n_ref, bf16[288,768]{1,0:T(8,128)(2,1)} %collective-permute-done.23.rest_0_, ...), custom_call_target="tpu_custom_call" | custom-call | flops 2717908992 | bytes 5898240 | tf_op jit(solution)/shard_map/project/pallas_call | solution.py:195
  126.2 1.6 collective-permute-start.36
  130.8 7.2 %project.6 = (bf16[3,384,768]{2,1,0:T(8,128)(2,1)S(1)}, bf16[3,768,384]{2,1,0:T(8,128)(2,1)S(1)}) custom-call(s32[3]{0:T(128)S(1)} %pad_add_fusion.at_ref, s32[1]{0:T(128)} %bitcast.5.plane_ref, bf16[1536,768]{1,0:T(8,128)(2,1)S(1)} %norm.1.n_ref, bf16[288,768]{1,0:T(8,128)(2,1)} %collective-permute-done.8.rest_0_, ...), custom_call_target="tpu_custom_call" | custom-call | flops 2717908992 | bytes 5898240 | tf_op jit(solution)/shard_map/project/pallas_call | solution.py:195
  138.6 10.1 %attend.1.att_ref = bf16[768,1536]{1,0:T(8,128)(2,1)S(1)} custom-call(s32[4]{0:T(128)S(1)} %pad_add_fusion.1.planes_ref, s32[12]{0:T(128)S(1)} %copy-done.28, bf16[3,384,768]{2,1,0:T(8,128)(2,1)S(1)} %copy-done.30, bf16[3,768,384]{2,1,0:T(8,128)(2,1)S(1)} %copy-done.32, bf16[3,384,768]{2,1,0:T(8,128)(2,1)S(1)} %copy-done.34, ...), custom_call_target="tpu_custom_call" | custom-call | flops 6039797760 | bytes 9437184 | tf_op jit(solution)/shard_map/attend/pallas_call | solution.py:269
  148.8 9.4 %output.1 = bf16[768,1536]{1,0:T(8,128)(2,1)} custom-call(s32[3]{0:T(128)S(1)} %pad_add_fusion.at_ref, s32[4]{0:T(128)S(1)} %pad_add_fusion.1.planes_ref, s32[12]{0:T(128)S(1)} %copy-done.28, s32[1]{0:T(128)S(6)} %copy.8.live_ref, bf16[768,1536]{1,0:T(8,128)(2,1)S(1)} %attend.1.att_ref, bf16[768,1536]{1,0:T(8,128)(2,1)S(1)} %bitcast.16, ...), custom_call_target="tpu_custom_call" | custom-call | flops 3623878656 | bytes 11796480 | tf_op jit(solution)/shard_map/output/pallas_call | solution.py:336
  (150 shorter events, 31.3 us)
Async XLA Ops:
  0.0 13.4 %collective-permute-start = (bf16[288,768]{1,0:T(8,128)(2,1)}, bf16[288,768]{1,0:T(8,128)(2,1)S(1)}, u32[]{:S(2)}, u32[]{:S(2)}) collective-permute-start(bf16[288,768]{1,0:T(8,128)(2,1)} %bitcast.17), channel_id=1, source_target_pairs={{0,4},{2,6},{4,0},{6,2},{8,12},{10,14},{12,8},{14,10},{16,20},{18,... | collective-permute-start | bytes 1327112 | tf_op jit(solution)/shard_map/ppermute | solution.py:369
  3.0 13.7 %collective-permute-start.1 = (bf16[288,768]{1,0:T(8,128)(2,1)}, bf16[288,768]{1,0:T(8,128)(2,1)S(1)}, u32[]{:S(2)}, u32[]{:S(2)}) collective-permute-start(bf16[288,768]{1,0:T(8,128)(2,1)} %bitcast.18), channel_id=1, source_target_pairs={{0,1},{1,0},{2,3},{3,2},{4,5},{5,4},{6,7},{7,6},{8,9},{9,8},{10,11... | collective-permute-start | bytes 1327112 | tf_op jit(solution)/shard_map/ppermute | solution.py:369
  4.5 22.2 %collective-permute-start.8 = (bf16[288,768]{1,0:T(8,128)(2,1)}, bf16[288,768]{1,0:T(8,128)(2,1)}, u32[]{:S(2)}, u32[]{:S(2)}) collective-permute-start(bf16[288,768]{1,0:T(8,128)(2,1)} %bitcast.19), channel_id=1, source_target_pairs={{0,16},{2,18},{4,20},{6,22},{8,24},{10,26},{12,28},{14,30},{16,0},... | collective-permute-start | bytes 1327112 | tf_op jit(solution)/shard_map/ppermute | solution.py:370
  13.4 14.0 %collective-permute-start.2 = (bf16[288,768]{1,0:T(8,128)(2,1)S(1)}, bf16[288,768]{1,0:T(8,128)(2,1)}, u32[]{:S(2)}, u32[]{:S(2)}) collective-permute-start(bf16[288,768]{1,0:T(8,128)(2,1)S(1)} %collective-permute-done.rest_2_), channel_id=1, source_target_pairs={{0,1},{1,0},{2,3},{3,2},{4,5},{5,4},{6,7},{7,6},{8,9},{9,8},{10,11... | collective-permute-start | bytes 1327112 | tf_op jit(solution)/shard_map/ppermute | solution.py:373
  15.1 30.3 %collective-permute-start.7 = (bf16[288,768]{1,0:T(8,128)(2,1)S(1)}, bf16[288,768]{1,0:T(8,128)(2,1)S(1)}, u32[]{:S(2)}, u32[]{:S(2)}) collective-permute-start(bf16[288,768]{1,0:T(8,128)(2,1)S(1)} %bitcast.21), channel_id=1, source_target_pairs={{0,8},{2,10},{4,12},{6,14},{8,0},{10,2},{12,4},{14,6},{16,24},{18,... | collective-permute-start | bytes 1327112 | tf_op jit(solution)/shard_map/ppermute | solution.py:369
  16.6 28.8 %collective-permute-start.4 = (bf16[288,768]{1,0:T(8,128)(2,1)S(1)}, bf16[288,768]{1,0:T(8,128)(2,1)S(1)}, u32[]{:S(2)}, u32[]{:S(2)}) collective-permute-start(bf16[288,768]{1,0:T(8,128)(2,1)S(1)} %collective-permute-done.1.rest_1_), channel_id=1, source_target_pairs={{0,2},{2,0},{4,6},{6,4},{8,10},{10,8},{12,14},{14,12},{16,18},{18,... | collective-permute-start | bytes 1327112 | tf_op jit(solution)/shard_map/ppermute | solution.py:379
  26.6 20.1 %collective-permute-start.5 = (bf16[288,768]{1,0:T(8,128)(2,1)S(1)}, bf16[288,768]{1,0:T(8,128)(2,1)S(1)}, u32[]{:S(2)}, u32[]{:S(2)}) collective-permute-start(bf16[288,768]{1,0:T(8,128)(2,1)S(1)} %collective-permute-done.rest_2_), channel_id=1, source_target_pairs={{0,2},{2,0},{4,6},{6,4},{8,10},{10,8},{12,14},{14,12},{16,18},{18,... | collective-permute-start | bytes 1327112 | tf_op jit(solution)/shard_map/ppermute | solution.py:379
  27.4 20.3 %collective-permute-start.9 = (bf16[288,768]{1,0:T(8,128)(2,1)}, bf16[288,768]{1,0:T(8,128)(2,1)}, u32[]{:S(2)}, u32[]{:S(2)}) collective-permute-start(bf16[288,768]{1,0:T(8,128)(2,1)} %collective-permute-done.8.rest_0_), channel_id=1, source_target_pairs={{0,1},{1,0},{2,3},{3,2},{4,5},{5,4},{6,7},{7,6},{8,9},{9,8},{10,11... | collective-permute-start | bytes 1327112 | tf_op jit(solution)/shard_map/ppermute | solution.py:376
  28.7 19.0 %collective-permute-start.23 = (bf16[288,768]{1,0:T(8,128)(2,1)S(1)}, bf16[288,768]{1,0:T(8,128)(2,1)}, u32[]{:S(2)}, u32[]{:S(2)}) collective-permute-start(bf16[288,768]{1,0:T(8,128)(2,1)S(1)} %bitcast.22), channel_id=1, source_target_pairs={{0,24},{2,26},{4,28},{6,30},{8,16},{10,18},{12,20},{14,22},{16,8},... | collective-permute-start | bytes 1327112 | tf_op jit(solution)/shard_map/ppermute | solution.py:375
  46.2 18.8 %collective-permute-start.11 = (bf16[288,768]{1,0:T(8,128)(2,1)S(1)}, bf16[288,768]{1,0:T(8,128)(2,1)}, u32[]{:S(2)}, u32[]{:S(2)}) collective-permute-start(bf16[288,768]{1,0:T(8,128)(2,1)S(1)} %collective-permute-done.7.rest_0_), channel_id=1, source_target_pairs={{0,4},{2,6},{4,0},{6,2},{8,12},{10,14},{12,8},{14,10},{16,20},{18,... | collective-permute-start | bytes 1327112 | tf_op jit(solution)/shard_map/ppermute | solution.py:374
  47.5 19.0 %collective-permute-start.13 = (bf16[288,768]{1,0:T(8,128)(2,1)S(1)}, bf16[288,768]{1,0:T(8,128)(2,1)}, u32[]{:S(2)}, u32[]{:S(2)}) collective-permute-start(bf16[288,768]{1,0:T(8,128)(2,1)S(1)} %collective-permute-done.7.rest_0_), channel_id=1, source_target_pairs={{0,2},{2,0},{4,6},{6,4},{8,10},{10,8},{12,14},{14,12},{16,18},{18,... | collective-permute-start | bytes 1327112 | tf_op jit(solution)/shard_map/ppermute | solution.py:383
  47.7 18.9 %collective-permute-start.12 = (bf16[288,768]{1,0:T(8,128)(2,1)}, bf16[288,768]{1,0:T(8,128)(2,1)}, u32[]{:S(2)}, u32[]{:S(2)}) collective-permute-start(bf16[288,768]{1,0:T(8,128)(2,1)} %collective-permute-done.2.rest_3_), channel_id=1, source_target_pairs={{0,8},{2,10},{4,12},{6,14},{8,0},{10,2},{12,4},{14,6},{16,24},{18,... | collective-permute-start | bytes 1327112 | tf_op jit(solution)/shard_map/ppermute | solution.py:377
  47.7 21.0 %collective-permute-start.10 = (bf16[288,768]{1,0:T(8,128)(2,1)S(1)}, bf16[288,768]{1,0:T(8,128)(2,1)}, u32[]{:S(2)}, u32[]{:S(2)}) collective-permute-start(bf16[288,768]{1,0:T(8,128)(2,1)S(1)} %collective-permute-done.7.rest_0_), channel_id=1, source_target_pairs={{0,1},{1,0},{2,3},{3,2},{4,5},{5,4},{6,7},{7,6},{8,9},{9,8},{10,11... | collective-permute-start | bytes 1327112 | tf_op jit(solution)/shard_map/ppermute | solution.py:381
  48.4 18.7 %collective-permute-start.33 = (bf16[96,768]{1,0:T(8,128)(2,1)S(1)}, bf16[96,768]{1,0:T(8,128)(2,1)S(1)}, u32[]{:S(2)}, u32[]{:S(2)}) collective-permute-start(bf16[96,768]{1,0:T(8,128)(2,1)S(1)} %bitcast.24), channel_id=1, source_target_pairs={{0,24},{2,26},{4,28},{6,30},{8,16},{10,18},{12,20},{14,22},{16,8},... | collective-permute-start | bytes 442376 | tf_op jit(solution)/shard_map/ppermute | solution.py:386
  65.0 17.7 %collective-permute-start.18 = (bf16[288,768]{1,0:T(8,128)(2,1)}, bf16[288,768]{1,0:T(8,128)(2,1)}, u32[]{:S(2)}, u32[]{:S(2)}) collective-permute-start(bf16[288,768]{1,0:T(8,128)(2,1)} %collective-permute-done.9.rest_1_), channel_id=1, source_target_pairs={{0,4},{2,6},{4,0},{6,2},{8,12},{10,14},{12,8},{14,10},{16,20},{18,... | collective-permute-start | bytes 1327112 | tf_op jit(solution)/shard_map/ppermute | solution.py:380
  66.5 17.7 %collective-permute-start.15 = (bf16[288,768]{1,0:T(8,128)(2,1)}, bf16[288,768]{1,0:T(8,128)(2,1)S(1)}, u32[]{:S(2)}, u32[]{:S(2)}) collective-permute-start(bf16[288,768]{1,0:T(8,128)(2,1)} %collective-permute-done.11.rest_2_), channel_id=1, source_target_pairs={{0,2},{2,0},{4,6},{6,4},{8,10},{10,8},{12,14},{14,12},{16,18},{18,... | collective-permute-start | bytes 1327112 | tf_op jit(solution)/shard_map/ppermute | solution.py:383
  66.6 19.9 %collective-permute-start.16 = (bf16[288,768]{1,0:T(8,128)(2,1)}, bf16[288,768]{1,0:T(8,128)(2,1)}, u32[]{:S(2)}, u32[]{:S(2)}) collective-permute-start(bf16[288,768]{1,0:T(8,128)(2,1)} %collective-permute-done.12.rest_3_), channel_id=1, source_target_pairs={{0,2},{2,0},{4,6},{6,4},{8,10},{10,8},{12,14},{14,12},{16,18},{18,... | collective-permute-start | bytes 1327112 | tf_op jit(solution)/shard_map/ppermute | solution.py:383
  68.7 19.0 %collective-permute-start.14 = (bf16[288,768]{1,0:T(8,128)(2,1)}, bf16[288,768]{1,0:T(8,128)(2,1)}, u32[]{:S(2)}, u32[]{:S(2)}) collective-permute-start(bf16[288,768]{1,0:T(8,128)(2,1)} %collective-permute-done.10.rest_1_), channel_id=1, source_target_pairs={{0,2},{2,0},{4,6},{6,4},{8,10},{10,8},{12,14},{14,12},{16,18},{18,... | collective-permute-start | bytes 1327112 | tf_op jit(solution)/shard_map/ppermute | solution.py:383
  82.1 15.5 %collective-permute-start.17 = (bf16[288,768]{1,0:T(8,128)(2,1)}, bf16[288,768]{1,0:T(8,128)(2,1)}, u32[]{:S(2)}, u32[]{:S(2)}) collective-permute-start(bf16[288,768]{1,0:T(8,128)(2,1)} %collective-permute-done.8.rest_0_), channel_id=1, source_target_pairs={{0,4},{2,6},{4,0},{6,2},{8,12},{10,14},{12,8},{14,10},{16,20},{18,... | collective-permute-start | bytes 1327112 | tf_op jit(solution)/shard_map/ppermute | solution.py:376
  82.8 15.5 %collective-permute-start.24 = (bf16[288,768]{1,0:T(8,128)(2,1)}, bf16[288,768]{1,0:T(8,128)(2,1)}, u32[]{:S(2)}, u32[]{:S(2)}) collective-permute-start(bf16[288,768]{1,0:T(8,128)(2,1)} %collective-permute-done.23.rest_0_), channel_id=1, source_target_pairs={{0,1},{1,0},{2,3},{3,2},{4,5},{5,4},{6,7},{7,6},{8,9},{9,8},{10,11... | collective-permute-start | bytes 1327112 | tf_op jit(solution)/shard_map/ppermute | solution.py:384
  85.0 18.1 %collective-permute-start.25 = (bf16[288,768]{1,0:T(8,128)(2,1)}, bf16[288,768]{1,0:T(8,128)(2,1)S(1)}, u32[]{:S(2)}, u32[]{:S(2)}) collective-permute-start(bf16[288,768]{1,0:T(8,128)(2,1)} %collective-permute-done.23.rest_0_), channel_id=1, source_target_pairs={{0,4},{2,6},{4,0},{6,2},{8,12},{10,14},{12,8},{14,10},{16,20},{18,... | collective-permute-start | bytes 1327112 | tf_op jit(solution)/shard_map/ppermute | solution.py:384
  86.4 17.5 %collective-permute-start.26 = (bf16[288,768]{1,0:T(8,128)(2,1)}, bf16[288,768]{1,0:T(8,128)(2,1)S(1)}, u32[]{:S(2)}, u32[]{:S(2)}) collective-permute-start(bf16[288,768]{1,0:T(8,128)(2,1)} %collective-permute-done.18.rest_3_), channel_id=1, source_target_pairs={{0,8},{2,10},{4,12},{6,14},{8,0},{10,2},{12,4},{14,6},{16,24},{18,... | collective-permute-start | bytes 1327112 | tf_op jit(solution)/shard_map/ppermute | solution.py:385
  87.7 17.5 %collective-permute-start.27 = (bf16[288,768]{1,0:T(8,128)(2,1)}, bf16[288,768]{1,0:T(8,128)(2,1)S(1)}, u32[]{:S(2)}, u32[]{:S(2)}) collective-permute-start(bf16[288,768]{1,0:T(8,128)(2,1)} %collective-permute-done.23.rest_0_), channel_id=1, source_target_pairs={{0,2},{2,0},{4,6},{6,4},{8,10},{10,8},{12,14},{14,12},{16,18},{18,... | collective-permute-start | bytes 1327112 | tf_op jit(solution)/shard_map/ppermute | solution.py:392
  97.6 17.0 %collective-permute-start.35 = (bf16[4,96,768]{2,1,0:T(8,128)(2,1)S(1)}, bf16[4,96,768]{2,1,0:T(8,128)(2,1)S(1)}, u32[]{:S(2)}, u32[]{:S(2)}) collective-permute-start(bf16[4,96,768]{2,1,0:T(8,128)(2,1)S(1)} %pad_maximum_fusion.rest_0_), channel_id=1, source_target_pairs={{0,4},{2,6},{4,0},{6,2},{8,12},{10,14},{12,8},{14,10},{16,20},{18,... | collective-permute-start | bytes 1769480 | tf_op jit(solution)/shard_map/ppermute | solution.py:390
  106.0 20.2 %collective-permute-start.34 = (bf16[4,96,768]{2,1,0:T(8,128)(2,1)S(1)}, bf16[4,96,768]{2,1,0:T(8,128)(2,1)}, u32[]{:S(2)}, u32[]{:S(2)}) collective-permute-start(bf16[4,96,768]{2,1,0:T(8,128)(2,1)S(1)} %pad_maximum_fusion.rest_0_), channel_id=1, source_target_pairs={{0,1},{1,0},{2,3},{3,2},{4,5},{5,4},{6,7},{7,6},{8,9},{9,8},{10,11... | collective-permute-start | bytes 1769480 | tf_op jit(solution)/shard_map/ppermute | solution.py:390
  109.3 19.5 %collective-permute-start.19 = (bf16[288,768]{1,0:T(8,128)(2,1)}, bf16[288,768]{1,0:T(8,128)(2,1)}, u32[]{:S(2)}, u32[]{:S(2)}) collective-permute-start(bf16[288,768]{1,0:T(8,128)(2,1)} %collective-permute-done.8.rest_0_), channel_id=1, source_target_pairs={{0,2},{2,0},{4,6},{6,4},{8,10},{10,8},{12,14},{14,12},{16,18},{18,... | collective-permute-start | bytes 1327112 | tf_op jit(solution)/shard_map/ppermute | solution.py:388
  110.0 20.1 %collective-permute-start.21 = (bf16[288,768]{1,0:T(8,128)(2,1)}, bf16[288,768]{1,0:T(8,128)(2,1)}, u32[]{:S(2)}, u32[]{:S(2)}) collective-permute-start(bf16[288,768]{1,0:T(8,128)(2,1)} %collective-permute-done.17.rest_2_), channel_id=1, source_target_pairs={{0,2},{2,0},{4,6},{6,4},{8,10},{10,8},{12,14},{14,12},{16,18},{18,... | collective-permute-start | bytes 1327112 | tf_op jit(solution)/shard_map/ppermute | solution.py:388
  111.3 18.9 %collective-permute-start.20 = (bf16[288,768]{1,0:T(8,128)(2,1)}, bf16[288,768]{1,0:T(8,128)(2,1)}, u32[]{:S(2)}, u32[]{:S(2)}) collective-permute-start(bf16[288,768]{1,0:T(8,128)(2,1)} %collective-permute-done.9.rest_1_), channel_id=1, source_target_pairs={{0,2},{2,0},{4,6},{6,4},{8,10},{10,8},{12,14},{14,12},{16,18},{18,... | collective-permute-start | bytes 1327112 | tf_op jit(solution)/shard_map/ppermute | solution.py:388
  114.6 16.1 %collective-permute-start.22 = (bf16[288,768]{1,0:T(8,128)(2,1)}, bf16[288,768]{1,0:T(8,128)(2,1)}, u32[]{:S(2)}, u32[]{:S(2)}) collective-permute-start(bf16[288,768]{1,0:T(8,128)(2,1)} %collective-permute-done.18.rest_3_), channel_id=1, source_target_pairs={{0,2},{2,0},{4,6},{6,4},{8,10},{10,8},{12,14},{14,12},{16,18},{18,... | collective-permute-start | bytes 1327112 | tf_op jit(solution)/shard_map/ppermute | solution.py:388
  130.2 18.6 %collective-permute-start.38 = (bf16[4,96,768]{2,1,0:T(8,128)(2,1)S(1)}, bf16[4,96,768]{2,1,0:T(8,128)(2,1)S(1)}, u32[]{:S(2)}, u32[]{:S(2)}) collective-permute-start(bf16[4,96,768]{2,1,0:T(8,128)(2,1)S(1)} %pad_maximum_fusion.rest_0_), channel_id=1, source_target_pairs={{0,2},{2,0},{4,6},{6,4},{8,10},{10,8},{12,14},{14,12},{16,18},{18,... | collective-permute-start | bytes 1769480 | tf_op jit(solution)/shard_map/ppermute | solution.py:396
  130.2 18.5 %collective-permute-start.39 = (bf16[4,96,768]{2,1,0:T(8,128)(2,1)}, bf16[4,96,768]{2,1,0:T(8,128)(2,1)S(1)}, u32[]{:S(2)}, u32[]{:S(2)}) collective-permute-start(bf16[4,96,768]{2,1,0:T(8,128)(2,1)} %collective-permute-done.34.rest_1_), channel_id=1, source_target_pairs={{0,2},{2,0},{4,6},{6,4},{8,10},{10,8},{12,14},{14,12},{16,18},{18,... | collective-permute-start | bytes 1769480 | tf_op jit(solution)/shard_map/ppermute | solution.py:396
  130.7 18.0 %collective-permute-start.40 = (bf16[4,96,768]{2,1,0:T(8,128)(2,1)S(1)}, bf16[4,96,768]{2,1,0:T(8,128)(2,1)S(1)}, u32[]{:S(2)}, u32[]{:S(2)}) collective-permute-start(bf16[4,96,768]{2,1,0:T(8,128)(2,1)S(1)} %collective-permute-done.35.rest_2_), channel_id=1, source_target_pairs={{0,2},{2,0},{4,6},{6,4},{8,10},{10,8},{12,14},{14,12},{16,18},{18,... | collective-permute-start | bytes 1769480 | tf_op jit(solution)/shard_map/ppermute | solution.py:396
  (52 other events, 246.3 us)

commit v3 on v2

--- a/solution.py
+++ b/solution.py
@@ -72,8 +72,8 @@
     return jnp.where(live_mask, finished, latents)
 
 
-def anyspec():
-    return pl.BlockSpec(memory_space=pl.ANY)
+def hspec():
+    return pl.BlockSpec(memory_space=pltpu.HBM)
 
 
 def vspec():
@@ -86,6 +86,10 @@
 
 def params(mib):
     return pltpu.CompilerParams(vmem_limit_bytes=mib * 1024 * 1024)
+
+
+def far(value):
+    return pltpu.with_memory_space_constraint(value, pltpu.HBM)
 
 
 def cost(flops, moved):
@@ -198,13 +202,13 @@
             jax.ShapeDtypeStruct((count, chunk, tokens), BF),
             jax.ShapeDtypeStruct((count, tokens, chunk), BF),
         ),
-        in_specs=[sspec(), sspec(), vspec()] + [anyspec()] * 8,
+        in_specs=[sspec(), sspec(), vspec()] + [hspec()] * 8,
         out_specs=(vspec(), vspec()),
         scratch_shapes=[pltpu.VMEM((rows, width), BF), pltpu.SemaphoreType.DMA((8,))],
         compiler_params=params(24),
         cost_estimate=cost(2 * rows * width * tokens, 2 * (rows + tokens) * width),
         name="project",
-    )(place, plane, normed, *pieces)
+    )(place, plane, normed, *map(far, pieces))
 
 
 def attend_kernel(
@@ -269,7 +273,7 @@
     return pl.pallas_call(
         attend_kernel,
         out_shape=jax.ShapeDtypeStruct((tokens, width), BF),
-        in_specs=[sspec()] * 2 + [anyspec()] * 8,
+        in_specs=[sspec()] * 2 + [hspec()] * 8,
         out_specs=vspec(),
         scratch_shapes=[
             pltpu.VMEM((4, chunk, tokens), BF),
@@ -281,7 +285,7 @@
         compiler_params=params(24),
         cost_estimate=cost(40 * 128 * tokens * width, 8 * tokens * width),
         name="attend",
-    )(planes, window_len, *[a for pair in parts for a in pair])
+    )(planes, window_len, *[far(a) for pair in parts for a in pair])
 
 
 def output_kernel(at_ref, planes_ref, lens_ref, live_ref, att_ref, lat_ref, *rest):
@@ -336,13 +340,13 @@
     return pl.pallas_call(
         output_kernel,
         out_shape=jax.ShapeDtypeStruct((tokens, width), BF),
-        in_specs=[sspec()] * 4 + [vspec()] * 2 + [anyspec()] * 10,
+        in_specs=[sspec()] * 4 + [vspec()] * 2 + [hspec()] * 10,
         out_specs=vspec(),
         scratch_shapes=[pltpu.VMEM((width, width), BF), pltpu.SemaphoreType.DMA((32,))],
         compiler_params=params(32),
         cost_estimate=cost(2 * width * width * tokens, 2 * width * (width + 3 * tokens)),
         name="output",
-    )(place, planes, lens, live, attended, latents, *pieces)
+    )(place, planes, lens, live, attended, latents, *map(far, pieces))
 
 
 def after(value, *earlier):
@@ -366,35 +370,33 @@
 
     u0 = w_qkv.T
     o0 = w_out.T
-    u1, x0, y0 = z1(u0), xs(u0), ys(u0)
-    u2 = z2(u0)
+    u1, x0, y0, u2 = z1(u0), xs(u0), ys(u0), z2(u0)
+    o1, o2 = z1(after(o0, x0)), z2(after(o0, x0))
     normed = normed_columns(latents, window_index, norm_gain)
-    y0, normed = lax.optimization_barrier((y0, normed))
-    d0 = xs(y0)
+    d0 = xs(after(y0, normed))
     y1 = ys(u1)
-    u3 = z3(after(u0, u2, y0))
-    x2, y2 = xs(after(u2, d0)), ys(u2)
+    x2, y2, u3 = xs(u2), ys(u2), z1(u2)
+    x1 = xs(after(u1, d0))
     d1 = z1(d0)
+    o3 = z1(after(o2, d0))
     s0 = [u0, x0, y0, d0]
     p0 = project(place, planes[0:1], normed, s0 + [core(a) for a in s0])
     d2 = ys(after(x2, p0[0]))
-    x1 = xs(after(u1, x2))
+    x3, y3 = xs(u3), ys(u3)
+    o4 = jnp.stack([after(o0, u3), o1, o2, o3])
+    xo, yo = xs(o4), ys(o4)
     s1 = [u1, x1, y1, d1]
     p1 = project(place, planes[1:2], normed, s1 + [core(a) for a in s1])
-    y3, x3 = ys(after(u3, d2)), xs(after(u3, x1))
     d3 = z1(d2)
-    o1, o2, o3 = (f(after(o0, u3)) for f in (z1, z2, z3))
     s2 = [u2, x2, y2, d2]
     p2 = project(place, planes[2:3], normed, s2 + [core(a) for a in s2])
-    o4 = after(jnp.stack([o0, o1, o2, o3]), p1[0])
-    xo, yo = xs(o4), ys(o4)
-    s3 = [u3, x3, y3, d3]
+    s3 = [u3, after(x3, p1[0]), after(y3, p2[0]), d3]
     p3 = project(place, planes[3:4], normed, s3 + [core(a) for a in s3])
     half = o4.shape[0] // 2
-    da, db = xs(after(yo[:half], p3[0])), ys(xo[half:])
+    da, db = xs(yo[:half]), ys(xo[half:])
     so = [o4, xo, yo, da, db]
     so = so + [core(a) for a in so]
-    attended = attend(planes, window_len, (p0, p1, p2, p3))
+    attended = attend(planes, after(window_len, xo, yo), (p0, p1, p2, p3))
     flat = latents.reshape(blocks * rows, width)
     out = output(place, planes, window_len, live_blocks, attended, flat, so)
     return out.reshape(latents.shape)

time: 159 us -> 147 us (0.925)
  local copies, waits for them, and re-layouts: 30.5 us -> 16.4 us
  Pallas kernels: 47.4 us -> 51 us
  starting transfers between devices: 34.4 us -> 31.8 us
  waiting for transfers between devices: 43.5 us -> 46 us
    unnamed x82 -> x62, local copies, waits for them, and re-layouts: 28.8 us -> 14.7 us
    ppermute x1, waiting for transfers between devices: 0.01 us -> 7.83 us  [local(): y1 = ys(u1)]
    ppermute x16, starting transfers between devices: 25.7 us -> 19.7 us  [the longest x4 8.62 us: local(): u1, x0, y0, u2 = (z1(u0), xs(u0), ys(u0), z2(u0))]
    ppermute x16, waiting for transfers between devices: 40.2 us -> 36.4 us  [the longest x4 12.3 us: local(): u1, x0, y0, u2 = (z1(u0), xs(u0), ys(u0), z2(u0))]
    ppermute x2, waiting for transfers between devices: 3.28 us -> 0.01 us  [local(): xo, yo = (xs(o4), ys(o4))]
    ppermute x1, starting transfers between devices: 0.01 us -> 2.24 us  [local(): d1 = z1(d0)]
    ppermute x1, starting transfers between devices: 0.14 us -> 2.33 us  [local(): d3 = z1(d2)]
  transfers between devices with their start and end apart: 43 -> 43, of which waited for: 6 -> 14; matrix products, arithmetic and copies ran while one was open for 2% -> 1% of each run, Pallas kernels for 24% -> 28%
where the time goes in v3:
time: 147 us; the launch traced here: 146 us
  Pallas kernels  51 us (35%)
  waiting for transfers between devices  46 us (31%)
  starting transfers between devices  31.8 us (22%)
  local copies, waits for them, and re-layouts  16.4 us (11%)
    pallas_call x4, Pallas kernels, project(): pl.pallas_call(functools.partial(project_kernel, 4, 8), out_shape=(jax.Sh...  25.8 us
    unnamed x62, local copies, waits for them, and re-layouts  14.7 us
    ppermute x4, waiting for transfers between devices, local(): u1, x0, y0, u2 = (z1(u0), xs(u0), ys(u0), z2(u0))  12.3 us
    pallas_call x1, Pallas kernels, attend(): pl.pallas_call(attend_kernel, out_shape=jax.ShapeDtypeStruct((tokens, wid...  11.3 us
    pallas_call x1, Pallas kernels, output(): pl.pallas_call(output_kernel, out_shape=jax.ShapeDtypeStruct((tokens, wid...  10.6 us
    ppermute x4, starting transfers between devices, local(): u1, x0, y0, u2 = (z1(u0), xs(u0), ys(u0), z2(u0))  8.62 us
    ppermute x1, waiting for transfers between devices, local(): x1 = xs(after(u1, d0))  7.87 us
    ppermute x1, waiting for transfers between devices, local(): y1 = ys(u1)  7.83 us
  transfers between devices with their start and end apart: 43, of which 14 were waited for; matrix products, arithmetic and copies ran while one was open for 1% of the time, Pallas kernels for 28%

profile of v3, /device:TPU:0, one launch (start us, length us, event | category | flops | bytes accessed | tf_op | source)
XLA Modules:
  0.0 146.4 jit_solution(3088697762641308602)
XLA Ops:
  0.0 3.0 %collective-permute-start.14 = (bf16[288,768]{1,0:T(8,128)(2,1)}, bf16[288,768]{1,0:T(8,128)(2,1)S(1)}, u32[]{:S(2)}, u32[]{:S(2)}) collective-permute-start(bf16[288,768]{1,0:T(8,128)(2,1)} %bitcast.22), channel_id=1, source_target_pairs={{0,8},{2,10},{4,12},{6,14},{8,0},{10,2},{12,4},{14,6},{16,24},{18,... | collective-permute-start | bytes 1327112 | tf_op jit(solution)/shard_map/ppermute | solution.py:373
  3.0 1.5 %collective-permute-start.5 = (bf16[288,768]{1,0:T(8,128)(2,1)}, bf16[288,768]{1,0:T(8,128)(2,1)S(1)}, u32[]{:S(2)}, u32[]{:S(2)}) collective-permute-start(bf16[288,768]{1,0:T(8,128)(2,1)} %bitcast.23), channel_id=1, source_target_pairs={{0,4},{2,6},{4,0},{6,2},{8,12},{10,14},{12,8},{14,10},{16,20},{18,... | collective-permute-start | bytes 1327112 | tf_op jit(solution)/shard_map/ppermute | solution.py:373
  4.5 1.5 %collective-permute-start.2 = (bf16[288,768]{1,0:T(8,128)(2,1)}, bf16[288,768]{1,0:T(8,128)(2,1)S(1)}, u32[]{:S(2)}, u32[]{:S(2)}) collective-permute-start(bf16[288,768]{1,0:T(8,128)(2,1)} %bitcast.24), channel_id=1, source_target_pairs={{0,1},{1,0},{2,3},{3,2},{4,5},{5,4},{6,7},{7,6},{8,9},{9,8},{10,11... | collective-permute-start | bytes 1327112 | tf_op jit(solution)/shard_map/ppermute | solution.py:373
  6.0 2.6 %collective-permute-start = (bf16[288,768]{1,0:T(8,128)(2,1)}, bf16[288,768]{1,0:T(8,128)(2,1)}, u32[]{:S(2)}, u32[]{:S(2)}) collective-permute-start(bf16[288,768]{1,0:T(8,128)(2,1)} %bitcast.26), channel_id=1, source_target_pairs={{0,16},{2,18},{4,20},{6,22},{8,24},{10,26},{12,28},{14,30},{16,0},... | collective-permute-start | bytes 1327112 | tf_op jit(solution)/shard_map/ppermute | solution.py:373
  9.4 1.7 %copy-done = bf16[6,128,1536]{2,1,0:T(8,128)(2,1)S(1)} copy-done((bf16[6,128,1536]{2,1,0:T(8,128)(2,1)S(1)}, bf16[6,128,1536]{2,1,0:T(8,128)(2,1)}, u32[]{:S(2)}) %copy-start) | copy-done | bytes 2359320
  11.7 3.3 %norm.1.n_ref = bf16[1536,768]{1,0:T(8,128)(2,1)S(1)} custom-call(s32[12]{0:T(128)S(1)} %copy-done.2, bf16[6,128,1536]{2,1,0:T(8,128)(2,1)S(1)} %copy-done, f32[1,1536]{1,0:T(1,128)S(1)} %reshape.20.gain_ref, f32[1,384]{1,0:T(1,128)S(1)} %multiply_exponential_fusion.freq_ref), custom_call_target="tpu_custom_call" | custom-call | flops 47185920 | bytes 4718592 | tf_op jit(solution)/shard_map/norm/pallas_call | solution.py:138
  14.9 3.9 %collective-permute-done.14.rest_0_ = bf16[288,768]{1,0:T(8,128)(2,1)S(1)} collective-permute-done((bf16[288,768]{1,0:T(8,128)(2,1)}, bf16[288,768]{1,0:T(8,128)(2,1)S(1)}, u32[]{:S(2)}, u32[]{:S(2)}) %collective-permute-start.14) | collective-permute-done | bytes 442400 | tf_op jit(solution)/shard_map/ppermute | solution.py:373
  18.8 2.7 %collective-permute-start.6 = (bf16[288,768]{1,0:T(8,128)(2,1)S(1)}, bf16[288,768]{1,0:T(8,128)(2,1)}, u32[]{:S(2)}, u32[]{:S(2)}) collective-permute-start(bf16[288,768]{1,0:T(8,128)(2,1)S(1)} %collective-permute-done.5.rest_2_), channel_id=1, source_target_pairs={{0,1},{1,0},{2,3},{3,2},{4,5},{5,4},{6,7},{7,6},{8,9},{9,8},{10,11... | collective-permute-start | bytes 1327112 | tf_op jit(solution)/shard_map/ppermute | solution.py:376
  22.2 2.4 %collective-permute-start.3 = (bf16[96,768]{1,0:T(8,128)(2,1)S(1)}, bf16[96,768]{1,0:T(8,128)(2,1)S(1)}, u32[]{:S(2)}, u32[]{:S(2)}) collective-permute-start(bf16[96,768]{1,0:T(8,128)(2,1)S(1)} %bitcast.17), channel_id=1, source_target_pairs={{0,8},{2,10},{4,12},{6,14},{8,0},{10,2},{12,4},{14,6},{16,24},{18,... | collective-permute-start | bytes 442376 | tf_op jit(solution)/shard_map/ppermute | solution.py:374
  24.6 8.4 %collective-permute-done.rest_0_ = bf16[288,768]{1,0:T(8,128)(2,1)} collective-permute-done((bf16[288,768]{1,0:T(8,128)(2,1)}, bf16[288,768]{1,0:T(8,128)(2,1)}, u32[]{:S(2)}, u32[]{:S(2)}) %collective-permute-start) | collective-permute-done | bytes 442400 | tf_op jit(solution)/shard_map/ppermute | solution.py:373
  33.5 2.2 %collective-permute-done.4 = bf16[96,768]{1,0:T(8,128)(2,1)S(1)} collective-permute-done((bf16[96,768]{1,0:T(8,128)(2,1)S(1)}, bf16[96,768]{1,0:T(8,128)(2,1)S(1)}, u32[]{:S(2)}, u32[]{:S(2)}) %collective-permute-start.4) | collective-permute-done | bytes 147488 | tf_op jit(solution)/shard_map/ppermute | solution.py:374
  36.6 7.8 %collective-permute-done.16.rest_2_ = bf16[288,768]{1,0:T(8,128)(2,1)} collective-permute-done((bf16[288,768]{1,0:T(8,128)(2,1)S(1)}, bf16[288,768]{1,0:T(8,128)(2,1)}, u32[]{:S(2)}, u32[]{:S(2)}) %collective-permute-start.16) | collective-permute-done | bytes 442400 | tf_op jit(solution)/shard_map/ppermute | solution.py:377
  46.0 2.7 %collective-permute-done.22.rest_1_ = bf16[288,768]{1,0:T(8,128)(2,1)} collective-permute-done((bf16[288,768]{1,0:T(8,128)(2,1)}, bf16[288,768]{1,0:T(8,128)(2,1)}, u32[]{:S(2)}, u32[]{:S(2)}) %collective-permute-start.22) | collective-permute-done | bytes 442400 | tf_op jit(solution)/shard_map/ppermute | solution.py:378
  48.7 6.3 %project.4 = (bf16[3,384,768]{2,1,0:T(8,128)(2,1)S(1)}, bf16[3,768,384]{2,1,0:T(8,128)(2,1)S(1)}) custom-call(s32[3]{0:T(128)S(1)} %pad_add_fusion.at_ref, s32[1]{0:T(128)} %bitcast.3.plane_ref, bf16[1536,768]{1,0:T(8,128)(2,1)S(1)} %norm.1.n_ref, bf16[288,768]{1,0:T(8,128)(2,1)} %bitcast.27, bf16[288,768]{1,0:T(8,128)(2,1)} %copy-done.21, ...), custom_call_target="tpu_custom_call" | custom-call | flops 2717908992 | bytes 5898240 | tf_op jit(solution)/shard_map/project/pallas_call | solution.py:199
  58.5 2.2 %collective-permute-start.17 = (bf16[288,768]{1,0:T(8,128)(2,1)}, bf16[288,768]{1,0:T(8,128)(2,1)}, u32[]{:S(2)}, u32[]{:S(2)}) collective-permute-start(bf16[288,768]{1,0:T(8,128)(2,1)} %collective-permute-done.6.rest_3_), channel_id=1, source_target_pairs={{0,8},{2,10},{4,12},{6,14},{8,0},{10,2},{12,4},{14,6},{16,24},{18,... | collective-permute-start | bytes 1327112 | tf_op jit(solution)/shard_map/ppermute | solution.py:380
  61.1 1.9 %collective-permute-start.24 = (bf16[288,768]{1,0:T(8,128)(2,1)}, bf16[288,768]{1,0:T(8,128)(2,1)}, u32[]{:S(2)}, u32[]{:S(2)}) collective-permute-start(bf16[288,768]{1,0:T(8,128)(2,1)} %collective-permute-done.22.rest_1_), channel_id=1, source_target_pairs={{0,4},{2,6},{4,0},{6,2},{8,12},{10,14},{12,8},{14,10},{16,20},{18,... | collective-permute-start | bytes 1327112 | tf_op jit(solution)/shard_map/ppermute | solution.py:384
  63.2 7.9 %collective-permute-done.15.rest_1_ = bf16[288,768]{1,0:T(8,128)(2,1)} collective-permute-done((bf16[288,768]{1,0:T(8,128)(2,1)S(1)}, bf16[288,768]{1,0:T(8,128)(2,1)}, u32[]{:S(2)}, u32[]{:S(2)}) %collective-permute-start.15) | collective-permute-done | bytes 442400 | tf_op jit(solution)/shard_map/ppermute | solution.py:379
  71.6 1.6 %collective-permute-done.24.rest_3_ = bf16[288,768]{1,0:T(8,128)(2,1)} collective-permute-done((bf16[288,768]{1,0:T(8,128)(2,1)}, bf16[288,768]{1,0:T(8,128)(2,1)}, u32[]{:S(2)}, u32[]{:S(2)}) %collective-permute-start.24) | collective-permute-done | bytes 442400 | tf_op jit(solution)/shard_map/ppermute | solution.py:384
  74.1 1.6 %collective-permute-start.9 = (bf16[4,96,768]{2,1,0:T(8,128)(2,1)S(1)}, bf16[4,96,768]{2,1,0:T(8,128)(2,1)}, u32[]{:S(2)}, u32[]{:S(2)}) collective-permute-start(bf16[4,96,768]{2,1,0:T(8,128)(2,1)S(1)} %pad_maximum_fusion.rest_0_), channel_id=1, source_target_pairs={{0,4},{2,6},{4,0},{6,2},{8,12},{10,14},{12,8},{14,10},{16,20},{18,... | collective-permute-start | bytes 1769480 | tf_op jit(solution)/shard_map/ppermute | solution.py:387
  75.7 4.0 %collective-permute-done.29.rest_1_ = bf16[288,768]{1,0:T(8,128)(2,1)} collective-permute-done((bf16[288,768]{1,0:T(8,128)(2,1)}, bf16[288,768]{1,0:T(8,128)(2,1)}, u32[]{:S(2)}, u32[]{:S(2)}) %collective-permute-start.29) | collective-permute-done | bytes 442400 | tf_op jit(solution)/shard_map/ppermute | solution.py:385
  80.6 2.3 %collective-permute-start.31 = (bf16[288,768]{1,0:T(8,128)(2,1)}, bf16[288,768]{1,0:T(8,128)(2,1)}, u32[]{:S(2)}, u32[]{:S(2)}) collective-permute-start(bf16[288,768]{1,0:T(8,128)(2,1)} %collective-permute-done.24.rest_3_), channel_id=1, source_target_pairs={{0,8},{2,10},{4,12},{6,14},{8,0},{10,2},{12,4},{14,6},{16,24},{18,... | collective-permute-start | bytes 1327112 | tf_op jit(solution)/shard_map/ppermute | solution.py:390
  83.0 6.6 %project.5 = (bf16[3,384,768]{2,1,0:T(8,128)(2,1)S(1)}, bf16[3,768,384]{2,1,0:T(8,128)(2,1)S(1)}) custom-call(s32[3]{0:T(128)S(1)} %pad_add_fusion.at_ref, s32[1]{0:T(128)} %bitcast.4.plane_ref, bf16[1536,768]{1,0:T(8,128)(2,1)S(1)} %norm.1.n_ref, bf16[288,768]{1,0:T(8,128)(2,1)} %copy-done.18, bf16[288,768]{1,0:T(8,128)(2,1)} %collective-permute-done.15.rest_1_, ...), custom_call_target="tpu_custom_call" | custom-call | flops 2717908992 | bytes 5898240 | tf_op jit(solution)/shard_map/project/pallas_call | solution.py:199
  90.8 6.6 %project.6 = (bf16[3,384,768]{2,1,0:T(8,128)(2,1)S(1)}, bf16[3,768,384]{2,1,0:T(8,128)(2,1)S(1)}) custom-call(s32[3]{0:T(128)S(1)} %pad_add_fusion.at_ref, s32[1]{0:T(128)} %bitcast.5.plane_ref, bf16[1536,768]{1,0:T(8,128)(2,1)S(1)} %norm.1.n_ref, bf16[288,768]{1,0:T(8,128)(2,1)} %collective-permute-done.rest_0_, ...), custom_call_target="tpu_custom_call" | custom-call | flops 2717908992 | bytes 5898240 | tf_op jit(solution)/shard_map/project/pallas_call | solution.py:199
  98.7 1.3 copy-done.9
  101.6 1.7 %collective-permute-start.36 = (bf16[2,96,768]{2,1,0:T(8,128)(2,1)S(1)}, bf16[2,96,768]{2,1,0:T(8,128)(2,1)}, u32[]{:S(2)}, u32[]{:S(2)}) collective-permute-start(bf16[2,96,768]{2,1,0:T(8,128)(2,1)S(1)} %slice.8), channel_id=1, source_target_pairs={{0,1},{1,0},{2,3},{3,2},{4,5},{5,4},{6,7},{7,6},{8,9},{9,8},{10,11... | collective-permute-start | bytes 884744 | tf_op jit(solution)/shard_map/ppermute | solution.py:396
  104.1 1.5 %collective-permute-start.37 = (bf16[2,96,768]{2,1,0:T(8,128)(2,1)S(1)}, bf16[2,96,768]{2,1,0:T(8,128)(2,1)}, u32[]{:S(2)}, u32[]{:S(2)}) collective-permute-start(bf16[2,96,768]{2,1,0:T(8,128)(2,1)S(1)} %slice.9), channel_id=1, source_target_pairs={{0,4},{2,6},{4,0},{6,2},{8,12},{10,14},{12,8},{14,10},{16,20},{18,... | collective-permute-start | bytes 884744 | tf_op jit(solution)/shard_map/ppermute | solution.py:396
  106.3 4.8 %collective-permute-done.36.rest_3_ = bf16[2,96,768]{2,1,0:T(8,128)(2,1)} collective-permute-done((bf16[2,96,768]{2,1,0:T(8,128)(2,1)S(1)}, bf16[2,96,768]{2,1,0:T(8,128)(2,1)}, u32[]{:S(2)}, u32[]{:S(2)}) %collective-permute-start.36) | collective-permute-done | bytes 294944 | tf_op jit(solution)/shard_map/ppermute | solution.py:396
  111.1 2.1 %collective-permute-done.37.rest_4_ = bf16[2,96,768]{2,1,0:T(8,128)(2,1)} collective-permute-done((bf16[2,96,768]{2,1,0:T(8,128)(2,1)S(1)}, bf16[2,96,768]{2,1,0:T(8,128)(2,1)}, u32[]{:S(2)}, u32[]{:S(2)}) %collective-permute-start.37) | collective-permute-done | bytes 294944 | tf_op jit(solution)/shard_map/ppermute | solution.py:396
  114.3 6.3 %project.7 = (bf16[3,384,768]{2,1,0:T(8,128)(2,1)S(1)}, bf16[3,768,384]{2,1,0:T(8,128)(2,1)S(1)}) custom-call(s32[3]{0:T(128)S(1)} %pad_add_fusion.at_ref, s32[1]{0:T(128)} %bitcast.6.plane_ref, bf16[1536,768]{1,0:T(8,128)(2,1)S(1)} %norm.1.n_ref, bf16[288,768]{1,0:T(8,128)(2,1)} %collective-permute-done.1.rest_0_, ...), custom_call_target="tpu_custom_call" | custom-call | flops 2717908992 | bytes 5898240 | tf_op jit(solution)/shard_map/project/pallas_call | solution.py:199
  121.8 1.3 copy-done.11
  123.1 11.3 %attend.1.att_ref = bf16[768,1536]{1,0:T(8,128)(2,1)S(1)} custom-call(s32[4]{0:T(128)S(1)} %pad_add_fusion.1.planes_ref, s32[12]{0:T(128)S(1)} %copy-done.3, bf16[3,384,768]{2,1,0:T(8,128)(2,1)} %copy-done.4, bf16[3,768,384]{2,1,0:T(8,128)(2,1)} %copy-done.5, bf16[3,384,768]{2,1,0:T(8,128)(2,1)} %copy-done.6, bf16[3,768,384]{2,1,0:T(8,128)(2,1)} %copy-done.7, ...), custom_call_target="tpu_custom_call" | custom-call | flops 6039797760 | bytes 9437184 | tf_op jit(solution)/shard_map/attend/pallas_call | solution.py:273
  135.8 10.6 %output.1 = bf16[768,1536]{1,0:T(8,128)(2,1)} custom-call(s32[3]{0:T(128)S(1)} %pad_add_fusion.at_ref, s32[4]{0:T(128)S(1)} %pad_add_fusion.1.planes_ref, s32[12]{0:T(128)S(1)} %copy-done.3, s32[1]{0:T(128)S(6)} %copy.8.live_ref, bf16[768,1536]{1,0:T(8,128)(2,1)S(1)} %attend.1.att_ref, bf16[768,1536]{1,0:T(8,128)(2,1)S(1)} %bitcast.15, ...), custom_call_target="tpu_custom_call" | custom-call | flops 3623878656 | bytes 11796480 | tf_op jit(solution)/shard_map/output/pallas_call | solution.py:340
  (130 shorter events, 19.9 us)
Async XLA Ops:
  0.0 18.8 %collective-permute-start.14 = (bf16[288,768]{1,0:T(8,128)(2,1)}, bf16[288,768]{1,0:T(8,128)(2,1)S(1)}, u32[]{:S(2)}, u32[]{:S(2)}) collective-permute-start(bf16[288,768]{1,0:T(8,128)(2,1)} %bitcast.22), channel_id=1, source_target_pairs={{0,8},{2,10},{4,12},{6,14},{8,0},{10,2},{12,4},{14,6},{16,24},{18,... | collective-permute-start | bytes 1327112 | tf_op jit(solution)/shard_map/ppermute | solution.py:373
  3.0 15.8 %collective-permute-start.5 = (bf16[288,768]{1,0:T(8,128)(2,1)}, bf16[288,768]{1,0:T(8,128)(2,1)S(1)}, u32[]{:S(2)}, u32[]{:S(2)}) collective-permute-start(bf16[288,768]{1,0:T(8,128)(2,1)} %bitcast.23), channel_id=1, source_target_pairs={{0,4},{2,6},{4,0},{6,2},{8,12},{10,14},{12,8},{14,10},{16,20},{18,... | collective-permute-start | bytes 1327112 | tf_op jit(solution)/shard_map/ppermute | solution.py:373
  4.5 17.0 %collective-permute-start.2 = (bf16[288,768]{1,0:T(8,128)(2,1)}, bf16[288,768]{1,0:T(8,128)(2,1)S(1)}, u32[]{:S(2)}, u32[]{:S(2)}) collective-permute-start(bf16[288,768]{1,0:T(8,128)(2,1)} %bitcast.24), channel_id=1, source_target_pairs={{0,1},{1,0},{2,3},{3,2},{4,5},{5,4},{6,7},{7,6},{8,9},{9,8},{10,11... | collective-permute-start | bytes 1327112 | tf_op jit(solution)/shard_map/ppermute | solution.py:373
  6.0 16.2 %collective-permute-start.10 = (bf16[288,768]{1,0:T(8,128)(2,1)}, bf16[288,768]{1,0:T(8,128)(2,1)S(1)}, u32[]{:S(2)}, u32[]{:S(2)}) collective-permute-start(bf16[288,768]{1,0:T(8,128)(2,1)} %bitcast.25), channel_id=1, source_target_pairs={{0,2},{2,0},{4,6},{6,4},{8,10},{10,8},{12,14},{14,12},{16,18},{18,... | collective-permute-start | bytes 1327112 | tf_op jit(solution)/shard_map/ppermute | solution.py:383
  6.0 27.0 %collective-permute-start = (bf16[288,768]{1,0:T(8,128)(2,1)}, bf16[288,768]{1,0:T(8,128)(2,1)}, u32[]{:S(2)}, u32[]{:S(2)}) collective-permute-start(bf16[288,768]{1,0:T(8,128)(2,1)} %bitcast.26), channel_id=1, source_target_pairs={{0,16},{2,18},{4,20},{6,22},{8,24},{10,26},{12,28},{14,30},{16,0},... | collective-permute-start | bytes 1327112 | tf_op jit(solution)/shard_map/ppermute | solution.py:373
  18.8 17.4 %collective-permute-start.18 = (bf16[288,768]{1,0:T(8,128)(2,1)S(1)}, bf16[288,768]{1,0:T(8,128)(2,1)S(1)}, u32[]{:S(2)}, u32[]{:S(2)}) collective-permute-start(bf16[288,768]{1,0:T(8,128)(2,1)S(1)} %collective-permute-done.14.rest_0_), channel_id=1, source_target_pairs={{0,2},{2,0},{4,6},{6,4},{8,10},{10,8},{12,14},{14,12},{16,18},{18,... | collective-permute-start | bytes 1327112 | tf_op jit(solution)/shard_map/ppermute | solution.py:389
  18.8 17.8 %collective-permute-start.6 = (bf16[288,768]{1,0:T(8,128)(2,1)S(1)}, bf16[288,768]{1,0:T(8,128)(2,1)}, u32[]{:S(2)}, u32[]{:S(2)}) collective-permute-start(bf16[288,768]{1,0:T(8,128)(2,1)S(1)} %collective-permute-done.5.rest_2_), channel_id=1, source_target_pairs={{0,1},{1,0},{2,3},{3,2},{4,5},{5,4},{6,7},{7,6},{8,9},{9,8},{10,11... | collective-permute-start | bytes 1327112 | tf_op jit(solution)/shard_map/ppermute | solution.py:376
  21.5 14.2 %collective-permute-start.4 = (bf16[96,768]{1,0:T(8,128)(2,1)S(1)}, bf16[96,768]{1,0:T(8,128)(2,1)S(1)}, u32[]{:S(2)}, u32[]{:S(2)}) collective-permute-start(bf16[96,768]{1,0:T(8,128)(2,1)S(1)} %bitcast.16), channel_id=1, source_target_pairs={{0,16},{2,18},{4,20},{6,22},{8,24},{10,26},{12,28},{14,30},{16,0},... | collective-permute-start | bytes 442376 | tf_op jit(solution)/shard_map/ppermute | solution.py:374
  22.2 13.5 %collective-permute-start.3 = (bf16[96,768]{1,0:T(8,128)(2,1)S(1)}, bf16[96,768]{1,0:T(8,128)(2,1)S(1)}, u32[]{:S(2)}, u32[]{:S(2)}) collective-permute-start(bf16[96,768]{1,0:T(8,128)(2,1)S(1)} %bitcast.17), channel_id=1, source_target_pairs={{0,8},{2,10},{4,12},{6,14},{8,0},{10,2},{12,4},{14,6},{16,24},{18,... | collective-permute-start | bytes 442376 | tf_op jit(solution)/shard_map/ppermute | solution.py:374
  36.2 12.5 %collective-permute-start.22 = (bf16[288,768]{1,0:T(8,128)(2,1)}, bf16[288,768]{1,0:T(8,128)(2,1)}, u32[]{:S(2)}, u32[]{:S(2)}) collective-permute-start(bf16[288,768]{1,0:T(8,128)(2,1)} %collective-permute-done.rest_0_), channel_id=1, source_target_pairs={{0,1},{1,0},{2,3},{3,2},{4,5},{5,4},{6,7},{7,6},{8,9},{9,8},{10,11... | collective-permute-start | bytes 1327112 | tf_op jit(solution)/shard_map/ppermute | solution.py:378
  44.5 13.0 %collective-permute-start.23 = (bf16[288,768]{1,0:T(8,128)(2,1)}, bf16[288,768]{1,0:T(8,128)(2,1)}, u32[]{:S(2)}, u32[]{:S(2)}) collective-permute-start(bf16[288,768]{1,0:T(8,128)(2,1)} %collective-permute-done.rest_0_), channel_id=1, source_target_pairs={{0,4},{2,6},{4,0},{6,2},{8,12},{10,14},{12,8},{14,10},{16,20},{18,... | collective-permute-start | bytes 1327112 | tf_op jit(solution)/shard_map/ppermute | solution.py:378
  45.0 12.9 %collective-permute-start.25 = (bf16[288,768]{1,0:T(8,128)(2,1)}, bf16[288,768]{1,0:T(8,128)(2,1)}, u32[]{:S(2)}, u32[]{:S(2)}) collective-permute-start(bf16[288,768]{1,0:T(8,128)(2,1)} %collective-permute-done.rest_0_), channel_id=1, source_target_pairs={{0,2},{2,0},{4,6},{6,4},{8,10},{10,8},{12,14},{14,12},{16,18},{18,... | collective-permute-start | bytes 1327112 | tf_op jit(solution)/shard_map/ppermute | solution.py:392
  45.1 13.4 %collective-permute-start.1 = (bf16[288,768]{1,0:T(8,128)(2,1)}, bf16[288,768]{1,0:T(8,128)(2,1)}, u32[]{:S(2)}, u32[]{:S(2)}) collective-permute-start(bf16[288,768]{1,0:T(8,128)(2,1)} %collective-permute-done.rest_0_), channel_id=1, source_target_pairs={{0,8},{2,10},{4,12},{6,14},{8,0},{10,2},{12,4},{14,6},{16,24},{18,... | collective-permute-start | bytes 1327112 | tf_op jit(solution)/shard_map/ppermute | solution.py:378
  48.7 12.4 %collective-permute-start.7 = (bf16[96,768]{1,0:T(8,128)(2,1)S(1)}, bf16[96,768]{1,0:T(8,128)(2,1)S(1)}, u32[]{:S(2)}, u32[]{:S(2)}) collective-permute-start(bf16[96,768]{1,0:T(8,128)(2,1)S(1)} %collective-permute-done.4), channel_id=1, source_target_pairs={{0,8},{2,10},{4,12},{6,14},{8,0},{10,2},{12,4},{14,6},{16,24},{18,... | collective-permute-start | bytes 442376 | tf_op jit(solution)/shard_map/ppermute | solution.py:381
  48.7 14.4 %collective-permute-start.20 = (bf16[288,768]{1,0:T(8,128)(2,1)}, bf16[288,768]{1,0:T(8,128)(2,1)S(1)}, u32[]{:S(2)}, u32[]{:S(2)}) collective-permute-start(bf16[288,768]{1,0:T(8,128)(2,1)} %collective-permute-done.16.rest_2_), channel_id=1, source_target_pairs={{0,2},{2,0},{4,6},{6,4},{8,10},{10,8},{12,14},{14,12},{16,18},{18,... | collective-permute-start | bytes 1327112 | tf_op jit(solution)/shard_map/ppermute | solution.py:389
  57.9 13.1 %collective-permute-start.15 = (bf16[288,768]{1,0:T(8,128)(2,1)S(1)}, bf16[288,768]{1,0:T(8,128)(2,1)}, u32[]{:S(2)}, u32[]{:S(2)}) collective-permute-start(bf16[288,768]{1,0:T(8,128)(2,1)S(1)} %collective-permute-done.14.rest_0_), channel_id=1, source_target_pairs={{0,1},{1,0},{2,3},{3,2},{4,5},{5,4},{6,7},{7,6},{8,9},{9,8},{10,11... | collective-permute-start | bytes 1327112 | tf_op jit(solution)/shard_map/ppermute | solution.py:379
  58.5 12.7 %collective-permute-start.17 = (bf16[288,768]{1,0:T(8,128)(2,1)}, bf16[288,768]{1,0:T(8,128)(2,1)}, u32[]{:S(2)}, u32[]{:S(2)}) collective-permute-start(bf16[288,768]{1,0:T(8,128)(2,1)} %collective-permute-done.6.rest_3_), channel_id=1, source_target_pairs={{0,8},{2,10},{4,12},{6,14},{8,0},{10,2},{12,4},{14,6},{16,24},{18,... | collective-permute-start | bytes 1327112 | tf_op jit(solution)/shard_map/ppermute | solution.py:380
  61.1 12.1 %collective-permute-start.24 = (bf16[288,768]{1,0:T(8,128)(2,1)}, bf16[288,768]{1,0:T(8,128)(2,1)}, u32[]{:S(2)}, u32[]{:S(2)}) collective-permute-start(bf16[288,768]{1,0:T(8,128)(2,1)} %collective-permute-done.22.rest_1_), channel_id=1, source_target_pairs={{0,4},{2,6},{4,0},{6,2},{8,12},{10,14},{12,8},{14,10},{16,20},{18,... | collective-permute-start | bytes 1327112 | tf_op jit(solution)/shard_map/ppermute | solution.py:384
  63.1 16.6 %collective-permute-start.29 = (bf16[288,768]{1,0:T(8,128)(2,1)}, bf16[288,768]{1,0:T(8,128)(2,1)}, u32[]{:S(2)}, u32[]{:S(2)}) collective-permute-start(bf16[288,768]{1,0:T(8,128)(2,1)} %collective-permute-done.1.rest_0_), channel_id=1, source_target_pairs={{0,1},{1,0},{2,3},{3,2},{4,5},{5,4},{6,7},{7,6},{8,9},{9,8},{10,11... | collective-permute-start | bytes 1327112 | tf_op jit(solution)/shard_map/ppermute | solution.py:385
  74.1 26.4 %collective-permute-start.9 = (bf16[4,96,768]{2,1,0:T(8,128)(2,1)S(1)}, bf16[4,96,768]{2,1,0:T(8,128)(2,1)}, u32[]{:S(2)}, u32[]{:S(2)}) collective-permute-start(bf16[4,96,768]{2,1,0:T(8,128)(2,1)S(1)} %pad_maximum_fusion.rest_0_), channel_id=1, source_target_pairs={{0,4},{2,6},{4,0},{6,2},{8,12},{10,14},{12,8},{14,10},{16,20},{18,... | collective-permute-start | bytes 1769480 | tf_op jit(solution)/shard_map/ppermute | solution.py:387
  79.7 23.6 %collective-permute-start.32 = (bf16[288,768]{1,0:T(8,128)(2,1)}, bf16[288,768]{1,0:T(8,128)(2,1)S(1)}, u32[]{:S(2)}, u32[]{:S(2)}) collective-permute-start(bf16[288,768]{1,0:T(8,128)(2,1)} %collective-permute-done.1.rest_0_), channel_id=1, source_target_pairs={{0,2},{2,0},{4,6},{6,4},{8,10},{10,8},{12,14},{14,12},{16,18},{18,... | collective-permute-start | bytes 1327112 | tf_op jit(solution)/shard_map/ppermute | solution.py:394
  79.7 20.3 %collective-permute-start.30 = (bf16[288,768]{1,0:T(8,128)(2,1)}, bf16[288,768]{1,0:T(8,128)(2,1)}, u32[]{:S(2)}, u32[]{:S(2)}) collective-permute-start(bf16[288,768]{1,0:T(8,128)(2,1)} %collective-permute-done.1.rest_0_), channel_id=1, source_target_pairs={{0,4},{2,6},{4,0},{6,2},{8,12},{10,14},{12,8},{14,10},{16,20},{18,... | collective-permute-start | bytes 1327112 | tf_op jit(solution)/shard_map/ppermute | solution.py:385
  80.2 21.4 %collective-permute-start.8 = (bf16[4,96,768]{2,1,0:T(8,128)(2,1)S(1)}, bf16[4,96,768]{2,1,0:T(8,128)(2,1)S(1)}, u32[]{:S(2)}, u32[]{:S(2)}) collective-permute-start(bf16[4,96,768]{2,1,0:T(8,128)(2,1)S(1)} %pad_maximum_fusion.rest_0_), channel_id=1, source_target_pairs={{0,1},{1,0},{2,3},{3,2},{4,5},{5,4},{6,7},{7,6},{8,9},{9,8},{10,11... | collective-permute-start | bytes 1769480 | tf_op jit(solution)/shard_map/ppermute | solution.py:387
  80.6 19.4 %collective-permute-start.31 = (bf16[288,768]{1,0:T(8,128)(2,1)}, bf16[288,768]{1,0:T(8,128)(2,1)}, u32[]{:S(2)}, u32[]{:S(2)}) collective-permute-start(bf16[288,768]{1,0:T(8,128)(2,1)} %collective-permute-done.24.rest_3_), channel_id=1, source_target_pairs={{0,8},{2,10},{4,12},{6,14},{8,0},{10,2},{12,4},{14,6},{16,24},{18,... | collective-permute-start | bytes 1327112 | tf_op jit(solution)/shard_map/ppermute | solution.py:390
  100.0 13.3 %collective-permute-start.33 = (bf16[288,768]{1,0:T(8,128)(2,1)}, bf16[288,768]{1,0:T(8,128)(2,1)}, u32[]{:S(2)}, u32[]{:S(2)}) collective-permute-start(bf16[288,768]{1,0:T(8,128)(2,1)} %collective-permute-done.29.rest_1_), channel_id=1, source_target_pairs={{0,2},{2,0},{4,6},{6,4},{8,10},{10,8},{12,14},{14,12},{16,18},{18,... | collective-permute-start | bytes 1327112 | tf_op jit(solution)/shard_map/ppermute | solution.py:394
  100.0 13.8 %collective-permute-start.35 = (bf16[288,768]{1,0:T(8,128)(2,1)}, bf16[288,768]{1,0:T(8,128)(2,1)}, u32[]{:S(2)}, u32[]{:S(2)}) collective-permute-start(bf16[288,768]{1,0:T(8,128)(2,1)} %collective-permute-done.31.rest_3_), channel_id=1, source_target_pairs={{0,2},{2,0},{4,6},{6,4},{8,10},{10,8},{12,14},{14,12},{16,18},{18,... | collective-permute-start | bytes 1327112 | tf_op jit(solution)/shard_map/ppermute | solution.py:394
  100.5 13.3 %collective-permute-start.34 = (bf16[288,768]{1,0:T(8,128)(2,1)}, bf16[288,768]{1,0:T(8,128)(2,1)}, u32[]{:S(2)}, u32[]{:S(2)}) collective-permute-start(bf16[288,768]{1,0:T(8,128)(2,1)} %collective-permute-done.30.rest_2_), channel_id=1, source_target_pairs={{0,2},{2,0},{4,6},{6,4},{8,10},{10,8},{12,14},{14,12},{16,18},{18,... | collective-permute-start | bytes 1327112 | tf_op jit(solution)/shard_map/ppermute | solution.py:394
  111.1 23.3 %collective-permute-start.38 = (bf16[4,96,768]{2,1,0:T(8,128)(2,1)S(1)}, bf16[4,96,768]{2,1,0:T(8,128)(2,1)S(1)}, u32[]{:S(2)}, u32[]{:S(2)}) collective-permute-start(bf16[4,96,768]{2,1,0:T(8,128)(2,1)S(1)} %pad_maximum_fusion.rest_0_), channel_id=1, source_target_pairs={{0,2},{2,0},{4,6},{6,4},{8,10},{10,8},{12,14},{14,12},{16,18},{18,... | collective-permute-start | bytes 1769480 | tf_op jit(solution)/shard_map/ppermute | solution.py:398
  113.2 21.2 %collective-permute-start.40 = (bf16[4,96,768]{2,1,0:T(8,128)(2,1)}, bf16[4,96,768]{2,1,0:T(8,128)(2,1)S(1)}, u32[]{:S(2)}, u32[]{:S(2)}) collective-permute-start(bf16[4,96,768]{2,1,0:T(8,128)(2,1)} %collective-permute-done.9.rest_2_), channel_id=1, source_target_pairs={{0,2},{2,0},{4,6},{6,4},{8,10},{10,8},{12,14},{14,12},{16,18},{18,... | collective-permute-start | bytes 1769480 | tf_op jit(solution)/shard_map/ppermute | solution.py:398
  113.3 21.2 %collective-permute-start.39 = (bf16[4,96,768]{2,1,0:T(8,128)(2,1)}, bf16[4,96,768]{2,1,0:T(8,128)(2,1)S(1)}, u32[]{:S(2)}, u32[]{:S(2)}) collective-permute-start(bf16[4,96,768]{2,1,0:T(8,128)(2,1)} %copy-done.14), channel_id=1, source_target_pairs={{0,2},{2,0},{4,6},{6,4},{8,10},{10,8},{12,14},{14,12},{16,18},{18,... | collective-permute-start | bytes 1769480 | tf_op jit(solution)/shard_map/ppermute | solution.py:398
  113.8 20.7 %collective-permute-start.41 = (bf16[2,96,768]{2,1,0:T(8,128)(2,1)}, bf16[2,96,768]{2,1,0:T(8,128)(2,1)S(1)}, u32[]{:S(2)}, u32[]{:S(2)}) collective-permute-start(bf16[2,96,768]{2,1,0:T(8,128)(2,1)} %collective-permute-done.36.rest_3_), channel_id=1, source_target_pairs={{0,2},{2,0},{4,6},{6,4},{8,10},{10,8},{12,14},{14,12},{16,18},{18,... | collective-permute-start | bytes 884744 | tf_op jit(solution)/shard_map/ppermute | solution.py:398
  113.8 20.6 %collective-permute-start.42 = (bf16[2,96,768]{2,1,0:T(8,128)(2,1)}, bf16[2,96,768]{2,1,0:T(8,128)(2,1)S(1)}, u32[]{:S(2)}, u32[]{:S(2)}) collective-permute-start(bf16[2,96,768]{2,1,0:T(8,128)(2,1)} %collective-permute-done.37.rest_4_), channel_id=1, source_target_pairs={{0,2},{2,0},{4,6},{6,4},{8,10},{10,8},{12,14},{14,12},{16,18},{18,... | collective-permute-start | bytes 884744 | tf_op jit(solution)/shard_map/ppermute | solution.py:398
  (42 other events, 347.1 us)

commit v4 on v3

--- a/solution.py
+++ b/solution.py
@@ -147,66 +147,80 @@
     )(window_index, latents, norm_gain.reshape(1, width), freq.reshape(1, quarter))
 
 
+def places(x, y):
+    return ((x, y), (1 - x, y), (x, 1 - y), (1 - x, 1 - y))
+
+
 def project_kernel(key_chunk, value_chunk, at_ref, plane_ref, n_ref, *rest):
-    pieces, (p_ref, k_ref, w_ref, sems) = rest[:8], rest[8:]
+    pieces, (p_ref, k_ref, w_ref, rows_ref, cols_ref, sems, out_sems) = rest[:8], rest[8:]
     x, y, core = at_ref[0], at_ref[1], at_ref[2]
-    rows, lanes = pieces[0].shape
-    copies = []
-    for owner in range(2):
-        c = core if owner == 0 else 1 - core
-        for i, (px, py) in enumerate(((x, y), (1 - x, y), (x, 1 - y), (1 - x, 1 - y))):
+    rows, lanes = w_ref.shape[0] // 4, w_ref.shape[1] // 2
+    for i, (px, py) in enumerate(places(x, y)):
+        for owner, c in ((0, core), (1, 1 - core)):
             row = pl.multiple_of((2 * py + c) * rows, 16)
             lane = pl.multiple_of(px * lanes, 128)
-            copies.append(
-                pltpu.make_async_copy(
-                    pieces[4 * owner + i],
-                    w_ref.at[pl.ds(row, rows), pl.ds(lane, lanes)],
-                    sems.at[len(copies)],
-                )
-            )
-    for c in copies:
-        c.start()
-    for c in copies:
-        c.wait()
+            pltpu.make_async_copy(
+                pieces[4 * owner + i].at[pl.ds(0, rows), :],
+                w_ref.at[pl.ds(row, rows), pl.ds(lane, lanes)],
+                sems.at[py * 4 + 2 * owner + i % 2],
+            ).start()
     count, chunk, tokens = p_ref.shape
-    cols = n_ref[...]
-
-    @pl.loop(0, count)
-    def _(m):
+
+    def landed(which):
+        for i in range(4):
+            pltpu.make_async_copy(
+                pieces[0].at[pl.ds(0, rows), :],
+                w_ref.at[pl.ds(0, rows), pl.ds(0, lanes)],
+                sems.at[4 * which + i],
+            ).wait()
+
+    for m in range(count):
+        if m < 2:
+            landed(m)
         which = plane_ref[0] * count + m
-        w = w_ref[pl.ds(pl.multiple_of(m * chunk, 128), chunk), :]
-        got = jnp.dot(w, cols, preferred_element_type=F32)
+        got = jnp.dot(w_ref[m * chunk : (m + 1) * chunk, :], n_ref[...], preferred_element_type=F32)
         got = got.reshape(chunk // HEAD_DIM, HEAD_DIM, tokens)
         ms = jnp.mean(got * got, axis=1, keepdims=True)
         scale = jnp.where(which < value_chunk, lax.rsqrt(ms + EPS), 1.0)
+        scale = jnp.where(which < key_chunk, scale * HEAD_DIM**-0.5, scale)
         out = (got * scale).astype(BF).reshape(chunk, tokens)
+        rows_ref[m] = out
+        cols_ref[m] = out.T
         is_key = (which >= key_chunk) & (which < value_chunk)
 
         @pl.when(is_key)
         def _():
-            k_ref[m] = out.T
+            pltpu.make_async_copy(cols_ref.at[m], k_ref.at[m], out_sems.at[m]).start()
 
         @pl.when(jnp.logical_not(is_key))
         def _():
-            p_ref[m] = out
-
-
-def project(place, plane, normed, pieces):
+            pltpu.make_async_copy(rows_ref.at[m], p_ref.at[m], out_sems.at[m]).start()
+
+    for m in range(count):
+        pltpu.make_async_copy(rows_ref.at[m], p_ref.at[m], out_sems.at[m]).wait()
+
+
+def project(place, plane, normed, pieces, rows):
     width, tokens = normed.shape
-    rows = 4 * pieces[0].shape[0]
     chunk = width // 4
-    count = rows // chunk
+    count = 4 * rows // chunk
     return pl.pallas_call(
         functools.partial(project_kernel, 4, 8),
         out_shape=(
-            jax.ShapeDtypeStruct((count, chunk, tokens), BF),
-            jax.ShapeDtypeStruct((count, tokens, chunk), BF),
+            pltpu.HBM((count, chunk, tokens), BF),
+            pltpu.HBM((count, tokens, chunk), BF),
         ),
         in_specs=[sspec(), sspec(), vspec()] + [hspec()] * 8,
-        out_specs=(vspec(), vspec()),
-        scratch_shapes=[pltpu.VMEM((rows, width), BF), pltpu.SemaphoreType.DMA((8,))],
+        out_specs=(hspec(), hspec()),
+        scratch_shapes=[
+            pltpu.VMEM((4 * rows, width), BF),
+            pltpu.VMEM((count, chunk, tokens), BF),
+            pltpu.VMEM((count, tokens, chunk), BF),
+            pltpu.SemaphoreType.DMA((8,)),
+            pltpu.SemaphoreType.DMA((count,)),
+        ],
         compiler_params=params(24),
-        cost_estimate=cost(2 * rows * width * tokens, 2 * (rows + tokens) * width),
+        cost_estimate=cost(8 * rows * width * tokens, 2 * (4 * rows + tokens) * width),
         name="project",
     )(place, plane, normed, *map(far, pieces))
 
@@ -218,7 +232,7 @@
     for s, (p, k) in enumerate(((p0, k0), (p1, k1), (p2, k2), (p3, k3))):
         for m in range(count):
             which = planes_ref[s] * count + m
-            sem = sems.at[s * count + m]
+            sem = sems.at[which]
 
             @pl.when(which < 4)
             def _():
@@ -241,30 +255,35 @@
         first = (key < WIN_TOK) & (query < WIN_TOK) & (key < lens_ref[2 * b])
         second = (key >= WIN_TOK) & (query >= WIN_TOK) & (key - WIN_TOK < lens_ref[2 * b + 1])
         mask_ref[b] = jnp.where(first | second, 1.0, 0.0).astype(F32)
-    for i in range(4 * count):
-        pltpu.make_async_copy(p0.at[0], q_ref.at[0], sems.at[i]).wait()
     ones = jnp.ones((16, 128), BF)
     blank = jnp.zeros((HEAD_DIM, 128), BF)
     pairs = chunk // 128
 
-    @pl.loop(0, 4 * pairs)
-    def _(pair):
-        part = pair // pairs
-        at = pl.ds(pl.multiple_of(pair % pairs * 128, 128), 128)
-        out_at = pl.ds(pl.multiple_of(pair * 128, 128), 128)
-        for b in range(blocks):
-            tok = pl.ds(b * 128, 128)
-            q = q_ref[part, at, tok]
-            k = k_ref[part, tok, at]
-            v = v_ref[part, at, tok]
-            q0 = jnp.concatenate([q[:HEAD_DIM], blank], axis=0)
-            q1 = jnp.concatenate([blank, q[HEAD_DIM:]], axis=0)
-            scores = jnp.dot(k, jnp.concatenate([q0, q1], axis=1), preferred_element_type=F32)
-            weights = (jnp.exp(scores * HEAD_DIM**-0.5) * mask_ref[b]).astype(BF)
-            got = jnp.dot(jnp.concatenate([v, ones], axis=0), weights, preferred_element_type=F32)
-            o0 = got[:HEAD_DIM, :128] / got[128:129, :128]
-            o1 = got[HEAD_DIM:128, 128:] / got[128:129, 128:]
-            out_ref[tok, out_at] = jnp.concatenate([o0, o1], axis=0).T.astype(BF)
+    @pl.loop(0, 4)
+    def _(part):
+        for kind in range(3):
+            pltpu.make_async_copy(p0.at[0], q_ref.at[0], sems.at[4 * kind + part]).wait()
+
+        @pl.loop(0, pairs)
+        def _(i):
+            at = pl.ds(pl.multiple_of(i * 128, 128), 128)
+            out_at = pl.ds(pl.multiple_of(part * chunk + i * 128, 128), 128)
+            for b in range(blocks):
+                tok = pl.ds(b * 128, 128)
+                q = q_ref[part, at, tok]
+                k = k_ref[part, tok, at]
+                v = v_ref[part, at, tok]
+                q0 = jnp.concatenate([q[:HEAD_DIM], blank], axis=0)
+                q1 = jnp.concatenate([blank, q[HEAD_DIM:]], axis=0)
+                scores = jnp.dot(k, jnp.concatenate([q0, q1], axis=1), preferred_element_type=F32)
+                weights = (jnp.exp(scores) * mask_ref[b]).astype(BF)
+                got = jnp.dot(
+                    jnp.concatenate([v, ones], axis=0), weights, preferred_element_type=F32
+                )
+                share = 1.0 / got[128:129, :]
+                o0 = got[:HEAD_DIM, :128] * share[:, :128]
+                o1 = got[HEAD_DIM:128, 128:] * share[:, 128:]
+                out_ref[tok, out_at] = jnp.concatenate([o0, o1], axis=0).astype(BF).T
 
 
 def attend(planes, window_len, parts):
@@ -289,50 +308,47 @@
 
 
 def output_kernel(at_ref, planes_ref, lens_ref, live_ref, att_ref, lat_ref, *rest):
-    pieces, (out_ref, w_ref, sems) = rest[:10], rest[10:]
+    pieces, (out_ref, w_ref, done_ref, sems, out_sems) = rest[:-5], rest[-5:]
     x, y, core = at_ref[0], at_ref[1], at_ref[2]
-    slots, rows, lanes = pieces[0].shape
+    slots = len(pieces) // 8
+    tokens, width = att_ref.shape
+    rows, lanes = width // (4 * slots), width // 2
+    skip = pieces[0].shape[0] - rows
     copies = []
-    for owner in range(2):
-        c = core if owner == 0 else 1 - core
-        own, xs, ys, da, db = pieces[5 * owner : 5 * owner + 5]
-        for s in range(slots):
-            diagonal = da.at[s] if s < slots // 2 else db.at[s - slots // 2]
-            for ref, px, py in (
-                (own.at[s], x, y),
-                (xs.at[s], 1 - x, y),
-                (ys.at[s], x, 1 - y),
-                (diagonal, 1 - x, 1 - y),
-            ):
-                row = pl.multiple_of((planes_ref[s] * 4 + 2 * py + c) * rows, 16)
+    for s in range(slots):
+        for owner, c in ((0, core), (1, 1 - core)):
+            for i, (px, py) in enumerate(places(x, y)):
+                src = pieces[8 * s + 4 * owner + i].at[pl.ds(skip, rows), :]
+                row = pl.multiple_of((2 * py + c) * rows, 16)
                 lane = pl.multiple_of(px * lanes, 128)
                 copies.append(
                     pltpu.make_async_copy(
-                        ref, w_ref.at[pl.ds(row, rows), pl.ds(lane, lanes)], sems.at[len(copies)]
+                        src, w_ref.at[s, pl.ds(row, rows), pl.ds(lane, lanes)], sems.at[len(copies)]
                     )
                 )
     for c in copies:
         c.start()
-    for c in copies:
-        c.wait()
-    tokens, width = att_ref.shape
     cols = 4 * rows
-    att = att_ref[...]
     token = lax.broadcasted_iota(jnp.int32, (tokens, 1), 0)
     stop = jnp.zeros((tokens, 1), jnp.int32)
     for w in range(tokens // WIN_TOK):
         length = jnp.where(w // 2 < live_ref[0], lens_ref[w], 0)
         stop = jnp.where(token // WIN_TOK == w, length + w * WIN_TOK, stop)
     keep = token < stop
-
-    @pl.loop(0, slots)
-    def _(s):
-        spot = pl.ds(pl.multiple_of(s * cols, 128), cols)
+    outs = []
+    for s in range(slots):
+        for c in copies[8 * s : 8 * s + 8]:
+            c.wait()
+        spot = pl.ds(pl.multiple_of(planes_ref[s] * cols, 128), cols)
         update = lax.dot_general(
-            att, w_ref[spot, :], (((1,), (1,)), ((), ())), preferred_element_type=F32
+            att_ref[...], w_ref[s], (((1,), (1,)), ((), ())), preferred_element_type=F32
         )
         base = lat_ref[:, spot].astype(F32)
-        out_ref[:, spot] = jnp.where(keep, base + update, base).astype(BF)
+        done_ref[s] = jnp.where(keep, base + update, base).astype(BF)
+        outs.append(pltpu.make_async_copy(done_ref.at[s], out_ref.at[:, spot], out_sems.at[s]))
+        outs[s].start()
+    for c in outs:
+        c.wait()
 
 
 def output(place, planes, lens, live, attended, latents, pieces):
@@ -340,63 +356,88 @@
     return pl.pallas_call(
         output_kernel,
         out_shape=jax.ShapeDtypeStruct((tokens, width), BF),
-        in_specs=[sspec()] * 4 + [vspec()] * 2 + [hspec()] * 10,
-        out_specs=vspec(),
-        scratch_shapes=[pltpu.VMEM((width, width), BF), pltpu.SemaphoreType.DMA((32,))],
+        in_specs=[sspec()] * 4 + [vspec()] * 2 + [hspec()] * len(pieces),
+        out_specs=hspec(),
+        scratch_shapes=[
+            pltpu.VMEM((4, width // 4, width), BF),
+            pltpu.VMEM((4, tokens, width // 4), BF),
+            pltpu.SemaphoreType.DMA((len(pieces),)),
+            pltpu.SemaphoreType.DMA((4,)),
+        ],
         compiler_params=params(32),
         cost_estimate=cost(2 * width * width * tokens, 2 * width * (width + 3 * tokens)),
         name="output",
     )(place, planes, lens, live, attended, latents, *map(far, pieces))
 
 
-def after(value, *earlier):
-    return lax.optimization_barrier((value, *earlier))[0]
-
-
 def local(tile_count, latents, window_index, window_len, live_blocks, norm_gain, w_qkv, w_out):
     blocks, rows, width = latents.shape
 
-    def along(bit):
-        pairs = [(i, i ^ bit) for i in range(tile_count)]
-        return functools.partial(lax.ppermute, axis_name="tile", perm=pairs)
-
-    core, ys, z1, z2, z3 = along(1), along(2), along(4), along(8), along(12)
-    xs = functools.partial(lax.ppermute, axis_name="group", perm=[(0, 1), (1, 0)])
+    def along(axis, pairs):
+        def move(value, name):
+            with jax.named_scope(name):
+                return lax.ppermute(value, axis, pairs)
+
+        return move
+
+    def across(bit):
+        return along("tile", [(i, i ^ bit) for i in range(tile_count)])
+
+    core, ys, z1 = across(1), across(2), across(4)
+    xs = along("group", [(0, 1), (1, 0)])
+    low, high = range(tile_count // 4, tile_count // 2), range(tile_count // 2, 3 * tile_count // 4)
+    step = tile_count // 4
+    mid = along("tile", [(i, i + step) for i in low] + [(i, i - step) for i in high])
+    ends = along("tile", [(i, i - step) for i in low] + [(i, i + step) for i in high])
     t = lax.axis_index("tile")
     x = lax.axis_index("group")
     z = t // 4
     place = jnp.stack([x, t // 2 % 2, t % 2]).astype(jnp.int32)
     planes = jnp.stack([z, z ^ 1, z ^ 2, z ^ 3]).astype(jnp.int32)
 
-    u0 = w_qkv.T
-    o0 = w_out.T
-    u1, x0, y0, u2 = z1(u0), xs(u0), ys(u0), z2(u0)
-    o1, o2 = z1(after(o0, x0)), z2(after(o0, x0))
+    nq = w_qkv.shape[1]
+
+    def sync(*values):
+        return lax.optimization_barrier(values)
+
+    def share(**values):
+        shared = []
+        for name, value in values.items():
+            if shared:
+                value = sync(value, shared[-1])[0]
+            shared.append(core(value, f"core_{name}"))
+        return shared
+
+    u0 = jnp.concatenate([w_qkv.T, w_out.T], axis=0)
+    u1, near, x0, y0 = z1(u0, "u1"), mid(u0, "near2"), xs(u0, "x0"), ys(u0, "y0")
     normed = normed_columns(latents, window_index, norm_gain)
-    d0 = xs(after(y0, normed))
-    y1 = ys(u1)
-    x2, y2, u3 = xs(u2), ys(u2), z1(u2)
-    x1 = xs(after(u1, d0))
-    d1 = z1(d0)
-    o3 = z1(after(o2, d0))
-    s0 = [u0, x0, y0, d0]
-    p0 = project(place, planes[0:1], normed, s0 + [core(a) for a in s0])
-    d2 = ys(after(x2, p0[0]))
-    x3, y3 = xs(u3), ys(u3)
-    o4 = jnp.stack([after(o0, u3), o1, o2, o3])
-    xo, yo = xs(o4), ys(o4)
-    s1 = [u1, x1, y1, d1]
-    p1 = project(place, planes[1:2], normed, s1 + [core(a) for a in s1])
-    d3 = z1(d2)
-    s2 = [u2, x2, y2, d2]
-    p2 = project(place, planes[2:3], normed, s2 + [core(a) for a in s2])
-    s3 = [u3, after(x3, p1[0]), after(y3, p2[0]), d3]
-    p3 = project(place, planes[3:4], normed, s3 + [core(a) for a in s3])
-    half = o4.shape[0] // 2
-    da, db = xs(yo[:half]), ys(xo[half:])
-    so = [o4, xo, yo, da, db]
-    so = so + [core(a) for a in so]
-    attended = attend(planes, after(window_len, xo, yo), (p0, p1, p2, p3))
+    cu0, = share(u0=u0)
+    u1, near, x0, y0, normed, cu0 = sync(u1, near, x0, y0, normed, cu0)
+    far2, near3, d0, y1 = ends(near, "far2"), mid(u1, "near3"), xs(y0, "d0"), ys(u1, "y1")
+    cx0, cy0 = share(x0=x0, y0=y0)
+    far2, near3, d0, y1, cx0, cy0, near, u1 = sync(far2, near3, d0, y1, cx0, cy0, near, u1)
+    u2 = near3 + far2
+    x2, y2, far3 = xs(u2, "x2"), ys(u2, "y2"), ends(near3, "far3")
+    cd0, cy1, cu1 = share(d0=d0, y1=y1, u1=u1)
+    x2, y2, far3, cd0, cy1, cu1, u1, u2, d0, near = sync(x2, y2, far3, cd0, cy1, cu1, u1, u2, d0, near)
+    x1, d2, d1 = xs(u1, "x1"), ys(x2, "d2"), z1(d0, "d1")
+    u3 = near + far3
+    s0 = [u0, x0, y0, d0, cu0, cx0, cy0, cd0]
+    p0 = project(place, planes[0:1], normed, s0, nq)
+    cu2, cx2, cy2 = share(u2=u2, x2=x2, y2=y2)
+    x1, d2, d1, u3, cu2, cx2, cy2, *p0 = sync(x1, d2, d1, u3, cu2, cx2, cy2, *p0)
+    x3, y3, d3 = xs(u3, "x3"), ys(u3, "y3"), z1(d2, "d3")
+    cx1, cd1, cd2, cu3 = share(x1=x1, d1=d1, d2=d2, u3=u3)
+    s1 = [u1, x1, y1, d1, cu1, cx1, cy1, cd1]
+    p1 = project(place, planes[1:2], normed, s1, nq)
+    s2 = [u2, x2, y2, d2, cu2, cx2, cy2, cd2]
+    p2 = project(place, planes[2:3], normed, s2, nq)
+    x3, y3, d3, cu3, p1, p2 = sync(x3, y3, d3, cu3, p1, p2)
+    cx3, cy3, cd3 = (share(**{name: value})[0] for name, value in (("x3", x3), ("y3", y3), ("d3", d3)))
+    s3 = [u3, x3, y3, d3, cu3, cx3, cy3, cd3]
+    p3 = project(place, planes[3:4], normed, s3, nq)
+    attended = attend(planes, window_len, (p0, p1, p2, p3))
+    so = s0 + s1 + s2 + s3
     flat = latents.reshape(blocks * rows, width)
     out = output(place, planes, window_len, live_blocks, attended, flat, so)
     return out.reshape(latents.shape)

time: 147 us -> 139 us (0.946)
  waiting for transfers between devices: 46 us -> 57.6 us
  starting transfers between devices: 31.8 us -> 22.1 us
  local copies, waits for them, and re-layouts: 16.4 us -> 6.95 us
  Pallas kernels: 51 us -> 47.7 us
  other arithmetic: 0.25 us -> 2.82 us
    ppermute x43 -> x33, waiting for transfers between devices: 46 us -> 57.6 us  [move(): return lax.ppermute(value, axis, pairs)]
    ppermute x43 -> x33, starting transfers between devices: 31.8 us -> 22.1 us  [move(): return lax.ppermute(value, axis, pairs)]
    unnamed x62 -> x50, local copies, waits for them, and re-layouts: 14.7 us -> 6.24 us
    pallas_call x1, Pallas kernels: 10.6 us -> 8.86 us  [output(): pl.pallas_call(output_kernel, out_shape=jax.ShapeDtypeStruct((tokens, wid...]
    add x0 -> x2, other arithmetic: none -> 1.51 us  [the longest x1 1.38 us: local(): u3 = near + far3]
  transfers between devices with their start and end apart: 43 -> 33, of which waited for: 14 -> 18; matrix products, arithmetic and copies ran while one was open for 1% -> 2% of each run, Pallas kernels for 28% -> 16%
where the time goes in v4:
time: 139 us; the launch traced here: 138 us
  waiting for transfers between devices  57.6 us (41%)
  Pallas kernels  47.7 us (34%)
  starting transfers between devices  22.1 us (16%)
  local copies, waits for them, and re-layouts  6.95 us (5%)
  other arithmetic  2.82 us (2%)
    ppermute x33, waiting for transfers between devices, move(): return lax.ppermute(value, axis, pairs)  57.6 us
    pallas_call x4, Pallas kernels, project(): pl.pallas_call(functools.partial(project_kernel, 4, 8), out_shape=(pltpu....  25.2 us
    ppermute x33, starting transfers between devices, move(): return lax.ppermute(value, axis, pairs)  22.1 us
    pallas_call x1, Pallas kernels, attend(): pl.pallas_call(attend_kernel, out_shape=jax.ShapeDtypeStruct((tokens, wid...  10.4 us
    pallas_call x1, Pallas kernels, output(): pl.pallas_call(output_kernel, out_shape=jax.ShapeDtypeStruct((tokens, wid...  8.86 us
    unnamed x50, local copies, waits for them, and re-layouts  6.24 us
    pallas_call x1, Pallas kernels, normed_columns(): pl.pallas_call(norm_kernel, out_shape=jax.ShapeDtypeStruct((width, blocks...  3.25 us
  transfers between devices with their start and end apart: 33, of which 18 were waited for; matrix products, arithmetic and copies ran while one was open for 2% of the time, Pallas kernels for 16%

profile of v4, /device:TPU:0, one launch (start us, length us, event | category | flops | bytes accessed | tf_op | source)
XLA Modules:
  0.0 138.3 jit_solution(7855158775686018978)
XLA Ops:
  0.0 1.1 pad_maximum_fusion.rest_0_
  1.7 2.6 %collective-permute-start.3 = (bf16[384,768]{1,0:T(8,128)(2,1)S(1)}, bf16[384,768]{1,0:T(8,128)(2,1)S(1)}, u32[]{:S(2)}, u32[]{:S(2)}) collective-permute-start(bf16[384,768]{1,0:T(8,128)(2,1)S(1)} %pad_maximum_fusion.rest_0_), channel_id=1, source_target_pairs={{0,4},{2,6},{4,0},{6,2},{8,12},{10,14},{12,8},{14,10},{16,20},{18,... | collective-permute-start | bytes 1769480 | tf_op jit(solution)/shard_map/y0/ppermute | solution.py:379
  4.3 1.5 %collective-permute-start.2 = (bf16[384,768]{1,0:T(8,128)(2,1)S(1)}, bf16[384,768]{1,0:T(8,128)(2,1)S(1)}, u32[]{:S(2)}, u32[]{:S(2)}) collective-permute-start(bf16[384,768]{1,0:T(8,128)(2,1)S(1)} %pad_maximum_fusion.rest_0_), channel_id=1, source_target_pairs={{0,1},{1,0},{2,3},{3,2},{4,5},{5,4},{6,7},{7,6},{8,9},{9,8},{10,11... | collective-permute-start | bytes 1769480 | tf_op jit(solution)/shard_map/x0/ppermute | solution.py:379
  6.4 4.4 %collective-permute-start = (bf16[384,768]{1,0:T(8,128)(2,1)S(1)}, bf16[384,768]{1,0:T(8,128)(2,1)}, u32[]{:S(2)}, u32[]{:S(2)}) collective-permute-start(bf16[384,768]{1,0:T(8,128)(2,1)S(1)} %pad_maximum_fusion.rest_0_), channel_id=1, source_target_pairs={{0,8},{2,10},{4,12},{6,14},{8,0},{10,2},{12,4},{14,6},{16,24},{18,... | collective-permute-start | bytes 1769480 | tf_op jit(solution)/shard_map/u1/ppermute | solution.py:379
  11.6 1.7 %copy-done = bf16[6,128,1536]{2,1,0:T(8,128)(2,1)S(1)} copy-done((bf16[6,128,1536]{2,1,0:T(8,128)(2,1)S(1)}, bf16[6,128,1536]{2,1,0:T(8,128)(2,1)}, u32[]{:S(2)}) %copy-start) | copy-done | bytes 2359320
  13.9 3.3 %norm.1.n_ref = bf16[1536,768]{1,0:T(8,128)(2,1)S(1)} custom-call(s32[12]{0:T(128)S(1)} %copy-done.3, bf16[6,128,1536]{2,1,0:T(8,128)(2,1)S(1)} %copy-done, f32[1,1536]{1,0:T(1,128)S(1)} %reshape.20.gain_ref, f32[1,384]{1,0:T(1,128)S(1)} %multiply_exponential_fusion.freq_ref), custom_call_target="tpu_custom_call" | custom-call | flops 47185920 | bytes 4718592 | tf_op jit(solution)/shard_map/norm/pallas_call | solution.py:138
  18.2 1.5 %collective-permute-done.2.rest_1_ = bf16[384,768]{1,0:T(8,128)(2,1)S(1)} collective-permute-done((bf16[384,768]{1,0:T(8,128)(2,1)S(1)}, bf16[384,768]{1,0:T(8,128)(2,1)S(1)}, u32[]{:S(2)}, u32[]{:S(2)}) %collective-permute-start.2) | collective-permute-done | bytes 589856 | tf_op jit(solution)/shard_map/x0/ppermute | solution.py:379
  19.7 4.4 %collective-permute-done.rest_0_.rest_8_ = bf16[384,768]{1,0:T(8,128)(2,1)} collective-permute-done((bf16[384,768]{1,0:T(8,128)(2,1)S(1)}, bf16[384,768]{1,0:T(8,128)(2,1)}, u32[]{:S(2)}, u32[]{:S(2)}) %collective-permute-start) | collective-permute-done | bytes 589856 | tf_op jit(solution)/shard_map/u1/ppermute | solution.py:379
  25.3 1.3 collective-permute-start.5
  27.2 16.2 %collective-permute-done.5 = bf16[384,768]{1,0:T(8,128)(2,1)S(1)} collective-permute-done((bf16[384,768]{1,0:T(8,128)(2,1)S(1)}, bf16[384,768]{1,0:T(8,128)(2,1)S(1)}, u32[]{:S(2)}, u32[]{:S(2)}) %collective-permute-start.5) | collective-permute-done | bytes 589856 | tf_op jit(solution)/shard_map/far2/ppermute | solution.py:379
  43.5 2.2 %collective-permute-done.14.rest_7_ = bf16[384,768]{1,0:T(8,128)(2,1)S(1)} collective-permute-done((bf16[384,768]{1,0:T(8,128)(2,1)}, bf16[384,768]{1,0:T(8,128)(2,1)S(1)}, u32[]{:S(2)}, u32[]{:S(2)}) %collective-permute-start.14) | collective-permute-done | bytes 589856 | tf_op jit(solution)/shard_map/core_d0/ppermute | solution.py:379
  46.8 1.6 %collective-permute-start.12 = (bf16[384,768]{1,0:T(8,128)(2,1)S(1)}, bf16[384,768]{1,0:T(8,128)(2,1)}, u32[]{:S(2)}, u32[]{:S(2)}) collective-permute-start(bf16[384,768]{1,0:T(8,128)(2,1)S(1)} %add.17.rest_0_.rest_16_), channel_id=1, source_target_pairs={{0,4},{2,6},{4,0},{6,2},{8,12},{10,14},{12,8},{14,10},{16,20},{18,... | collective-permute-start | bytes 1769480 | tf_op jit(solution)/shard_map/y2/ppermute | solution.py:379
  49.0 1.5 %collective-permute-start.13 = (bf16[384,768]{1,0:T(8,128)(2,1)S(1)}, bf16[384,768]{1,0:T(8,128)(2,1)S(1)}, u32[]{:S(2)}, u32[]{:S(2)}) collective-permute-start(bf16[384,768]{1,0:T(8,128)(2,1)S(1)} %collective-permute-done.6), channel_id=1, source_target_pairs={{8,0},{10,2},{12,4},{14,6},{16,24},{18,26},{20,28},{22,30},{9,1},{... | collective-permute-start | bytes 1769480 | tf_op jit(solution)/shard_map/far3/ppermute | solution.py:379
  50.5 12.1 %collective-permute-done.12.rest_2_.rest_18_ = bf16[384,768]{1,0:T(8,128)(2,1)} collective-permute-done((bf16[384,768]{1,0:T(8,128)(2,1)S(1)}, bf16[384,768]{1,0:T(8,128)(2,1)}, u32[]{:S(2)}, u32[]{:S(2)}) %collective-permute-start.12) | collective-permute-done | bytes 589856 | tf_op jit(solution)/shard_map/y2/ppermute | solution.py:379
  62.6 1.2 collective-permute-done.11.rest_1_.rest_17_
  63.9 2.0 %collective-permute-done.13 = bf16[384,768]{1,0:T(8,128)(2,1)S(1)} collective-permute-done((bf16[384,768]{1,0:T(8,128)(2,1)S(1)}, bf16[384,768]{1,0:T(8,128)(2,1)S(1)}, u32[]{:S(2)}, u32[]{:S(2)}) %collective-permute-start.13) | collective-permute-done | bytes 589856 | tf_op jit(solution)/shard_map/far3/ppermute | solution.py:379
  66.7 2.0 %collective-permute-done.20.rest_4_.rest_20_ = bf16[384,768]{1,0:T(8,128)(2,1)S(1)} collective-permute-done((bf16[384,768]{1,0:T(8,128)(2,1)S(1)}, bf16[384,768]{1,0:T(8,128)(2,1)S(1)}, u32[]{:S(2)}, u32[]{:S(2)}) %collective-permute-start.20) | collective-permute-done | bytes 589856 | tf_op jit(solution)/shard_map/core_u2/ppermute | solution.py:379
  69.4 1.5 %collective-permute-start.17 = (bf16[384,768]{1,0:T(8,128)(2,1)}, bf16[384,768]{1,0:T(8,128)(2,1)}, u32[]{:S(2)}, u32[]{:S(2)}) collective-permute-start(bf16[384,768]{1,0:T(8,128)(2,1)} %collective-permute-done.rest_0_.rest_8_), channel_id=1, source_target_pairs={{0,1},{1,0},{2,3},{3,2},{4,5},{5,4},{6,7},{7,6},{8,9},{9,8},{10,11... | collective-permute-start | bytes 1769480 | tf_op jit(solution)/shard_map/x1/ppermute | solution.py:379
  71.9 1.4 add.18.rest_0_.rest_24_
  73.3 6.3 %project.4 = (bf16[3,384,768]{2,1,0:T(8,128)(2,1)}, bf16[3,768,384]{2,1,0:T(8,128)(2,1)}) custom-call(s32[3]{0:T(128)S(1)} %pad_add_fusion.at_ref, s32[1]{0:T(128)} %bitcast.3.plane_ref, bf16[1536,768]{1,0:T(8,128)(2,1)S(1)} %norm.1.n_ref, bf16[384,768]{1,0:T(8,128)(2,1)} %copy-done.6, bf16[384,768]{1,0:T(8,128)(2,1)} %copy-done.9, ...), custom_call_target="tpu_custom_call" | custom-call | flops 2717908992 | bytes 5898240 | tf_op jit(solution)/shard_map/project/pallas_call | solution.py:207
  79.6 5.5 %collective-permute-done.17.rest_1_.rest_9_ = bf16[384,768]{1,0:T(8,128)(2,1)} collective-permute-done((bf16[384,768]{1,0:T(8,128)(2,1)}, bf16[384,768]{1,0:T(8,128)(2,1)}, u32[]{:S(2)}, u32[]{:S(2)}) %collective-permute-start.17) | collective-permute-done | bytes 589856 | tf_op jit(solution)/shard_map/x1/ppermute | solution.py:379
  85.0 1.2 collective-permute-done.19.rest_3_.rest_11_
  86.3 2.2 %collective-permute-done.26.rest_5_.rest_13_ = bf16[384,768]{1,0:T(8,128)(2,1)S(1)} collective-permute-done((bf16[384,768]{1,0:T(8,128)(2,1)}, bf16[384,768]{1,0:T(8,128)(2,1)S(1)}, u32[]{:S(2)}, u32[]{:S(2)}) %collective-permute-start.26) | collective-permute-done | bytes 589856 | tf_op jit(solution)/shard_map/core_x1/ppermute | solution.py:379
  88.6 2.1 %collective-permute-done.27.rest_7_.rest_15_ = bf16[384,768]{1,0:T(8,128)(2,1)S(1)} collective-permute-done((bf16[384,768]{1,0:T(8,128)(2,1)}, bf16[384,768]{1,0:T(8,128)(2,1)S(1)}, u32[]{:S(2)}, u32[]{:S(2)}) %collective-permute-start.27) | collective-permute-done | bytes 589856 | tf_op jit(solution)/shard_map/core_d1/ppermute | solution.py:379
  91.1 1.5 %collective-permute-start.24 = (bf16[384,768]{1,0:T(8,128)(2,1)S(1)}, bf16[384,768]{1,0:T(8,128)(2,1)}, u32[]{:S(2)}, u32[]{:S(2)}) collective-permute-start(bf16[384,768]{1,0:T(8,128)(2,1)S(1)} %add.18.rest_0_.rest_24_), channel_id=1, source_target_pairs={{0,4},{2,6},{4,0},{6,2},{8,12},{10,14},{12,8},{14,10},{16,20},{18,... | collective-permute-start | bytes 1769480 | tf_op jit(solution)/shard_map/y3/ppermute | solution.py:379
  94.0 6.3 %project.5 = (bf16[3,384,768]{2,1,0:T(8,128)(2,1)}, bf16[3,768,384]{2,1,0:T(8,128)(2,1)}) custom-call(s32[3]{0:T(128)S(1)} %pad_add_fusion.at_ref, s32[1]{0:T(128)} %bitcast.4.plane_ref, bf16[1536,768]{1,0:T(8,128)(2,1)S(1)} %norm.1.n_ref, bf16[384,768]{1,0:T(8,128)(2,1)} %collective-permute-done.rest_0_.rest_8_, ...), custom_call_target="tpu_custom_call" | custom-call | flops 2717908992 | bytes 5898240 | tf_op jit(solution)/shard_map/project/pallas_call | solution.py:207
  100.3 6.3 %project.6 = (bf16[3,384,768]{2,1,0:T(8,128)(2,1)}, bf16[3,768,384]{2,1,0:T(8,128)(2,1)}) custom-call(s32[3]{0:T(128)S(1)} %pad_add_fusion.at_ref, s32[1]{0:T(128)} %bitcast.5.plane_ref, bf16[1536,768]{1,0:T(8,128)(2,1)S(1)} %norm.1.n_ref, bf16[384,768]{1,0:T(8,128)(2,1)} %copy-done.4, bf16[384,768]{1,0:T(8,128)(2,1)} %collective-permute-done.11.rest_1_.rest_17_, ...), custom_call_target="tpu_custom_call" | custom-call | flops 2717908992 | bytes 5898240 | tf_op jit(solution)/shard_map/project/pallas_call | solution.py:207
  106.7 1.0 collective-permute-done.23.rest_1_.rest_25_
  110.0 1.7 %collective-permute-done.31.rest_6_.rest_30_ = bf16[384,768]{1,0:T(8,128)(2,1)S(1)} collective-permute-done((bf16[384,768]{1,0:T(8,128)(2,1)}, bf16[384,768]{1,0:T(8,128)(2,1)S(1)}, u32[]{:S(2)}, u32[]{:S(2)}) %collective-permute-start.31) | collective-permute-done | bytes 589856 | tf_op jit(solution)/shard_map/core_y3/ppermute | solution.py:379
  112.5 6.3 %project.7 = (bf16[3,384,768]{2,1,0:T(8,128)(2,1)}, bf16[3,768,384]{2,1,0:T(8,128)(2,1)}) custom-call(s32[3]{0:T(128)S(1)} %pad_add_fusion.at_ref, s32[1]{0:T(128)} %bitcast.6.plane_ref, bf16[1536,768]{1,0:T(8,128)(2,1)S(1)} %norm.1.n_ref, bf16[384,768]{1,0:T(8,128)(2,1)} %copy-done.5, bf16[384,768]{1,0:T(8,128)(2,1)} %collective-permute-done.23.rest_1_.rest_25_, ...), custom_call_target="tpu_custom_call" | custom-call | flops 2717908992 | bytes 5898240 | tf_op jit(solution)/shard_map/project/pallas_call | solution.py:207
  118.8 10.4 %attend.1.att_ref = bf16[768,1536]{1,0:T(8,128)(2,1)S(1)} custom-call(s32[4]{0:T(128)S(1)} %pad_add_fusion.1.planes_ref, s32[12]{0:T(128)S(1)} %copy-done.2, bf16[3,384,768]{2,1,0:T(8,128)(2,1)} %get-tuple-element.91.p0, bf16[3,768,384]{2,1,0:T(8,128)(2,1)} %get-tuple-element.92.k0, bf16[3,384,768]{2,1,0:T(8,128)(2,1)} %get-tuple-element.109.p1, ...), custom_call_target="tpu_custom_call" | custom-call | flops 6039797760 | bytes 9437184 | tf_op jit(solution)/shard_map/attend/pallas_call | solution.py:292
  129.2 8.9 %output.1 = bf16[768,1536]{1,0:T(8,128)(2,1)} custom-call(s32[3]{0:T(128)S(1)} %pad_add_fusion.at_ref, s32[4]{0:T(128)S(1)} %pad_add_fusion.1.planes_ref, s32[12]{0:T(128)S(1)} %copy-done.2, s32[1]{0:T(128)S(6)} %copy.8.live_ref, bf16[768,1536]{1,0:T(8,128)(2,1)S(1)} %attend.1.att_ref, bf16[768,1536]{1,0:T(8,128)(2,1)S(1)} %bitcast.11, ...), custom_call_target="tpu_custom_call" | custom-call | flops 3623878656 | bytes 11796480 | tf_op jit(solution)/shard_map/output/pallas_call | solution.py:356
  (98 shorter events, 14.1 us)
Async XLA Ops:
  1.1 16.0 %collective-permute-start.4 = (bf16[384,768]{1,0:T(8,128)(2,1)S(1)}, bf16[384,768]{1,0:T(8,128)(2,1)S(1)}, u32[]{:S(2)}, u32[]{:S(2)}) collective-permute-start(bf16[384,768]{1,0:T(8,128)(2,1)S(1)} %pad_maximum_fusion.rest_0_), channel_id=1, source_target_pairs={{0,2},{2,0},{4,6},{6,4},{8,10},{10,8},{12,14},{14,12},{16,18},{18,... | collective-permute-start | bytes 1769480 | tf_op jit(solution)/shard_map/core_u0/ppermute | solution.py:379
  1.7 16.5 %collective-permute-start.3 = (bf16[384,768]{1,0:T(8,128)(2,1)S(1)}, bf16[384,768]{1,0:T(8,128)(2,1)S(1)}, u32[]{:S(2)}, u32[]{:S(2)}) collective-permute-start(bf16[384,768]{1,0:T(8,128)(2,1)S(1)} %pad_maximum_fusion.rest_0_), channel_id=1, source_target_pairs={{0,4},{2,6},{4,0},{6,2},{8,12},{10,14},{12,8},{14,10},{16,20},{18,... | collective-permute-start | bytes 1769480 | tf_op jit(solution)/shard_map/y0/ppermute | solution.py:379
  4.3 15.4 %collective-permute-start.2 = (bf16[384,768]{1,0:T(8,128)(2,1)S(1)}, bf16[384,768]{1,0:T(8,128)(2,1)S(1)}, u32[]{:S(2)}, u32[]{:S(2)}) collective-permute-start(bf16[384,768]{1,0:T(8,128)(2,1)S(1)} %pad_maximum_fusion.rest_0_), channel_id=1, source_target_pairs={{0,1},{1,0},{2,3},{3,2},{4,5},{5,4},{6,7},{7,6},{8,9},{9,8},{10,11... | collective-permute-start | bytes 1769480 | tf_op jit(solution)/shard_map/x0/ppermute | solution.py:379
  5.8 13.9 %collective-permute-start.1 = (bf16[384,768]{1,0:T(8,128)(2,1)S(1)}, bf16[384,768]{1,0:T(8,128)(2,1)S(1)}, u32[]{:S(2)}, u32[]{:S(2)}) collective-permute-start(bf16[384,768]{1,0:T(8,128)(2,1)S(1)} %pad_maximum_fusion.rest_0_), channel_id=1, source_target_pairs={{8,16},{10,18},{12,20},{14,22},{16,8},{18,10},{20,12},{22,14},{9,1... | collective-permute-start | bytes 1769480 | tf_op jit(solution)/shard_map/near2/ppermute | solution.py:379
  6.4 17.6 %collective-permute-start = (bf16[384,768]{1,0:T(8,128)(2,1)S(1)}, bf16[384,768]{1,0:T(8,128)(2,1)}, u32[]{:S(2)}, u32[]{:S(2)}) collective-permute-start(bf16[384,768]{1,0:T(8,128)(2,1)S(1)} %pad_maximum_fusion.rest_0_), channel_id=1, source_target_pairs={{0,8},{2,10},{4,12},{6,14},{8,0},{10,2},{12,4},{14,6},{16,24},{18,... | collective-permute-start | bytes 1769480 | tf_op jit(solution)/shard_map/u1/ppermute | solution.py:379
  24.1 3.1 %collective-permute-start.9 = (bf16[384,768]{1,0:T(8,128)(2,1)S(1)}, bf16[384,768]{1,0:T(8,128)(2,1)S(1)}, u32[]{:S(2)}, u32[]{:S(2)}) collective-permute-start(bf16[384,768]{1,0:T(8,128)(2,1)S(1)} %collective-permute-done.2.rest_1_), channel_id=1, source_target_pairs={{0,2},{2,0},{4,6},{6,4},{8,10},{10,8},{12,14},{14,12},{16,18},{18,... | collective-permute-start | bytes 1769480 | tf_op jit(solution)/shard_map/core_x0/ppermute | solution.py:379
  24.1 19.3 %collective-permute-start.8 = (bf16[384,768]{1,0:T(8,128)(2,1)}, bf16[384,768]{1,0:T(8,128)(2,1)S(1)}, u32[]{:S(2)}, u32[]{:S(2)}) collective-permute-start(bf16[384,768]{1,0:T(8,128)(2,1)} %collective-permute-done.rest_0_.rest_8_), channel_id=1, source_target_pairs={{0,4},{2,6},{4,0},{6,2},{8,12},{10,14},{12,8},{14,10},{16,20},{18,... | collective-permute-start | bytes 1769480 | tf_op jit(solution)/shard_map/y1/ppermute | solution.py:379
  24.6 18.8 %collective-permute-start.6 = (bf16[384,768]{1,0:T(8,128)(2,1)}, bf16[384,768]{1,0:T(8,128)(2,1)S(1)}, u32[]{:S(2)}, u32[]{:S(2)}) collective-permute-start(bf16[384,768]{1,0:T(8,128)(2,1)} %collective-permute-done.rest_0_.rest_8_), channel_id=1, source_target_pairs={{8,16},{10,18},{12,20},{14,22},{16,8},{18,10},{20,12},{22,14},{9,1... | collective-permute-start | bytes 1769480 | tf_op jit(solution)/shard_map/near3/ppermute | solution.py:379
  25.3 18.1 %collective-permute-start.5 = (bf16[384,768]{1,0:T(8,128)(2,1)S(1)}, bf16[384,768]{1,0:T(8,128)(2,1)S(1)}, u32[]{:S(2)}, u32[]{:S(2)}) collective-permute-start(bf16[384,768]{1,0:T(8,128)(2,1)S(1)} %collective-permute-done.1), channel_id=1, source_target_pairs={{8,0},{10,2},{12,4},{14,6},{16,24},{18,26},{20,28},{22,30},{9,1},{... | collective-permute-start | bytes 1769480 | tf_op jit(solution)/shard_map/far2/ppermute | solution.py:379
  26.6 16.8 %collective-permute-start.7 = (bf16[384,768]{1,0:T(8,128)(2,1)S(1)}, bf16[384,768]{1,0:T(8,128)(2,1)}, u32[]{:S(2)}, u32[]{:S(2)}) collective-permute-start(bf16[384,768]{1,0:T(8,128)(2,1)S(1)} %collective-permute-done.3.rest_2_), channel_id=1, source_target_pairs={{0,1},{1,0},{2,3},{3,2},{4,5},{5,4},{6,7},{7,6},{8,9},{9,8},{10,11... | collective-permute-start | bytes 1769480 | tf_op jit(solution)/shard_map/d0/ppermute | solution.py:379
  27.2 16.2 %collective-permute-start.10 = (bf16[384,768]{1,0:T(8,128)(2,1)S(1)}, bf16[384,768]{1,0:T(8,128)(2,1)S(1)}, u32[]{:S(2)}, u32[]{:S(2)}) collective-permute-start(bf16[384,768]{1,0:T(8,128)(2,1)S(1)} %collective-permute-done.3.rest_2_), channel_id=1, source_target_pairs={{0,2},{2,0},{4,6},{6,4},{8,10},{10,8},{12,14},{14,12},{16,18},{18,... | collective-permute-start | bytes 1769480 | tf_op jit(solution)/shard_map/core_y0/ppermute | solution.py:379
  43.4 2.3 %collective-permute-start.14 = (bf16[384,768]{1,0:T(8,128)(2,1)}, bf16[384,768]{1,0:T(8,128)(2,1)S(1)}, u32[]{:S(2)}, u32[]{:S(2)}) collective-permute-start(bf16[384,768]{1,0:T(8,128)(2,1)} %collective-permute-done.7.rest_3_), channel_id=1, source_target_pairs={{0,2},{2,0},{4,6},{6,4},{8,10},{10,8},{12,14},{14,12},{16,18},{18,... | collective-permute-start | bytes 1769480 | tf_op jit(solution)/shard_map/core_d0/ppermute | solution.py:379
  46.6 3.9 %collective-permute-start.15 = (bf16[384,768]{1,0:T(8,128)(2,1)S(1)}, bf16[384,768]{1,0:T(8,128)(2,1)S(1)}, u32[]{:S(2)}, u32[]{:S(2)}) collective-permute-start(bf16[384,768]{1,0:T(8,128)(2,1)S(1)} %collective-permute-done.8.rest_2_.rest_10_), channel_id=1, source_target_pairs={{0,2},{2,0},{4,6},{6,4},{8,10},{10,8},{12,14},{14,12},{16,18},{18,... | collective-permute-start | bytes 1769480 | tf_op jit(solution)/shard_map/core_y1/ppermute | solution.py:379
  46.8 15.8 %collective-permute-start.12 = (bf16[384,768]{1,0:T(8,128)(2,1)S(1)}, bf16[384,768]{1,0:T(8,128)(2,1)}, u32[]{:S(2)}, u32[]{:S(2)}) collective-permute-start(bf16[384,768]{1,0:T(8,128)(2,1)S(1)} %add.17.rest_0_.rest_16_), channel_id=1, source_target_pairs={{0,4},{2,6},{4,0},{6,2},{8,12},{10,14},{12,8},{14,10},{16,20},{18,... | collective-permute-start | bytes 1769480 | tf_op jit(solution)/shard_map/y2/ppermute | solution.py:379
  48.4 15.4 %collective-permute-start.11 = (bf16[384,768]{1,0:T(8,128)(2,1)S(1)}, bf16[384,768]{1,0:T(8,128)(2,1)}, u32[]{:S(2)}, u32[]{:S(2)}) collective-permute-start(bf16[384,768]{1,0:T(8,128)(2,1)S(1)} %add.17.rest_0_.rest_16_), channel_id=1, source_target_pairs={{0,1},{1,0},{2,3},{3,2},{4,5},{5,4},{6,7},{7,6},{8,9},{9,8},{10,11... | collective-permute-start | bytes 1769480 | tf_op jit(solution)/shard_map/x2/ppermute | solution.py:379
  49.0 16.9 %collective-permute-start.13 = (bf16[384,768]{1,0:T(8,128)(2,1)S(1)}, bf16[384,768]{1,0:T(8,128)(2,1)S(1)}, u32[]{:S(2)}, u32[]{:S(2)}) collective-permute-start(bf16[384,768]{1,0:T(8,128)(2,1)S(1)} %collective-permute-done.6), channel_id=1, source_target_pairs={{8,0},{10,2},{12,4},{14,6},{16,24},{18,26},{20,28},{22,30},{9,1},{... | collective-permute-start | bytes 1769480 | tf_op jit(solution)/shard_map/far3/ppermute | solution.py:379
  50.5 16.3 %collective-permute-start.16 = (bf16[384,768]{1,0:T(8,128)(2,1)}, bf16[384,768]{1,0:T(8,128)(2,1)S(1)}, u32[]{:S(2)}, u32[]{:S(2)}) collective-permute-start(bf16[384,768]{1,0:T(8,128)(2,1)} %collective-permute-done.rest_0_.rest_8_), channel_id=1, source_target_pairs={{0,2},{2,0},{4,6},{6,4},{8,10},{10,8},{12,14},{14,12},{16,18},{18,... | collective-permute-start | bytes 1769480 | tf_op jit(solution)/shard_map/core_u1/ppermute | solution.py:379
  68.7 2.2 %collective-permute-start.21 = (bf16[384,768]{1,0:T(8,128)(2,1)}, bf16[384,768]{1,0:T(8,128)(2,1)S(1)}, u32[]{:S(2)}, u32[]{:S(2)}) collective-permute-start(bf16[384,768]{1,0:T(8,128)(2,1)} %collective-permute-done.11.rest_1_.rest_17_), channel_id=1, source_target_pairs={{0,2},{2,0},{4,6},{6,4},{8,10},{10,8},{12,14},{14,12},{16,18},{18,... | collective-permute-start | bytes 1769480 | tf_op jit(solution)/shard_map/core_x2/ppermute | solution.py:379
  68.9 17.4 %collective-permute-start.18 = (bf16[384,768]{1,0:T(8,128)(2,1)}, bf16[384,768]{1,0:T(8,128)(2,1)}, u32[]{:S(2)}, u32[]{:S(2)}) collective-permute-start(bf16[384,768]{1,0:T(8,128)(2,1)} %collective-permute-done.11.rest_1_.rest_17_), channel_id=1, source_target_pairs={{0,4},{2,6},{4,0},{6,2},{8,12},{10,14},{12,8},{14,10},{16,20},{18,... | collective-permute-start | bytes 1769480 | tf_op jit(solution)/shard_map/d2/ppermute | solution.py:379
  69.4 15.6 %collective-permute-start.17 = (bf16[384,768]{1,0:T(8,128)(2,1)}, bf16[384,768]{1,0:T(8,128)(2,1)}, u32[]{:S(2)}, u32[]{:S(2)}) collective-permute-start(bf16[384,768]{1,0:T(8,128)(2,1)} %collective-permute-done.rest_0_.rest_8_), channel_id=1, source_target_pairs={{0,1},{1,0},{2,3},{3,2},{4,5},{5,4},{6,7},{7,6},{8,9},{9,8},{10,11... | collective-permute-start | bytes 1769480 | tf_op jit(solution)/shard_map/x1/ppermute | solution.py:379
  70.9 15.3 %collective-permute-start.19 = (bf16[384,768]{1,0:T(8,128)(2,1)}, bf16[384,768]{1,0:T(8,128)(2,1)}, u32[]{:S(2)}, u32[]{:S(2)}) collective-permute-start(bf16[384,768]{1,0:T(8,128)(2,1)} %collective-permute-done.7.rest_3_), channel_id=1, source_target_pairs={{0,8},{2,10},{4,12},{6,14},{8,0},{10,2},{12,4},{14,6},{16,24},{18,... | collective-permute-start | bytes 1769480 | tf_op jit(solution)/shard_map/d1/ppermute | solution.py:379
  71.0 15.3 %collective-permute-start.22 = (bf16[384,768]{1,0:T(8,128)(2,1)}, bf16[384,768]{1,0:T(8,128)(2,1)}, u32[]{:S(2)}, u32[]{:S(2)}) collective-permute-start(bf16[384,768]{1,0:T(8,128)(2,1)} %collective-permute-done.12.rest_2_.rest_18_), channel_id=1, source_target_pairs={{0,2},{2,0},{4,6},{6,4},{8,10},{10,8},{12,14},{14,12},{16,18},{18,... | collective-permute-start | bytes 1769480 | tf_op jit(solution)/shard_map/core_y2/ppermute | solution.py:379
  86.2 2.2 %collective-permute-start.26 = (bf16[384,768]{1,0:T(8,128)(2,1)}, bf16[384,768]{1,0:T(8,128)(2,1)S(1)}, u32[]{:S(2)}, u32[]{:S(2)}) collective-permute-start(bf16[384,768]{1,0:T(8,128)(2,1)} %collective-permute-done.17.rest_1_.rest_9_), channel_id=1, source_target_pairs={{0,2},{2,0},{4,6},{6,4},{8,10},{10,8},{12,14},{14,12},{16,18},{18,... | collective-permute-start | bytes 1769480 | tf_op jit(solution)/shard_map/core_x1/ppermute | solution.py:379
  88.5 2.2 %collective-permute-start.27 = (bf16[384,768]{1,0:T(8,128)(2,1)}, bf16[384,768]{1,0:T(8,128)(2,1)S(1)}, u32[]{:S(2)}, u32[]{:S(2)}) collective-permute-start(bf16[384,768]{1,0:T(8,128)(2,1)} %collective-permute-done.19.rest_3_.rest_11_), channel_id=1, source_target_pairs={{0,2},{2,0},{4,6},{6,4},{8,10},{10,8},{12,14},{14,12},{16,18},{18,... | collective-permute-start | bytes 1769480 | tf_op jit(solution)/shard_map/core_d1/ppermute | solution.py:379
  90.7 2.5 %collective-permute-start.28 = (bf16[384,768]{1,0:T(8,128)(2,1)}, bf16[384,768]{1,0:T(8,128)(2,1)S(1)}, u32[]{:S(2)}, u32[]{:S(2)}) collective-permute-start(bf16[384,768]{1,0:T(8,128)(2,1)} %collective-permute-done.18.rest_3_.rest_19_), channel_id=1, source_target_pairs={{0,2},{2,0},{4,6},{6,4},{8,10},{10,8},{12,14},{14,12},{16,18},{18,... | collective-permute-start | bytes 1769480 | tf_op jit(solution)/shard_map/core_d2/ppermute | solution.py:379
  90.8 15.9 %collective-permute-start.25 = (bf16[384,768]{1,0:T(8,128)(2,1)}, bf16[384,768]{1,0:T(8,128)(2,1)}, u32[]{:S(2)}, u32[]{:S(2)}) collective-permute-start(bf16[384,768]{1,0:T(8,128)(2,1)} %collective-permute-done.18.rest_3_.rest_19_), channel_id=1, source_target_pairs={{0,8},{2,10},{4,12},{6,14},{8,0},{10,2},{12,4},{14,6},{16,24},{18,... | collective-permute-start | bytes 1769480 | tf_op jit(solution)/shard_map/d3/ppermute | solution.py:379
  91.1 15.6 %collective-permute-start.24 = (bf16[384,768]{1,0:T(8,128)(2,1)S(1)}, bf16[384,768]{1,0:T(8,128)(2,1)}, u32[]{:S(2)}, u32[]{:S(2)}) collective-permute-start(bf16[384,768]{1,0:T(8,128)(2,1)S(1)} %add.18.rest_0_.rest_24_), channel_id=1, source_target_pairs={{0,4},{2,6},{4,0},{6,2},{8,12},{10,14},{12,8},{14,10},{16,20},{18,... | collective-permute-start | bytes 1769480 | tf_op jit(solution)/shard_map/y3/ppermute | solution.py:379
  92.6 15.1 %collective-permute-start.23 = (bf16[384,768]{1,0:T(8,128)(2,1)S(1)}, bf16[384,768]{1,0:T(8,128)(2,1)}, u32[]{:S(2)}, u32[]{:S(2)}) collective-permute-start(bf16[384,768]{1,0:T(8,128)(2,1)S(1)} %add.18.rest_0_.rest_24_), channel_id=1, source_target_pairs={{0,1},{1,0},{2,3},{3,2},{4,5},{5,4},{6,7},{7,6},{8,9},{9,8},{10,11... | collective-permute-start | bytes 1769480 | tf_op jit(solution)/shard_map/x3/ppermute | solution.py:379
  94.0 13.8 %collective-permute-start.29 = (bf16[384,768]{1,0:T(8,128)(2,1)S(1)}, bf16[384,768]{1,0:T(8,128)(2,1)}, u32[]{:S(2)}, u32[]{:S(2)}) collective-permute-start(bf16[384,768]{1,0:T(8,128)(2,1)S(1)} %add.18.rest_0_.rest_24_), channel_id=1, source_target_pairs={{0,2},{2,0},{4,6},{6,4},{8,10},{10,8},{12,14},{14,12},{16,18},{18,... | collective-permute-start | bytes 1769480 | tf_op jit(solution)/shard_map/core_u3/ppermute | solution.py:379
  107.8 2.2 %collective-permute-start.30 = (bf16[384,768]{1,0:T(8,128)(2,1)}, bf16[384,768]{1,0:T(8,128)(2,1)S(1)}, u32[]{:S(2)}, u32[]{:S(2)}) collective-permute-start(bf16[384,768]{1,0:T(8,128)(2,1)} %collective-permute-done.23.rest_1_.rest_25_), channel_id=1, source_target_pairs={{0,2},{2,0},{4,6},{6,4},{8,10},{10,8},{12,14},{14,12},{16,18},{18,... | collective-permute-start | bytes 1769480 | tf_op jit(solution)/shard_map/core_x3/ppermute | solution.py:379
  107.8 3.9 %collective-permute-start.31 = (bf16[384,768]{1,0:T(8,128)(2,1)}, bf16[384,768]{1,0:T(8,128)(2,1)S(1)}, u32[]{:S(2)}, u32[]{:S(2)}) collective-permute-start(bf16[384,768]{1,0:T(8,128)(2,1)} %collective-permute-done.24.rest_2_.rest_26_), channel_id=1, source_target_pairs={{0,2},{2,0},{4,6},{6,4},{8,10},{10,8},{12,14},{14,12},{16,18},{18,... | collective-permute-start | bytes 1769480 | tf_op jit(solution)/shard_map/core_y3/ppermute | solution.py:379
  108.3 3.5 %collective-permute-start.32 = (bf16[384,768]{1,0:T(8,128)(2,1)}, bf16[384,768]{1,0:T(8,128)(2,1)}, u32[]{:S(2)}, u32[]{:S(2)}) collective-permute-start(bf16[384,768]{1,0:T(8,128)(2,1)} %collective-permute-done.25.rest_3_.rest_27_), channel_id=1, source_target_pairs={{0,2},{2,0},{4,6},{6,4},{8,10},{10,8},{12,14},{14,12},{16,18},{18,... | collective-permute-start | bytes 1769480 | tf_op jit(solution)/shard_map/core_d3/ppermute | solution.py:379
  (26 other events, 386.0 us)

commit v5 on v4

--- a/solution.py
+++ b/solution.py
@@ -151,42 +151,59 @@
     return ((x, y), (1 - x, y), (x, 1 - y), (1 - x, 1 - y))
 
 
-def project_kernel(key_chunk, value_chunk, at_ref, plane_ref, n_ref, *rest):
-    pieces, (p_ref, k_ref, w_ref, rows_ref, cols_ref, sems, out_sems) = rest[:8], rest[8:]
+def piece_rows(ref, spot, start, rows):
+    part = pl.ds(start, rows)
+    return ref.at[part, :] if spot is None else ref.at[spot, part, :]
+
+
+def start_columns(at_ref, pieces, spots, rows, w_ref, sems):
     x, y, core = at_ref[0], at_ref[1], at_ref[2]
-    rows, lanes = w_ref.shape[0] // 4, w_ref.shape[1] // 2
+    lanes = w_ref.shape[1] // 2
     for i, (px, py) in enumerate(places(x, y)):
         for owner, c in ((0, core), (1, 1 - core)):
             row = pl.multiple_of((2 * py + c) * rows, 16)
             lane = pl.multiple_of(px * lanes, 128)
             pltpu.make_async_copy(
-                pieces[4 * owner + i].at[pl.ds(0, rows), :],
+                piece_rows(pieces[4 * owner + i], spots[4 * owner + i], 0, rows),
                 w_ref.at[pl.ds(row, rows), pl.ds(lane, lanes)],
                 sems.at[py * 4 + 2 * owner + i % 2],
             ).start()
-    count, chunk, tokens = p_ref.shape
-
-    def landed(which):
-        for i in range(4):
-            pltpu.make_async_copy(
-                pieces[0].at[pl.ds(0, rows), :],
-                w_ref.at[pl.ds(0, rows), pl.ds(0, lanes)],
-                sems.at[4 * which + i],
-            ).wait()
-
+
+
+def wait_columns(half, pieces, spots, rows, w_ref, sems):
+    lanes = w_ref.shape[1] // 2
+    for i in range(4):
+        pltpu.make_async_copy(
+            piece_rows(pieces[0], spots[0], 0, rows),
+            w_ref.at[pl.ds(0, rows), pl.ds(0, lanes)],
+            sems.at[4 * half + i],
+        ).wait()
+
+
+def project_chunk(m, which, parts, w_ref, n_ref):
+    tokens = n_ref.shape[1]
+    chunk = n_ref.shape[0] // parts
+    got = jnp.dot(w_ref[m * chunk : (m + 1) * chunk, :], n_ref[...], preferred_element_type=F32)
+    got = got.reshape(chunk // HEAD_DIM, HEAD_DIM, tokens)
+    ms = jnp.mean(got * got, axis=1, keepdims=True)
+    scale = jnp.where(which < 2 * parts, lax.rsqrt(ms + EPS), 1.0)
+    scale = jnp.where(which < parts, scale * HEAD_DIM**-0.5, scale)
+    return (got * scale).astype(BF).reshape(chunk, tokens)
+
+
+def project_kernel(spots, parts, at_ref, plane_ref, n_ref, *rest):
+    pieces, (p_ref, k_ref, w_ref, rows_ref, cols_ref, sems, out_sems) = rest[:8], rest[8:]
+    rows = w_ref.shape[0] // 4
+    start_columns(at_ref, pieces, spots, rows, w_ref, sems)
+    count = p_ref.shape[0]
     for m in range(count):
         if m < 2:
-            landed(m)
+            wait_columns(m, pieces, spots, rows, w_ref, sems)
         which = plane_ref[0] * count + m
-        got = jnp.dot(w_ref[m * chunk : (m + 1) * chunk, :], n_ref[...], preferred_element_type=F32)
-        got = got.reshape(chunk // HEAD_DIM, HEAD_DIM, tokens)
-        ms = jnp.mean(got * got, axis=1, keepdims=True)
-        scale = jnp.where(which < value_chunk, lax.rsqrt(ms + EPS), 1.0)
-        scale = jnp.where(which < key_chunk, scale * HEAD_DIM**-0.5, scale)
-        out = (got * scale).astype(BF).reshape(chunk, tokens)
+        out = project_chunk(m, which, parts, w_ref, n_ref)
         rows_ref[m] = out
         cols_ref[m] = out.T
-        is_key = (which >= key_chunk) & (which < value_chunk)
+        is_key = (which >= parts) & (which < 2 * parts)
 
         @pl.when(is_key)
         def _():
@@ -202,10 +219,11 @@
 
 def project(place, plane, normed, pieces, rows):
     width, tokens = normed.shape
-    chunk = width // 4
+    parts = 4
+    chunk = width // parts
     count = 4 * rows // chunk
     return pl.pallas_call(
-        functools.partial(project_kernel, 4, 8),
+        functools.partial(project_kernel, [spot for _, spot in pieces], parts),
         out_shape=(
             pltpu.HBM((count, chunk, tokens), BF),
             pltpu.HBM((count, tokens, chunk), BF),
@@ -222,31 +240,55 @@
         compiler_params=params(24),
         cost_estimate=cost(8 * rows * width * tokens, 2 * (4 * rows + tokens) * width),
         name="project",
-    )(place, plane, normed, *map(far, pieces))
-
-
-def attend_kernel(
-    planes_ref, lens_ref, p0, k0, p1, k1, p2, k2, p3, k3, out_ref, q_ref, k_ref, v_ref, mask_ref, sems
+    )(place, plane, normed, *[far(value) for value, _ in pieces])
+
+
+def finish_kernel(
+    spots, rows, at_ref, planes_ref, lens_ref, live_ref, n_ref, lat_ref, p0, k0, p1, k1, p2, k2, *rest
 ):
-    count, chunk, tokens = p0.shape
-    for s, (p, k) in enumerate(((p0, k0), (p1, k1), (p2, k2), (p3, k3))):
-        for m in range(count):
-            which = planes_ref[s] * count + m
-            sem = sems.at[which]
-
-            @pl.when(which < 4)
-            def _():
-                pltpu.make_async_copy(p.at[m], q_ref.at[jnp.minimum(which, 3)], sem).start()
-
-            @pl.when((which >= 4) & (which < 8))
-            def _():
-                to = k_ref.at[jnp.clip(which - 4, 0, 3)]
-                pltpu.make_async_copy(k.at[m], to, sem).start()
-
-            @pl.when(which >= 8)
-            def _():
-                to = v_ref.at[jnp.clip(which - 8, 0, 3)]
-                pltpu.make_async_copy(p.at[m], to, sem).start()
+    pieces, rest = rest[:-15], rest[-15:]
+    out_ref, w_ref, q_ref, k_ref, v_ref, mask_ref, e_ref, att_ref, wo_ref, done_ref = rest[:10]
+    w_sems, part_sems, wo_sems, out_sems, base_sems = rest[10:]
+    parts, chunk, tokens = q_ref.shape
+    count = p0.shape[0]
+    slots = wo_ref.shape[0]
+    last = slots - 1
+    x, y, core = at_ref[0], at_ref[1], at_ref[2]
+
+    start_columns(at_ref, pieces[8 * last :], spots[8 * last :], rows, w_ref, w_sems)
+    for part in range(parts):
+        for kind, to in ((0, q_ref), (1, k_ref), (2, v_ref)):
+            which = parts * kind + part
+            for s, (p, k) in enumerate(((p0, k0), (p1, k1), (p2, k2))):
+
+                @pl.when(planes_ref[which // count] == s)
+                def _():
+                    src = (k if kind == 1 else p).at[which % count]
+                    pltpu.make_async_copy(src, to.at[part], part_sems.at[which]).start()
+
+    cols, lanes = wo_ref.shape[1], wo_ref.shape[2] // 2
+    ours = cols // 4
+    skip = pieces[0].shape[-2] - ours
+    copies = []
+    for s in range(slots):
+        for owner, c in ((0, core), (1, 1 - core)):
+            for i, (px, py) in enumerate(places(x, y)):
+                at = 8 * s + 4 * owner + i
+                row = pl.multiple_of((2 * py + c) * ours, 16)
+                lane = pl.multiple_of(px * lanes, 128)
+                copies.append(
+                    pltpu.make_async_copy(
+                        piece_rows(pieces[at], spots[at], skip, ours),
+                        wo_ref.at[s, pl.ds(row, ours), pl.ds(lane, lanes)],
+                        wo_sems.at[at],
+                    )
+                )
+    bases = []
+    for s in range(slots):
+        spot = pl.ds(pl.multiple_of(planes_ref[s] * cols, 128), cols)
+        bases.append(pltpu.make_async_copy(lat_ref.at[:, spot], done_ref.at[s], base_sems.at[s]))
+    for c in copies + bases:
+        c.start()
 
     blocks = tokens // 128
     key = lax.broadcasted_iota(jnp.int32, (128, 256), 0)
@@ -255,14 +297,30 @@
         first = (key < WIN_TOK) & (query < WIN_TOK) & (key < lens_ref[2 * b])
         second = (key >= WIN_TOK) & (query >= WIN_TOK) & (key - WIN_TOK < lens_ref[2 * b + 1])
         mask_ref[b] = jnp.where(first | second, 1.0, 0.0).astype(F32)
+
+    for m in range(count):
+        if m < 2:
+            wait_columns(m, pieces[8 * last :], spots[8 * last :], rows, w_ref, w_sems)
+        which = planes_ref[last] * count + m
+        out = project_chunk(m, which, parts, w_ref, n_ref)
+        for kind, to in ((0, q_ref), (1, k_ref), (2, v_ref)):
+
+            @pl.when(which // parts == kind)
+            def _():
+                to[which % parts] = out.T if kind == 1 else out
+
     ones = jnp.ones((16, 128), BF)
     blank = jnp.zeros((HEAD_DIM, 128), BF)
     pairs = chunk // 128
 
-    @pl.loop(0, 4)
+    @pl.loop(0, parts)
     def _(part):
         for kind in range(3):
-            pltpu.make_async_copy(p0.at[0], q_ref.at[0], sems.at[4 * kind + part]).wait()
+            which = parts * kind + part
+
+            @pl.when(planes_ref[which // count] != last)
+            def _():
+                pltpu.make_async_copy(p0.at[0], q_ref.at[0], part_sems.at[which]).wait()
 
         @pl.loop(0, pairs)
         def _(i):
@@ -272,102 +330,78 @@
                 tok = pl.ds(b * 128, 128)
                 q = q_ref[part, at, tok]
                 k = k_ref[part, tok, at]
-                v = v_ref[part, at, tok]
                 q0 = jnp.concatenate([q[:HEAD_DIM], blank], axis=0)
                 q1 = jnp.concatenate([blank, q[HEAD_DIM:]], axis=0)
                 scores = jnp.dot(k, jnp.concatenate([q0, q1], axis=1), preferred_element_type=F32)
-                weights = (jnp.exp(scores) * mask_ref[b]).astype(BF)
+                e_ref[b] = (jnp.exp(scores) * mask_ref[b]).astype(BF)
+            for b in range(blocks):
+                tok = pl.ds(b * 128, 128)
+                v = v_ref[part, at, tok]
                 got = jnp.dot(
-                    jnp.concatenate([v, ones], axis=0), weights, preferred_element_type=F32
+                    jnp.concatenate([v, ones], axis=0), e_ref[b], preferred_element_type=F32
                 )
-                share = 1.0 / got[128:129, :]
+                token = lax.broadcasted_iota(jnp.int32, (1, 256), 1) % 128
+                first = (token < WIN_TOK) & (token < lens_ref[2 * b])
+                second = (token >= WIN_TOK) & (token - WIN_TOK < lens_ref[2 * b + 1])
+                keep = (first | second) & (b < live_ref[0])
+                share = jnp.where(keep, 1.0 / got[128:129, :], 0.0)
                 o0 = got[:HEAD_DIM, :128] * share[:, :128]
                 o1 = got[HEAD_DIM:128, 128:] * share[:, 128:]
-                out_ref[tok, out_at] = jnp.concatenate([o0, o1], axis=0).astype(BF).T
-
-
-def attend(planes, window_len, parts):
+                att_ref[tok, out_at] = jnp.concatenate([o0, o1], axis=0).astype(BF).T
+
+    outs = []
+    for s in range(slots):
+        for c in copies[8 * s : 8 * s + 8] + [bases[s]]:
+            c.wait()
+        spot = pl.ds(pl.multiple_of(planes_ref[s] * cols, 128), cols)
+        update = lax.dot_general(
+            att_ref[...], wo_ref[s], (((1,), (1,)), ((), ())), preferred_element_type=F32
+        )
+        done_ref[s] = (done_ref[s].astype(F32) + update).astype(BF)
+        outs.append(pltpu.make_async_copy(done_ref.at[s], out_ref.at[:, spot], out_sems.at[s]))
+        outs[s].start()
+    for c in outs:
+        c.wait()
+
+
+def finish(place, planes, window_len, live_blocks, normed, latents, parts, pieces, rows):
     count, chunk, tokens = parts[0][0].shape
-    width = 4 * chunk
+    width = normed.shape[0]
+    slots = len(pieces) // 8
     return pl.pallas_call(
-        attend_kernel,
+        functools.partial(finish_kernel, [spot for _, spot in pieces], rows),
         out_shape=jax.ShapeDtypeStruct((tokens, width), BF),
-        in_specs=[sspec()] * 2 + [hspec()] * 8,
-        out_specs=vspec(),
+        in_specs=[sspec()] * 4 + [vspec()] + [hspec()] * (7 + len(pieces)),
+        out_specs=hspec(),
         scratch_shapes=[
+            pltpu.VMEM((4 * rows, width), BF),
             pltpu.VMEM((4, chunk, tokens), BF),
             pltpu.VMEM((4, tokens, chunk), BF),
             pltpu.VMEM((4, chunk, tokens), BF),
             pltpu.VMEM((tokens // 128, 128, 256), F32),
+            pltpu.VMEM((tokens // 128, 128, 256), BF),
+            pltpu.VMEM((tokens, width), BF),
+            pltpu.VMEM((slots, width // slots, width), BF),
+            pltpu.VMEM((slots, tokens, width // slots), BF),
+            pltpu.SemaphoreType.DMA((8,)),
             pltpu.SemaphoreType.DMA((4 * count,)),
+            pltpu.SemaphoreType.DMA((len(pieces),)),
+            pltpu.SemaphoreType.DMA((slots,)),
+            pltpu.SemaphoreType.DMA((slots,)),
         ],
-        compiler_params=params(24),
-        cost_estimate=cost(40 * 128 * tokens * width, 8 * tokens * width),
-        name="attend",
-    )(planes, window_len, *[far(a) for pair in parts for a in pair])
-
-
-def output_kernel(at_ref, planes_ref, lens_ref, live_ref, att_ref, lat_ref, *rest):
-    pieces, (out_ref, w_ref, done_ref, sems, out_sems) = rest[:-5], rest[-5:]
-    x, y, core = at_ref[0], at_ref[1], at_ref[2]
-    slots = len(pieces) // 8
-    tokens, width = att_ref.shape
-    rows, lanes = width // (4 * slots), width // 2
-    skip = pieces[0].shape[0] - rows
-    copies = []
-    for s in range(slots):
-        for owner, c in ((0, core), (1, 1 - core)):
-            for i, (px, py) in enumerate(places(x, y)):
-                src = pieces[8 * s + 4 * owner + i].at[pl.ds(skip, rows), :]
-                row = pl.multiple_of((2 * py + c) * rows, 16)
-                lane = pl.multiple_of(px * lanes, 128)
-                copies.append(
-                    pltpu.make_async_copy(
-                        src, w_ref.at[s, pl.ds(row, rows), pl.ds(lane, lanes)], sems.at[len(copies)]
-                    )
-                )
-    for c in copies:
-        c.start()
-    cols = 4 * rows
-    token = lax.broadcasted_iota(jnp.int32, (tokens, 1), 0)
-    stop = jnp.zeros((tokens, 1), jnp.int32)
-    for w in range(tokens // WIN_TOK):
-        length = jnp.where(w // 2 < live_ref[0], lens_ref[w], 0)
-        stop = jnp.where(token // WIN_TOK == w, length + w * WIN_TOK, stop)
-    keep = token < stop
-    outs = []
-    for s in range(slots):
-        for c in copies[8 * s : 8 * s + 8]:
-            c.wait()
-        spot = pl.ds(pl.multiple_of(planes_ref[s] * cols, 128), cols)
-        update = lax.dot_general(
-            att_ref[...], w_ref[s], (((1,), (1,)), ((), ())), preferred_element_type=F32
-        )
-        base = lat_ref[:, spot].astype(F32)
-        done_ref[s] = jnp.where(keep, base + update, base).astype(BF)
-        outs.append(pltpu.make_async_copy(done_ref.at[s], out_ref.at[:, spot], out_sems.at[s]))
-        outs[s].start()
-    for c in outs:
-        c.wait()
-
-
-def output(place, planes, lens, live, attended, latents, pieces):
-    tokens, width = attended.shape
-    return pl.pallas_call(
-        output_kernel,
-        out_shape=jax.ShapeDtypeStruct((tokens, width), BF),
-        in_specs=[sspec()] * 4 + [vspec()] * 2 + [hspec()] * len(pieces),
-        out_specs=hspec(),
-        scratch_shapes=[
-            pltpu.VMEM((4, width // 4, width), BF),
-            pltpu.VMEM((4, tokens, width // 4), BF),
-            pltpu.SemaphoreType.DMA((len(pieces),)),
-            pltpu.SemaphoreType.DMA((4,)),
-        ],
-        compiler_params=params(32),
-        cost_estimate=cost(2 * width * width * tokens, 2 * width * (width + 3 * tokens)),
-        name="output",
-    )(place, planes, lens, live, attended, latents, *map(far, pieces))
+        compiler_params=params(44),
+        cost_estimate=cost(6 * width * width * tokens, 8 * width * tokens),
+        name="finish",
+    )(
+        place,
+        planes,
+        window_len,
+        live_blocks,
+        normed,
+        far(latents),
+        *[far(a) for pair in parts for a in pair],
+        *[far(value) for value, _ in pieces],
+    )
 
 
 def local(tile_count, latents, window_index, window_len, live_blocks, norm_gain, w_qkv, w_out):
@@ -383,12 +417,12 @@
     def across(bit):
         return along("tile", [(i, i ^ bit) for i in range(tile_count)])
 
-    core, ys, z1 = across(1), across(2), across(4)
+    core, ys, z1, z2 = across(1), across(2), across(4), across(8)
     xs = along("group", [(0, 1), (1, 0)])
-    low, high = range(tile_count // 4, tile_count // 2), range(tile_count // 2, 3 * tile_count // 4)
-    step = tile_count // 4
-    mid = along("tile", [(i, i + step) for i in low] + [(i, i - step) for i in high])
-    ends = along("tile", [(i, i - step) for i in low] + [(i, i + step) for i in high])
+    xy = along(
+        ("tile", "group"),
+        [(2 * i + g, 2 * (i ^ 2) + 1 - g) for i in range(tile_count) for g in range(2)],
+    )
     t = lax.axis_index("tile")
     x = lax.axis_index("group")
     z = t // 4
@@ -408,38 +442,36 @@
             shared.append(core(value, f"core_{name}"))
         return shared
 
+    def slot(index, *values):
+        return [(value, index if value.ndim == 3 else None) for value in values]
+
     u0 = jnp.concatenate([w_qkv.T, w_out.T], axis=0)
-    u1, near, x0, y0 = z1(u0, "u1"), mid(u0, "near2"), xs(u0, "x0"), ys(u0, "y0")
+    u1, d0, x0, y0, u2 = z1(u0, "u1"), xy(u0, "d0"), xs(u0, "x0"), ys(u0, "y0"), z2(u0, "u2")
     normed = normed_columns(latents, window_index, norm_gain)
-    cu0, = share(u0=u0)
-    u1, near, x0, y0, normed, cu0 = sync(u1, near, x0, y0, normed, cu0)
-    far2, near3, d0, y1 = ends(near, "far2"), mid(u1, "near3"), xs(y0, "d0"), ys(u1, "y1")
+    cu0 = core(u0, "core_u0")
+    u1, d0, x0, y0, u2, normed, cu0 = sync(u1, d0, x0, y0, u2, normed, cu0)
+    u12 = jnp.stack([u1, u2])
+    x2, y12, u3, d1 = xs(u2, "x2"), ys(u12, "y12"), z1(u2, "u3"), z1(d0, "d1")
     cx0, cy0 = share(x0=x0, y0=y0)
-    far2, near3, d0, y1, cx0, cy0, near, u1 = sync(far2, near3, d0, y1, cx0, cy0, near, u1)
-    u2 = near3 + far2
-    x2, y2, far3 = xs(u2, "x2"), ys(u2, "y2"), ends(near3, "far3")
-    cd0, cy1, cu1 = share(d0=d0, y1=y1, u1=u1)
-    x2, y2, far3, cd0, cy1, cu1, u1, u2, d0, near = sync(x2, y2, far3, cd0, cy1, cu1, u1, u2, d0, near)
-    x1, d2, d1 = xs(u1, "x1"), ys(x2, "d2"), z1(d0, "d1")
-    u3 = near + far3
-    s0 = [u0, x0, y0, d0, cu0, cx0, cy0, cd0]
+    x2, y12, u3, d1, cx0, cy0, u12 = sync(x2, y12, u3, d1, cx0, cy0, u12)
+    x1, d2 = xs(u1, "x1"), ys(x2, "d2")
+    cd0, cx2, cy12 = core(d0, "core_d0"), core(x2, "core_x2"), core(y12, "core_y12")
+    s0 = slot(0, u0, x0, y0, d0, cu0, cx0, cy0, cd0)
     p0 = project(place, planes[0:1], normed, s0, nq)
-    cu2, cx2, cy2 = share(u2=u2, x2=x2, y2=y2)
-    x1, d2, d1, u3, cu2, cx2, cy2, *p0 = sync(x1, d2, d1, u3, cu2, cx2, cy2, *p0)
+    x1, d2, cx2, cy12, d1, u3, p0, u12 = sync(x1, d2, cx2, cy12, d1, u3, p0, u12)
     x3, y3, d3 = xs(u3, "x3"), ys(u3, "y3"), z1(d2, "d3")
-    cx1, cd1, cd2, cu3 = share(x1=x1, d1=d1, d2=d2, u3=u3)
-    s1 = [u1, x1, y1, d1, cu1, cx1, cy1, cd1]
+    cu12, cx1 = share(u12=u12, x1=x1)
+    cd2, cd1 = share(d2=d2, d1=d1)
+    s2 = slot(1, u12, x2, y12, d2, cu12, cx2, cy12, cd2)
+    p2 = project(place, planes[2:3], normed, s2, nq)
+    x3, y3, d3, u3, p2, cx1, cd1 = sync(x3, y3, d3, u3, p2, cx1, cd1)
+    cu3, cx3, cy3, cd3 = core(u3, "core_u3"), core(x3, "core_x3"), core(y3, "core_y3"), core(d3, "core_d3")
+    s1 = slot(0, u12, x1, y12, d1, cu12, cx1, cy12, cd1)
     p1 = project(place, planes[1:2], normed, s1, nq)
-    s2 = [u2, x2, y2, d2, cu2, cx2, cy2, cd2]
-    p2 = project(place, planes[2:3], normed, s2, nq)
-    x3, y3, d3, cu3, p1, p2 = sync(x3, y3, d3, cu3, p1, p2)
-    cx3, cy3, cd3 = (share(**{name: value})[0] for name, value in (("x3", x3), ("y3", y3), ("d3", d3)))
-    s3 = [u3, x3, y3, d3, cu3, cx3, cy3, cd3]
-    p3 = project(place, planes[3:4], normed, s3, nq)
-    attended = attend(planes, window_len, (p0, p1, p2, p3))
+    s3 = slot(0, u3, x3, y3, d3, cu3, cx3, cy3, cd3)
+    flat = latents.reshape(blocks * rows, width)
     so = s0 + s1 + s2 + s3
-    flat = latents.reshape(blocks * rows, width)
-    out = output(place, planes, window_len, live_blocks, attended, flat, so)
+    out = finish(place, planes, window_len, live_blocks, normed, flat, (p0, p1, p2), so, nq)
     return out.reshape(latents.shape)
 
 

time: 139 us -> 134 us (0.964)
  Pallas kernels: 47.7 us -> 44.6 us
  local copies, waits for them, and re-layouts: 6.95 us -> 5.04 us
    pallas_call x6 -> x4, Pallas kernels: 44.4 us -> 41.4 us  [the longest x1 22.4 us: finish(): pl.pallas_call(functools.partial(finish_kernel, [spot for _, spot in piec...]
    add x2 -> x0, other arithmetic: 1.51 us -> none  [the longest x1 1.38 us: local(): u3 = near + far3]
    ppermute x33 -> x28, starting transfers between devices: 22.1 us -> 20.9 us  [move(): return lax.ppermute(value, axis, pairs)]
    unnamed x50 -> x30, local copies, waits for them, and re-layouts: 6.24 us -> 5.03 us
    ppermute x33 -> x28, waiting for transfers between devices: 57.6 us -> 58.5 us  [move(): return lax.ppermute(value, axis, pairs)]
  transfers between devices with their start and end apart: 33 -> 28, of which waited for: 18 -> 13; matrix products, arithmetic and copies ran while one was open for 2% -> 1% of each run, Pallas kernels for 16% -> 17%
where the time goes in v5:
time: 134 us; the launch traced here: 133 us
  waiting for transfers between devices  58.5 us (44%)
  Pallas kernels  44.6 us (33%)
  starting transfers between devices  20.9 us (16%)
  local copies, waits for them, and re-layouts  5.04 us (4%)
  other arithmetic  2.49 us (2%)
    ppermute x28, waiting for transfers between devices, move(): return lax.ppermute(value, axis, pairs)  58.5 us
    pallas_call x1, Pallas kernels, finish(): pl.pallas_call(functools.partial(finish_kernel, [spot for _, spot in piec...  22.4 us
    ppermute x28, starting transfers between devices, move(): return lax.ppermute(value, axis, pairs)  20.9 us
    pallas_call x3, Pallas kernels, project(): pl.pallas_call(functools.partial(project_kernel, [spot for _, spot in pie...  18.9 us
    unnamed x30, local copies, waits for them, and re-layouts  5.03 us
    pallas_call x1, Pallas kernels, normed_columns(): pl.pallas_call(norm_kernel, out_shape=jax.ShapeDtypeStruct((width, blocks...  3.26 us
  transfers between devices with their start and end apart: 28, of which 13 were waited for; matrix products, arithmetic and copies ran while one was open for 1% of the time, Pallas kernels for 17%

profile of v5, /device:TPU:0, one launch (start us, length us, event | category | flops | bytes accessed | tf_op | source)
XLA Modules:
  0.0 132.6 jit_solution(6952021271635654976)
XLA Ops:
  0.0 1.2 pad_maximum_fusion.1.rest_0_
  1.2 0.5 collective-permute-start.5
  1.7 3.7 %collective-permute-start.4 = (bf16[384,768]{1,0:T(8,128)(2,1)S(1)}, bf16[384,768]{1,0:T(8,128)(2,1)S(1)}, u32[]{:S(2)}, u32[]{:S(2)}) collective-permute-start(bf16[384,768]{1,0:T(8,128)(2,1)S(1)} %pad_maximum_fusion.1.rest_0_), channel_id=1, source_target_pairs={{0,16},{2,18},{4,20},{6,22},{8,24},{10,26},{12,28},{14,30},{16,0},... | collective-permute-start | bytes 1769480 | tf_op jit(solution)/shard_map/u2/ppermute | solution.py:413
  5.4 1.5 %collective-permute-start.3 = (bf16[384,768]{1,0:T(8,128)(2,1)S(1)}, bf16[384,768]{1,0:T(8,128)(2,1)S(1)}, u32[]{:S(2)}, u32[]{:S(2)}) collective-permute-start(bf16[384,768]{1,0:T(8,128)(2,1)S(1)} %pad_maximum_fusion.1.rest_0_), channel_id=1, source_target_pairs={{0,4},{2,6},{4,0},{6,2},{8,12},{10,14},{12,8},{14,10},{16,20},{18,... | collective-permute-start | bytes 1769480 | tf_op jit(solution)/shard_map/y0/ppermute | solution.py:413
  6.9 1.5 %collective-permute-start.2 = (bf16[384,768]{1,0:T(8,128)(2,1)S(1)}, bf16[384,768]{1,0:T(8,128)(2,1)S(1)}, u32[]{:S(2)}, u32[]{:S(2)}) collective-permute-start(bf16[384,768]{1,0:T(8,128)(2,1)S(1)} %pad_maximum_fusion.1.rest_0_), channel_id=1, source_target_pairs={{0,1},{1,0},{2,3},{3,2},{4,5},{5,4},{6,7},{7,6},{8,9},{9,8},{10,11... | collective-permute-start | bytes 1769480 | tf_op jit(solution)/shard_map/x0/ppermute | solution.py:413
  8.8 1.6 %collective-permute-start = (bf16[384,768]{1,0:T(8,128)(2,1)S(1)}, bf16[384,768]{1,0:T(8,128)(2,1)}, u32[]{:S(2)}, u32[]{:S(2)}) collective-permute-start(bf16[384,768]{1,0:T(8,128)(2,1)S(1)} %pad_maximum_fusion.1.rest_0_), channel_id=1, source_target_pairs={{0,8},{2,10},{4,12},{6,14},{8,0},{10,2},{12,4},{14,6},{16,24},{18,... | collective-permute-start | bytes 1769480 | tf_op jit(solution)/shard_map/u1/ppermute | solution.py:413
  10.5 1.7 %copy-done = bf16[6,128,1536]{2,1,0:T(8,128)(2,1)S(1)} copy-done((bf16[6,128,1536]{2,1,0:T(8,128)(2,1)S(1)}, bf16[6,128,1536]{2,1,0:T(8,128)(2,1)}, u32[]{:S(2)}) %copy-start) | copy-done | bytes 2359320
  12.1 3.3 %norm.1.n_ref = bf16[1536,768]{1,0:T(8,128)(2,1)S(1)} custom-call(s32[12]{0:T(128)S(1)} %copy-done.1, bf16[6,128,1536]{2,1,0:T(8,128)(2,1)S(1)} %copy-done, f32[1,1536]{1,0:T(1,128)S(1)} %reshape.20.gain_ref, f32[1,384]{1,0:T(1,128)S(1)} %multiply_exponential_fusion.freq_ref), custom_call_target="tpu_custom_call" | custom-call | flops 47185920 | bytes 4718592 | tf_op jit(solution)/shard_map/norm/pallas_call | solution.py:138
  15.4 16.6 %collective-permute-done.4 = bf16[384,768]{1,0:T(8,128)(2,1)S(1)} collective-permute-done((bf16[384,768]{1,0:T(8,128)(2,1)S(1)}, bf16[384,768]{1,0:T(8,128)(2,1)S(1)}, u32[]{:S(2)}, u32[]{:S(2)}) %collective-permute-start.4) | collective-permute-done | bytes 589856 | tf_op jit(solution)/shard_map/u2/ppermute | solution.py:413
  32.0 2.6 %collective-permute-done.1.rest_3_ = bf16[384,768]{1,0:T(8,128)(2,1)} collective-permute-done((bf16[384,768]{1,0:T(8,128)(2,1)S(1)}, bf16[384,768]{1,0:T(8,128)(2,1)}, u32[]{:S(2)}, u32[]{:S(2)}) %collective-permute-start.1) | collective-permute-done | bytes 589856 | tf_op jit(solution)/shard_map/d0/ppermute | solution.py:413
  35.0 1.2 pad_maximum_fusion.rest_0_.rest_8_.rest_16_
  36.2 1.7 %collective-permute-start.8 = (bf16[2,384,768]{2,1,0:T(8,128)(2,1)S(1)}, bf16[2,384,768]{2,1,0:T(8,128)(2,1)}, u32[]{:S(2)}, u32[]{:S(2)}) collective-permute-start(bf16[2,384,768]{2,1,0:T(8,128)(2,1)S(1)} %pad_maximum_fusion.rest_0_.rest_8_.rest_16_), channel_id=1, source_target_pairs={{0,4},{2,6},{4,0},{6,2},{8,12},{10,14},{12,8},{14,10},{16,20},{18,... | collective-permute-start | bytes 3538952 | tf_op jit(solution)/shard_map/y12/ppermute | solution.py:413
  37.8 1.2 collective-permute-start.9
  39.0 1.5 %collective-permute-start.7 = (bf16[384,768]{1,0:T(8,128)(2,1)S(1)}, bf16[384,768]{1,0:T(8,128)(2,1)}, u32[]{:S(2)}, u32[]{:S(2)}) collective-permute-start(bf16[384,768]{1,0:T(8,128)(2,1)S(1)} %collective-permute-done.4), channel_id=1, source_target_pairs={{0,1},{1,0},{2,3},{3,2},{4,5},{5,4},{6,7},{7,6},{8,9},{9,8},{10,11... | collective-permute-start | bytes 1769480 | tf_op jit(solution)/shard_map/x2/ppermute | solution.py:413
  40.5 0.8 collective-permute-start.10
  41.4 12.7 %collective-permute-done.9.rest_24_ = bf16[384,768]{1,0:T(8,128)(2,1)} collective-permute-done((bf16[384,768]{1,0:T(8,128)(2,1)S(1)}, bf16[384,768]{1,0:T(8,128)(2,1)}, u32[]{:S(2)}, u32[]{:S(2)}) %collective-permute-start.9) | collective-permute-done | bytes 589856 | tf_op jit(solution)/shard_map/u3/ppermute | solution.py:413
  54.3 11.7 %collective-permute-done.10.rest_3_.rest_11_ = bf16[384,768]{1,0:T(8,128)(2,1)} collective-permute-done((bf16[384,768]{1,0:T(8,128)(2,1)}, bf16[384,768]{1,0:T(8,128)(2,1)}, u32[]{:S(2)}, u32[]{:S(2)}) %collective-permute-start.10) | collective-permute-done | bytes 589856 | tf_op jit(solution)/shard_map/d1/ppermute | solution.py:413
  66.1 0.7 copy-done.10
  66.9 1.5 %collective-permute-start.6 = (bf16[384,768]{1,0:T(8,128)(2,1)}, bf16[384,768]{1,0:T(8,128)(2,1)}, u32[]{:S(2)}, u32[]{:S(2)}) collective-permute-start(bf16[384,768]{1,0:T(8,128)(2,1)} %collective-permute-done), channel_id=1, source_target_pairs={{0,1},{1,0},{2,3},{3,2},{4,5},{5,4},{6,7},{7,6},{8,9},{9,8},{10,11... | collective-permute-start | bytes 1769480 | tf_op jit(solution)/shard_map/x1/ppermute | solution.py:413
  69.2 1.0 collective-permute-done.16.rest_7_
  70.1 6.3 %project.3 = (bf16[3,384,768]{2,1,0:T(8,128)(2,1)}, bf16[3,768,384]{2,1,0:T(8,128)(2,1)}) custom-call(s32[3]{0:T(128)S(1)} %pad_add_fusion.at_ref, s32[1]{0:T(128)} %bitcast.3.plane_ref, bf16[1536,768]{1,0:T(8,128)(2,1)S(1)} %norm.1.n_ref, bf16[384,768]{1,0:T(8,128)(2,1)} %copy-done.5, bf16[384,768]{1,0:T(8,128)(2,1)} %copy-done.8, ...), custom_call_target="tpu_custom_call" | custom-call | flops 2717908992 | bytes 5898240 | tf_op jit(solution)/shard_map/project/pallas_call | solution.py:225
  76.5 6.5 %collective-permute-done.6.rest_1_.rest_9_ = bf16[384,768]{1,0:T(8,128)(2,1)} collective-permute-done((bf16[384,768]{1,0:T(8,128)(2,1)}, bf16[384,768]{1,0:T(8,128)(2,1)}, u32[]{:S(2)}, u32[]{:S(2)}) %collective-permute-start.6) | collective-permute-done | bytes 589856 | tf_op jit(solution)/shard_map/x1/ppermute | solution.py:413
  82.9 1.5 %collective-permute-done.13.rest_3_.rest_19_ = bf16[384,768]{1,0:T(8,128)(2,1)} collective-permute-done((bf16[384,768]{1,0:T(8,128)(2,1)}, bf16[384,768]{1,0:T(8,128)(2,1)}, u32[]{:S(2)}, u32[]{:S(2)}) %collective-permute-start.13) | collective-permute-done | bytes 589856 | tf_op jit(solution)/shard_map/d2/ppermute | solution.py:413
  85.9 1.3 collective-permute-start.20
  87.2 1.0 collective-permute-done.21.rest_7_.rest_23_
  88.4 0.7 copy-done.11
  89.1 1.0 copy-done.4
  90.3 6.3 %project.4 = (bf16[3,384,768]{2,1,0:T(8,128)(2,1)}, bf16[3,768,384]{2,1,0:T(8,128)(2,1)}) custom-call(s32[3]{0:T(128)S(1)} %pad_add_fusion.at_ref, s32[1]{0:T(128)} %bitcast.5.plane_ref, bf16[1536,768]{1,0:T(8,128)(2,1)S(1)} %norm.1.n_ref, bf16[2,384,768]{2,1,0:T(8,128)(2,1)} %copy-done.3, bf16[384,768]{1,0:T(8,128)(2,1)} %collective-permute-done.7.rest_1_.rest_17_, ...), custom_call_target="tpu_custom_call" | custom-call | flops 2717908992 | bytes 5898240 | tf_op jit(solution)/shard_map/project/pallas_call | solution.py:225
  96.6 3.9 %collective-permute-done.19.rest_26_ = bf16[384,768]{1,0:T(8,128)(2,1)} collective-permute-done((bf16[384,768]{1,0:T(8,128)(2,1)}, bf16[384,768]{1,0:T(8,128)(2,1)}, u32[]{:S(2)}, u32[]{:S(2)}) %collective-permute-start.19) | collective-permute-done | bytes 589856 | tf_op jit(solution)/shard_map/y3/ppermute | solution.py:413
  102.8 6.3 %project.5 = (bf16[3,384,768]{2,1,0:T(8,128)(2,1)}, bf16[3,768,384]{2,1,0:T(8,128)(2,1)}) custom-call(s32[3]{0:T(128)S(1)} %pad_add_fusion.at_ref, s32[1]{0:T(128)} %bitcast.4.plane_ref, bf16[1536,768]{1,0:T(8,128)(2,1)S(1)} %norm.1.n_ref, bf16[2,384,768]{2,1,0:T(8,128)(2,1)} %copy-done.3, bf16[384,768]{1,0:T(8,128)(2,1)} %collective-permute-done.6.rest_1_.rest_9_, ...), custom_call_target="tpu_custom_call" | custom-call | flops 2717908992 | bytes 5898240 | tf_op jit(solution)/shard_map/project/pallas_call | solution.py:225
  109.2 0.8 copy-done.13
  110.0 22.4 %finish.1 = bf16[768,1536]{1,0:T(8,128)(2,1)} custom-call(s32[3]{0:T(128)S(1)} %pad_add_fusion.at_ref, s32[4]{0:T(128)S(1)} %pad_add_fusion.1.planes_ref, s32[12]{0:T(128)S(1)} %copy-done.2, s32[1]{0:T(128)S(6)} %copy.8.live_ref, bf16[1536,768]{1,0:T(8,128)(2,1)S(1)} %norm.1.n_ref, bf16[768,1536]{1,0:T(8,128)(2,1)} %bitcast.13, ...), custom_call_target="tpu_custom_call" | custom-call | flops 10871635968 | bytes 9437184 | tf_op jit(solution)/shard_map/finish/pallas_call | solution.py:371
  (65 shorter events, 5.4 us)
Async XLA Ops:
  0.0 10.5 %copy-start.1 = (s32[12]{0:T(128)S(1)}, s32[12]{0:T(128)}, u32[]{:S(2)}) copy-start(s32[12]{0:T(128)} %ids_ref.1) | copy-start | bytes 148
  1.2 14.3 %copy-start.5 = (bf16[384,768]{1,0:T(8,128)(2,1)}, bf16[384,768]{1,0:T(8,128)(2,1)S(1)}, u32[]{:S(2)}) copy-start(bf16[384,768]{1,0:T(8,128)(2,1)S(1)} %pad_maximum_fusion.1.rest_0_) | copy-start | bytes 1769476
  1.2 7.7 %collective-permute-start.5 = (bf16[384,768]{1,0:T(8,128)(2,1)S(1)}, bf16[384,768]{1,0:T(8,128)(2,1)S(1)}, u32[]{:S(2)}, u32[]{:S(2)}) collective-permute-start(bf16[384,768]{1,0:T(8,128)(2,1)S(1)} %pad_maximum_fusion.1.rest_0_), channel_id=1, source_target_pairs={{0,2},{2,0},{4,6},{6,4},{8,10},{10,8},{12,14},{14,12},{16,18},{18,... | collective-permute-start | bytes 1769480 | tf_op jit(solution)/shard_map/core_u0/ppermute | solution.py:413
  1.7 30.3 %collective-permute-start.4 = (bf16[384,768]{1,0:T(8,128)(2,1)S(1)}, bf16[384,768]{1,0:T(8,128)(2,1)S(1)}, u32[]{:S(2)}, u32[]{:S(2)}) collective-permute-start(bf16[384,768]{1,0:T(8,128)(2,1)S(1)} %pad_maximum_fusion.1.rest_0_), channel_id=1, source_target_pairs={{0,16},{2,18},{4,20},{6,22},{8,24},{10,26},{12,28},{14,30},{16,0},... | collective-permute-start | bytes 1769480 | tf_op jit(solution)/shard_map/u2/ppermute | solution.py:413
  5.4 26.7 %collective-permute-start.3 = (bf16[384,768]{1,0:T(8,128)(2,1)S(1)}, bf16[384,768]{1,0:T(8,128)(2,1)S(1)}, u32[]{:S(2)}, u32[]{:S(2)}) collective-permute-start(bf16[384,768]{1,0:T(8,128)(2,1)S(1)} %pad_maximum_fusion.1.rest_0_), channel_id=1, source_target_pairs={{0,4},{2,6},{4,0},{6,2},{8,12},{10,14},{12,8},{14,10},{16,20},{18,... | collective-permute-start | bytes 1769480 | tf_op jit(solution)/shard_map/y0/ppermute | solution.py:413
  6.9 25.2 %collective-permute-start.2 = (bf16[384,768]{1,0:T(8,128)(2,1)S(1)}, bf16[384,768]{1,0:T(8,128)(2,1)S(1)}, u32[]{:S(2)}, u32[]{:S(2)}) collective-permute-start(bf16[384,768]{1,0:T(8,128)(2,1)S(1)} %pad_maximum_fusion.1.rest_0_), channel_id=1, source_target_pairs={{0,1},{1,0},{2,3},{3,2},{4,5},{5,4},{6,7},{7,6},{8,9},{9,8},{10,11... | collective-permute-start | bytes 1769480 | tf_op jit(solution)/shard_map/x0/ppermute | solution.py:413
  8.4 26.3 %collective-permute-start.1 = (bf16[384,768]{1,0:T(8,128)(2,1)S(1)}, bf16[384,768]{1,0:T(8,128)(2,1)}, u32[]{:S(2)}, u32[]{:S(2)}) collective-permute-start(bf16[384,768]{1,0:T(8,128)(2,1)S(1)} %pad_maximum_fusion.1.rest_0_), channel_id=1, source_target_pairs={{0,5},{1,4},{2,7},{3,6},{4,1},{5,0},{6,3},{7,2},{8,13},{9,12},{10,... | collective-permute-start | bytes 1769480 | tf_op jit(solution)/shard_map/d0/ppermute | solution.py:413
  8.8 26.1 %collective-permute-start = (bf16[384,768]{1,0:T(8,128)(2,1)S(1)}, bf16[384,768]{1,0:T(8,128)(2,1)}, u32[]{:S(2)}, u32[]{:S(2)}) collective-permute-start(bf16[384,768]{1,0:T(8,128)(2,1)S(1)} %pad_maximum_fusion.1.rest_0_), channel_id=1, source_target_pairs={{0,8},{2,10},{4,12},{6,14},{8,0},{10,2},{12,4},{14,6},{16,24},{18,... | collective-permute-start | bytes 1769480 | tf_op jit(solution)/shard_map/u1/ppermute | solution.py:413
  35.0 6.4 %collective-permute-start.11 = (bf16[384,768]{1,0:T(8,128)(2,1)S(1)}, bf16[384,768]{1,0:T(8,128)(2,1)S(1)}, u32[]{:S(2)}, u32[]{:S(2)}) collective-permute-start(bf16[384,768]{1,0:T(8,128)(2,1)S(1)} %collective-permute-done.2.rest_1_), channel_id=1, source_target_pairs={{0,2},{2,0},{4,6},{6,4},{8,10},{10,8},{12,14},{14,12},{16,18},{18,... | collective-permute-start | bytes 1769480 | tf_op jit(solution)/shard_map/core_x0/ppermute | solution.py:413
  36.2 48.3 %copy-start.3 = (bf16[2,384,768]{2,1,0:T(8,128)(2,1)}, bf16[2,384,768]{2,1,0:T(8,128)(2,1)S(1)}, u32[]{:S(2)}) copy-start(bf16[2,384,768]{2,1,0:T(8,128)(2,1)S(1)} %pad_maximum_fusion.rest_0_.rest_8_.rest_16_) | copy-start | bytes 3538948
  36.2 29.9 %collective-permute-start.8 = (bf16[2,384,768]{2,1,0:T(8,128)(2,1)S(1)}, bf16[2,384,768]{2,1,0:T(8,128)(2,1)}, u32[]{:S(2)}, u32[]{:S(2)}) collective-permute-start(bf16[2,384,768]{2,1,0:T(8,128)(2,1)S(1)} %pad_maximum_fusion.rest_0_.rest_8_.rest_16_), channel_id=1, source_target_pairs={{0,4},{2,6},{4,0},{6,2},{8,12},{10,14},{12,8},{14,10},{16,20},{18,... | collective-permute-start | bytes 3538952 | tf_op jit(solution)/shard_map/y12/ppermute | solution.py:413
  37.8 16.3 %collective-permute-start.9 = (bf16[384,768]{1,0:T(8,128)(2,1)S(1)}, bf16[384,768]{1,0:T(8,128)(2,1)}, u32[]{:S(2)}, u32[]{:S(2)}) collective-permute-start(bf16[384,768]{1,0:T(8,128)(2,1)S(1)} %collective-permute-done.4), channel_id=1, source_target_pairs={{0,8},{2,10},{4,12},{6,14},{8,0},{10,2},{12,4},{14,6},{16,24},{18,... | collective-permute-start | bytes 1769480 | tf_op jit(solution)/shard_map/u3/ppermute | solution.py:413
  39.0 15.3 %collective-permute-start.7 = (bf16[384,768]{1,0:T(8,128)(2,1)S(1)}, bf16[384,768]{1,0:T(8,128)(2,1)}, u32[]{:S(2)}, u32[]{:S(2)}) collective-permute-start(bf16[384,768]{1,0:T(8,128)(2,1)S(1)} %collective-permute-done.4), channel_id=1, source_target_pairs={{0,1},{1,0},{2,3},{3,2},{4,5},{5,4},{6,7},{7,6},{8,9},{9,8},{10,11... | collective-permute-start | bytes 1769480 | tf_op jit(solution)/shard_map/x2/ppermute | solution.py:413
  40.5 25.5 %collective-permute-start.10 = (bf16[384,768]{1,0:T(8,128)(2,1)}, bf16[384,768]{1,0:T(8,128)(2,1)}, u32[]{:S(2)}, u32[]{:S(2)}) collective-permute-start(bf16[384,768]{1,0:T(8,128)(2,1)} %collective-permute-done.1.rest_3_), channel_id=1, source_target_pairs={{0,8},{2,10},{4,12},{6,14},{8,0},{10,2},{12,4},{14,6},{16,24},{18,... | collective-permute-start | bytes 1769480 | tf_op jit(solution)/shard_map/d1/ppermute | solution.py:413
  41.3 24.7 %copy-start.9 = (bf16[384,768]{1,0:T(8,128)(2,1)}, bf16[384,768]{1,0:T(8,128)(2,1)S(1)}, u32[]{:S(2)}) copy-start(bf16[384,768]{1,0:T(8,128)(2,1)S(1)} %collective-permute-done.11.rest_5_) | copy-start | bytes 1769476
  41.4 24.7 %collective-permute-start.12 = (bf16[384,768]{1,0:T(8,128)(2,1)S(1)}, bf16[384,768]{1,0:T(8,128)(2,1)S(1)}, u32[]{:S(2)}, u32[]{:S(2)}) collective-permute-start(bf16[384,768]{1,0:T(8,128)(2,1)S(1)} %collective-permute-done.3.rest_2_), channel_id=1, source_target_pairs={{0,2},{2,0},{4,6},{6,4},{8,10},{10,8},{12,14},{14,12},{16,18},{18,... | collective-permute-start | bytes 1769480 | tf_op jit(solution)/shard_map/core_y0/ppermute | solution.py:413
  66.0 18.4 %collective-permute-start.15 = (bf16[2,384,768]{2,1,0:T(8,128)(2,1)}, bf16[2,384,768]{2,1,0:T(8,128)(2,1)}, u32[]{:S(2)}, u32[]{:S(2)}) collective-permute-start(bf16[2,384,768]{2,1,0:T(8,128)(2,1)} %collective-permute-done.8.rest_2_.rest_10_.rest_18_), channel_id=1, source_target_pairs={{0,2},{2,0},{4,6},{6,4},{8,10},{10,8},{12,14},{14,12},{16,18},{18,... | collective-permute-start | bytes 3538952 | tf_op jit(solution)/shard_map/core_y12/ppermute | solution.py:413
  66.9 3.3 %collective-permute-start.16 = (bf16[384,768]{1,0:T(8,128)(2,1)}, bf16[384,768]{1,0:T(8,128)(2,1)}, u32[]{:S(2)}, u32[]{:S(2)}) collective-permute-start(bf16[384,768]{1,0:T(8,128)(2,1)} %collective-permute-done.1.rest_3_), channel_id=1, source_target_pairs={{0,2},{2,0},{4,6},{6,4},{8,10},{10,8},{12,14},{14,12},{16,18},{18,... | collective-permute-start | bytes 1769480 | tf_op jit(solution)/shard_map/core_d0/ppermute | solution.py:413
  66.9 16.1 %collective-permute-start.6 = (bf16[384,768]{1,0:T(8,128)(2,1)}, bf16[384,768]{1,0:T(8,128)(2,1)}, u32[]{:S(2)}, u32[]{:S(2)}) collective-permute-start(bf16[384,768]{1,0:T(8,128)(2,1)} %collective-permute-done), channel_id=1, source_target_pairs={{0,1},{1,0},{2,3},{3,2},{4,5},{5,4},{6,7},{7,6},{8,9},{9,8},{10,11... | collective-permute-start | bytes 1769480 | tf_op jit(solution)/shard_map/x1/ppermute | solution.py:413
  68.4 14.6 %collective-permute-start.14 = (bf16[384,768]{1,0:T(8,128)(2,1)}, bf16[384,768]{1,0:T(8,128)(2,1)}, u32[]{:S(2)}, u32[]{:S(2)}) collective-permute-start(bf16[384,768]{1,0:T(8,128)(2,1)} %collective-permute-done.7.rest_1_.rest_17_), channel_id=1, source_target_pairs={{0,2},{2,0},{4,6},{6,4},{8,10},{10,8},{12,14},{14,12},{16,18},{18,... | collective-permute-start | bytes 1769480 | tf_op jit(solution)/shard_map/core_x2/ppermute | solution.py:413
  68.6 15.8 %collective-permute-start.13 = (bf16[384,768]{1,0:T(8,128)(2,1)}, bf16[384,768]{1,0:T(8,128)(2,1)}, u32[]{:S(2)}, u32[]{:S(2)}) collective-permute-start(bf16[384,768]{1,0:T(8,128)(2,1)} %collective-permute-done.7.rest_1_.rest_17_), channel_id=1, source_target_pairs={{0,4},{2,6},{4,0},{6,2},{8,12},{10,14},{12,8},{14,10},{16,20},{18,... | collective-permute-start | bytes 1769480 | tf_op jit(solution)/shard_map/d2/ppermute | solution.py:413
  84.4 3.9 %collective-permute-start.17 = (bf16[2,384,768]{2,1,0:T(8,128)(2,1)S(1)}, bf16[2,384,768]{2,1,0:T(8,128)(2,1)S(1)}, u32[]{:S(2)}, u32[]{:S(2)}) collective-permute-start(bf16[2,384,768]{2,1,0:T(8,128)(2,1)S(1)} %pad_maximum_fusion.rest_0_.rest_8_.rest_16_), channel_id=1, source_target_pairs={{0,2},{2,0},{4,6},{6,4},{8,10},{10,8},{12,14},{14,12},{16,18},{18,... | collective-permute-start | bytes 3538952 | tf_op jit(solution)/shard_map/core_u12/ppermute | solution.py:413
  84.4 3.8 %collective-permute-start.21 = (bf16[384,768]{1,0:T(8,128)(2,1)}, bf16[384,768]{1,0:T(8,128)(2,1)S(1)}, u32[]{:S(2)}, u32[]{:S(2)}) collective-permute-start(bf16[384,768]{1,0:T(8,128)(2,1)} %collective-permute-done.13.rest_3_.rest_19_), channel_id=1, source_target_pairs={{0,2},{2,0},{4,6},{6,4},{8,10},{10,8},{12,14},{14,12},{16,18},{18,... | collective-permute-start | bytes 1769480 | tf_op jit(solution)/shard_map/core_d2/ppermute | solution.py:413
  84.9 15.6 %collective-permute-start.19 = (bf16[384,768]{1,0:T(8,128)(2,1)}, bf16[384,768]{1,0:T(8,128)(2,1)}, u32[]{:S(2)}, u32[]{:S(2)}) collective-permute-start(bf16[384,768]{1,0:T(8,128)(2,1)} %collective-permute-done.9.rest_24_), channel_id=1, source_target_pairs={{0,4},{2,6},{4,0},{6,2},{8,12},{10,14},{12,8},{14,10},{16,20},{18,... | collective-permute-start | bytes 1769480 | tf_op jit(solution)/shard_map/y3/ppermute | solution.py:413
  85.4 15.3 %collective-permute-start.18 = (bf16[384,768]{1,0:T(8,128)(2,1)}, bf16[384,768]{1,0:T(8,128)(2,1)}, u32[]{:S(2)}, u32[]{:S(2)}) collective-permute-start(bf16[384,768]{1,0:T(8,128)(2,1)} %collective-permute-done.9.rest_24_), channel_id=1, source_target_pairs={{0,1},{1,0},{2,3},{3,2},{4,5},{5,4},{6,7},{7,6},{8,9},{9,8},{10,11... | collective-permute-start | bytes 1769480 | tf_op jit(solution)/shard_map/x3/ppermute | solution.py:413
  85.9 15.1 %collective-permute-start.20 = (bf16[384,768]{1,0:T(8,128)(2,1)}, bf16[384,768]{1,0:T(8,128)(2,1)}, u32[]{:S(2)}, u32[]{:S(2)}) collective-permute-start(bf16[384,768]{1,0:T(8,128)(2,1)} %collective-permute-done.13.rest_3_.rest_19_), channel_id=1, source_target_pairs={{0,8},{2,10},{4,12},{6,14},{8,0},{10,2},{12,4},{14,6},{16,24},{18,... | collective-permute-start | bytes 1769480 | tf_op jit(solution)/shard_map/d3/ppermute | solution.py:413
  88.2 12.8 %collective-permute-start.23 = (bf16[384,768]{1,0:T(8,128)(2,1)}, bf16[384,768]{1,0:T(8,128)(2,1)}, u32[]{:S(2)}, u32[]{:S(2)}) collective-permute-start(bf16[384,768]{1,0:T(8,128)(2,1)} %collective-permute-done.10.rest_3_.rest_11_), channel_id=1, source_target_pairs={{0,2},{2,0},{4,6},{6,4},{8,10},{10,8},{12,14},{14,12},{16,18},{18,... | collective-permute-start | bytes 1769480 | tf_op jit(solution)/shard_map/core_d1/ppermute | solution.py:413
  90.1 10.9 %collective-permute-start.22 = (bf16[384,768]{1,0:T(8,128)(2,1)}, bf16[384,768]{1,0:T(8,128)(2,1)S(1)}, u32[]{:S(2)}, u32[]{:S(2)}) collective-permute-start(bf16[384,768]{1,0:T(8,128)(2,1)} %collective-permute-done.6.rest_1_.rest_9_), channel_id=1, source_target_pairs={{0,2},{2,0},{4,6},{6,4},{8,10},{10,8},{12,14},{14,12},{16,18},{18,... | collective-permute-start | bytes 1769480 | tf_op jit(solution)/shard_map/core_x1/ppermute | solution.py:413
  101.0 8.1 %collective-permute-start.24 = (bf16[384,768]{1,0:T(8,128)(2,1)}, bf16[384,768]{1,0:T(8,128)(2,1)S(1)}, u32[]{:S(2)}, u32[]{:S(2)}) collective-permute-start(bf16[384,768]{1,0:T(8,128)(2,1)} %collective-permute-done.9.rest_24_), channel_id=1, source_target_pairs={{0,2},{2,0},{4,6},{6,4},{8,10},{10,8},{12,14},{14,12},{16,18},{18,... | collective-permute-start | bytes 1769480 | tf_op jit(solution)/shard_map/core_u3/ppermute | solution.py:413
  101.1 8.1 %collective-permute-start.25 = (bf16[384,768]{1,0:T(8,128)(2,1)}, bf16[384,768]{1,0:T(8,128)(2,1)}, u32[]{:S(2)}, u32[]{:S(2)}) collective-permute-start(bf16[384,768]{1,0:T(8,128)(2,1)} %collective-permute-done.18.rest_25_), channel_id=1, source_target_pairs={{0,2},{2,0},{4,6},{6,4},{8,10},{10,8},{12,14},{14,12},{16,18},{18,... | collective-permute-start | bytes 1769480 | tf_op jit(solution)/shard_map/core_x3/ppermute | solution.py:413
  101.6 7.6 %collective-permute-start.26 = (bf16[384,768]{1,0:T(8,128)(2,1)}, bf16[384,768]{1,0:T(8,128)(2,1)}, u32[]{:S(2)}, u32[]{:S(2)}) collective-permute-start(bf16[384,768]{1,0:T(8,128)(2,1)} %collective-permute-done.19.rest_26_), channel_id=1, source_target_pairs={{0,2},{2,0},{4,6},{6,4},{8,10},{10,8},{12,14},{14,12},{16,18},{18,... | collective-permute-start | bytes 1769480 | tf_op jit(solution)/shard_map/core_y3/ppermute | solution.py:413
  101.6 7.5 %collective-permute-start.27 = (bf16[384,768]{1,0:T(8,128)(2,1)}, bf16[384,768]{1,0:T(8,128)(2,1)}, u32[]{:S(2)}, u32[]{:S(2)}) collective-permute-start(bf16[384,768]{1,0:T(8,128)(2,1)} %collective-permute-done.20.rest_27_), channel_id=1, source_target_pairs={{0,2},{2,0},{4,6},{6,4},{8,10},{10,8},{12,14},{14,12},{16,18},{18,... | collective-permute-start | bytes 1769480 | tf_op jit(solution)/shard_map/core_d3/ppermute | solution.py:413
  (11 other events, 39.8 us)

commit v6 on v5

--- a/solution.py
+++ b/solution.py
@@ -400,7 +400,8 @@
         normed,
         far(latents),
         *[far(a) for pair in parts for a in pair],
-        *[far(value) for value, _ in pieces],
+        *[far(value) for value, _ in pieces[:-8]],
+        *[value for value, _ in pieces[-8:]],
     )
 
 
@@ -455,19 +456,20 @@
     cx0, cy0 = share(x0=x0, y0=y0)
     x2, y12, u3, d1, cx0, cy0, u12 = sync(x2, y12, u3, d1, cx0, cy0, u12)
     x1, d2 = xs(u1, "x1"), ys(x2, "d2")
-    cd0, cx2, cy12 = core(d0, "core_d0"), core(x2, "core_x2"), core(y12, "core_y12")
+    cd0, cx2, cy12, cu12 = (
+        core(value, name) for value, name in ((d0, "core_d0"), (x2, "core_x2"), (y12, "core_y12"), (u12, "core_u12"))
+    )
     s0 = slot(0, u0, x0, y0, d0, cu0, cx0, cy0, cd0)
     p0 = project(place, planes[0:1], normed, s0, nq)
-    x1, d2, cx2, cy12, d1, u3, p0, u12 = sync(x1, d2, cx2, cy12, d1, u3, p0, u12)
+    x1, d2, cx2, cy12, cu12, d1, u3, p0 = sync(x1, d2, cx2, cy12, cu12, d1, u3, p0)
     x3, y3, d3 = xs(u3, "x3"), ys(u3, "y3"), z1(d2, "d3")
-    cu12, cx1 = share(u12=u12, x1=x1)
-    cd2, cd1 = share(d2=d2, d1=d1)
+    cd2, cx1, cd1 = core(d2, "core_d2"), core(x1, "core_x1"), core(d1, "core_d1")
     s2 = slot(1, u12, x2, y12, d2, cu12, cx2, cy12, cd2)
     p2 = project(place, planes[2:3], normed, s2, nq)
-    x3, y3, d3, u3, p2, cx1, cd1 = sync(x3, y3, d3, u3, p2, cx1, cd1)
-    cu3, cx3, cy3, cd3 = core(u3, "core_u3"), core(x3, "core_x3"), core(y3, "core_y3"), core(d3, "core_d3")
     s1 = slot(0, u12, x1, y12, d1, cu12, cx1, cy12, cd1)
     p1 = project(place, planes[1:2], normed, s1, nq)
+    x3, y3, d3, u3, p2, p1 = sync(x3, y3, d3, u3, p2, p1)
+    cu3, cx3, cy3, cd3 = core(u3, "core_u3"), core(x3, "core_x3"), core(y3, "core_y3"), core(d3, "core_d3")
     s3 = slot(0, u3, x3, y3, d3, cu3, cx3, cy3, cd3)
     flat = latents.reshape(blocks * rows, width)
     so = s0 + s1 + s2 + s3

time: 134 us -> 130 us (0.970)
  local copies, waits for them, and re-layouts: 5.04 us -> 1.94 us
    unnamed x30 -> x24, local copies, waits for them, and re-layouts: 5.03 us -> 1.94 us
  transfers between devices with their start and end apart: 28 -> 28, of which waited for: 13 -> 16; matrix products, arithmetic and copies ran while one was open for 1% -> 2% of each run, Pallas kernels for 17% -> 17%
where the time goes in v6:
time: 130 us
  waiting for transfers between devices  58.8 us (45%)
  Pallas kernels  43.6 us (34%)
  starting transfers between devices  20.7 us (16%)
  other arithmetic  3.5 us (3%)
  local copies, waits for them, and re-layouts  1.94 us (1%)
    ppermute x28, waiting for transfers between devices, move(): return lax.ppermute(value, axis, pairs)  58.8 us
    pallas_call x1, Pallas kernels, finish(): pl.pallas_call(functools.partial(finish_kernel, [spot for _, spot in piec...  21.4 us
    ppermute x28, starting transfers between devices, move(): return lax.ppermute(value, axis, pairs)  20.7 us
    pallas_call x3, Pallas kernels, project(): pl.pallas_call(functools.partial(project_kernel, [spot for _, spot in pie...  19 us
    pallas_call x1, Pallas kernels, normed_columns(): pl.pallas_call(norm_kernel, out_shape=jax.ShapeDtypeStruct((width, blocks...  3.26 us
  transfers between devices with their start and end apart: 28, of which 16 were waited for; matrix products, arithmetic and copies ran while one was open for 2% of the time, Pallas kernels for 17%

profile of v6, /device:TPU:0, one launch (start us, length us, event | category | flops | bytes accessed | tf_op | source)
XLA Modules:
  0.0 129.6 jit_solution(15747354961407296162)
XLA Ops:
  0.0 1.2 pad_maximum_fusion.1.rest_0_
  1.2 0.5 collective-permute-start.5
  1.7 3.7 %collective-permute-start.4 = (bf16[384,768]{1,0:T(8,128)(2,1)S(1)}, bf16[384,768]{1,0:T(8,128)(2,1)S(1)}, u32[]{:S(2)}, u32[]{:S(2)}) collective-permute-start(bf16[384,768]{1,0:T(8,128)(2,1)S(1)} %pad_maximum_fusion.1.rest_0_), channel_id=1, source_target_pairs={{0,16},{2,18},{4,20},{6,22},{8,24},{10,26},{12,28},{14,30},{16,0},... | collective-permute-start | bytes 1769480 | tf_op jit(solution)/shard_map/u2/ppermute | solution.py:414
  5.4 1.5 %collective-permute-start.3 = (bf16[384,768]{1,0:T(8,128)(2,1)S(1)}, bf16[384,768]{1,0:T(8,128)(2,1)S(1)}, u32[]{:S(2)}, u32[]{:S(2)}) collective-permute-start(bf16[384,768]{1,0:T(8,128)(2,1)S(1)} %pad_maximum_fusion.1.rest_0_), channel_id=1, source_target_pairs={{0,4},{2,6},{4,0},{6,2},{8,12},{10,14},{12,8},{14,10},{16,20},{18,... | collective-permute-start | bytes 1769480 | tf_op jit(solution)/shard_map/y0/ppermute | solution.py:414
  6.9 1.5 %collective-permute-start.2 = (bf16[384,768]{1,0:T(8,128)(2,1)S(1)}, bf16[384,768]{1,0:T(8,128)(2,1)S(1)}, u32[]{:S(2)}, u32[]{:S(2)}) collective-permute-start(bf16[384,768]{1,0:T(8,128)(2,1)S(1)} %pad_maximum_fusion.1.rest_0_), channel_id=1, source_target_pairs={{0,1},{1,0},{2,3},{3,2},{4,5},{5,4},{6,7},{7,6},{8,9},{9,8},{10,11... | collective-permute-start | bytes 1769480 | tf_op jit(solution)/shard_map/x0/ppermute | solution.py:414
  8.8 1.6 %collective-permute-start = (bf16[384,768]{1,0:T(8,128)(2,1)S(1)}, bf16[384,768]{1,0:T(8,128)(2,1)}, u32[]{:S(2)}, u32[]{:S(2)}) collective-permute-start(bf16[384,768]{1,0:T(8,128)(2,1)S(1)} %pad_maximum_fusion.1.rest_0_), channel_id=1, source_target_pairs={{0,8},{2,10},{4,12},{6,14},{8,0},{10,2},{12,4},{14,6},{16,24},{18,... | collective-permute-start | bytes 1769480 | tf_op jit(solution)/shard_map/u1/ppermute | solution.py:414
  10.5 1.7 %copy-done = bf16[6,128,1536]{2,1,0:T(8,128)(2,1)S(1)} copy-done((bf16[6,128,1536]{2,1,0:T(8,128)(2,1)S(1)}, bf16[6,128,1536]{2,1,0:T(8,128)(2,1)}, u32[]{:S(2)}) %copy-start) | copy-done | bytes 2359320
  12.1 3.3 %norm.1.n_ref = bf16[1536,768]{1,0:T(8,128)(2,1)S(1)} custom-call(s32[12]{0:T(128)S(1)} %copy-done.1, bf16[6,128,1536]{2,1,0:T(8,128)(2,1)S(1)} %copy-done, f32[1,1536]{1,0:T(1,128)S(1)} %reshape.20.gain_ref, f32[1,384]{1,0:T(1,128)S(1)} %multiply_exponential_fusion.freq_ref), custom_call_target="tpu_custom_call" | custom-call | flops 47185920 | bytes 4718592 | tf_op jit(solution)/shard_map/norm/pallas_call | solution.py:138
  15.4 16.6 %collective-permute-done.4 = bf16[384,768]{1,0:T(8,128)(2,1)S(1)} collective-permute-done((bf16[384,768]{1,0:T(8,128)(2,1)S(1)}, bf16[384,768]{1,0:T(8,128)(2,1)S(1)}, u32[]{:S(2)}, u32[]{:S(2)}) %collective-permute-start.4) | collective-permute-done | bytes 589856 | tf_op jit(solution)/shard_map/u2/ppermute | solution.py:414
  32.0 2.5 %collective-permute-done.1.rest_3_ = bf16[384,768]{1,0:T(8,128)(2,1)S(1)} collective-permute-done((bf16[384,768]{1,0:T(8,128)(2,1)S(1)}, bf16[384,768]{1,0:T(8,128)(2,1)S(1)}, u32[]{:S(2)}, u32[]{:S(2)}) %collective-permute-start.1) | collective-permute-done | bytes 589856 | tf_op jit(solution)/shard_map/d0/ppermute | solution.py:414
  35.0 2.2 %pad_maximum_fusion.rest_0_.rest_8_.rest_16_ = bf16[2,384,768]{2,1,0:T(8,128)(2,1)} fusion(bf16[1,384,768]{2,1,0:T(8,128)(2,1)S(1)} %bitcast.14, bf16[1,384,768]{2,1,0:T(8,128)(2,1)} %bitcast.10), kind=kLoop, calls=%fused_computation | loop fusion | flops 589824 | bytes 2359296 | tf_op jit(solution)/shard_map/stack | solution.py:454
  37.2 1.6 %collective-permute-start.8 = (bf16[2,384,768]{2,1,0:T(8,128)(2,1)}, bf16[2,384,768]{2,1,0:T(8,128)(2,1)}, u32[]{:S(2)}, u32[]{:S(2)}) collective-permute-start(bf16[2,384,768]{2,1,0:T(8,128)(2,1)} %pad_maximum_fusion.rest_0_.rest_8_.rest_16_), channel_id=1, source_target_pairs={{0,4},{2,6},{4,0},{6,2},{8,12},{10,14},{12,8},{14,10},{16,20},{18,... | collective-permute-start | bytes 3538952 | tf_op jit(solution)/shard_map/y12/ppermute | solution.py:414
  38.7 1.3 %collective-permute-start.9 = (bf16[384,768]{1,0:T(8,128)(2,1)S(1)}, bf16[384,768]{1,0:T(8,128)(2,1)S(1)}, u32[]{:S(2)}, u32[]{:S(2)}) collective-permute-start(bf16[384,768]{1,0:T(8,128)(2,1)S(1)} %collective-permute-done.4), channel_id=1, source_target_pairs={{0,8},{2,10},{4,12},{6,14},{8,0},{10,2},{12,4},{14,6},{16,24},{18,... | collective-permute-start | bytes 1769480 | tf_op jit(solution)/shard_map/u3/ppermute | solution.py:414
  40.1 1.5 %collective-permute-start.7 = (bf16[384,768]{1,0:T(8,128)(2,1)S(1)}, bf16[384,768]{1,0:T(8,128)(2,1)}, u32[]{:S(2)}, u32[]{:S(2)}) collective-permute-start(bf16[384,768]{1,0:T(8,128)(2,1)S(1)} %collective-permute-done.4), channel_id=1, source_target_pairs={{0,1},{1,0},{2,3},{3,2},{4,5},{5,4},{6,7},{7,6},{8,9},{9,8},{10,11... | collective-permute-start | bytes 1769480 | tf_op jit(solution)/shard_map/x2/ppermute | solution.py:414
  41.6 0.7 collective-permute-start.10
  42.3 12.6 %collective-permute-done.9.rest_24_ = bf16[384,768]{1,0:T(8,128)(2,1)S(1)} collective-permute-done((bf16[384,768]{1,0:T(8,128)(2,1)S(1)}, bf16[384,768]{1,0:T(8,128)(2,1)S(1)}, u32[]{:S(2)}, u32[]{:S(2)}) %collective-permute-start.9) | collective-permute-done | bytes 589856 | tf_op jit(solution)/shard_map/u3/ppermute | solution.py:414
  55.1 11.8 %collective-permute-done.10.rest_3_.rest_11_ = bf16[384,768]{1,0:T(8,128)(2,1)} collective-permute-done((bf16[384,768]{1,0:T(8,128)(2,1)S(1)}, bf16[384,768]{1,0:T(8,128)(2,1)}, u32[]{:S(2)}, u32[]{:S(2)}) %collective-permute-start.10) | collective-permute-done | bytes 589856 | tf_op jit(solution)/shard_map/d1/ppermute | solution.py:414
  67.5 1.5 %collective-permute-start.6 = (bf16[384,768]{1,0:T(8,128)(2,1)}, bf16[384,768]{1,0:T(8,128)(2,1)}, u32[]{:S(2)}, u32[]{:S(2)}) collective-permute-start(bf16[384,768]{1,0:T(8,128)(2,1)} %collective-permute-done), channel_id=1, source_target_pairs={{0,1},{1,0},{2,3},{3,2},{4,5},{5,4},{6,7},{7,6},{8,9},{9,8},{10,11... | collective-permute-start | bytes 1769480 | tf_op jit(solution)/shard_map/x1/ppermute | solution.py:414
  69.0 0.6 collective-permute-start.13
  69.9 6.3 %project.3 = (bf16[3,384,768]{2,1,0:T(8,128)(2,1)}, bf16[3,768,384]{2,1,0:T(8,128)(2,1)}) custom-call(s32[3]{0:T(128)S(1)} %pad_add_fusion.at_ref, s32[1]{0:T(128)} %bitcast.3.plane_ref, bf16[1536,768]{1,0:T(8,128)(2,1)S(1)} %norm.1.n_ref, bf16[384,768]{1,0:T(8,128)(2,1)} %copy-done.3, bf16[384,768]{1,0:T(8,128)(2,1)} %copy-done.6, ...), custom_call_target="tpu_custom_call" | custom-call | flops 2717908992 | bytes 5898240 | tf_op jit(solution)/shard_map/project/pallas_call | solution.py:225
  76.3 6.9 %collective-permute-done.6.rest_1_.rest_9_ = bf16[384,768]{1,0:T(8,128)(2,1)} collective-permute-done((bf16[384,768]{1,0:T(8,128)(2,1)}, bf16[384,768]{1,0:T(8,128)(2,1)}, u32[]{:S(2)}, u32[]{:S(2)}) %collective-permute-start.6) | collective-permute-done | bytes 589856 | tf_op jit(solution)/shard_map/x1/ppermute | solution.py:414
  83.2 2.0 %collective-permute-done.13.rest_3_.rest_19_ = bf16[384,768]{1,0:T(8,128)(2,1)} collective-permute-done((bf16[384,768]{1,0:T(8,128)(2,1)}, bf16[384,768]{1,0:T(8,128)(2,1)}, u32[]{:S(2)}, u32[]{:S(2)}) %collective-permute-start.13) | collective-permute-done | bytes 589856 | tf_op jit(solution)/shard_map/d2/ppermute | solution.py:414
  86.7 0.8 collective-permute-done.21.rest_7_.rest_23_
  87.5 1.1 collective-permute-start.20
  88.6 6.4 %project.4 = (bf16[3,384,768]{2,1,0:T(8,128)(2,1)}, bf16[3,768,384]{2,1,0:T(8,128)(2,1)}) custom-call(s32[3]{0:T(128)S(1)} %pad_add_fusion.at_ref, s32[1]{0:T(128)} %bitcast.5.plane_ref, bf16[1536,768]{1,0:T(8,128)(2,1)S(1)} %norm.1.n_ref, bf16[2,384,768]{2,1,0:T(8,128)(2,1)} %pad_maximum_fusion.rest_0_.rest_8_.rest_16_, ...), custom_call_target="tpu_custom_call" | custom-call | flops 2717908992 | bytes 5898240 | tf_op jit(solution)/shard_map/project/pallas_call | solution.py:225
  95.0 6.3 %project.5 = (bf16[3,384,768]{2,1,0:T(8,128)(2,1)}, bf16[3,768,384]{2,1,0:T(8,128)(2,1)}) custom-call(s32[3]{0:T(128)S(1)} %pad_add_fusion.at_ref, s32[1]{0:T(128)} %bitcast.4.plane_ref, bf16[1536,768]{1,0:T(8,128)(2,1)S(1)} %norm.1.n_ref, bf16[2,384,768]{2,1,0:T(8,128)(2,1)} %pad_maximum_fusion.rest_0_.rest_8_.rest_16_, ...), custom_call_target="tpu_custom_call" | custom-call | flops 2717908992 | bytes 5898240 | tf_op jit(solution)/shard_map/project/pallas_call | solution.py:225
  101.8 1.4 %collective-permute-done.20.rest_27_ = bf16[384,768]{1,0:T(8,128)(2,1)} collective-permute-done((bf16[384,768]{1,0:T(8,128)(2,1)}, bf16[384,768]{1,0:T(8,128)(2,1)}, u32[]{:S(2)}, u32[]{:S(2)}) %collective-permute-start.20) | collective-permute-done | bytes 589856 | tf_op jit(solution)/shard_map/d3/ppermute | solution.py:414
  103.2 0.5 collective-permute-start.25
  104.9 1.2 collective-permute-done.24.rest_28_
  106.1 0.7 collective-permute-done.25.rest_29_
  106.9 1.0 collective-permute-done.26.rest_30_
  108.1 21.4 %finish.1 = bf16[768,1536]{1,0:T(8,128)(2,1)} custom-call(s32[3]{0:T(128)S(1)} %pad_add_fusion.at_ref, s32[4]{0:T(128)S(1)} %pad_add_fusion.1.planes_ref, s32[12]{0:T(128)S(1)} %copy-done.2, s32[1]{0:T(128)S(6)} %copy.8.live_ref, bf16[1536,768]{1,0:T(8,128)(2,1)S(1)} %norm.1.n_ref, bf16[768,1536]{1,0:T(8,128)(2,1)} %bitcast.13, ...), custom_call_target="tpu_custom_call" | custom-call | flops 10871635968 | bytes 9437184 | tf_op jit(solution)/shard_map/finish/pallas_call | solution.py:371
  (59 shorter events, 5.0 us)
Async XLA Ops:
  1.2 14.3 %copy-start.3 = (bf16[384,768]{1,0:T(8,128)(2,1)}, bf16[384,768]{1,0:T(8,128)(2,1)S(1)}, u32[]{:S(2)}) copy-start(bf16[384,768]{1,0:T(8,128)(2,1)S(1)} %pad_maximum_fusion.1.rest_0_) | copy-start | bytes 1769476
  1.2 7.7 %collective-permute-start.5 = (bf16[384,768]{1,0:T(8,128)(2,1)S(1)}, bf16[384,768]{1,0:T(8,128)(2,1)S(1)}, u32[]{:S(2)}, u32[]{:S(2)}) collective-permute-start(bf16[384,768]{1,0:T(8,128)(2,1)S(1)} %pad_maximum_fusion.1.rest_0_), channel_id=1, source_target_pairs={{0,2},{2,0},{4,6},{6,4},{8,10},{10,8},{12,14},{14,12},{16,18},{18,... | collective-permute-start | bytes 1769480 | tf_op jit(solution)/shard_map/core_u0/ppermute | solution.py:414
  1.7 30.3 %collective-permute-start.4 = (bf16[384,768]{1,0:T(8,128)(2,1)S(1)}, bf16[384,768]{1,0:T(8,128)(2,1)S(1)}, u32[]{:S(2)}, u32[]{:S(2)}) collective-permute-start(bf16[384,768]{1,0:T(8,128)(2,1)S(1)} %pad_maximum_fusion.1.rest_0_), channel_id=1, source_target_pairs={{0,16},{2,18},{4,20},{6,22},{8,24},{10,26},{12,28},{14,30},{16,0},... | collective-permute-start | bytes 1769480 | tf_op jit(solution)/shard_map/u2/ppermute | solution.py:414
  5.4 26.7 %collective-permute-start.3 = (bf16[384,768]{1,0:T(8,128)(2,1)S(1)}, bf16[384,768]{1,0:T(8,128)(2,1)S(1)}, u32[]{:S(2)}, u32[]{:S(2)}) collective-permute-start(bf16[384,768]{1,0:T(8,128)(2,1)S(1)} %pad_maximum_fusion.1.rest_0_), channel_id=1, source_target_pairs={{0,4},{2,6},{4,0},{6,2},{8,12},{10,14},{12,8},{14,10},{16,20},{18,... | collective-permute-start | bytes 1769480 | tf_op jit(solution)/shard_map/y0/ppermute | solution.py:414
  6.9 25.2 %collective-permute-start.2 = (bf16[384,768]{1,0:T(8,128)(2,1)S(1)}, bf16[384,768]{1,0:T(8,128)(2,1)S(1)}, u32[]{:S(2)}, u32[]{:S(2)}) collective-permute-start(bf16[384,768]{1,0:T(8,128)(2,1)S(1)} %pad_maximum_fusion.1.rest_0_), channel_id=1, source_target_pairs={{0,1},{1,0},{2,3},{3,2},{4,5},{5,4},{6,7},{7,6},{8,9},{9,8},{10,11... | collective-permute-start | bytes 1769480 | tf_op jit(solution)/shard_map/x0/ppermute | solution.py:414
  8.4 26.2 %collective-permute-start.1 = (bf16[384,768]{1,0:T(8,128)(2,1)S(1)}, bf16[384,768]{1,0:T(8,128)(2,1)S(1)}, u32[]{:S(2)}, u32[]{:S(2)}) collective-permute-start(bf16[384,768]{1,0:T(8,128)(2,1)S(1)} %pad_maximum_fusion.1.rest_0_), channel_id=1, source_target_pairs={{0,5},{1,4},{2,7},{3,6},{4,1},{5,0},{6,3},{7,2},{8,13},{9,12},{10,... | collective-permute-start | bytes 1769480 | tf_op jit(solution)/shard_map/d0/ppermute | solution.py:414
  8.8 26.1 %collective-permute-start = (bf16[384,768]{1,0:T(8,128)(2,1)S(1)}, bf16[384,768]{1,0:T(8,128)(2,1)}, u32[]{:S(2)}, u32[]{:S(2)}) collective-permute-start(bf16[384,768]{1,0:T(8,128)(2,1)S(1)} %pad_maximum_fusion.1.rest_0_), channel_id=1, source_target_pairs={{0,8},{2,10},{4,12},{6,14},{8,0},{10,2},{12,4},{14,6},{16,24},{18,... | collective-permute-start | bytes 1769480 | tf_op jit(solution)/shard_map/u1/ppermute | solution.py:414
  34.6 20.3 %copy-start.7 = (bf16[384,768]{1,0:T(8,128)(2,1)}, bf16[384,768]{1,0:T(8,128)(2,1)S(1)}, u32[]{:S(2)}) copy-start(bf16[384,768]{1,0:T(8,128)(2,1)S(1)} %collective-permute-done.1.rest_3_) | copy-start | bytes 1769476
  35.0 7.3 %collective-permute-start.11 = (bf16[384,768]{1,0:T(8,128)(2,1)S(1)}, bf16[384,768]{1,0:T(8,128)(2,1)S(1)}, u32[]{:S(2)}, u32[]{:S(2)}) collective-permute-start(bf16[384,768]{1,0:T(8,128)(2,1)S(1)} %collective-permute-done.2.rest_1_), channel_id=1, source_target_pairs={{0,2},{2,0},{4,6},{6,4},{8,10},{10,8},{12,14},{14,12},{16,18},{18,... | collective-permute-start | bytes 1769480 | tf_op jit(solution)/shard_map/core_x0/ppermute | solution.py:414
  37.2 29.8 %collective-permute-start.8 = (bf16[2,384,768]{2,1,0:T(8,128)(2,1)}, bf16[2,384,768]{2,1,0:T(8,128)(2,1)}, u32[]{:S(2)}, u32[]{:S(2)}) collective-permute-start(bf16[2,384,768]{2,1,0:T(8,128)(2,1)} %pad_maximum_fusion.rest_0_.rest_8_.rest_16_), channel_id=1, source_target_pairs={{0,4},{2,6},{4,0},{6,2},{8,12},{10,14},{12,8},{14,10},{16,20},{18,... | collective-permute-start | bytes 3538952 | tf_op jit(solution)/shard_map/y12/ppermute | solution.py:414
  38.7 16.2 %collective-permute-start.9 = (bf16[384,768]{1,0:T(8,128)(2,1)S(1)}, bf16[384,768]{1,0:T(8,128)(2,1)S(1)}, u32[]{:S(2)}, u32[]{:S(2)}) collective-permute-start(bf16[384,768]{1,0:T(8,128)(2,1)S(1)} %collective-permute-done.4), channel_id=1, source_target_pairs={{0,8},{2,10},{4,12},{6,14},{8,0},{10,2},{12,4},{14,6},{16,24},{18,... | collective-permute-start | bytes 1769480 | tf_op jit(solution)/shard_map/u3/ppermute | solution.py:414
  40.1 15.1 %collective-permute-start.7 = (bf16[384,768]{1,0:T(8,128)(2,1)S(1)}, bf16[384,768]{1,0:T(8,128)(2,1)}, u32[]{:S(2)}, u32[]{:S(2)}) collective-permute-start(bf16[384,768]{1,0:T(8,128)(2,1)S(1)} %collective-permute-done.4), channel_id=1, source_target_pairs={{0,1},{1,0},{2,3},{3,2},{4,5},{5,4},{6,7},{7,6},{8,9},{9,8},{10,11... | collective-permute-start | bytes 1769480 | tf_op jit(solution)/shard_map/x2/ppermute | solution.py:414
  41.6 25.4 %collective-permute-start.10 = (bf16[384,768]{1,0:T(8,128)(2,1)S(1)}, bf16[384,768]{1,0:T(8,128)(2,1)}, u32[]{:S(2)}, u32[]{:S(2)}) collective-permute-start(bf16[384,768]{1,0:T(8,128)(2,1)S(1)} %collective-permute-done.1.rest_3_), channel_id=1, source_target_pairs={{0,8},{2,10},{4,12},{6,14},{8,0},{10,2},{12,4},{14,6},{16,24},{18,... | collective-permute-start | bytes 1769480 | tf_op jit(solution)/shard_map/d1/ppermute | solution.py:414
  42.3 27.7 %copy-start.8 = (bf16[384,768]{1,0:T(8,128)(2,1)}, bf16[384,768]{1,0:T(8,128)(2,1)S(1)}, u32[]{:S(2)}) copy-start(bf16[384,768]{1,0:T(8,128)(2,1)S(1)} %collective-permute-done.11.rest_5_) | copy-start | bytes 1769476
  42.3 24.7 %collective-permute-start.12 = (bf16[384,768]{1,0:T(8,128)(2,1)S(1)}, bf16[384,768]{1,0:T(8,128)(2,1)S(1)}, u32[]{:S(2)}, u32[]{:S(2)}) collective-permute-start(bf16[384,768]{1,0:T(8,128)(2,1)S(1)} %collective-permute-done.3.rest_2_), channel_id=1, source_target_pairs={{0,2},{2,0},{4,6},{6,4},{8,10},{10,8},{12,14},{14,12},{16,18},{18,... | collective-permute-start | bytes 1769480 | tf_op jit(solution)/shard_map/core_y0/ppermute | solution.py:414
  54.9 14.1 %collective-permute-start.17 = (bf16[384,768]{1,0:T(8,128)(2,1)S(1)}, bf16[384,768]{1,0:T(8,128)(2,1)S(1)}, u32[]{:S(2)}, u32[]{:S(2)}) collective-permute-start(bf16[384,768]{1,0:T(8,128)(2,1)S(1)} %collective-permute-done.1.rest_3_), channel_id=1, source_target_pairs={{0,2},{2,0},{4,6},{6,4},{8,10},{10,8},{12,14},{14,12},{16,18},{18,... | collective-permute-start | bytes 1769480 | tf_op jit(solution)/shard_map/core_d0/ppermute | solution.py:414
  67.0 18.2 %collective-permute-start.15 = (bf16[2,384,768]{2,1,0:T(8,128)(2,1)}, bf16[2,384,768]{2,1,0:T(8,128)(2,1)}, u32[]{:S(2)}, u32[]{:S(2)}) collective-permute-start(bf16[2,384,768]{2,1,0:T(8,128)(2,1)} %collective-permute-done.8.rest_2_.rest_10_.rest_18_), channel_id=1, source_target_pairs={{0,2},{2,0},{4,6},{6,4},{8,10},{10,8},{12,14},{14,12},{16,18},{18,... | collective-permute-start | bytes 3538952 | tf_op jit(solution)/shard_map/core_y12/ppermute | solution.py:414
  67.0 18.1 %collective-permute-start.16 = (bf16[2,384,768]{2,1,0:T(8,128)(2,1)}, bf16[2,384,768]{2,1,0:T(8,128)(2,1)}, u32[]{:S(2)}, u32[]{:S(2)}) collective-permute-start(bf16[2,384,768]{2,1,0:T(8,128)(2,1)} %pad_maximum_fusion.rest_0_.rest_8_.rest_16_), channel_id=1, source_target_pairs={{0,2},{2,0},{4,6},{6,4},{8,10},{10,8},{12,14},{14,12},{16,18},{18,... | collective-permute-start | bytes 3538952 | tf_op jit(solution)/shard_map/core_u12/ppermute | solution.py:414
  67.5 15.6 %collective-permute-start.6 = (bf16[384,768]{1,0:T(8,128)(2,1)}, bf16[384,768]{1,0:T(8,128)(2,1)}, u32[]{:S(2)}, u32[]{:S(2)}) collective-permute-start(bf16[384,768]{1,0:T(8,128)(2,1)} %collective-permute-done), channel_id=1, source_target_pairs={{0,1},{1,0},{2,3},{3,2},{4,5},{5,4},{6,7},{7,6},{8,9},{9,8},{10,11... | collective-permute-start | bytes 1769480 | tf_op jit(solution)/shard_map/x1/ppermute | solution.py:414
  69.0 14.1 %collective-permute-start.14 = (bf16[384,768]{1,0:T(8,128)(2,1)}, bf16[384,768]{1,0:T(8,128)(2,1)}, u32[]{:S(2)}, u32[]{:S(2)}) collective-permute-start(bf16[384,768]{1,0:T(8,128)(2,1)} %collective-permute-done.7.rest_1_.rest_17_), channel_id=1, source_target_pairs={{0,2},{2,0},{4,6},{6,4},{8,10},{10,8},{12,14},{14,12},{16,18},{18,... | collective-permute-start | bytes 1769480 | tf_op jit(solution)/shard_map/core_x2/ppermute | solution.py:414
  69.0 16.1 %collective-permute-start.13 = (bf16[384,768]{1,0:T(8,128)(2,1)}, bf16[384,768]{1,0:T(8,128)(2,1)}, u32[]{:S(2)}, u32[]{:S(2)}) collective-permute-start(bf16[384,768]{1,0:T(8,128)(2,1)} %collective-permute-done.7.rest_1_.rest_17_), channel_id=1, source_target_pairs={{0,4},{2,6},{4,0},{6,2},{8,12},{10,14},{12,8},{14,10},{16,20},{18,... | collective-permute-start | bytes 1769480 | tf_op jit(solution)/shard_map/d2/ppermute | solution.py:414
  85.2 2.3 %collective-permute-start.21 = (bf16[384,768]{1,0:T(8,128)(2,1)}, bf16[384,768]{1,0:T(8,128)(2,1)}, u32[]{:S(2)}, u32[]{:S(2)}) collective-permute-start(bf16[384,768]{1,0:T(8,128)(2,1)} %collective-permute-done.13.rest_3_.rest_19_), channel_id=1, source_target_pairs={{0,2},{2,0},{4,6},{6,4},{8,10},{10,8},{12,14},{14,12},{16,18},{18,... | collective-permute-start | bytes 1769480 | tf_op jit(solution)/shard_map/core_d2/ppermute | solution.py:414
  85.2 9.8 %collective-permute-start.22 = (bf16[384,768]{1,0:T(8,128)(2,1)}, bf16[384,768]{1,0:T(8,128)(2,1)}, u32[]{:S(2)}, u32[]{:S(2)}) collective-permute-start(bf16[384,768]{1,0:T(8,128)(2,1)} %collective-permute-done.6.rest_1_.rest_9_), channel_id=1, source_target_pairs={{0,2},{2,0},{4,6},{6,4},{8,10},{10,8},{12,14},{14,12},{16,18},{18,... | collective-permute-start | bytes 1769480 | tf_op jit(solution)/shard_map/core_x1/ppermute | solution.py:414
  85.7 9.3 %collective-permute-start.23 = (bf16[384,768]{1,0:T(8,128)(2,1)}, bf16[384,768]{1,0:T(8,128)(2,1)}, u32[]{:S(2)}, u32[]{:S(2)}) collective-permute-start(bf16[384,768]{1,0:T(8,128)(2,1)} %collective-permute-done.10.rest_3_.rest_11_), channel_id=1, source_target_pairs={{0,2},{2,0},{4,6},{6,4},{8,10},{10,8},{12,14},{14,12},{16,18},{18,... | collective-permute-start | bytes 1769480 | tf_op jit(solution)/shard_map/core_d1/ppermute | solution.py:414
  85.7 15.7 %collective-permute-start.19 = (bf16[384,768]{1,0:T(8,128)(2,1)S(1)}, bf16[384,768]{1,0:T(8,128)(2,1)S(1)}, u32[]{:S(2)}, u32[]{:S(2)}) collective-permute-start(bf16[384,768]{1,0:T(8,128)(2,1)S(1)} %collective-permute-done.9.rest_24_), channel_id=1, source_target_pairs={{0,4},{2,6},{4,0},{6,2},{8,12},{10,14},{12,8},{14,10},{16,20},{18,... | collective-permute-start | bytes 1769480 | tf_op jit(solution)/shard_map/y3/ppermute | solution.py:414
  86.3 15.5 %collective-permute-start.18 = (bf16[384,768]{1,0:T(8,128)(2,1)S(1)}, bf16[384,768]{1,0:T(8,128)(2,1)}, u32[]{:S(2)}, u32[]{:S(2)}) collective-permute-start(bf16[384,768]{1,0:T(8,128)(2,1)S(1)} %collective-permute-done.9.rest_24_), channel_id=1, source_target_pairs={{0,1},{1,0},{2,3},{3,2},{4,5},{5,4},{6,7},{7,6},{8,9},{9,8},{10,11... | collective-permute-start | bytes 1769480 | tf_op jit(solution)/shard_map/x3/ppermute | solution.py:414
  87.5 15.7 %collective-permute-start.20 = (bf16[384,768]{1,0:T(8,128)(2,1)}, bf16[384,768]{1,0:T(8,128)(2,1)}, u32[]{:S(2)}, u32[]{:S(2)}) collective-permute-start(bf16[384,768]{1,0:T(8,128)(2,1)} %collective-permute-done.13.rest_3_.rest_19_), channel_id=1, source_target_pairs={{0,8},{2,10},{4,12},{6,14},{8,0},{10,2},{12,4},{14,6},{16,24},{18,... | collective-permute-start | bytes 1769480 | tf_op jit(solution)/shard_map/d3/ppermute | solution.py:414
  95.0 13.1 %copy-start.2 = (s32[12]{0:T(128)S(1)}, s32[12]{0:T(128)}, u32[]{:S(2)}) copy-start(s32[12]{0:T(128)} %lens_ref.1) | copy-start | bytes 148
  103.2 2.9 %collective-permute-start.24 = (bf16[384,768]{1,0:T(8,128)(2,1)S(1)}, bf16[384,768]{1,0:T(8,128)(2,1)}, u32[]{:S(2)}, u32[]{:S(2)}) collective-permute-start(bf16[384,768]{1,0:T(8,128)(2,1)S(1)} %collective-permute-done.9.rest_24_), channel_id=1, source_target_pairs={{0,2},{2,0},{4,6},{6,4},{8,10},{10,8},{12,14},{14,12},{16,18},{18,... | collective-permute-start | bytes 1769480 | tf_op jit(solution)/shard_map/core_u3/ppermute | solution.py:414
  103.2 3.7 %collective-permute-start.25 = (bf16[384,768]{1,0:T(8,128)(2,1)}, bf16[384,768]{1,0:T(8,128)(2,1)}, u32[]{:S(2)}, u32[]{:S(2)}) collective-permute-start(bf16[384,768]{1,0:T(8,128)(2,1)} %collective-permute-done.18.rest_25_), channel_id=1, source_target_pairs={{0,2},{2,0},{4,6},{6,4},{8,10},{10,8},{12,14},{14,12},{16,18},{18,... | collective-permute-start | bytes 1769480 | tf_op jit(solution)/shard_map/core_x3/ppermute | solution.py:414
  103.7 4.1 %collective-permute-start.26 = (bf16[384,768]{1,0:T(8,128)(2,1)S(1)}, bf16[384,768]{1,0:T(8,128)(2,1)}, u32[]{:S(2)}, u32[]{:S(2)}) collective-permute-start(bf16[384,768]{1,0:T(8,128)(2,1)S(1)} %collective-permute-done.19.rest_26_), channel_id=1, source_target_pairs={{0,2},{2,0},{4,6},{6,4},{8,10},{10,8},{12,14},{14,12},{16,18},{18,... | collective-permute-start | bytes 1769480 | tf_op jit(solution)/shard_map/core_y3/ppermute | solution.py:414
  103.7 4.4 %collective-permute-start.27 = (bf16[384,768]{1,0:T(8,128)(2,1)}, bf16[384,768]{1,0:T(8,128)(2,1)}, u32[]{:S(2)}, u32[]{:S(2)}) collective-permute-start(bf16[384,768]{1,0:T(8,128)(2,1)} %collective-permute-done.20.rest_27_), channel_id=1, source_target_pairs={{0,2},{2,0},{4,6},{6,4},{8,10},{10,8},{12,14},{14,12},{16,18},{18,... | collective-permute-start | bytes 1769480 | tf_op jit(solution)/shard_map/core_d3/ppermute | solution.py:414
  (8 other events, 42.4 us)

commit v7 on v6

--- a/solution.py
+++ b/solution.py
@@ -287,9 +287,6 @@
     for s in range(slots):
         spot = pl.ds(pl.multiple_of(planes_ref[s] * cols, 128), cols)
         bases.append(pltpu.make_async_copy(lat_ref.at[:, spot], done_ref.at[s], base_sems.at[s]))
-    for c in copies + bases:
-        c.start()
-
     blocks = tokens // 128
     key = lax.broadcasted_iota(jnp.int32, (128, 256), 0)
     query = lax.broadcasted_iota(jnp.int32, (128, 256), 1) % 128
@@ -302,6 +299,8 @@
         if m < 2:
             wait_columns(m, pieces[8 * last :], spots[8 * last :], rows, w_ref, w_sems)
         which = planes_ref[last] * count + m
+        for c in (copies + bases)[m::count]:
+            c.start()
         out = project_chunk(m, which, parts, w_ref, n_ref)
         for kind, to in ((0, q_ref), (1, k_ref), (2, v_ref)):
 
@@ -354,12 +353,18 @@
         for c in copies[8 * s : 8 * s + 8] + [bases[s]]:
             c.wait()
         spot = pl.ds(pl.multiple_of(planes_ref[s] * cols, 128), cols)
-        update = lax.dot_general(
-            att_ref[...], wo_ref[s], (((1,), (1,)), ((), ())), preferred_element_type=F32
-        )
-        done_ref[s] = (done_ref[s].astype(F32) + update).astype(BF)
-        outs.append(pltpu.make_async_copy(done_ref.at[s], out_ref.at[:, spot], out_sems.at[s]))
-        outs[s].start()
+        for h in range(2):
+            part = pl.ds(h * tokens // 2, tokens // 2)
+            update = lax.dot_general(
+                att_ref[part, :], wo_ref[s], (((1,), (1,)), ((), ())), preferred_element_type=F32
+            )
+            done_ref[s, part, :] = (done_ref[s, part, :].astype(F32) + update).astype(BF)
+            outs.append(
+                pltpu.make_async_copy(
+                    done_ref.at[s, part], out_ref.at[part, spot], out_sems.at[2 * s + h]
+                )
+            )
+            outs[-1].start()
     for c in outs:
         c.wait()
 
@@ -386,7 +391,7 @@
             pltpu.SemaphoreType.DMA((8,)),
             pltpu.SemaphoreType.DMA((4 * count,)),
             pltpu.SemaphoreType.DMA((len(pieces),)),
-            pltpu.SemaphoreType.DMA((slots,)),
+            pltpu.SemaphoreType.DMA((2 * slots,)),
             pltpu.SemaphoreType.DMA((slots,)),
         ],
         compiler_params=params(44),
@@ -453,7 +458,7 @@
     u1, d0, x0, y0, u2, normed, cu0 = sync(u1, d0, x0, y0, u2, normed, cu0)
     u12 = jnp.stack([u1, u2])
     x2, y12, u3, d1 = xs(u2, "x2"), ys(u12, "y12"), z1(u2, "u3"), z1(d0, "d1")
-    cx0, cy0 = share(x0=x0, y0=y0)
+    cx0, cy0 = core(x0, "core_x0"), core(y0, "core_y0")
     x2, y12, u3, d1, cx0, cy0, u12 = sync(x2, y12, u3, d1, cx0, cy0, u12)
     x1, d2 = xs(u1, "x1"), ys(x2, "d2")
     cd0, cx2, cy12, cu12 = (
@@ -464,12 +469,13 @@
     x1, d2, cx2, cy12, cu12, d1, u3, p0 = sync(x1, d2, cx2, cy12, cu12, d1, u3, p0)
     x3, y3, d3 = xs(u3, "x3"), ys(u3, "y3"), z1(d2, "d3")
     cd2, cx1, cd1 = core(d2, "core_d2"), core(x1, "core_x1"), core(d1, "core_d1")
+    cu3 = core(u3, "core_u3")
     s2 = slot(1, u12, x2, y12, d2, cu12, cx2, cy12, cd2)
     p2 = project(place, planes[2:3], normed, s2, nq)
     s1 = slot(0, u12, x1, y12, d1, cu12, cx1, cy12, cd1)
     p1 = project(place, planes[1:2], normed, s1, nq)
-    x3, y3, d3, u3, p2, p1 = sync(x3, y3, d3, u3, p2, p1)
-    cu3, cx3, cy3, cd3 = core(u3, "core_u3"), core(x3, "core_x3"), core(y3, "core_y3"), core(d3, "core_d3")
+    x3, y3, d3, u3, cu3, p2, p1 = sync(x3, y3, d3, u3, cu3, p2, p1)
+    cx3, cy3, cd3 = core(x3, "core_x3"), core(y3, "core_y3"), core(d3, "core_d3")
     s3 = slot(0, u3, x3, y3, d3, cu3, cx3, cy3, cd3)
     flat = latents.reshape(blocks * rows, width)
     so = s0 + s1 + s2 + s3

time: 130 us -> 128 us (0.985)
  waiting for transfers between devices: 58.8 us -> 55.5 us
  starting transfers between devices: 20.7 us -> 23.2 us
    ppermute x28, waiting for transfers between devices: 58.8 us -> 55.5 us  [move(): return lax.ppermute(value, axis, pairs)]
    ppermute x28, starting transfers between devices: 20.7 us -> 23.2 us  [move(): return lax.ppermute(value, axis, pairs)]
  transfers between devices with their start and end apart: 28 -> 28, of which waited for: 16 -> 15; matrix products, arithmetic and copies ran while one was open for 2% -> 2% of each run, Pallas kernels for 17% -> 17%
where the time goes in v7:
time: 128 us
  waiting for transfers between devices  55.5 us (43%)
  Pallas kernels  43.3 us (34%)
  starting transfers between devices  23.2 us (18%)
  other arithmetic  3.5 us (3%)
  local copies, waits for them, and re-layouts  1.72 us (1%)
    ppermute x28, waiting for transfers between devices, move(): return lax.ppermute(value, axis, pairs)  55.5 us
    ppermute x28, starting transfers between devices, move(): return lax.ppermute(value, axis, pairs)  23.2 us
    pallas_call x1, Pallas kernels, finish(): pl.pallas_call(functools.partial(finish_kernel, [spot for _, spot in piec...  21.1 us
    pallas_call x3, Pallas kernels, project(): pl.pallas_call(functools.partial(project_kernel, [spot for _, spot in pie...  19 us
    pallas_call x1, Pallas kernels, normed_columns(): pl.pallas_call(norm_kernel, out_shape=jax.ShapeDtypeStruct((width, blocks...  3.26 us
  transfers between devices with their start and end apart: 28, of which 15 were waited for; matrix products, arithmetic and copies ran while one was open for 2% of the time, Pallas kernels for 17%

profile of v7, /device:TPU:0, one launch (start us, length us, event | category | flops | bytes accessed | tf_op | source)
XLA Modules:
  0.0 128.2 jit_solution(55559330856157747)
XLA Ops:
  0.0 1.2 pad_maximum_fusion.1.rest_0_
  1.7 3.7 %collective-permute-start.4 = (bf16[384,768]{1,0:T(8,128)(2,1)S(1)}, bf16[384,768]{1,0:T(8,128)(2,1)S(1)}, u32[]{:S(2)}, u32[]{:S(2)}) collective-permute-start(bf16[384,768]{1,0:T(8,128)(2,1)S(1)} %pad_maximum_fusion.1.rest_0_), channel_id=1, source_target_pairs={{0,16},{2,18},{4,20},{6,22},{8,24},{10,26},{12,28},{14,30},{16,0},... | collective-permute-start | bytes 1769480 | tf_op jit(solution)/shard_map/u2/ppermute | solution.py:419
  5.4 1.5 %collective-permute-start.3 = (bf16[384,768]{1,0:T(8,128)(2,1)S(1)}, bf16[384,768]{1,0:T(8,128)(2,1)S(1)}, u32[]{:S(2)}, u32[]{:S(2)}) collective-permute-start(bf16[384,768]{1,0:T(8,128)(2,1)S(1)} %pad_maximum_fusion.1.rest_0_), channel_id=1, source_target_pairs={{0,4},{2,6},{4,0},{6,2},{8,12},{10,14},{12,8},{14,10},{16,20},{18,... | collective-permute-start | bytes 1769480 | tf_op jit(solution)/shard_map/y0/ppermute | solution.py:419
  6.9 1.5 %collective-permute-start.2 = (bf16[384,768]{1,0:T(8,128)(2,1)S(1)}, bf16[384,768]{1,0:T(8,128)(2,1)S(1)}, u32[]{:S(2)}, u32[]{:S(2)}) collective-permute-start(bf16[384,768]{1,0:T(8,128)(2,1)S(1)} %pad_maximum_fusion.1.rest_0_), channel_id=1, source_target_pairs={{0,1},{1,0},{2,3},{3,2},{4,5},{5,4},{6,7},{7,6},{8,9},{9,8},{10,11... | collective-permute-start | bytes 1769480 | tf_op jit(solution)/shard_map/x0/ppermute | solution.py:419
  8.8 1.6 %collective-permute-start = (bf16[384,768]{1,0:T(8,128)(2,1)S(1)}, bf16[384,768]{1,0:T(8,128)(2,1)}, u32[]{:S(2)}, u32[]{:S(2)}) collective-permute-start(bf16[384,768]{1,0:T(8,128)(2,1)S(1)} %pad_maximum_fusion.1.rest_0_), channel_id=1, source_target_pairs={{0,8},{2,10},{4,12},{6,14},{8,0},{10,2},{12,4},{14,6},{16,24},{18,... | collective-permute-start | bytes 1769480 | tf_op jit(solution)/shard_map/u1/ppermute | solution.py:419
  10.5 1.7 %copy-done = bf16[6,128,1536]{2,1,0:T(8,128)(2,1)S(1)} copy-done((bf16[6,128,1536]{2,1,0:T(8,128)(2,1)S(1)}, bf16[6,128,1536]{2,1,0:T(8,128)(2,1)}, u32[]{:S(2)}) %copy-start) | copy-done | bytes 2359320
  12.1 3.3 %norm.1.n_ref = bf16[1536,768]{1,0:T(8,128)(2,1)S(1)} custom-call(s32[12]{0:T(128)S(1)} %copy-done.1, bf16[6,128,1536]{2,1,0:T(8,128)(2,1)S(1)} %copy-done, f32[1,1536]{1,0:T(1,128)S(1)} %reshape.20.gain_ref, f32[1,384]{1,0:T(1,128)S(1)} %multiply_exponential_fusion.freq_ref), custom_call_target="tpu_custom_call" | custom-call | flops 47185920 | bytes 4718592 | tf_op jit(solution)/shard_map/norm/pallas_call | solution.py:138
  15.4 16.6 %collective-permute-done.4 = bf16[384,768]{1,0:T(8,128)(2,1)S(1)} collective-permute-done((bf16[384,768]{1,0:T(8,128)(2,1)S(1)}, bf16[384,768]{1,0:T(8,128)(2,1)S(1)}, u32[]{:S(2)}, u32[]{:S(2)}) %collective-permute-start.4) | collective-permute-done | bytes 589856 | tf_op jit(solution)/shard_map/u2/ppermute | solution.py:419
  32.0 2.5 %collective-permute-done.1.rest_3_ = bf16[384,768]{1,0:T(8,128)(2,1)S(1)} collective-permute-done((bf16[384,768]{1,0:T(8,128)(2,1)S(1)}, bf16[384,768]{1,0:T(8,128)(2,1)S(1)}, u32[]{:S(2)}, u32[]{:S(2)}) %collective-permute-start.1) | collective-permute-done | bytes 589856 | tf_op jit(solution)/shard_map/d0/ppermute | solution.py:419
  35.0 1.2 collective-permute-start.9
  36.2 2.2 %pad_maximum_fusion.rest_0_.rest_8_.rest_16_ = bf16[2,384,768]{2,1,0:T(8,128)(2,1)} fusion(bf16[1,384,768]{2,1,0:T(8,128)(2,1)S(1)} %bitcast.14, bf16[1,384,768]{2,1,0:T(8,128)(2,1)} %bitcast.10), kind=kLoop, calls=%fused_computation | loop fusion | flops 589824 | bytes 2359296 | tf_op jit(solution)/shard_map/stack | solution.py:459
  38.3 1.5 %collective-permute-start.8 = (bf16[2,384,768]{2,1,0:T(8,128)(2,1)}, bf16[2,384,768]{2,1,0:T(8,128)(2,1)}, u32[]{:S(2)}, u32[]{:S(2)}) collective-permute-start(bf16[2,384,768]{2,1,0:T(8,128)(2,1)} %pad_maximum_fusion.rest_0_.rest_8_.rest_16_), channel_id=1, source_target_pairs={{0,4},{2,6},{4,0},{6,2},{8,12},{10,14},{12,8},{14,10},{16,20},{18,... | collective-permute-start | bytes 3538952 | tf_op jit(solution)/shard_map/y12/ppermute | solution.py:419
  39.9 1.5 %collective-permute-start.7 = (bf16[384,768]{1,0:T(8,128)(2,1)S(1)}, bf16[384,768]{1,0:T(8,128)(2,1)S(1)}, u32[]{:S(2)}, u32[]{:S(2)}) collective-permute-start(bf16[384,768]{1,0:T(8,128)(2,1)S(1)} %collective-permute-done.4), channel_id=1, source_target_pairs={{0,1},{1,0},{2,3},{3,2},{4,5},{5,4},{6,7},{7,6},{8,9},{9,8},{10,11... | collective-permute-start | bytes 1769480 | tf_op jit(solution)/shard_map/x2/ppermute | solution.py:419
  41.9 7.0 %collective-permute-done.9.rest_24_ = bf16[384,768]{1,0:T(8,128)(2,1)S(1)} collective-permute-done((bf16[384,768]{1,0:T(8,128)(2,1)S(1)}, bf16[384,768]{1,0:T(8,128)(2,1)S(1)}, u32[]{:S(2)}, u32[]{:S(2)}) %collective-permute-start.9) | collective-permute-done | bytes 589856 | tf_op jit(solution)/shard_map/u3/ppermute | solution.py:419
  48.8 1.6 %collective-permute-start.10 = (bf16[384,768]{1,0:T(8,128)(2,1)S(1)}, bf16[384,768]{1,0:T(8,128)(2,1)}, u32[]{:S(2)}, u32[]{:S(2)}) collective-permute-start(bf16[384,768]{1,0:T(8,128)(2,1)S(1)} %collective-permute-done.1.rest_3_), channel_id=1, source_target_pairs={{0,8},{2,10},{4,12},{6,14},{8,0},{10,2},{12,4},{14,6},{16,24},{18,... | collective-permute-start | bytes 1769480 | tf_op jit(solution)/shard_map/d1/ppermute | solution.py:419
  50.4 3.1 %collective-permute-done.7.rest_1_.rest_17_ = bf16[384,768]{1,0:T(8,128)(2,1)S(1)} collective-permute-done((bf16[384,768]{1,0:T(8,128)(2,1)S(1)}, bf16[384,768]{1,0:T(8,128)(2,1)S(1)}, u32[]{:S(2)}, u32[]{:S(2)}) %collective-permute-start.7) | collective-permute-done | bytes 589856 | tf_op jit(solution)/shard_map/x2/ppermute | solution.py:419
  53.6 8.6 %collective-permute-done.10.rest_3_.rest_11_ = bf16[384,768]{1,0:T(8,128)(2,1)} collective-permute-done((bf16[384,768]{1,0:T(8,128)(2,1)S(1)}, bf16[384,768]{1,0:T(8,128)(2,1)}, u32[]{:S(2)}, u32[]{:S(2)}) %collective-permute-start.10) | collective-permute-done | bytes 589856 | tf_op jit(solution)/shard_map/d1/ppermute | solution.py:419
  62.2 3.1 %collective-permute-done.8.rest_2_.rest_10_.rest_18_ = bf16[2,384,768]{2,1,0:T(8,128)(2,1)} collective-permute-done((bf16[2,384,768]{2,1,0:T(8,128)(2,1)}, bf16[2,384,768]{2,1,0:T(8,128)(2,1)}, u32[]{:S(2)}, u32[]{:S(2)}) %collective-permute-start.8) | collective-permute-done | bytes 1179680 | tf_op jit(solution)/shard_map/y12/ppermute | solution.py:419
  65.8 1.5 %collective-permute-start.6 = (bf16[384,768]{1,0:T(8,128)(2,1)}, bf16[384,768]{1,0:T(8,128)(2,1)}, u32[]{:S(2)}, u32[]{:S(2)}) collective-permute-start(bf16[384,768]{1,0:T(8,128)(2,1)} %collective-permute-done), channel_id=1, source_target_pairs={{0,1},{1,0},{2,3},{3,2},{4,5},{5,4},{6,7},{7,6},{8,9},{9,8},{10,11... | collective-permute-start | bytes 1769480 | tf_op jit(solution)/shard_map/x1/ppermute | solution.py:419
  67.3 1.6 %collective-permute-start.13 = (bf16[384,768]{1,0:T(8,128)(2,1)S(1)}, bf16[384,768]{1,0:T(8,128)(2,1)}, u32[]{:S(2)}, u32[]{:S(2)}) collective-permute-start(bf16[384,768]{1,0:T(8,128)(2,1)S(1)} %collective-permute-done.7.rest_1_.rest_17_), channel_id=1, source_target_pairs={{0,4},{2,6},{4,0},{6,2},{8,12},{10,14},{12,8},{14,10},{16,20},{18,... | collective-permute-start | bytes 1769480 | tf_op jit(solution)/shard_map/d2/ppermute | solution.py:419
  69.0 6.3 %project.3 = (bf16[3,384,768]{2,1,0:T(8,128)(2,1)}, bf16[3,768,384]{2,1,0:T(8,128)(2,1)}) custom-call(s32[3]{0:T(128)S(1)} %pad_add_fusion.at_ref, s32[1]{0:T(128)} %bitcast.3.plane_ref, bf16[1536,768]{1,0:T(8,128)(2,1)S(1)} %norm.1.n_ref, bf16[384,768]{1,0:T(8,128)(2,1)} %copy-done.3, bf16[384,768]{1,0:T(8,128)(2,1)} %copy-done.6, ...), custom_call_target="tpu_custom_call" | custom-call | flops 2717908992 | bytes 5898240 | tf_op jit(solution)/shard_map/project/pallas_call | solution.py:225
  75.3 6.0 %collective-permute-done.6.rest_1_.rest_9_ = bf16[384,768]{1,0:T(8,128)(2,1)} collective-permute-done((bf16[384,768]{1,0:T(8,128)(2,1)}, bf16[384,768]{1,0:T(8,128)(2,1)}, u32[]{:S(2)}, u32[]{:S(2)}) %collective-permute-start.6) | collective-permute-done | bytes 589856 | tf_op jit(solution)/shard_map/x1/ppermute | solution.py:419
  81.3 1.9 %collective-permute-done.13.rest_3_.rest_19_ = bf16[384,768]{1,0:T(8,128)(2,1)} collective-permute-done((bf16[384,768]{1,0:T(8,128)(2,1)S(1)}, bf16[384,768]{1,0:T(8,128)(2,1)}, u32[]{:S(2)}, u32[]{:S(2)}) %collective-permute-start.13) | collective-permute-done | bytes 589856 | tf_op jit(solution)/shard_map/d2/ppermute | solution.py:419
  84.2 1.5 %collective-permute-start.19 = (bf16[384,768]{1,0:T(8,128)(2,1)S(1)}, bf16[384,768]{1,0:T(8,128)(2,1)}, u32[]{:S(2)}, u32[]{:S(2)}) collective-permute-start(bf16[384,768]{1,0:T(8,128)(2,1)S(1)} %collective-permute-done.9.rest_24_), channel_id=1, source_target_pairs={{0,4},{2,6},{4,0},{6,2},{8,12},{10,14},{12,8},{14,10},{16,20},{18,... | collective-permute-start | bytes 1769480 | tf_op jit(solution)/shard_map/y3/ppermute | solution.py:419
  86.3 1.0 collective-permute-done.22.rest_7_.rest_23_
  87.7 6.3 %project.4 = (bf16[3,384,768]{2,1,0:T(8,128)(2,1)}, bf16[3,768,384]{2,1,0:T(8,128)(2,1)}) custom-call(s32[3]{0:T(128)S(1)} %pad_add_fusion.at_ref, s32[1]{0:T(128)} %bitcast.5.plane_ref, bf16[1536,768]{1,0:T(8,128)(2,1)S(1)} %norm.1.n_ref, bf16[2,384,768]{2,1,0:T(8,128)(2,1)} %pad_maximum_fusion.rest_0_.rest_8_.rest_16_, bf16[384,768]{1,0:T(8,128)(2,1)} %copy-done.8, ...), custom_call_target="tpu_custom_call" | custom-call | flops 2717908992 | bytes 5898240 | tf_op jit(solution)/shard_map/project/pallas_call | solution.py:225
  94.1 6.3 %project.5 = (bf16[3,384,768]{2,1,0:T(8,128)(2,1)}, bf16[3,768,384]{2,1,0:T(8,128)(2,1)}) custom-call(s32[3]{0:T(128)S(1)} %pad_add_fusion.at_ref, s32[1]{0:T(128)} %bitcast.4.plane_ref, bf16[1536,768]{1,0:T(8,128)(2,1)S(1)} %norm.1.n_ref, bf16[2,384,768]{2,1,0:T(8,128)(2,1)} %pad_maximum_fusion.rest_0_.rest_8_.rest_16_, ...), custom_call_target="tpu_custom_call" | custom-call | flops 2717908992 | bytes 5898240 | tf_op jit(solution)/shard_map/project/pallas_call | solution.py:225
  101.0 1.9 %collective-permute-done.20.rest_27_ = bf16[384,768]{1,0:T(8,128)(2,1)} collective-permute-done((bf16[384,768]{1,0:T(8,128)(2,1)}, bf16[384,768]{1,0:T(8,128)(2,1)}, u32[]{:S(2)}, u32[]{:S(2)}) %collective-permute-start.20) | collective-permute-done | bytes 589856 | tf_op jit(solution)/shard_map/d3/ppermute | solution.py:419
  104.2 1.1 collective-permute-done.25.rest_29_
  105.3 0.8 collective-permute-done.26.rest_30_
  106.1 0.8 collective-permute-done.27.rest_31_
  107.0 21.1 %finish.1 = bf16[768,1536]{1,0:T(8,128)(2,1)} custom-call(s32[3]{0:T(128)S(1)} %pad_add_fusion.at_ref, s32[4]{0:T(128)S(1)} %pad_add_fusion.1.planes_ref, s32[12]{0:T(128)S(1)} %copy-done.2, s32[1]{0:T(128)S(6)} %copy.8.live_ref, bf16[1536,768]{1,0:T(8,128)(2,1)S(1)} %norm.1.n_ref, bf16[768,1536]{1,0:T(8,128)(2,1)} %bitcast.13, ...), custom_call_target="tpu_custom_call" | custom-call | flops 10871635968 | bytes 9437184 | tf_op jit(solution)/shard_map/finish/pallas_call | solution.py:376
  (61 shorter events, 5.8 us)
Async XLA Ops:
  1.2 14.3 %copy-start.3 = (bf16[384,768]{1,0:T(8,128)(2,1)}, bf16[384,768]{1,0:T(8,128)(2,1)S(1)}, u32[]{:S(2)}) copy-start(bf16[384,768]{1,0:T(8,128)(2,1)S(1)} %pad_maximum_fusion.1.rest_0_) | copy-start | bytes 1769476
  1.2 7.7 %collective-permute-start.5 = (bf16[384,768]{1,0:T(8,128)(2,1)S(1)}, bf16[384,768]{1,0:T(8,128)(2,1)S(1)}, u32[]{:S(2)}, u32[]{:S(2)}) collective-permute-start(bf16[384,768]{1,0:T(8,128)(2,1)S(1)} %pad_maximum_fusion.1.rest_0_), channel_id=1, source_target_pairs={{0,2},{2,0},{4,6},{6,4},{8,10},{10,8},{12,14},{14,12},{16,18},{18,... | collective-permute-start | bytes 1769480 | tf_op jit(solution)/shard_map/core_u0/ppermute | solution.py:419
  1.7 30.3 %collective-permute-start.4 = (bf16[384,768]{1,0:T(8,128)(2,1)S(1)}, bf16[384,768]{1,0:T(8,128)(2,1)S(1)}, u32[]{:S(2)}, u32[]{:S(2)}) collective-permute-start(bf16[384,768]{1,0:T(8,128)(2,1)S(1)} %pad_maximum_fusion.1.rest_0_), channel_id=1, source_target_pairs={{0,16},{2,18},{4,20},{6,22},{8,24},{10,26},{12,28},{14,30},{16,0},... | collective-permute-start | bytes 1769480 | tf_op jit(solution)/shard_map/u2/ppermute | solution.py:419
  5.4 26.7 %collective-permute-start.3 = (bf16[384,768]{1,0:T(8,128)(2,1)S(1)}, bf16[384,768]{1,0:T(8,128)(2,1)S(1)}, u32[]{:S(2)}, u32[]{:S(2)}) collective-permute-start(bf16[384,768]{1,0:T(8,128)(2,1)S(1)} %pad_maximum_fusion.1.rest_0_), channel_id=1, source_target_pairs={{0,4},{2,6},{4,0},{6,2},{8,12},{10,14},{12,8},{14,10},{16,20},{18,... | collective-permute-start | bytes 1769480 | tf_op jit(solution)/shard_map/y0/ppermute | solution.py:419
  6.9 25.2 %collective-permute-start.2 = (bf16[384,768]{1,0:T(8,128)(2,1)S(1)}, bf16[384,768]{1,0:T(8,128)(2,1)S(1)}, u32[]{:S(2)}, u32[]{:S(2)}) collective-permute-start(bf16[384,768]{1,0:T(8,128)(2,1)S(1)} %pad_maximum_fusion.1.rest_0_), channel_id=1, source_target_pairs={{0,1},{1,0},{2,3},{3,2},{4,5},{5,4},{6,7},{7,6},{8,9},{9,8},{10,11... | collective-permute-start | bytes 1769480 | tf_op jit(solution)/shard_map/x0/ppermute | solution.py:419
  8.4 26.2 %collective-permute-start.1 = (bf16[384,768]{1,0:T(8,128)(2,1)S(1)}, bf16[384,768]{1,0:T(8,128)(2,1)S(1)}, u32[]{:S(2)}, u32[]{:S(2)}) collective-permute-start(bf16[384,768]{1,0:T(8,128)(2,1)S(1)} %pad_maximum_fusion.1.rest_0_), channel_id=1, source_target_pairs={{0,5},{1,4},{2,7},{3,6},{4,1},{5,0},{6,3},{7,2},{8,13},{9,12},{10,... | collective-permute-start | bytes 1769480 | tf_op jit(solution)/shard_map/d0/ppermute | solution.py:419
  8.8 26.1 %collective-permute-start = (bf16[384,768]{1,0:T(8,128)(2,1)S(1)}, bf16[384,768]{1,0:T(8,128)(2,1)}, u32[]{:S(2)}, u32[]{:S(2)}) collective-permute-start(bf16[384,768]{1,0:T(8,128)(2,1)S(1)} %pad_maximum_fusion.1.rest_0_), channel_id=1, source_target_pairs={{0,8},{2,10},{4,12},{6,14},{8,0},{10,2},{12,4},{14,6},{16,24},{18,... | collective-permute-start | bytes 1769480 | tf_op jit(solution)/shard_map/u1/ppermute | solution.py:419
  34.6 19.0 %copy-start.7 = (bf16[384,768]{1,0:T(8,128)(2,1)}, bf16[384,768]{1,0:T(8,128)(2,1)S(1)}, u32[]{:S(2)}) copy-start(bf16[384,768]{1,0:T(8,128)(2,1)S(1)} %collective-permute-done.1.rest_3_) | copy-start | bytes 1769476
  35.0 13.9 %collective-permute-start.9 = (bf16[384,768]{1,0:T(8,128)(2,1)S(1)}, bf16[384,768]{1,0:T(8,128)(2,1)S(1)}, u32[]{:S(2)}, u32[]{:S(2)}) collective-permute-start(bf16[384,768]{1,0:T(8,128)(2,1)S(1)} %collective-permute-done.4), channel_id=1, source_target_pairs={{0,8},{2,10},{4,12},{6,14},{8,0},{10,2},{12,4},{14,6},{16,24},{18,... | collective-permute-start | bytes 1769480 | tf_op jit(solution)/shard_map/u3/ppermute | solution.py:419
  38.3 26.9 %collective-permute-start.8 = (bf16[2,384,768]{2,1,0:T(8,128)(2,1)}, bf16[2,384,768]{2,1,0:T(8,128)(2,1)}, u32[]{:S(2)}, u32[]{:S(2)}) collective-permute-start(bf16[2,384,768]{2,1,0:T(8,128)(2,1)} %pad_maximum_fusion.rest_0_.rest_8_.rest_16_), channel_id=1, source_target_pairs={{0,4},{2,6},{4,0},{6,2},{8,12},{10,14},{12,8},{14,10},{16,20},{18,... | collective-permute-start | bytes 3538952 | tf_op jit(solution)/shard_map/y12/ppermute | solution.py:419
  39.9 13.7 %collective-permute-start.7 = (bf16[384,768]{1,0:T(8,128)(2,1)S(1)}, bf16[384,768]{1,0:T(8,128)(2,1)S(1)}, u32[]{:S(2)}, u32[]{:S(2)}) collective-permute-start(bf16[384,768]{1,0:T(8,128)(2,1)S(1)} %collective-permute-done.4), channel_id=1, source_target_pairs={{0,1},{1,0},{2,3},{3,2},{4,5},{5,4},{6,7},{7,6},{8,9},{9,8},{10,11... | collective-permute-start | bytes 1769480 | tf_op jit(solution)/shard_map/x2/ppermute | solution.py:419
  41.4 12.2 %collective-permute-start.11 = (bf16[384,768]{1,0:T(8,128)(2,1)S(1)}, bf16[384,768]{1,0:T(8,128)(2,1)S(1)}, u32[]{:S(2)}, u32[]{:S(2)}) collective-permute-start(bf16[384,768]{1,0:T(8,128)(2,1)S(1)} %collective-permute-done.2.rest_1_), channel_id=1, source_target_pairs={{0,2},{2,0},{4,6},{6,4},{8,10},{10,8},{12,14},{14,12},{16,18},{18,... | collective-permute-start | bytes 1769480 | tf_op jit(solution)/shard_map/core_x0/ppermute | solution.py:419
  41.4 12.2 %collective-permute-start.12 = (bf16[384,768]{1,0:T(8,128)(2,1)S(1)}, bf16[384,768]{1,0:T(8,128)(2,1)S(1)}, u32[]{:S(2)}, u32[]{:S(2)}) collective-permute-start(bf16[384,768]{1,0:T(8,128)(2,1)S(1)} %collective-permute-done.3.rest_2_), channel_id=1, source_target_pairs={{0,2},{2,0},{4,6},{6,4},{8,10},{10,8},{12,14},{14,12},{16,18},{18,... | collective-permute-start | bytes 1769480 | tf_op jit(solution)/shard_map/core_y0/ppermute | solution.py:419
  48.8 13.4 %collective-permute-start.10 = (bf16[384,768]{1,0:T(8,128)(2,1)S(1)}, bf16[384,768]{1,0:T(8,128)(2,1)}, u32[]{:S(2)}, u32[]{:S(2)}) collective-permute-start(bf16[384,768]{1,0:T(8,128)(2,1)S(1)} %collective-permute-done.1.rest_3_), channel_id=1, source_target_pairs={{0,8},{2,10},{4,12},{6,14},{8,0},{10,2},{12,4},{14,6},{16,24},{18,... | collective-permute-start | bytes 1769480 | tf_op jit(solution)/shard_map/d1/ppermute | solution.py:419
  53.6 21.7 %copy-start.8 = (bf16[384,768]{1,0:T(8,128)(2,1)}, bf16[384,768]{1,0:T(8,128)(2,1)S(1)}, u32[]{:S(2)}) copy-start(bf16[384,768]{1,0:T(8,128)(2,1)S(1)} %collective-permute-done.7.rest_1_.rest_17_) | copy-start | bytes 1769476
  53.6 13.7 %collective-permute-start.17 = (bf16[384,768]{1,0:T(8,128)(2,1)S(1)}, bf16[384,768]{1,0:T(8,128)(2,1)S(1)}, u32[]{:S(2)}, u32[]{:S(2)}) collective-permute-start(bf16[384,768]{1,0:T(8,128)(2,1)S(1)} %collective-permute-done.1.rest_3_), channel_id=1, source_target_pairs={{0,2},{2,0},{4,6},{6,4},{8,10},{10,8},{12,14},{14,12},{16,18},{18,... | collective-permute-start | bytes 1769480 | tf_op jit(solution)/shard_map/core_d0/ppermute | solution.py:419
  53.6 15.3 %copy-start.10 = (bf16[384,768]{1,0:T(8,128)(2,1)}, bf16[384,768]{1,0:T(8,128)(2,1)S(1)}, u32[]{:S(2)}) copy-start(bf16[384,768]{1,0:T(8,128)(2,1)S(1)} %collective-permute-done.12.rest_6_) | copy-start | bytes 1769476
  65.3 17.9 %collective-permute-start.15 = (bf16[2,384,768]{2,1,0:T(8,128)(2,1)}, bf16[2,384,768]{2,1,0:T(8,128)(2,1)}, u32[]{:S(2)}, u32[]{:S(2)}) collective-permute-start(bf16[2,384,768]{2,1,0:T(8,128)(2,1)} %collective-permute-done.8.rest_2_.rest_10_.rest_18_), channel_id=1, source_target_pairs={{0,2},{2,0},{4,6},{6,4},{8,10},{10,8},{12,14},{14,12},{16,18},{18,... | collective-permute-start | bytes 3538952 | tf_op jit(solution)/shard_map/core_y12/ppermute | solution.py:419
  65.3 17.9 %collective-permute-start.16 = (bf16[2,384,768]{2,1,0:T(8,128)(2,1)}, bf16[2,384,768]{2,1,0:T(8,128)(2,1)}, u32[]{:S(2)}, u32[]{:S(2)}) collective-permute-start(bf16[2,384,768]{2,1,0:T(8,128)(2,1)} %pad_maximum_fusion.rest_0_.rest_8_.rest_16_), channel_id=1, source_target_pairs={{0,2},{2,0},{4,6},{6,4},{8,10},{10,8},{12,14},{14,12},{16,18},{18,... | collective-permute-start | bytes 3538952 | tf_op jit(solution)/shard_map/core_u12/ppermute | solution.py:419
  65.8 15.6 %collective-permute-start.6 = (bf16[384,768]{1,0:T(8,128)(2,1)}, bf16[384,768]{1,0:T(8,128)(2,1)}, u32[]{:S(2)}, u32[]{:S(2)}) collective-permute-start(bf16[384,768]{1,0:T(8,128)(2,1)} %collective-permute-done), channel_id=1, source_target_pairs={{0,1},{1,0},{2,3},{3,2},{4,5},{5,4},{6,7},{7,6},{8,9},{9,8},{10,11... | collective-permute-start | bytes 1769480 | tf_op jit(solution)/shard_map/x1/ppermute | solution.py:419
  67.3 14.1 %collective-permute-start.14 = (bf16[384,768]{1,0:T(8,128)(2,1)S(1)}, bf16[384,768]{1,0:T(8,128)(2,1)}, u32[]{:S(2)}, u32[]{:S(2)}) collective-permute-start(bf16[384,768]{1,0:T(8,128)(2,1)S(1)} %collective-permute-done.7.rest_1_.rest_17_), channel_id=1, source_target_pairs={{0,2},{2,0},{4,6},{6,4},{8,10},{10,8},{12,14},{14,12},{16,18},{18,... | collective-permute-start | bytes 1769480 | tf_op jit(solution)/shard_map/core_x2/ppermute | solution.py:419
  67.3 15.9 %collective-permute-start.13 = (bf16[384,768]{1,0:T(8,128)(2,1)S(1)}, bf16[384,768]{1,0:T(8,128)(2,1)}, u32[]{:S(2)}, u32[]{:S(2)}) collective-permute-start(bf16[384,768]{1,0:T(8,128)(2,1)S(1)} %collective-permute-done.7.rest_1_.rest_17_), channel_id=1, source_target_pairs={{0,4},{2,6},{4,0},{6,2},{8,12},{10,14},{12,8},{14,10},{16,20},{18,... | collective-permute-start | bytes 1769480 | tf_op jit(solution)/shard_map/d2/ppermute | solution.py:419
  83.2 2.5 %collective-permute-start.23 = (bf16[384,768]{1,0:T(8,128)(2,1)}, bf16[384,768]{1,0:T(8,128)(2,1)}, u32[]{:S(2)}, u32[]{:S(2)}) collective-permute-start(bf16[384,768]{1,0:T(8,128)(2,1)} %collective-permute-done.6.rest_1_.rest_9_), channel_id=1, source_target_pairs={{0,2},{2,0},{4,6},{6,4},{8,10},{10,8},{12,14},{14,12},{16,18},{18,... | collective-permute-start | bytes 1769480 | tf_op jit(solution)/shard_map/core_x1/ppermute | solution.py:419
  83.2 4.0 %collective-permute-start.22 = (bf16[384,768]{1,0:T(8,128)(2,1)}, bf16[384,768]{1,0:T(8,128)(2,1)}, u32[]{:S(2)}, u32[]{:S(2)}) collective-permute-start(bf16[384,768]{1,0:T(8,128)(2,1)} %collective-permute-done.13.rest_3_.rest_19_), channel_id=1, source_target_pairs={{0,2},{2,0},{4,6},{6,4},{8,10},{10,8},{12,14},{14,12},{16,18},{18,... | collective-permute-start | bytes 1769480 | tf_op jit(solution)/shard_map/core_d2/ppermute | solution.py:419
  83.7 10.4 %collective-permute-start.24 = (bf16[384,768]{1,0:T(8,128)(2,1)}, bf16[384,768]{1,0:T(8,128)(2,1)}, u32[]{:S(2)}, u32[]{:S(2)}) collective-permute-start(bf16[384,768]{1,0:T(8,128)(2,1)} %collective-permute-done.10.rest_3_.rest_11_), channel_id=1, source_target_pairs={{0,2},{2,0},{4,6},{6,4},{8,10},{10,8},{12,14},{14,12},{16,18},{18,... | collective-permute-start | bytes 1769480 | tf_op jit(solution)/shard_map/core_d1/ppermute | solution.py:419
  83.8 16.6 %collective-permute-start.21 = (bf16[384,768]{1,0:T(8,128)(2,1)S(1)}, bf16[384,768]{1,0:T(8,128)(2,1)S(1)}, u32[]{:S(2)}, u32[]{:S(2)}) collective-permute-start(bf16[384,768]{1,0:T(8,128)(2,1)S(1)} %collective-permute-done.9.rest_24_), channel_id=1, source_target_pairs={{0,2},{2,0},{4,6},{6,4},{8,10},{10,8},{12,14},{14,12},{16,18},{18,... | collective-permute-start | bytes 1769480 | tf_op jit(solution)/shard_map/core_u3/ppermute | solution.py:419
  84.2 16.2 %collective-permute-start.19 = (bf16[384,768]{1,0:T(8,128)(2,1)S(1)}, bf16[384,768]{1,0:T(8,128)(2,1)}, u32[]{:S(2)}, u32[]{:S(2)}) collective-permute-start(bf16[384,768]{1,0:T(8,128)(2,1)S(1)} %collective-permute-done.9.rest_24_), channel_id=1, source_target_pairs={{0,4},{2,6},{4,0},{6,2},{8,12},{10,14},{12,8},{14,10},{16,20},{18,... | collective-permute-start | bytes 1769480 | tf_op jit(solution)/shard_map/y3/ppermute | solution.py:419
  85.7 15.3 %collective-permute-start.18 = (bf16[384,768]{1,0:T(8,128)(2,1)S(1)}, bf16[384,768]{1,0:T(8,128)(2,1)}, u32[]{:S(2)}, u32[]{:S(2)}) collective-permute-start(bf16[384,768]{1,0:T(8,128)(2,1)S(1)} %collective-permute-done.9.rest_24_), channel_id=1, source_target_pairs={{0,1},{1,0},{2,3},{3,2},{4,5},{5,4},{6,7},{7,6},{8,9},{9,8},{10,11... | collective-permute-start | bytes 1769480 | tf_op jit(solution)/shard_map/x3/ppermute | solution.py:419
  87.2 15.7 %collective-permute-start.20 = (bf16[384,768]{1,0:T(8,128)(2,1)}, bf16[384,768]{1,0:T(8,128)(2,1)}, u32[]{:S(2)}, u32[]{:S(2)}) collective-permute-start(bf16[384,768]{1,0:T(8,128)(2,1)} %collective-permute-done.13.rest_3_.rest_19_), channel_id=1, source_target_pairs={{0,8},{2,10},{4,12},{6,14},{8,0},{10,2},{12,4},{14,6},{16,24},{18,... | collective-permute-start | bytes 1769480 | tf_op jit(solution)/shard_map/d3/ppermute | solution.py:419
  102.9 2.3 %collective-permute-start.25 = (bf16[384,768]{1,0:T(8,128)(2,1)}, bf16[384,768]{1,0:T(8,128)(2,1)}, u32[]{:S(2)}, u32[]{:S(2)}) collective-permute-start(bf16[384,768]{1,0:T(8,128)(2,1)} %collective-permute-done.18.rest_25_), channel_id=1, source_target_pairs={{0,2},{2,0},{4,6},{6,4},{8,10},{10,8},{12,14},{14,12},{16,18},{18,... | collective-permute-start | bytes 1769480 | tf_op jit(solution)/shard_map/core_x3/ppermute | solution.py:419
  102.9 3.2 %collective-permute-start.26 = (bf16[384,768]{1,0:T(8,128)(2,1)}, bf16[384,768]{1,0:T(8,128)(2,1)}, u32[]{:S(2)}, u32[]{:S(2)}) collective-permute-start(bf16[384,768]{1,0:T(8,128)(2,1)} %collective-permute-done.19.rest_26_), channel_id=1, source_target_pairs={{0,2},{2,0},{4,6},{6,4},{8,10},{10,8},{12,14},{14,12},{16,18},{18,... | collective-permute-start | bytes 1769480 | tf_op jit(solution)/shard_map/core_y3/ppermute | solution.py:419
  103.4 3.5 %collective-permute-start.27 = (bf16[384,768]{1,0:T(8,128)(2,1)}, bf16[384,768]{1,0:T(8,128)(2,1)}, u32[]{:S(2)}, u32[]{:S(2)}) collective-permute-start(bf16[384,768]{1,0:T(8,128)(2,1)} %collective-permute-done.20.rest_27_), channel_id=1, source_target_pairs={{0,2},{2,0},{4,6},{6,4},{8,10},{10,8},{12,14},{14,12},{16,18},{18,... | collective-permute-start | bytes 1769480 | tf_op jit(solution)/shard_map/core_d3/ppermute | solution.py:419
  (9 other events, 71.0 us)

commit v8 on v7

--- a/solution.py
+++ b/solution.py
@@ -312,41 +312,49 @@
     blank = jnp.zeros((HEAD_DIM, 128), BF)
     pairs = chunk // 128
 
-    @pl.loop(0, parts)
-    def _(part):
-        for kind in range(3):
-            which = parts * kind + part
-
-            @pl.when(planes_ref[which // count] != last)
-            def _():
-                pltpu.make_async_copy(p0.at[0], q_ref.at[0], part_sems.at[which]).wait()
-
-        @pl.loop(0, pairs)
-        def _(i):
-            at = pl.ds(pl.multiple_of(i * 128, 128), 128)
-            out_at = pl.ds(pl.multiple_of(part * chunk + i * 128, 128), 128)
-            for b in range(blocks):
-                tok = pl.ds(b * 128, 128)
-                q = q_ref[part, at, tok]
-                k = k_ref[part, tok, at]
-                q0 = jnp.concatenate([q[:HEAD_DIM], blank], axis=0)
-                q1 = jnp.concatenate([blank, q[HEAD_DIM:]], axis=0)
-                scores = jnp.dot(k, jnp.concatenate([q0, q1], axis=1), preferred_element_type=F32)
-                e_ref[b] = (jnp.exp(scores) * mask_ref[b]).astype(BF)
-            for b in range(blocks):
-                tok = pl.ds(b * 128, 128)
-                v = v_ref[part, at, tok]
-                got = jnp.dot(
-                    jnp.concatenate([v, ones], axis=0), e_ref[b], preferred_element_type=F32
-                )
-                token = lax.broadcasted_iota(jnp.int32, (1, 256), 1) % 128
-                first = (token < WIN_TOK) & (token < lens_ref[2 * b])
-                second = (token >= WIN_TOK) & (token - WIN_TOK < lens_ref[2 * b + 1])
-                keep = (first | second) & (b < live_ref[0])
-                share = jnp.where(keep, 1.0 / got[128:129, :], 0.0)
-                o0 = got[:HEAD_DIM, :128] * share[:, :128]
-                o1 = got[HEAD_DIM:128, 128:] * share[:, 128:]
-                att_ref[tok, out_at] = jnp.concatenate([o0, o1], axis=0).astype(BF).T
+    for which in range(3 * parts):
+
+        @pl.when(planes_ref[which // count] != last)
+        def _():
+            pltpu.make_async_copy(p0.at[0], q_ref.at[0], part_sems.at[which]).wait()
+
+    def weigh(pair):
+        part = pair // pairs
+        at = pl.ds(pl.multiple_of(pair % pairs * 128, 128), 128)
+        for b in range(blocks):
+            tok = pl.ds(b * 128, 128)
+            q = q_ref[part, at, tok]
+            k = k_ref[part, tok, at]
+            q0 = jnp.concatenate([q[:HEAD_DIM], blank], axis=0)
+            q1 = jnp.concatenate([blank, q[HEAD_DIM:]], axis=0)
+            scores = jnp.dot(k, jnp.concatenate([q0, q1], axis=1), preferred_element_type=F32)
+            e_ref[pair % 2, b] = (jnp.exp(scores) * mask_ref[b]).astype(BF)
+
+    def gather(pair):
+        part = pair // pairs
+        at = pl.ds(pl.multiple_of(pair % pairs * 128, 128), 128)
+        out_at = pl.ds(pl.multiple_of(pair * 128, 128), 128)
+        for b in range(blocks):
+            tok = pl.ds(b * 128, 128)
+            v = v_ref[part, at, tok]
+            got = jnp.dot(
+                jnp.concatenate([v, ones], axis=0), e_ref[pair % 2, b], preferred_element_type=F32
+            )
+            token = lax.broadcasted_iota(jnp.int32, (1, 256), 1) % 128
+            first = (token < WIN_TOK) & (token < lens_ref[2 * b])
+            second = (token >= WIN_TOK) & (token - WIN_TOK < lens_ref[2 * b + 1])
+            keep = (first | second) & (b < live_ref[0])
+            share = jnp.where(keep, 1.0 / got[128:129, :], 0.0)
+            o0 = got[:HEAD_DIM, :128] * share[:, :128]
+            o1 = got[HEAD_DIM:128, 128:] * share[:, 128:]
+            att_ref[tok, out_at] = jnp.concatenate([o0, o1], axis=0).astype(BF).T
+
+    weigh(0)
+
+    @pl.loop(0, parts * pairs)
+    def _(pair):
+        gather(pair)
+        weigh(jnp.minimum(pair + 1, parts * pairs - 1))
 
     outs = []
     for s in range(slots):
@@ -384,7 +392,7 @@
             pltpu.VMEM((4, tokens, chunk), BF),
             pltpu.VMEM((4, chunk, tokens), BF),
             pltpu.VMEM((tokens // 128, 128, 256), F32),
-            pltpu.VMEM((tokens // 128, 128, 256), BF),
+            pltpu.VMEM((2, tokens // 128, 128, 256), BF),
             pltpu.VMEM((tokens, width), BF),
             pltpu.VMEM((slots, width // slots, width), BF),
             pltpu.VMEM((slots, tokens, width // slots), BF),

time: 128 us -> 127 us (level)
  Pallas kernels: 43.3 us -> 41.9 us
    pallas_call x1, Pallas kernels: 21.1 us -> 19.7 us  [finish(): pl.pallas_call(functools.partial(finish_kernel, [spot for _, spot in piec...]
  transfers between devices with their start and end apart: 28 -> 28, of which waited for: 15 -> 15; matrix products, arithmetic and copies ran while one was open for 2% -> 2% of each run, Pallas kernels for 17% -> 18%
where the time goes in v8:
time: 127 us
  waiting for transfers between devices  55.5 us (44%)
  Pallas kernels  41.9 us (33%)
  starting transfers between devices  23.2 us (18%)
  other arithmetic  3.5 us (3%)
  local copies, waits for them, and re-layouts  1.72 us (1%)
    ppermute x28, waiting for transfers between devices, move(): return lax.ppermute(value, axis, pairs)  55.5 us
    ppermute x28, starting transfers between devices, move(): return lax.ppermute(value, axis, pairs)  23.2 us
    pallas_call x1, Pallas kernels, finish(): pl.pallas_call(functools.partial(finish_kernel, [spot for _, spot in piec...  19.7 us
    pallas_call x3, Pallas kernels, project(): pl.pallas_call(functools.partial(project_kernel, [spot for _, spot in pie...  19 us
    pallas_call x1, Pallas kernels, normed_columns(): pl.pallas_call(norm_kernel, out_shape=jax.ShapeDtypeStruct((width, blocks...  3.26 us
  transfers between devices with their start and end apart: 28, of which 15 were waited for; matrix products, arithmetic and copies ran while one was open for 2% of the time, Pallas kernels for 18%

profile of v8, /device:TPU:0, one launch (start us, length us, event | category | flops | bytes accessed | tf_op | source)
XLA Modules:
  0.0 126.8 jit_solution(8674068655972442379)
XLA Ops:
  0.0 1.2 pad_maximum_fusion.1.rest_0_
  1.7 3.7 %collective-permute-start.4 = (bf16[384,768]{1,0:T(8,128)(2,1)S(1)}, bf16[384,768]{1,0:T(8,128)(2,1)S(1)}, u32[]{:S(2)}, u32[]{:S(2)}) collective-permute-start(bf16[384,768]{1,0:T(8,128)(2,1)S(1)} %pad_maximum_fusion.1.rest_0_), channel_id=1, source_target_pairs={{0,16},{2,18},{4,20},{6,22},{8,24},{10,26},{12,28},{14,30},{16,0},... | collective-permute-start | bytes 1769480 | tf_op jit(solution)/shard_map/u2/ppermute | solution.py:427
  5.4 1.5 %collective-permute-start.3 = (bf16[384,768]{1,0:T(8,128)(2,1)S(1)}, bf16[384,768]{1,0:T(8,128)(2,1)S(1)}, u32[]{:S(2)}, u32[]{:S(2)}) collective-permute-start(bf16[384,768]{1,0:T(8,128)(2,1)S(1)} %pad_maximum_fusion.1.rest_0_), channel_id=1, source_target_pairs={{0,4},{2,6},{4,0},{6,2},{8,12},{10,14},{12,8},{14,10},{16,20},{18,... | collective-permute-start | bytes 1769480 | tf_op jit(solution)/shard_map/y0/ppermute | solution.py:427
  6.9 1.5 %collective-permute-start.2 = (bf16[384,768]{1,0:T(8,128)(2,1)S(1)}, bf16[384,768]{1,0:T(8,128)(2,1)S(1)}, u32[]{:S(2)}, u32[]{:S(2)}) collective-permute-start(bf16[384,768]{1,0:T(8,128)(2,1)S(1)} %pad_maximum_fusion.1.rest_0_), channel_id=1, source_target_pairs={{0,1},{1,0},{2,3},{3,2},{4,5},{5,4},{6,7},{7,6},{8,9},{9,8},{10,11... | collective-permute-start | bytes 1769480 | tf_op jit(solution)/shard_map/x0/ppermute | solution.py:427
  8.8 1.6 %collective-permute-start = (bf16[384,768]{1,0:T(8,128)(2,1)S(1)}, bf16[384,768]{1,0:T(8,128)(2,1)}, u32[]{:S(2)}, u32[]{:S(2)}) collective-permute-start(bf16[384,768]{1,0:T(8,128)(2,1)S(1)} %pad_maximum_fusion.1.rest_0_), channel_id=1, source_target_pairs={{0,8},{2,10},{4,12},{6,14},{8,0},{10,2},{12,4},{14,6},{16,24},{18,... | collective-permute-start | bytes 1769480 | tf_op jit(solution)/shard_map/u1/ppermute | solution.py:427
  10.5 1.7 %copy-done = bf16[6,128,1536]{2,1,0:T(8,128)(2,1)S(1)} copy-done((bf16[6,128,1536]{2,1,0:T(8,128)(2,1)S(1)}, bf16[6,128,1536]{2,1,0:T(8,128)(2,1)}, u32[]{:S(2)}) %copy-start) | copy-done | bytes 2359320
  12.1 3.3 %norm.1.n_ref = bf16[1536,768]{1,0:T(8,128)(2,1)S(1)} custom-call(s32[12]{0:T(128)S(1)} %copy-done.1, bf16[6,128,1536]{2,1,0:T(8,128)(2,1)S(1)} %copy-done, f32[1,1536]{1,0:T(1,128)S(1)} %reshape.20.gain_ref, f32[1,384]{1,0:T(1,128)S(1)} %multiply_exponential_fusion.freq_ref), custom_call_target="tpu_custom_call" | custom-call | flops 47185920 | bytes 4718592 | tf_op jit(solution)/shard_map/norm/pallas_call | solution.py:138
  15.4 16.6 %collective-permute-done.4 = bf16[384,768]{1,0:T(8,128)(2,1)S(1)} collective-permute-done((bf16[384,768]{1,0:T(8,128)(2,1)S(1)}, bf16[384,768]{1,0:T(8,128)(2,1)S(1)}, u32[]{:S(2)}, u32[]{:S(2)}) %collective-permute-start.4) | collective-permute-done | bytes 589856 | tf_op jit(solution)/shard_map/u2/ppermute | solution.py:427
  32.0 2.5 %collective-permute-done.1.rest_3_ = bf16[384,768]{1,0:T(8,128)(2,1)S(1)} collective-permute-done((bf16[384,768]{1,0:T(8,128)(2,1)S(1)}, bf16[384,768]{1,0:T(8,128)(2,1)S(1)}, u32[]{:S(2)}, u32[]{:S(2)}) %collective-permute-start.1) | collective-permute-done | bytes 589856 | tf_op jit(solution)/shard_map/d0/ppermute | solution.py:427
  35.0 1.2 collective-permute-start.9
  36.2 2.2 %pad_maximum_fusion.rest_0_.rest_8_.rest_16_ = bf16[2,384,768]{2,1,0:T(8,128)(2,1)} fusion(bf16[1,384,768]{2,1,0:T(8,128)(2,1)S(1)} %bitcast.14, bf16[1,384,768]{2,1,0:T(8,128)(2,1)} %bitcast.10), kind=kLoop, calls=%fused_computation | loop fusion | flops 589824 | bytes 2359296 | tf_op jit(solution)/shard_map/stack | solution.py:467
  38.3 1.5 %collective-permute-start.8 = (bf16[2,384,768]{2,1,0:T(8,128)(2,1)}, bf16[2,384,768]{2,1,0:T(8,128)(2,1)}, u32[]{:S(2)}, u32[]{:S(2)}) collective-permute-start(bf16[2,384,768]{2,1,0:T(8,128)(2,1)} %pad_maximum_fusion.rest_0_.rest_8_.rest_16_), channel_id=1, source_target_pairs={{0,4},{2,6},{4,0},{6,2},{8,12},{10,14},{12,8},{14,10},{16,20},{18,... | collective-permute-start | bytes 3538952 | tf_op jit(solution)/shard_map/y12/ppermute | solution.py:427
  39.9 1.5 %collective-permute-start.7 = (bf16[384,768]{1,0:T(8,128)(2,1)S(1)}, bf16[384,768]{1,0:T(8,128)(2,1)S(1)}, u32[]{:S(2)}, u32[]{:S(2)}) collective-permute-start(bf16[384,768]{1,0:T(8,128)(2,1)S(1)} %collective-permute-done.4), channel_id=1, source_target_pairs={{0,1},{1,0},{2,3},{3,2},{4,5},{5,4},{6,7},{7,6},{8,9},{9,8},{10,11... | collective-permute-start | bytes 1769480 | tf_op jit(solution)/shard_map/x2/ppermute | solution.py:427
  41.9 7.0 %collective-permute-done.9.rest_24_ = bf16[384,768]{1,0:T(8,128)(2,1)S(1)} collective-permute-done((bf16[384,768]{1,0:T(8,128)(2,1)S(1)}, bf16[384,768]{1,0:T(8,128)(2,1)S(1)}, u32[]{:S(2)}, u32[]{:S(2)}) %collective-permute-start.9) | collective-permute-done | bytes 589856 | tf_op jit(solution)/shard_map/u3/ppermute | solution.py:427
  48.8 1.6 %collective-permute-start.10 = (bf16[384,768]{1,0:T(8,128)(2,1)S(1)}, bf16[384,768]{1,0:T(8,128)(2,1)}, u32[]{:S(2)}, u32[]{:S(2)}) collective-permute-start(bf16[384,768]{1,0:T(8,128)(2,1)S(1)} %collective-permute-done.1.rest_3_), channel_id=1, source_target_pairs={{0,8},{2,10},{4,12},{6,14},{8,0},{10,2},{12,4},{14,6},{16,24},{18,... | collective-permute-start | bytes 1769480 | tf_op jit(solution)/shard_map/d1/ppermute | solution.py:427
  50.4 3.1 %collective-permute-done.7.rest_1_.rest_17_ = bf16[384,768]{1,0:T(8,128)(2,1)S(1)} collective-permute-done((bf16[384,768]{1,0:T(8,128)(2,1)S(1)}, bf16[384,768]{1,0:T(8,128)(2,1)S(1)}, u32[]{:S(2)}, u32[]{:S(2)}) %collective-permute-start.7) | collective-permute-done | bytes 589856 | tf_op jit(solution)/shard_map/x2/ppermute | solution.py:427
  53.6 8.6 %collective-permute-done.10.rest_3_.rest_11_ = bf16[384,768]{1,0:T(8,128)(2,1)} collective-permute-done((bf16[384,768]{1,0:T(8,128)(2,1)S(1)}, bf16[384,768]{1,0:T(8,128)(2,1)}, u32[]{:S(2)}, u32[]{:S(2)}) %collective-permute-start.10) | collective-permute-done | bytes 589856 | tf_op jit(solution)/shard_map/d1/ppermute | solution.py:427
  62.2 3.1 %collective-permute-done.8.rest_2_.rest_10_.rest_18_ = bf16[2,384,768]{2,1,0:T(8,128)(2,1)} collective-permute-done((bf16[2,384,768]{2,1,0:T(8,128)(2,1)}, bf16[2,384,768]{2,1,0:T(8,128)(2,1)}, u32[]{:S(2)}, u32[]{:S(2)}) %collective-permute-start.8) | collective-permute-done | bytes 1179680 | tf_op jit(solution)/shard_map/y12/ppermute | solution.py:427
  65.8 1.5 %collective-permute-start.6 = (bf16[384,768]{1,0:T(8,128)(2,1)}, bf16[384,768]{1,0:T(8,128)(2,1)}, u32[]{:S(2)}, u32[]{:S(2)}) collective-permute-start(bf16[384,768]{1,0:T(8,128)(2,1)} %collective-permute-done), channel_id=1, source_target_pairs={{0,1},{1,0},{2,3},{3,2},{4,5},{5,4},{6,7},{7,6},{8,9},{9,8},{10,11... | collective-permute-start | bytes 1769480 | tf_op jit(solution)/shard_map/x1/ppermute | solution.py:427
  67.3 1.6 %collective-permute-start.13 = (bf16[384,768]{1,0:T(8,128)(2,1)S(1)}, bf16[384,768]{1,0:T(8,128)(2,1)}, u32[]{:S(2)}, u32[]{:S(2)}) collective-permute-start(bf16[384,768]{1,0:T(8,128)(2,1)S(1)} %collective-permute-done.7.rest_1_.rest_17_), channel_id=1, source_target_pairs={{0,4},{2,6},{4,0},{6,2},{8,12},{10,14},{12,8},{14,10},{16,20},{18,... | collective-permute-start | bytes 1769480 | tf_op jit(solution)/shard_map/d2/ppermute | solution.py:427
  69.0 6.3 %project.3 = (bf16[3,384,768]{2,1,0:T(8,128)(2,1)}, bf16[3,768,384]{2,1,0:T(8,128)(2,1)}) custom-call(s32[3]{0:T(128)S(1)} %pad_add_fusion.at_ref, s32[1]{0:T(128)} %bitcast.3.plane_ref, bf16[1536,768]{1,0:T(8,128)(2,1)S(1)} %norm.1.n_ref, bf16[384,768]{1,0:T(8,128)(2,1)} %copy-done.3, bf16[384,768]{1,0:T(8,128)(2,1)} %copy-done.6, ...), custom_call_target="tpu_custom_call" | custom-call | flops 2717908992 | bytes 5898240 | tf_op jit(solution)/shard_map/project/pallas_call | solution.py:225
  75.3 6.0 %collective-permute-done.6.rest_1_.rest_9_ = bf16[384,768]{1,0:T(8,128)(2,1)} collective-permute-done((bf16[384,768]{1,0:T(8,128)(2,1)}, bf16[384,768]{1,0:T(8,128)(2,1)}, u32[]{:S(2)}, u32[]{:S(2)}) %collective-permute-start.6) | collective-permute-done | bytes 589856 | tf_op jit(solution)/shard_map/x1/ppermute | solution.py:427
  81.3 1.9 %collective-permute-done.13.rest_3_.rest_19_ = bf16[384,768]{1,0:T(8,128)(2,1)} collective-permute-done((bf16[384,768]{1,0:T(8,128)(2,1)S(1)}, bf16[384,768]{1,0:T(8,128)(2,1)}, u32[]{:S(2)}, u32[]{:S(2)}) %collective-permute-start.13) | collective-permute-done | bytes 589856 | tf_op jit(solution)/shard_map/d2/ppermute | solution.py:427
  84.2 1.5 %collective-permute-start.19 = (bf16[384,768]{1,0:T(8,128)(2,1)S(1)}, bf16[384,768]{1,0:T(8,128)(2,1)}, u32[]{:S(2)}, u32[]{:S(2)}) collective-permute-start(bf16[384,768]{1,0:T(8,128)(2,1)S(1)} %collective-permute-done.9.rest_24_), channel_id=1, source_target_pairs={{0,4},{2,6},{4,0},{6,2},{8,12},{10,14},{12,8},{14,10},{16,20},{18,... | collective-permute-start | bytes 1769480 | tf_op jit(solution)/shard_map/y3/ppermute | solution.py:427
  86.3 1.0 collective-permute-done.22.rest_7_.rest_23_
  87.7 6.3 %project.4 = (bf16[3,384,768]{2,1,0:T(8,128)(2,1)}, bf16[3,768,384]{2,1,0:T(8,128)(2,1)}) custom-call(s32[3]{0:T(128)S(1)} %pad_add_fusion.at_ref, s32[1]{0:T(128)} %bitcast.5.plane_ref, bf16[1536,768]{1,0:T(8,128)(2,1)S(1)} %norm.1.n_ref, bf16[2,384,768]{2,1,0:T(8,128)(2,1)} %pad_maximum_fusion.rest_0_.rest_8_.rest_16_, bf16[384,768]{1,0:T(8,128)(2,1)} %copy-done.8, ...), custom_call_target="tpu_custom_call" | custom-call | flops 2717908992 | bytes 5898240 | tf_op jit(solution)/shard_map/project/pallas_call | solution.py:225
  94.1 6.3 %project.5 = (bf16[3,384,768]{2,1,0:T(8,128)(2,1)}, bf16[3,768,384]{2,1,0:T(8,128)(2,1)}) custom-call(s32[3]{0:T(128)S(1)} %pad_add_fusion.at_ref, s32[1]{0:T(128)} %bitcast.4.plane_ref, bf16[1536,768]{1,0:T(8,128)(2,1)S(1)} %norm.1.n_ref, bf16[2,384,768]{2,1,0:T(8,128)(2,1)} %pad_maximum_fusion.rest_0_.rest_8_.rest_16_, ...), custom_call_target="tpu_custom_call" | custom-call | flops 2717908992 | bytes 5898240 | tf_op jit(solution)/shard_map/project/pallas_call | solution.py:225
  101.0 1.9 %collective-permute-done.20.rest_27_ = bf16[384,768]{1,0:T(8,128)(2,1)} collective-permute-done((bf16[384,768]{1,0:T(8,128)(2,1)}, bf16[384,768]{1,0:T(8,128)(2,1)}, u32[]{:S(2)}, u32[]{:S(2)}) %collective-permute-start.20) | collective-permute-done | bytes 589856 | tf_op jit(solution)/shard_map/d3/ppermute | solution.py:427
  104.2 1.1 collective-permute-done.25.rest_29_
  105.3 0.8 collective-permute-done.26.rest_30_
  106.1 0.8 collective-permute-done.27.rest_31_
  107.0 19.7 %finish.1 = bf16[768,1536]{1,0:T(8,128)(2,1)} custom-call(s32[3]{0:T(128)S(1)} %pad_add_fusion.at_ref, s32[4]{0:T(128)S(1)} %pad_add_fusion.1.planes_ref, s32[12]{0:T(128)S(1)} %copy-done.2, s32[1]{0:T(128)S(6)} %copy.8.live_ref, bf16[1536,768]{1,0:T(8,128)(2,1)S(1)} %norm.1.n_ref, bf16[768,1536]{1,0:T(8,128)(2,1)} %bitcast.13, ...), custom_call_target="tpu_custom_call" | custom-call | flops 10871635968 | bytes 9437184 | tf_op jit(solution)/shard_map/finish/pallas_call | solution.py:384
  (61 shorter events, 5.8 us)
Async XLA Ops:
  1.2 14.3 %copy-start.3 = (bf16[384,768]{1,0:T(8,128)(2,1)}, bf16[384,768]{1,0:T(8,128)(2,1)S(1)}, u32[]{:S(2)}) copy-start(bf16[384,768]{1,0:T(8,128)(2,1)S(1)} %pad_maximum_fusion.1.rest_0_) | copy-start | bytes 1769476
  1.2 7.7 %collective-permute-start.5 = (bf16[384,768]{1,0:T(8,128)(2,1)S(1)}, bf16[384,768]{1,0:T(8,128)(2,1)S(1)}, u32[]{:S(2)}, u32[]{:S(2)}) collective-permute-start(bf16[384,768]{1,0:T(8,128)(2,1)S(1)} %pad_maximum_fusion.1.rest_0_), channel_id=1, source_target_pairs={{0,2},{2,0},{4,6},{6,4},{8,10},{10,8},{12,14},{14,12},{16,18},{18,... | collective-permute-start | bytes 1769480 | tf_op jit(solution)/shard_map/core_u0/ppermute | solution.py:427
  1.7 30.3 %collective-permute-start.4 = (bf16[384,768]{1,0:T(8,128)(2,1)S(1)}, bf16[384,768]{1,0:T(8,128)(2,1)S(1)}, u32[]{:S(2)}, u32[]{:S(2)}) collective-permute-start(bf16[384,768]{1,0:T(8,128)(2,1)S(1)} %pad_maximum_fusion.1.rest_0_), channel_id=1, source_target_pairs={{0,16},{2,18},{4,20},{6,22},{8,24},{10,26},{12,28},{14,30},{16,0},... | collective-permute-start | bytes 1769480 | tf_op jit(solution)/shard_map/u2/ppermute | solution.py:427
  5.4 26.7 %collective-permute-start.3 = (bf16[384,768]{1,0:T(8,128)(2,1)S(1)}, bf16[384,768]{1,0:T(8,128)(2,1)S(1)}, u32[]{:S(2)}, u32[]{:S(2)}) collective-permute-start(bf16[384,768]{1,0:T(8,128)(2,1)S(1)} %pad_maximum_fusion.1.rest_0_), channel_id=1, source_target_pairs={{0,4},{2,6},{4,0},{6,2},{8,12},{10,14},{12,8},{14,10},{16,20},{18,... | collective-permute-start | bytes 1769480 | tf_op jit(solution)/shard_map/y0/ppermute | solution.py:427
  6.9 25.2 %collective-permute-start.2 = (bf16[384,768]{1,0:T(8,128)(2,1)S(1)}, bf16[384,768]{1,0:T(8,128)(2,1)S(1)}, u32[]{:S(2)}, u32[]{:S(2)}) collective-permute-start(bf16[384,768]{1,0:T(8,128)(2,1)S(1)} %pad_maximum_fusion.1.rest_0_), channel_id=1, source_target_pairs={{0,1},{1,0},{2,3},{3,2},{4,5},{5,4},{6,7},{7,6},{8,9},{9,8},{10,11... | collective-permute-start | bytes 1769480 | tf_op jit(solution)/shard_map/x0/ppermute | solution.py:427
  8.4 26.2 %collective-permute-start.1 = (bf16[384,768]{1,0:T(8,128)(2,1)S(1)}, bf16[384,768]{1,0:T(8,128)(2,1)S(1)}, u32[]{:S(2)}, u32[]{:S(2)}) collective-permute-start(bf16[384,768]{1,0:T(8,128)(2,1)S(1)} %pad_maximum_fusion.1.rest_0_), channel_id=1, source_target_pairs={{0,5},{1,4},{2,7},{3,6},{4,1},{5,0},{6,3},{7,2},{8,13},{9,12},{10,... | collective-permute-start | bytes 1769480 | tf_op jit(solution)/shard_map/d0/ppermute | solution.py:427
  8.8 26.1 %collective-permute-start = (bf16[384,768]{1,0:T(8,128)(2,1)S(1)}, bf16[384,768]{1,0:T(8,128)(2,1)}, u32[]{:S(2)}, u32[]{:S(2)}) collective-permute-start(bf16[384,768]{1,0:T(8,128)(2,1)S(1)} %pad_maximum_fusion.1.rest_0_), channel_id=1, source_target_pairs={{0,8},{2,10},{4,12},{6,14},{8,0},{10,2},{12,4},{14,6},{16,24},{18,... | collective-permute-start | bytes 1769480 | tf_op jit(solution)/shard_map/u1/ppermute | solution.py:427
  34.6 19.0 %copy-start.7 = (bf16[384,768]{1,0:T(8,128)(2,1)}, bf16[384,768]{1,0:T(8,128)(2,1)S(1)}, u32[]{:S(2)}) copy-start(bf16[384,768]{1,0:T(8,128)(2,1)S(1)} %collective-permute-done.1.rest_3_) | copy-start | bytes 1769476
  35.0 13.9 %collective-permute-start.9 = (bf16[384,768]{1,0:T(8,128)(2,1)S(1)}, bf16[384,768]{1,0:T(8,128)(2,1)S(1)}, u32[]{:S(2)}, u32[]{:S(2)}) collective-permute-start(bf16[384,768]{1,0:T(8,128)(2,1)S(1)} %collective-permute-done.4), channel_id=1, source_target_pairs={{0,8},{2,10},{4,12},{6,14},{8,0},{10,2},{12,4},{14,6},{16,24},{18,... | collective-permute-start | bytes 1769480 | tf_op jit(solution)/shard_map/u3/ppermute | solution.py:427
  38.3 26.9 %collective-permute-start.8 = (bf16[2,384,768]{2,1,0:T(8,128)(2,1)}, bf16[2,384,768]{2,1,0:T(8,128)(2,1)}, u32[]{:S(2)}, u32[]{:S(2)}) collective-permute-start(bf16[2,384,768]{2,1,0:T(8,128)(2,1)} %pad_maximum_fusion.rest_0_.rest_8_.rest_16_), channel_id=1, source_target_pairs={{0,4},{2,6},{4,0},{6,2},{8,12},{10,14},{12,8},{14,10},{16,20},{18,... | collective-permute-start | bytes 3538952 | tf_op jit(solution)/shard_map/y12/ppermute | solution.py:427
  39.9 13.7 %collective-permute-start.7 = (bf16[384,768]{1,0:T(8,128)(2,1)S(1)}, bf16[384,768]{1,0:T(8,128)(2,1)S(1)}, u32[]{:S(2)}, u32[]{:S(2)}) collective-permute-start(bf16[384,768]{1,0:T(8,128)(2,1)S(1)} %collective-permute-done.4), channel_id=1, source_target_pairs={{0,1},{1,0},{2,3},{3,2},{4,5},{5,4},{6,7},{7,6},{8,9},{9,8},{10,11... | collective-permute-start | bytes 1769480 | tf_op jit(solution)/shard_map/x2/ppermute | solution.py:427
  41.4 12.2 %collective-permute-start.11 = (bf16[384,768]{1,0:T(8,128)(2,1)S(1)}, bf16[384,768]{1,0:T(8,128)(2,1)S(1)}, u32[]{:S(2)}, u32[]{:S(2)}) collective-permute-start(bf16[384,768]{1,0:T(8,128)(2,1)S(1)} %collective-permute-done.2.rest_1_), channel_id=1, source_target_pairs={{0,2},{2,0},{4,6},{6,4},{8,10},{10,8},{12,14},{14,12},{16,18},{18,... | collective-permute-start | bytes 1769480 | tf_op jit(solution)/shard_map/core_x0/ppermute | solution.py:427
  41.4 12.2 %collective-permute-start.12 = (bf16[384,768]{1,0:T(8,128)(2,1)S(1)}, bf16[384,768]{1,0:T(8,128)(2,1)S(1)}, u32[]{:S(2)}, u32[]{:S(2)}) collective-permute-start(bf16[384,768]{1,0:T(8,128)(2,1)S(1)} %collective-permute-done.3.rest_2_), channel_id=1, source_target_pairs={{0,2},{2,0},{4,6},{6,4},{8,10},{10,8},{12,14},{14,12},{16,18},{18,... | collective-permute-start | bytes 1769480 | tf_op jit(solution)/shard_map/core_y0/ppermute | solution.py:427
  48.8 13.4 %collective-permute-start.10 = (bf16[384,768]{1,0:T(8,128)(2,1)S(1)}, bf16[384,768]{1,0:T(8,128)(2,1)}, u32[]{:S(2)}, u32[]{:S(2)}) collective-permute-start(bf16[384,768]{1,0:T(8,128)(2,1)S(1)} %collective-permute-done.1.rest_3_), channel_id=1, source_target_pairs={{0,8},{2,10},{4,12},{6,14},{8,0},{10,2},{12,4},{14,6},{16,24},{18,... | collective-permute-start | bytes 1769480 | tf_op jit(solution)/shard_map/d1/ppermute | solution.py:427
  53.6 21.7 %copy-start.8 = (bf16[384,768]{1,0:T(8,128)(2,1)}, bf16[384,768]{1,0:T(8,128)(2,1)S(1)}, u32[]{:S(2)}) copy-start(bf16[384,768]{1,0:T(8,128)(2,1)S(1)} %collective-permute-done.7.rest_1_.rest_17_) | copy-start | bytes 1769476
  53.6 13.7 %collective-permute-start.17 = (bf16[384,768]{1,0:T(8,128)(2,1)S(1)}, bf16[384,768]{1,0:T(8,128)(2,1)S(1)}, u32[]{:S(2)}, u32[]{:S(2)}) collective-permute-start(bf16[384,768]{1,0:T(8,128)(2,1)S(1)} %collective-permute-done.1.rest_3_), channel_id=1, source_target_pairs={{0,2},{2,0},{4,6},{6,4},{8,10},{10,8},{12,14},{14,12},{16,18},{18,... | collective-permute-start | bytes 1769480 | tf_op jit(solution)/shard_map/core_d0/ppermute | solution.py:427
  53.6 15.3 %copy-start.10 = (bf16[384,768]{1,0:T(8,128)(2,1)}, bf16[384,768]{1,0:T(8,128)(2,1)S(1)}, u32[]{:S(2)}) copy-start(bf16[384,768]{1,0:T(8,128)(2,1)S(1)} %collective-permute-done.12.rest_6_) | copy-start | bytes 1769476
  65.3 17.9 %collective-permute-start.15 = (bf16[2,384,768]{2,1,0:T(8,128)(2,1)}, bf16[2,384,768]{2,1,0:T(8,128)(2,1)}, u32[]{:S(2)}, u32[]{:S(2)}) collective-permute-start(bf16[2,384,768]{2,1,0:T(8,128)(2,1)} %collective-permute-done.8.rest_2_.rest_10_.rest_18_), channel_id=1, source_target_pairs={{0,2},{2,0},{4,6},{6,4},{8,10},{10,8},{12,14},{14,12},{16,18},{18,... | collective-permute-start | bytes 3538952 | tf_op jit(solution)/shard_map/core_y12/ppermute | solution.py:427
  65.3 17.9 %collective-permute-start.16 = (bf16[2,384,768]{2,1,0:T(8,128)(2,1)}, bf16[2,384,768]{2,1,0:T(8,128)(2,1)}, u32[]{:S(2)}, u32[]{:S(2)}) collective-permute-start(bf16[2,384,768]{2,1,0:T(8,128)(2,1)} %pad_maximum_fusion.rest_0_.rest_8_.rest_16_), channel_id=1, source_target_pairs={{0,2},{2,0},{4,6},{6,4},{8,10},{10,8},{12,14},{14,12},{16,18},{18,... | collective-permute-start | bytes 3538952 | tf_op jit(solution)/shard_map/core_u12/ppermute | solution.py:427
  65.8 15.6 %collective-permute-start.6 = (bf16[384,768]{1,0:T(8,128)(2,1)}, bf16[384,768]{1,0:T(8,128)(2,1)}, u32[]{:S(2)}, u32[]{:S(2)}) collective-permute-start(bf16[384,768]{1,0:T(8,128)(2,1)} %collective-permute-done), channel_id=1, source_target_pairs={{0,1},{1,0},{2,3},{3,2},{4,5},{5,4},{6,7},{7,6},{8,9},{9,8},{10,11... | collective-permute-start | bytes 1769480 | tf_op jit(solution)/shard_map/x1/ppermute | solution.py:427
  67.3 14.1 %collective-permute-start.14 = (bf16[384,768]{1,0:T(8,128)(2,1)S(1)}, bf16[384,768]{1,0:T(8,128)(2,1)}, u32[]{:S(2)}, u32[]{:S(2)}) collective-permute-start(bf16[384,768]{1,0:T(8,128)(2,1)S(1)} %collective-permute-done.7.rest_1_.rest_17_), channel_id=1, source_target_pairs={{0,2},{2,0},{4,6},{6,4},{8,10},{10,8},{12,14},{14,12},{16,18},{18,... | collective-permute-start | bytes 1769480 | tf_op jit(solution)/shard_map/core_x2/ppermute | solution.py:427
  67.3 15.9 %collective-permute-start.13 = (bf16[384,768]{1,0:T(8,128)(2,1)S(1)}, bf16[384,768]{1,0:T(8,128)(2,1)}, u32[]{:S(2)}, u32[]{:S(2)}) collective-permute-start(bf16[384,768]{1,0:T(8,128)(2,1)S(1)} %collective-permute-done.7.rest_1_.rest_17_), channel_id=1, source_target_pairs={{0,4},{2,6},{4,0},{6,2},{8,12},{10,14},{12,8},{14,10},{16,20},{18,... | collective-permute-start | bytes 1769480 | tf_op jit(solution)/shard_map/d2/ppermute | solution.py:427
  83.2 2.5 %collective-permute-start.23 = (bf16[384,768]{1,0:T(8,128)(2,1)}, bf16[384,768]{1,0:T(8,128)(2,1)}, u32[]{:S(2)}, u32[]{:S(2)}) collective-permute-start(bf16[384,768]{1,0:T(8,128)(2,1)} %collective-permute-done.6.rest_1_.rest_9_), channel_id=1, source_target_pairs={{0,2},{2,0},{4,6},{6,4},{8,10},{10,8},{12,14},{14,12},{16,18},{18,... | collective-permute-start | bytes 1769480 | tf_op jit(solution)/shard_map/core_x1/ppermute | solution.py:427
  83.2 4.0 %collective-permute-start.22 = (bf16[384,768]{1,0:T(8,128)(2,1)}, bf16[384,768]{1,0:T(8,128)(2,1)}, u32[]{:S(2)}, u32[]{:S(2)}) collective-permute-start(bf16[384,768]{1,0:T(8,128)(2,1)} %collective-permute-done.13.rest_3_.rest_19_), channel_id=1, source_target_pairs={{0,2},{2,0},{4,6},{6,4},{8,10},{10,8},{12,14},{14,12},{16,18},{18,... | collective-permute-start | bytes 1769480 | tf_op jit(solution)/shard_map/core_d2/ppermute | solution.py:427
  83.7 10.4 %collective-permute-start.24 = (bf16[384,768]{1,0:T(8,128)(2,1)}, bf16[384,768]{1,0:T(8,128)(2,1)}, u32[]{:S(2)}, u32[]{:S(2)}) collective-permute-start(bf16[384,768]{1,0:T(8,128)(2,1)} %collective-permute-done.10.rest_3_.rest_11_), channel_id=1, source_target_pairs={{0,2},{2,0},{4,6},{6,4},{8,10},{10,8},{12,14},{14,12},{16,18},{18,... | collective-permute-start | bytes 1769480 | tf_op jit(solution)/shard_map/core_d1/ppermute | solution.py:427
  83.8 16.6 %collective-permute-start.21 = (bf16[384,768]{1,0:T(8,128)(2,1)S(1)}, bf16[384,768]{1,0:T(8,128)(2,1)S(1)}, u32[]{:S(2)}, u32[]{:S(2)}) collective-permute-start(bf16[384,768]{1,0:T(8,128)(2,1)S(1)} %collective-permute-done.9.rest_24_), channel_id=1, source_target_pairs={{0,2},{2,0},{4,6},{6,4},{8,10},{10,8},{12,14},{14,12},{16,18},{18,... | collective-permute-start | bytes 1769480 | tf_op jit(solution)/shard_map/core_u3/ppermute | solution.py:427
  84.2 16.2 %collective-permute-start.19 = (bf16[384,768]{1,0:T(8,128)(2,1)S(1)}, bf16[384,768]{1,0:T(8,128)(2,1)}, u32[]{:S(2)}, u32[]{:S(2)}) collective-permute-start(bf16[384,768]{1,0:T(8,128)(2,1)S(1)} %collective-permute-done.9.rest_24_), channel_id=1, source_target_pairs={{0,4},{2,6},{4,0},{6,2},{8,12},{10,14},{12,8},{14,10},{16,20},{18,... | collective-permute-start | bytes 1769480 | tf_op jit(solution)/shard_map/y3/ppermute | solution.py:427
  85.7 15.3 %collective-permute-start.18 = (bf16[384,768]{1,0:T(8,128)(2,1)S(1)}, bf16[384,768]{1,0:T(8,128)(2,1)}, u32[]{:S(2)}, u32[]{:S(2)}) collective-permute-start(bf16[384,768]{1,0:T(8,128)(2,1)S(1)} %collective-permute-done.9.rest_24_), channel_id=1, source_target_pairs={{0,1},{1,0},{2,3},{3,2},{4,5},{5,4},{6,7},{7,6},{8,9},{9,8},{10,11... | collective-permute-start | bytes 1769480 | tf_op jit(solution)/shard_map/x3/ppermute | solution.py:427
  87.2 15.7 %collective-permute-start.20 = (bf16[384,768]{1,0:T(8,128)(2,1)}, bf16[384,768]{1,0:T(8,128)(2,1)}, u32[]{:S(2)}, u32[]{:S(2)}) collective-permute-start(bf16[384,768]{1,0:T(8,128)(2,1)} %collective-permute-done.13.rest_3_.rest_19_), channel_id=1, source_target_pairs={{0,8},{2,10},{4,12},{6,14},{8,0},{10,2},{12,4},{14,6},{16,24},{18,... | collective-permute-start | bytes 1769480 | tf_op jit(solution)/shard_map/d3/ppermute | solution.py:427
  102.9 2.3 %collective-permute-start.25 = (bf16[384,768]{1,0:T(8,128)(2,1)}, bf16[384,768]{1,0:T(8,128)(2,1)}, u32[]{:S(2)}, u32[]{:S(2)}) collective-permute-start(bf16[384,768]{1,0:T(8,128)(2,1)} %collective-permute-done.18.rest_25_), channel_id=1, source_target_pairs={{0,2},{2,0},{4,6},{6,4},{8,10},{10,8},{12,14},{14,12},{16,18},{18,... | collective-permute-start | bytes 1769480 | tf_op jit(solution)/shard_map/core_x3/ppermute | solution.py:427
  102.9 3.2 %collective-permute-start.26 = (bf16[384,768]{1,0:T(8,128)(2,1)}, bf16[384,768]{1,0:T(8,128)(2,1)}, u32[]{:S(2)}, u32[]{:S(2)}) collective-permute-start(bf16[384,768]{1,0:T(8,128)(2,1)} %collective-permute-done.19.rest_26_), channel_id=1, source_target_pairs={{0,2},{2,0},{4,6},{6,4},{8,10},{10,8},{12,14},{14,12},{16,18},{18,... | collective-permute-start | bytes 1769480 | tf_op jit(solution)/shard_map/core_y3/ppermute | solution.py:427
  103.4 3.5 %collective-permute-start.27 = (bf16[384,768]{1,0:T(8,128)(2,1)}, bf16[384,768]{1,0:T(8,128)(2,1)}, u32[]{:S(2)}, u32[]{:S(2)}) collective-permute-start(bf16[384,768]{1,0:T(8,128)(2,1)} %collective-permute-done.20.rest_27_), channel_id=1, source_target_pairs={{0,2},{2,0},{4,6},{6,4},{8,10},{10,8},{12,14},{14,12},{16,18},{18,... | collective-permute-start | bytes 1769480 | tf_op jit(solution)/shard_map/core_d3/ppermute | solution.py:427
  (9 other events, 71.0 us)

commit v9 on v8

--- a/solution.py
+++ b/solution.py
@@ -256,15 +256,14 @@
     x, y, core = at_ref[0], at_ref[1], at_ref[2]
 
     start_columns(at_ref, pieces[8 * last :], spots[8 * last :], rows, w_ref, w_sems)
-    for part in range(parts):
-        for kind, to in ((0, q_ref), (1, k_ref), (2, v_ref)):
-            which = parts * kind + part
-            for s, (p, k) in enumerate(((p0, k0), (p1, k1), (p2, k2))):
-
-                @pl.when(planes_ref[which // count] == s)
+    for s, (p, k) in enumerate(((p0, k0), (p1, k1), (p2, k2))):
+        for m in range(count):
+            which = planes_ref[s] * count + m
+            for kind, (src, to) in enumerate(((p, q_ref), (k, k_ref), (p, v_ref))):
+
+                @pl.when(which // parts == kind)
                 def _():
-                    src = (k if kind == 1 else p).at[which % count]
-                    pltpu.make_async_copy(src, to.at[part], part_sems.at[which]).start()
+                    pltpu.make_async_copy(src.at[m], to.at[which % parts], part_sems.at[which]).start()
 
     cols, lanes = wo_ref.shape[1], wo_ref.shape[2] // 2
     ours = cols // 4
@@ -351,10 +350,12 @@
 
     weigh(0)
 
-    @pl.loop(0, parts * pairs)
-    def _(pair):
-        gather(pair)
-        weigh(jnp.minimum(pair + 1, parts * pairs - 1))
+    @pl.loop(0, parts)
+    def _(part):
+        for i in range(pairs):
+            pair = part * pairs + i
+            gather(pair)
+            weigh(jnp.minimum(pair + 1, parts * pairs - 1))
 
     outs = []
     for s in range(slots):

time: 127 us -> 127 us (level)
  no operation moved by 1% of the time
where the time goes in v9:
time: 127 us
  waiting for transfers between devices  55.5 us (44%)
  Pallas kernels  41.9 us (33%)
  starting transfers between devices  23.2 us (18%)
  other arithmetic  3.5 us (3%)
  local copies, waits for them, and re-layouts  1.72 us (1%)
    ppermute x28, waiting for transfers between devices, move(): return lax.ppermute(value, axis, pairs)  55.5 us
    ppermute x28, starting transfers between devices, move(): return lax.ppermute(value, axis, pairs)  23.2 us
    pallas_call x1, Pallas kernels, finish(): pl.pallas_call(functools.partial(finish_kernel, [spot for _, spot in piec...  19.7 us
    pallas_call x3, Pallas kernels, project(): pl.pallas_call(functools.partial(project_kernel, [spot for _, spot in pie...  19 us
    pallas_call x1, Pallas kernels, normed_columns(): pl.pallas_call(norm_kernel, out_shape=jax.ShapeDtypeStruct((width, blocks...  3.26 us
  transfers between devices with their start and end apart: 28, of which 15 were waited for; matrix products, arithmetic and copies ran while one was open for 2% of the time, Pallas kernels for 18%

profile of v9, /device:TPU:0, one launch (start us, length us, event | category | flops | bytes accessed | tf_op | source)
XLA Modules:
  0.0 126.8 jit_solution(15168113662632989820)
XLA Ops:
  0.0 1.2 pad_maximum_fusion.1.rest_0_
  1.7 3.7 %collective-permute-start.4 = (bf16[384,768]{1,0:T(8,128)(2,1)S(1)}, bf16[384,768]{1,0:T(8,128)(2,1)S(1)}, u32[]{:S(2)}, u32[]{:S(2)}) collective-permute-start(bf16[384,768]{1,0:T(8,128)(2,1)S(1)} %pad_maximum_fusion.1.rest_0_), channel_id=1, source_target_pairs={{0,16},{2,18},{4,20},{6,22},{8,24},{10,26},{12,28},{14,30},{16,0},... | collective-permute-start | bytes 1769480 | tf_op jit(solution)/shard_map/u2/ppermute | solution.py:428
  5.4 1.5 %collective-permute-start.3 = (bf16[384,768]{1,0:T(8,128)(2,1)S(1)}, bf16[384,768]{1,0:T(8,128)(2,1)S(1)}, u32[]{:S(2)}, u32[]{:S(2)}) collective-permute-start(bf16[384,768]{1,0:T(8,128)(2,1)S(1)} %pad_maximum_fusion.1.rest_0_), channel_id=1, source_target_pairs={{0,4},{2,6},{4,0},{6,2},{8,12},{10,14},{12,8},{14,10},{16,20},{18,... | collective-permute-start | bytes 1769480 | tf_op jit(solution)/shard_map/y0/ppermute | solution.py:428
  6.9 1.5 %collective-permute-start.2 = (bf16[384,768]{1,0:T(8,128)(2,1)S(1)}, bf16[384,768]{1,0:T(8,128)(2,1)S(1)}, u32[]{:S(2)}, u32[]{:S(2)}) collective-permute-start(bf16[384,768]{1,0:T(8,128)(2,1)S(1)} %pad_maximum_fusion.1.rest_0_), channel_id=1, source_target_pairs={{0,1},{1,0},{2,3},{3,2},{4,5},{5,4},{6,7},{7,6},{8,9},{9,8},{10,11... | collective-permute-start | bytes 1769480 | tf_op jit(solution)/shard_map/x0/ppermute | solution.py:428
  8.8 1.6 %collective-permute-start = (bf16[384,768]{1,0:T(8,128)(2,1)S(1)}, bf16[384,768]{1,0:T(8,128)(2,1)}, u32[]{:S(2)}, u32[]{:S(2)}) collective-permute-start(bf16[384,768]{1,0:T(8,128)(2,1)S(1)} %pad_maximum_fusion.1.rest_0_), channel_id=1, source_target_pairs={{0,8},{2,10},{4,12},{6,14},{8,0},{10,2},{12,4},{14,6},{16,24},{18,... | collective-permute-start | bytes 1769480 | tf_op jit(solution)/shard_map/u1/ppermute | solution.py:428
  10.5 1.7 %copy-done = bf16[6,128,1536]{2,1,0:T(8,128)(2,1)S(1)} copy-done((bf16[6,128,1536]{2,1,0:T(8,128)(2,1)S(1)}, bf16[6,128,1536]{2,1,0:T(8,128)(2,1)}, u32[]{:S(2)}) %copy-start) | copy-done | bytes 2359320
  12.1 3.3 %norm.1.n_ref = bf16[1536,768]{1,0:T(8,128)(2,1)S(1)} custom-call(s32[12]{0:T(128)S(1)} %copy-done.1, bf16[6,128,1536]{2,1,0:T(8,128)(2,1)S(1)} %copy-done, f32[1,1536]{1,0:T(1,128)S(1)} %reshape.20.gain_ref, f32[1,384]{1,0:T(1,128)S(1)} %multiply_exponential_fusion.freq_ref), custom_call_target="tpu_custom_call" | custom-call | flops 47185920 | bytes 4718592 | tf_op jit(solution)/shard_map/norm/pallas_call | solution.py:138
  15.4 16.6 %collective-permute-done.4 = bf16[384,768]{1,0:T(8,128)(2,1)S(1)} collective-permute-done((bf16[384,768]{1,0:T(8,128)(2,1)S(1)}, bf16[384,768]{1,0:T(8,128)(2,1)S(1)}, u32[]{:S(2)}, u32[]{:S(2)}) %collective-permute-start.4) | collective-permute-done | bytes 589856 | tf_op jit(solution)/shard_map/u2/ppermute | solution.py:428
  32.0 2.5 %collective-permute-done.1.rest_3_ = bf16[384,768]{1,0:T(8,128)(2,1)S(1)} collective-permute-done((bf16[384,768]{1,0:T(8,128)(2,1)S(1)}, bf16[384,768]{1,0:T(8,128)(2,1)S(1)}, u32[]{:S(2)}, u32[]{:S(2)}) %collective-permute-start.1) | collective-permute-done | bytes 589856 | tf_op jit(solution)/shard_map/d0/ppermute | solution.py:428
  35.0 1.2 collective-permute-start.9
  36.2 2.2 %pad_maximum_fusion.rest_0_.rest_8_.rest_16_ = bf16[2,384,768]{2,1,0:T(8,128)(2,1)} fusion(bf16[1,384,768]{2,1,0:T(8,128)(2,1)S(1)} %bitcast.14, bf16[1,384,768]{2,1,0:T(8,128)(2,1)} %bitcast.10), kind=kLoop, calls=%fused_computation | loop fusion | flops 589824 | bytes 2359296 | tf_op jit(solution)/shard_map/stack | solution.py:468
  38.3 1.5 %collective-permute-start.8 = (bf16[2,384,768]{2,1,0:T(8,128)(2,1)}, bf16[2,384,768]{2,1,0:T(8,128)(2,1)}, u32[]{:S(2)}, u32[]{:S(2)}) collective-permute-start(bf16[2,384,768]{2,1,0:T(8,128)(2,1)} %pad_maximum_fusion.rest_0_.rest_8_.rest_16_), channel_id=1, source_target_pairs={{0,4},{2,6},{4,0},{6,2},{8,12},{10,14},{12,8},{14,10},{16,20},{18,... | collective-permute-start | bytes 3538952 | tf_op jit(solution)/shard_map/y12/ppermute | solution.py:428
  39.9 1.5 %collective-permute-start.7 = (bf16[384,768]{1,0:T(8,128)(2,1)S(1)}, bf16[384,768]{1,0:T(8,128)(2,1)S(1)}, u32[]{:S(2)}, u32[]{:S(2)}) collective-permute-start(bf16[384,768]{1,0:T(8,128)(2,1)S(1)} %collective-permute-done.4), channel_id=1, source_target_pairs={{0,1},{1,0},{2,3},{3,2},{4,5},{5,4},{6,7},{7,6},{8,9},{9,8},{10,11... | collective-permute-start | bytes 1769480 | tf_op jit(solution)/shard_map/x2/ppermute | solution.py:428
  41.9 7.0 %collective-permute-done.9.rest_24_ = bf16[384,768]{1,0:T(8,128)(2,1)S(1)} collective-permute-done((bf16[384,768]{1,0:T(8,128)(2,1)S(1)}, bf16[384,768]{1,0:T(8,128)(2,1)S(1)}, u32[]{:S(2)}, u32[]{:S(2)}) %collective-permute-start.9) | collective-permute-done | bytes 589856 | tf_op jit(solution)/shard_map/u3/ppermute | solution.py:428
  48.8 1.6 %collective-permute-start.10 = (bf16[384,768]{1,0:T(8,128)(2,1)S(1)}, bf16[384,768]{1,0:T(8,128)(2,1)}, u32[]{:S(2)}, u32[]{:S(2)}) collective-permute-start(bf16[384,768]{1,0:T(8,128)(2,1)S(1)} %collective-permute-done.1.rest_3_), channel_id=1, source_target_pairs={{0,8},{2,10},{4,12},{6,14},{8,0},{10,2},{12,4},{14,6},{16,24},{18,... | collective-permute-start | bytes 1769480 | tf_op jit(solution)/shard_map/d1/ppermute | solution.py:428
  50.4 3.1 %collective-permute-done.7.rest_1_.rest_17_ = bf16[384,768]{1,0:T(8,128)(2,1)S(1)} collective-permute-done((bf16[384,768]{1,0:T(8,128)(2,1)S(1)}, bf16[384,768]{1,0:T(8,128)(2,1)S(1)}, u32[]{:S(2)}, u32[]{:S(2)}) %collective-permute-start.7) | collective-permute-done | bytes 589856 | tf_op jit(solution)/shard_map/x2/ppermute | solution.py:428
  53.6 8.6 %collective-permute-done.10.rest_3_.rest_11_ = bf16[384,768]{1,0:T(8,128)(2,1)} collective-permute-done((bf16[384,768]{1,0:T(8,128)(2,1)S(1)}, bf16[384,768]{1,0:T(8,128)(2,1)}, u32[]{:S(2)}, u32[]{:S(2)}) %collective-permute-start.10) | collective-permute-done | bytes 589856 | tf_op jit(solution)/shard_map/d1/ppermute | solution.py:428
  62.2 3.1 %collective-permute-done.8.rest_2_.rest_10_.rest_18_ = bf16[2,384,768]{2,1,0:T(8,128)(2,1)} collective-permute-done((bf16[2,384,768]{2,1,0:T(8,128)(2,1)}, bf16[2,384,768]{2,1,0:T(8,128)(2,1)}, u32[]{:S(2)}, u32[]{:S(2)}) %collective-permute-start.8) | collective-permute-done | bytes 1179680 | tf_op jit(solution)/shard_map/y12/ppermute | solution.py:428
  65.8 1.5 %collective-permute-start.6 = (bf16[384,768]{1,0:T(8,128)(2,1)}, bf16[384,768]{1,0:T(8,128)(2,1)}, u32[]{:S(2)}, u32[]{:S(2)}) collective-permute-start(bf16[384,768]{1,0:T(8,128)(2,1)} %collective-permute-done), channel_id=1, source_target_pairs={{0,1},{1,0},{2,3},{3,2},{4,5},{5,4},{6,7},{7,6},{8,9},{9,8},{10,11... | collective-permute-start | bytes 1769480 | tf_op jit(solution)/shard_map/x1/ppermute | solution.py:428
  67.3 1.6 %collective-permute-start.13 = (bf16[384,768]{1,0:T(8,128)(2,1)S(1)}, bf16[384,768]{1,0:T(8,128)(2,1)}, u32[]{:S(2)}, u32[]{:S(2)}) collective-permute-start(bf16[384,768]{1,0:T(8,128)(2,1)S(1)} %collective-permute-done.7.rest_1_.rest_17_), channel_id=1, source_target_pairs={{0,4},{2,6},{4,0},{6,2},{8,12},{10,14},{12,8},{14,10},{16,20},{18,... | collective-permute-start | bytes 1769480 | tf_op jit(solution)/shard_map/d2/ppermute | solution.py:428
  69.0 6.3 %project.3 = (bf16[3,384,768]{2,1,0:T(8,128)(2,1)}, bf16[3,768,384]{2,1,0:T(8,128)(2,1)}) custom-call(s32[3]{0:T(128)S(1)} %pad_add_fusion.at_ref, s32[1]{0:T(128)} %bitcast.3.plane_ref, bf16[1536,768]{1,0:T(8,128)(2,1)S(1)} %norm.1.n_ref, bf16[384,768]{1,0:T(8,128)(2,1)} %copy-done.3, bf16[384,768]{1,0:T(8,128)(2,1)} %copy-done.6, ...), custom_call_target="tpu_custom_call" | custom-call | flops 2717908992 | bytes 5898240 | tf_op jit(solution)/shard_map/project/pallas_call | solution.py:225
  75.3 6.0 %collective-permute-done.6.rest_1_.rest_9_ = bf16[384,768]{1,0:T(8,128)(2,1)} collective-permute-done((bf16[384,768]{1,0:T(8,128)(2,1)}, bf16[384,768]{1,0:T(8,128)(2,1)}, u32[]{:S(2)}, u32[]{:S(2)}) %collective-permute-start.6) | collective-permute-done | bytes 589856 | tf_op jit(solution)/shard_map/x1/ppermute | solution.py:428
  81.3 1.9 %collective-permute-done.13.rest_3_.rest_19_ = bf16[384,768]{1,0:T(8,128)(2,1)} collective-permute-done((bf16[384,768]{1,0:T(8,128)(2,1)S(1)}, bf16[384,768]{1,0:T(8,128)(2,1)}, u32[]{:S(2)}, u32[]{:S(2)}) %collective-permute-start.13) | collective-permute-done | bytes 589856 | tf_op jit(solution)/shard_map/d2/ppermute | solution.py:428
  84.2 1.5 %collective-permute-start.19 = (bf16[384,768]{1,0:T(8,128)(2,1)S(1)}, bf16[384,768]{1,0:T(8,128)(2,1)}, u32[]{:S(2)}, u32[]{:S(2)}) collective-permute-start(bf16[384,768]{1,0:T(8,128)(2,1)S(1)} %collective-permute-done.9.rest_24_), channel_id=1, source_target_pairs={{0,4},{2,6},{4,0},{6,2},{8,12},{10,14},{12,8},{14,10},{16,20},{18,... | collective-permute-start | bytes 1769480 | tf_op jit(solution)/shard_map/y3/ppermute | solution.py:428
  86.3 1.0 collective-permute-done.22.rest_7_.rest_23_
  87.7 6.3 %project.4 = (bf16[3,384,768]{2,1,0:T(8,128)(2,1)}, bf16[3,768,384]{2,1,0:T(8,128)(2,1)}) custom-call(s32[3]{0:T(128)S(1)} %pad_add_fusion.at_ref, s32[1]{0:T(128)} %bitcast.5.plane_ref, bf16[1536,768]{1,0:T(8,128)(2,1)S(1)} %norm.1.n_ref, bf16[2,384,768]{2,1,0:T(8,128)(2,1)} %pad_maximum_fusion.rest_0_.rest_8_.rest_16_, bf16[384,768]{1,0:T(8,128)(2,1)} %copy-done.8, ...), custom_call_target="tpu_custom_call" | custom-call | flops 2717908992 | bytes 5898240 | tf_op jit(solution)/shard_map/project/pallas_call | solution.py:225
  94.1 6.3 %project.5 = (bf16[3,384,768]{2,1,0:T(8,128)(2,1)}, bf16[3,768,384]{2,1,0:T(8,128)(2,1)}) custom-call(s32[3]{0:T(128)S(1)} %pad_add_fusion.at_ref, s32[1]{0:T(128)} %bitcast.4.plane_ref, bf16[1536,768]{1,0:T(8,128)(2,1)S(1)} %norm.1.n_ref, bf16[2,384,768]{2,1,0:T(8,128)(2,1)} %pad_maximum_fusion.rest_0_.rest_8_.rest_16_, ...), custom_call_target="tpu_custom_call" | custom-call | flops 2717908992 | bytes 5898240 | tf_op jit(solution)/shard_map/project/pallas_call | solution.py:225
  101.0 1.9 %collective-permute-done.20.rest_27_ = bf16[384,768]{1,0:T(8,128)(2,1)} collective-permute-done((bf16[384,768]{1,0:T(8,128)(2,1)}, bf16[384,768]{1,0:T(8,128)(2,1)}, u32[]{:S(2)}, u32[]{:S(2)}) %collective-permute-start.20) | collective-permute-done | bytes 589856 | tf_op jit(solution)/shard_map/d3/ppermute | solution.py:428
  104.2 1.1 collective-permute-done.25.rest_29_
  105.3 0.8 collective-permute-done.26.rest_30_
  106.1 0.8 collective-permute-done.27.rest_31_
  107.0 19.7 %finish.1 = bf16[768,1536]{1,0:T(8,128)(2,1)} custom-call(s32[3]{0:T(128)S(1)} %pad_add_fusion.at_ref, s32[4]{0:T(128)S(1)} %pad_add_fusion.1.planes_ref, s32[12]{0:T(128)S(1)} %copy-done.2, s32[1]{0:T(128)S(6)} %copy.8.live_ref, bf16[1536,768]{1,0:T(8,128)(2,1)S(1)} %norm.1.n_ref, bf16[768,1536]{1,0:T(8,128)(2,1)} %bitcast.13, ...), custom_call_target="tpu_custom_call" | custom-call | flops 10871635968 | bytes 9437184 | tf_op jit(solution)/shard_map/finish/pallas_call | solution.py:385
  (61 shorter events, 5.8 us)
Async XLA Ops:
  1.2 14.3 %copy-start.3 = (bf16[384,768]{1,0:T(8,128)(2,1)}, bf16[384,768]{1,0:T(8,128)(2,1)S(1)}, u32[]{:S(2)}) copy-start(bf16[384,768]{1,0:T(8,128)(2,1)S(1)} %pad_maximum_fusion.1.rest_0_) | copy-start | bytes 1769476
  1.2 7.7 %collective-permute-start.5 = (bf16[384,768]{1,0:T(8,128)(2,1)S(1)}, bf16[384,768]{1,0:T(8,128)(2,1)S(1)}, u32[]{:S(2)}, u32[]{:S(2)}) collective-permute-start(bf16[384,768]{1,0:T(8,128)(2,1)S(1)} %pad_maximum_fusion.1.rest_0_), channel_id=1, source_target_pairs={{0,2},{2,0},{4,6},{6,4},{8,10},{10,8},{12,14},{14,12},{16,18},{18,... | collective-permute-start | bytes 1769480 | tf_op jit(solution)/shard_map/core_u0/ppermute | solution.py:428
  1.7 30.3 %collective-permute-start.4 = (bf16[384,768]{1,0:T(8,128)(2,1)S(1)}, bf16[384,768]{1,0:T(8,128)(2,1)S(1)}, u32[]{:S(2)}, u32[]{:S(2)}) collective-permute-start(bf16[384,768]{1,0:T(8,128)(2,1)S(1)} %pad_maximum_fusion.1.rest_0_), channel_id=1, source_target_pairs={{0,16},{2,18},{4,20},{6,22},{8,24},{10,26},{12,28},{14,30},{16,0},... | collective-permute-start | bytes 1769480 | tf_op jit(solution)/shard_map/u2/ppermute | solution.py:428
  5.4 26.7 %collective-permute-start.3 = (bf16[384,768]{1,0:T(8,128)(2,1)S(1)}, bf16[384,768]{1,0:T(8,128)(2,1)S(1)}, u32[]{:S(2)}, u32[]{:S(2)}) collective-permute-start(bf16[384,768]{1,0:T(8,128)(2,1)S(1)} %pad_maximum_fusion.1.rest_0_), channel_id=1, source_target_pairs={{0,4},{2,6},{4,0},{6,2},{8,12},{10,14},{12,8},{14,10},{16,20},{18,... | collective-permute-start | bytes 1769480 | tf_op jit(solution)/shard_map/y0/ppermute | solution.py:428
  6.9 25.2 %collective-permute-start.2 = (bf16[384,768]{1,0:T(8,128)(2,1)S(1)}, bf16[384,768]{1,0:T(8,128)(2,1)S(1)}, u32[]{:S(2)}, u32[]{:S(2)}) collective-permute-start(bf16[384,768]{1,0:T(8,128)(2,1)S(1)} %pad_maximum_fusion.1.rest_0_), channel_id=1, source_target_pairs={{0,1},{1,0},{2,3},{3,2},{4,5},{5,4},{6,7},{7,6},{8,9},{9,8},{10,11... | collective-permute-start | bytes 1769480 | tf_op jit(solution)/shard_map/x0/ppermute | solution.py:428
  8.4 26.2 %collective-permute-start.1 = (bf16[384,768]{1,0:T(8,128)(2,1)S(1)}, bf16[384,768]{1,0:T(8,128)(2,1)S(1)}, u32[]{:S(2)}, u32[]{:S(2)}) collective-permute-start(bf16[384,768]{1,0:T(8,128)(2,1)S(1)} %pad_maximum_fusion.1.rest_0_), channel_id=1, source_target_pairs={{0,5},{1,4},{2,7},{3,6},{4,1},{5,0},{6,3},{7,2},{8,13},{9,12},{10,... | collective-permute-start | bytes 1769480 | tf_op jit(solution)/shard_map/d0/ppermute | solution.py:428
  8.8 26.1 %collective-permute-start = (bf16[384,768]{1,0:T(8,128)(2,1)S(1)}, bf16[384,768]{1,0:T(8,128)(2,1)}, u32[]{:S(2)}, u32[]{:S(2)}) collective-permute-start(bf16[384,768]{1,0:T(8,128)(2,1)S(1)} %pad_maximum_fusion.1.rest_0_), channel_id=1, source_target_pairs={{0,8},{2,10},{4,12},{6,14},{8,0},{10,2},{12,4},{14,6},{16,24},{18,... | collective-permute-start | bytes 1769480 | tf_op jit(solution)/shard_map/u1/ppermute | solution.py:428
  34.6 19.0 %copy-start.7 = (bf16[384,768]{1,0:T(8,128)(2,1)}, bf16[384,768]{1,0:T(8,128)(2,1)S(1)}, u32[]{:S(2)}) copy-start(bf16[384,768]{1,0:T(8,128)(2,1)S(1)} %collective-permute-done.1.rest_3_) | copy-start | bytes 1769476
  35.0 13.9 %collective-permute-start.9 = (bf16[384,768]{1,0:T(8,128)(2,1)S(1)}, bf16[384,768]{1,0:T(8,128)(2,1)S(1)}, u32[]{:S(2)}, u32[]{:S(2)}) collective-permute-start(bf16[384,768]{1,0:T(8,128)(2,1)S(1)} %collective-permute-done.4), channel_id=1, source_target_pairs={{0,8},{2,10},{4,12},{6,14},{8,0},{10,2},{12,4},{14,6},{16,24},{18,... | collective-permute-start | bytes 1769480 | tf_op jit(solution)/shard_map/u3/ppermute | solution.py:428
  38.3 26.9 %collective-permute-start.8 = (bf16[2,384,768]{2,1,0:T(8,128)(2,1)}, bf16[2,384,768]{2,1,0:T(8,128)(2,1)}, u32[]{:S(2)}, u32[]{:S(2)}) collective-permute-start(bf16[2,384,768]{2,1,0:T(8,128)(2,1)} %pad_maximum_fusion.rest_0_.rest_8_.rest_16_), channel_id=1, source_target_pairs={{0,4},{2,6},{4,0},{6,2},{8,12},{10,14},{12,8},{14,10},{16,20},{18,... | collective-permute-start | bytes 3538952 | tf_op jit(solution)/shard_map/y12/ppermute | solution.py:428
  39.9 13.7 %collective-permute-start.7 = (bf16[384,768]{1,0:T(8,128)(2,1)S(1)}, bf16[384,768]{1,0:T(8,128)(2,1)S(1)}, u32[]{:S(2)}, u32[]{:S(2)}) collective-permute-start(bf16[384,768]{1,0:T(8,128)(2,1)S(1)} %collective-permute-done.4), channel_id=1, source_target_pairs={{0,1},{1,0},{2,3},{3,2},{4,5},{5,4},{6,7},{7,6},{8,9},{9,8},{10,11... | collective-permute-start | bytes 1769480 | tf_op jit(solution)/shard_map/x2/ppermute | solution.py:428
  41.4 12.2 %collective-permute-start.11 = (bf16[384,768]{1,0:T(8,128)(2,1)S(1)}, bf16[384,768]{1,0:T(8,128)(2,1)S(1)}, u32[]{:S(2)}, u32[]{:S(2)}) collective-permute-start(bf16[384,768]{1,0:T(8,128)(2,1)S(1)} %collective-permute-done.2.rest_1_), channel_id=1, source_target_pairs={{0,2},{2,0},{4,6},{6,4},{8,10},{10,8},{12,14},{14,12},{16,18},{18,... | collective-permute-start | bytes 1769480 | tf_op jit(solution)/shard_map/core_x0/ppermute | solution.py:428
  41.4 12.2 %collective-permute-start.12 = (bf16[384,768]{1,0:T(8,128)(2,1)S(1)}, bf16[384,768]{1,0:T(8,128)(2,1)S(1)}, u32[]{:S(2)}, u32[]{:S(2)}) collective-permute-start(bf16[384,768]{1,0:T(8,128)(2,1)S(1)} %collective-permute-done.3.rest_2_), channel_id=1, source_target_pairs={{0,2},{2,0},{4,6},{6,4},{8,10},{10,8},{12,14},{14,12},{16,18},{18,... | collective-permute-start | bytes 1769480 | tf_op jit(solution)/shard_map/core_y0/ppermute | solution.py:428
  48.8 13.4 %collective-permute-start.10 = (bf16[384,768]{1,0:T(8,128)(2,1)S(1)}, bf16[384,768]{1,0:T(8,128)(2,1)}, u32[]{:S(2)}, u32[]{:S(2)}) collective-permute-start(bf16[384,768]{1,0:T(8,128)(2,1)S(1)} %collective-permute-done.1.rest_3_), channel_id=1, source_target_pairs={{0,8},{2,10},{4,12},{6,14},{8,0},{10,2},{12,4},{14,6},{16,24},{18,... | collective-permute-start | bytes 1769480 | tf_op jit(solution)/shard_map/d1/ppermute | solution.py:428
  53.6 21.7 %copy-start.8 = (bf16[384,768]{1,0:T(8,128)(2,1)}, bf16[384,768]{1,0:T(8,128)(2,1)S(1)}, u32[]{:S(2)}) copy-start(bf16[384,768]{1,0:T(8,128)(2,1)S(1)} %collective-permute-done.7.rest_1_.rest_17_) | copy-start | bytes 1769476
  53.6 13.7 %collective-permute-start.17 = (bf16[384,768]{1,0:T(8,128)(2,1)S(1)}, bf16[384,768]{1,0:T(8,128)(2,1)S(1)}, u32[]{:S(2)}, u32[]{:S(2)}) collective-permute-start(bf16[384,768]{1,0:T(8,128)(2,1)S(1)} %collective-permute-done.1.rest_3_), channel_id=1, source_target_pairs={{0,2},{2,0},{4,6},{6,4},{8,10},{10,8},{12,14},{14,12},{16,18},{18,... | collective-permute-start | bytes 1769480 | tf_op jit(solution)/shard_map/core_d0/ppermute | solution.py:428
  53.6 15.3 %copy-start.10 = (bf16[384,768]{1,0:T(8,128)(2,1)}, bf16[384,768]{1,0:T(8,128)(2,1)S(1)}, u32[]{:S(2)}) copy-start(bf16[384,768]{1,0:T(8,128)(2,1)S(1)} %collective-permute-done.12.rest_6_) | copy-start | bytes 1769476
  65.3 17.9 %collective-permute-start.15 = (bf16[2,384,768]{2,1,0:T(8,128)(2,1)}, bf16[2,384,768]{2,1,0:T(8,128)(2,1)}, u32[]{:S(2)}, u32[]{:S(2)}) collective-permute-start(bf16[2,384,768]{2,1,0:T(8,128)(2,1)} %collective-permute-done.8.rest_2_.rest_10_.rest_18_), channel_id=1, source_target_pairs={{0,2},{2,0},{4,6},{6,4},{8,10},{10,8},{12,14},{14,12},{16,18},{18,... | collective-permute-start | bytes 3538952 | tf_op jit(solution)/shard_map/core_y12/ppermute | solution.py:428
  65.3 17.9 %collective-permute-start.16 = (bf16[2,384,768]{2,1,0:T(8,128)(2,1)}, bf16[2,384,768]{2,1,0:T(8,128)(2,1)}, u32[]{:S(2)}, u32[]{:S(2)}) collective-permute-start(bf16[2,384,768]{2,1,0:T(8,128)(2,1)} %pad_maximum_fusion.rest_0_.rest_8_.rest_16_), channel_id=1, source_target_pairs={{0,2},{2,0},{4,6},{6,4},{8,10},{10,8},{12,14},{14,12},{16,18},{18,... | collective-permute-start | bytes 3538952 | tf_op jit(solution)/shard_map/core_u12/ppermute | solution.py:428
  65.8 15.6 %collective-permute-start.6 = (bf16[384,768]{1,0:T(8,128)(2,1)}, bf16[384,768]{1,0:T(8,128)(2,1)}, u32[]{:S(2)}, u32[]{:S(2)}) collective-permute-start(bf16[384,768]{1,0:T(8,128)(2,1)} %collective-permute-done), channel_id=1, source_target_pairs={{0,1},{1,0},{2,3},{3,2},{4,5},{5,4},{6,7},{7,6},{8,9},{9,8},{10,11... | collective-permute-start | bytes 1769480 | tf_op jit(solution)/shard_map/x1/ppermute | solution.py:428
  67.3 14.1 %collective-permute-start.14 = (bf16[384,768]{1,0:T(8,128)(2,1)S(1)}, bf16[384,768]{1,0:T(8,128)(2,1)}, u32[]{:S(2)}, u32[]{:S(2)}) collective-permute-start(bf16[384,768]{1,0:T(8,128)(2,1)S(1)} %collective-permute-done.7.rest_1_.rest_17_), channel_id=1, source_target_pairs={{0,2},{2,0},{4,6},{6,4},{8,10},{10,8},{12,14},{14,12},{16,18},{18,... | collective-permute-start | bytes 1769480 | tf_op jit(solution)/shard_map/core_x2/ppermute | solution.py:428
  67.3 15.9 %collective-permute-start.13 = (bf16[384,768]{1,0:T(8,128)(2,1)S(1)}, bf16[384,768]{1,0:T(8,128)(2,1)}, u32[]{:S(2)}, u32[]{:S(2)}) collective-permute-start(bf16[384,768]{1,0:T(8,128)(2,1)S(1)} %collective-permute-done.7.rest_1_.rest_17_), channel_id=1, source_target_pairs={{0,4},{2,6},{4,0},{6,2},{8,12},{10,14},{12,8},{14,10},{16,20},{18,... | collective-permute-start | bytes 1769480 | tf_op jit(solution)/shard_map/d2/ppermute | solution.py:428
  83.2 2.5 %collective-permute-start.23 = (bf16[384,768]{1,0:T(8,128)(2,1)}, bf16[384,768]{1,0:T(8,128)(2,1)}, u32[]{:S(2)}, u32[]{:S(2)}) collective-permute-start(bf16[384,768]{1,0:T(8,128)(2,1)} %collective-permute-done.6.rest_1_.rest_9_), channel_id=1, source_target_pairs={{0,2},{2,0},{4,6},{6,4},{8,10},{10,8},{12,14},{14,12},{16,18},{18,... | collective-permute-start | bytes 1769480 | tf_op jit(solution)/shard_map/core_x1/ppermute | solution.py:428
  83.2 4.0 %collective-permute-start.22 = (bf16[384,768]{1,0:T(8,128)(2,1)}, bf16[384,768]{1,0:T(8,128)(2,1)}, u32[]{:S(2)}, u32[]{:S(2)}) collective-permute-start(bf16[384,768]{1,0:T(8,128)(2,1)} %collective-permute-done.13.rest_3_.rest_19_), channel_id=1, source_target_pairs={{0,2},{2,0},{4,6},{6,4},{8,10},{10,8},{12,14},{14,12},{16,18},{18,... | collective-permute-start | bytes 1769480 | tf_op jit(solution)/shard_map/core_d2/ppermute | solution.py:428
  83.7 10.4 %collective-permute-start.24 = (bf16[384,768]{1,0:T(8,128)(2,1)}, bf16[384,768]{1,0:T(8,128)(2,1)}, u32[]{:S(2)}, u32[]{:S(2)}) collective-permute-start(bf16[384,768]{1,0:T(8,128)(2,1)} %collective-permute-done.10.rest_3_.rest_11_), channel_id=1, source_target_pairs={{0,2},{2,0},{4,6},{6,4},{8,10},{10,8},{12,14},{14,12},{16,18},{18,... | collective-permute-start | bytes 1769480 | tf_op jit(solution)/shard_map/core_d1/ppermute | solution.py:428
  83.8 16.6 %collective-permute-start.21 = (bf16[384,768]{1,0:T(8,128)(2,1)S(1)}, bf16[384,768]{1,0:T(8,128)(2,1)S(1)}, u32[]{:S(2)}, u32[]{:S(2)}) collective-permute-start(bf16[384,768]{1,0:T(8,128)(2,1)S(1)} %collective-permute-done.9.rest_24_), channel_id=1, source_target_pairs={{0,2},{2,0},{4,6},{6,4},{8,10},{10,8},{12,14},{14,12},{16,18},{18,... | collective-permute-start | bytes 1769480 | tf_op jit(solution)/shard_map/core_u3/ppermute | solution.py:428
  84.2 16.2 %collective-permute-start.19 = (bf16[384,768]{1,0:T(8,128)(2,1)S(1)}, bf16[384,768]{1,0:T(8,128)(2,1)}, u32[]{:S(2)}, u32[]{:S(2)}) collective-permute-start(bf16[384,768]{1,0:T(8,128)(2,1)S(1)} %collective-permute-done.9.rest_24_), channel_id=1, source_target_pairs={{0,4},{2,6},{4,0},{6,2},{8,12},{10,14},{12,8},{14,10},{16,20},{18,... | collective-permute-start | bytes 1769480 | tf_op jit(solution)/shard_map/y3/ppermute | solution.py:428
  85.7 15.3 %collective-permute-start.18 = (bf16[384,768]{1,0:T(8,128)(2,1)S(1)}, bf16[384,768]{1,0:T(8,128)(2,1)}, u32[]{:S(2)}, u32[]{:S(2)}) collective-permute-start(bf16[384,768]{1,0:T(8,128)(2,1)S(1)} %collective-permute-done.9.rest_24_), channel_id=1, source_target_pairs={{0,1},{1,0},{2,3},{3,2},{4,5},{5,4},{6,7},{7,6},{8,9},{9,8},{10,11... | collective-permute-start | bytes 1769480 | tf_op jit(solution)/shard_map/x3/ppermute | solution.py:428
  87.2 15.7 %collective-permute-start.20 = (bf16[384,768]{1,0:T(8,128)(2,1)}, bf16[384,768]{1,0:T(8,128)(2,1)}, u32[]{:S(2)}, u32[]{:S(2)}) collective-permute-start(bf16[384,768]{1,0:T(8,128)(2,1)} %collective-permute-done.13.rest_3_.rest_19_), channel_id=1, source_target_pairs={{0,8},{2,10},{4,12},{6,14},{8,0},{10,2},{12,4},{14,6},{16,24},{18,... | collective-permute-start | bytes 1769480 | tf_op jit(solution)/shard_map/d3/ppermute | solution.py:428
  102.9 2.3 %collective-permute-start.25 = (bf16[384,768]{1,0:T(8,128)(2,1)}, bf16[384,768]{1,0:T(8,128)(2,1)}, u32[]{:S(2)}, u32[]{:S(2)}) collective-permute-start(bf16[384,768]{1,0:T(8,128)(2,1)} %collective-permute-done.18.rest_25_), channel_id=1, source_target_pairs={{0,2},{2,0},{4,6},{6,4},{8,10},{10,8},{12,14},{14,12},{16,18},{18,... | collective-permute-start | bytes 1769480 | tf_op jit(solution)/shard_map/core_x3/ppermute | solution.py:428
  102.9 3.2 %collective-permute-start.26 = (bf16[384,768]{1,0:T(8,128)(2,1)}, bf16[384,768]{1,0:T(8,128)(2,1)}, u32[]{:S(2)}, u32[]{:S(2)}) collective-permute-start(bf16[384,768]{1,0:T(8,128)(2,1)} %collective-permute-done.19.rest_26_), channel_id=1, source_target_pairs={{0,2},{2,0},{4,6},{6,4},{8,10},{10,8},{12,14},{14,12},{16,18},{18,... | collective-permute-start | bytes 1769480 | tf_op jit(solution)/shard_map/core_y3/ppermute | solution.py:428
  103.4 3.5 %collective-permute-start.27 = (bf16[384,768]{1,0:T(8,128)(2,1)}, bf16[384,768]{1,0:T(8,128)(2,1)}, u32[]{:S(2)}, u32[]{:S(2)}) collective-permute-start(bf16[384,768]{1,0:T(8,128)(2,1)} %collective-permute-done.20.rest_27_), channel_id=1, source_target_pairs={{0,2},{2,0},{4,6},{6,4},{8,10},{10,8},{12,14},{14,12},{16,18},{18,... | collective-permute-start | bytes 1769480 | tf_op jit(solution)/shard_map/core_d3/ppermute | solution.py:428
  (9 other events, 71.0 us)

commit v10 on v9

--- a/solution.py
+++ b/solution.py
@@ -473,12 +473,12 @@
     cd0, cx2, cy12, cu12 = (
         core(value, name) for value, name in ((d0, "core_d0"), (x2, "core_x2"), (y12, "core_y12"), (u12, "core_u12"))
     )
+    cu3 = core(sync(u3, cd0)[0], "core_u3")
     s0 = slot(0, u0, x0, y0, d0, cu0, cx0, cy0, cd0)
     p0 = project(place, planes[0:1], normed, s0, nq)
-    x1, d2, cx2, cy12, cu12, d1, u3, p0 = sync(x1, d2, cx2, cy12, cu12, d1, u3, p0)
+    x1, d2, cx2, cy12, cu12, cu3, d1, u3, p0 = sync(x1, d2, cx2, cy12, cu12, cu3, d1, u3, p0)
     x3, y3, d3 = xs(u3, "x3"), ys(u3, "y3"), z1(d2, "d3")
     cd2, cx1, cd1 = core(d2, "core_d2"), core(x1, "core_x1"), core(d1, "core_d1")
-    cu3 = core(u3, "core_u3")
     s2 = slot(1, u12, x2, y12, d2, cu12, cx2, cy12, cd2)
     p2 = project(place, planes[2:3], normed, s2, nq)
     s1 = slot(0, u12, x1, y12, d1, cu12, cx1, cy12, cd1)

time: 127 us -> 126 us (level)
  transfers between devices with their start and end apart: 28 -> 28, of which waited for: 15 -> 15; matrix products, arithmetic and copies ran while one was open for 2% -> 1% of each run, Pallas kernels for 18% -> 18%
where the time goes in v10:
time: 126 us
  waiting for transfers between devices  56.3 us (45%)
  Pallas kernels  41.9 us (33%)
  starting transfers between devices  22.3 us (18%)
  other arithmetic  2.43 us (2%)
  local copies, waits for them, and re-layouts  1.71 us (1%)
    ppermute x28, waiting for transfers between devices, move(): return lax.ppermute(value, axis, pairs)  56.3 us
    ppermute x28, starting transfers between devices, move(): return lax.ppermute(value, axis, pairs)  22.3 us
    pallas_call x1, Pallas kernels, finish(): pl.pallas_call(functools.partial(finish_kernel, [spot for _, spot in piec...  19.7 us
    pallas_call x3, Pallas kernels, project(): pl.pallas_call(functools.partial(project_kernel, [spot for _, spot in pie...  19 us
    pallas_call x1, Pallas kernels, normed_columns(): pl.pallas_call(norm_kernel, out_shape=jax.ShapeDtypeStruct((width, blocks...  3.26 us
  transfers between devices with their start and end apart: 28, of which 15 were waited for; matrix products, arithmetic and copies ran while one was open for 1% of the time, Pallas kernels for 18%

profile of v10, /device:TPU:0, one launch (start us, length us, event | category | flops | bytes accessed | tf_op | source)
XLA Modules:
  0.0 125.6 jit_solution(17385087049326372813)
XLA Ops:
  0.0 1.2 pad_maximum_fusion.1.rest_0_
  1.2 0.5 collective-permute-start.5
  1.7 3.7 %collective-permute-start.4 = (bf16[384,768]{1,0:T(8,128)(2,1)S(1)}, bf16[384,768]{1,0:T(8,128)(2,1)S(1)}, u32[]{:S(2)}, u32[]{:S(2)}) collective-permute-start(bf16[384,768]{1,0:T(8,128)(2,1)S(1)} %pad_maximum_fusion.1.rest_0_), channel_id=1, source_target_pairs={{0,16},{2,18},{4,20},{6,22},{8,24},{10,26},{12,28},{14,30},{16,0},... | collective-permute-start | bytes 1769480 | tf_op jit(solution)/shard_map/u2/ppermute | solution.py:428
  5.4 1.5 %collective-permute-start.3 = (bf16[384,768]{1,0:T(8,128)(2,1)S(1)}, bf16[384,768]{1,0:T(8,128)(2,1)S(1)}, u32[]{:S(2)}, u32[]{:S(2)}) collective-permute-start(bf16[384,768]{1,0:T(8,128)(2,1)S(1)} %pad_maximum_fusion.1.rest_0_), channel_id=1, source_target_pairs={{0,4},{2,6},{4,0},{6,2},{8,12},{10,14},{12,8},{14,10},{16,20},{18,... | collective-permute-start | bytes 1769480 | tf_op jit(solution)/shard_map/y0/ppermute | solution.py:428
  6.9 1.5 %collective-permute-start.2 = (bf16[384,768]{1,0:T(8,128)(2,1)S(1)}, bf16[384,768]{1,0:T(8,128)(2,1)S(1)}, u32[]{:S(2)}, u32[]{:S(2)}) collective-permute-start(bf16[384,768]{1,0:T(8,128)(2,1)S(1)} %pad_maximum_fusion.1.rest_0_), channel_id=1, source_target_pairs={{0,1},{1,0},{2,3},{3,2},{4,5},{5,4},{6,7},{7,6},{8,9},{9,8},{10,11... | collective-permute-start | bytes 1769480 | tf_op jit(solution)/shard_map/x0/ppermute | solution.py:428
  8.8 1.6 %collective-permute-start = (bf16[384,768]{1,0:T(8,128)(2,1)S(1)}, bf16[384,768]{1,0:T(8,128)(2,1)S(1)}, u32[]{:S(2)}, u32[]{:S(2)}) collective-permute-start(bf16[384,768]{1,0:T(8,128)(2,1)S(1)} %pad_maximum_fusion.1.rest_0_), channel_id=1, source_target_pairs={{0,8},{2,10},{4,12},{6,14},{8,0},{10,2},{12,4},{14,6},{16,24},{18,... | collective-permute-start | bytes 1769480 | tf_op jit(solution)/shard_map/u1/ppermute | solution.py:428
  10.5 1.7 %copy-done = bf16[6,128,1536]{2,1,0:T(8,128)(2,1)S(1)} copy-done((bf16[6,128,1536]{2,1,0:T(8,128)(2,1)S(1)}, bf16[6,128,1536]{2,1,0:T(8,128)(2,1)}, u32[]{:S(2)}) %copy-start) | copy-done | bytes 2359320
  12.1 3.3 %norm.1.n_ref = bf16[1536,768]{1,0:T(8,128)(2,1)S(1)} custom-call(s32[12]{0:T(128)S(1)} %copy-done.1, bf16[6,128,1536]{2,1,0:T(8,128)(2,1)S(1)} %copy-done, f32[1,1536]{1,0:T(1,128)S(1)} %reshape.20.gain_ref, f32[1,384]{1,0:T(1,128)S(1)} %multiply_exponential_fusion.freq_ref), custom_call_target="tpu_custom_call" | custom-call | flops 47185920 | bytes 4718592 | tf_op jit(solution)/shard_map/norm/pallas_call | solution.py:138
  15.4 16.6 %collective-permute-done.4 = bf16[384,768]{1,0:T(8,128)(2,1)S(1)} collective-permute-done((bf16[384,768]{1,0:T(8,128)(2,1)S(1)}, bf16[384,768]{1,0:T(8,128)(2,1)S(1)}, u32[]{:S(2)}, u32[]{:S(2)}) %collective-permute-start.4) | collective-permute-done | bytes 589856 | tf_op jit(solution)/shard_map/u2/ppermute | solution.py:428
  32.0 2.5 %collective-permute-done.1.rest_3_ = bf16[384,768]{1,0:T(8,128)(2,1)S(1)} collective-permute-done((bf16[384,768]{1,0:T(8,128)(2,1)S(1)}, bf16[384,768]{1,0:T(8,128)(2,1)S(1)}, u32[]{:S(2)}, u32[]{:S(2)}) %collective-permute-start.1) | collective-permute-done | bytes 589856 | tf_op jit(solution)/shard_map/d0/ppermute | solution.py:428
  34.9 1.3 %collective-permute-start.9 = (bf16[384,768]{1,0:T(8,128)(2,1)S(1)}, bf16[384,768]{1,0:T(8,128)(2,1)S(1)}, u32[]{:S(2)}, u32[]{:S(2)}) collective-permute-start(bf16[384,768]{1,0:T(8,128)(2,1)S(1)} %collective-permute-done.4), channel_id=1, source_target_pairs={{0,8},{2,10},{4,12},{6,14},{8,0},{10,2},{12,4},{14,6},{16,24},{18,... | collective-permute-start | bytes 1769480 | tf_op jit(solution)/shard_map/u3/ppermute | solution.py:428
  36.2 1.1 pad_maximum_fusion.rest_0_.rest_8_.rest_16_
  37.3 1.5 %collective-permute-start.8 = (bf16[2,384,768]{2,1,0:T(8,128)(2,1)}, bf16[2,384,768]{2,1,0:T(8,128)(2,1)}, u32[]{:S(2)}, u32[]{:S(2)}) collective-permute-start(bf16[2,384,768]{2,1,0:T(8,128)(2,1)} %pad_maximum_fusion.rest_0_.rest_8_.rest_16_), channel_id=1, source_target_pairs={{0,4},{2,6},{4,0},{6,2},{8,12},{10,14},{12,8},{14,10},{16,20},{18,... | collective-permute-start | bytes 3538952 | tf_op jit(solution)/shard_map/y12/ppermute | solution.py:428
  38.8 1.5 %collective-permute-start.7 = (bf16[384,768]{1,0:T(8,128)(2,1)S(1)}, bf16[384,768]{1,0:T(8,128)(2,1)}, u32[]{:S(2)}, u32[]{:S(2)}) collective-permute-start(bf16[384,768]{1,0:T(8,128)(2,1)S(1)} %collective-permute-done.4), channel_id=1, source_target_pairs={{0,1},{1,0},{2,3},{3,2},{4,5},{5,4},{6,7},{7,6},{8,9},{9,8},{10,11... | collective-permute-start | bytes 1769480 | tf_op jit(solution)/shard_map/x2/ppermute | solution.py:428
  40.8 8.0 %collective-permute-done.9.rest_24_ = bf16[384,768]{1,0:T(8,128)(2,1)S(1)} collective-permute-done((bf16[384,768]{1,0:T(8,128)(2,1)S(1)}, bf16[384,768]{1,0:T(8,128)(2,1)S(1)}, u32[]{:S(2)}, u32[]{:S(2)}) %collective-permute-start.9) | collective-permute-done | bytes 589856 | tf_op jit(solution)/shard_map/u3/ppermute | solution.py:428
  48.8 1.6 %collective-permute-start.10 = (bf16[384,768]{1,0:T(8,128)(2,1)S(1)}, bf16[384,768]{1,0:T(8,128)(2,1)}, u32[]{:S(2)}, u32[]{:S(2)}) collective-permute-start(bf16[384,768]{1,0:T(8,128)(2,1)S(1)} %collective-permute-done.1.rest_3_), channel_id=1, source_target_pairs={{0,8},{2,10},{4,12},{6,14},{8,0},{10,2},{12,4},{14,6},{16,24},{18,... | collective-permute-start | bytes 1769480 | tf_op jit(solution)/shard_map/d1/ppermute | solution.py:428
  50.4 2.2 %collective-permute-done.7.rest_1_.rest_17_ = bf16[384,768]{1,0:T(8,128)(2,1)} collective-permute-done((bf16[384,768]{1,0:T(8,128)(2,1)S(1)}, bf16[384,768]{1,0:T(8,128)(2,1)}, u32[]{:S(2)}, u32[]{:S(2)}) %collective-permute-start.7) | collective-permute-done | bytes 589856 | tf_op jit(solution)/shard_map/x2/ppermute | solution.py:428
  52.6 1.6 %collective-permute-start.6 = (bf16[384,768]{1,0:T(8,128)(2,1)S(1)}, bf16[384,768]{1,0:T(8,128)(2,1)}, u32[]{:S(2)}, u32[]{:S(2)}) collective-permute-start(bf16[384,768]{1,0:T(8,128)(2,1)S(1)} %collective-permute-done), channel_id=1, source_target_pairs={{0,1},{1,0},{2,3},{3,2},{4,5},{5,4},{6,7},{7,6},{8,9},{9,8},{10,11... | collective-permute-start | bytes 1769480 | tf_op jit(solution)/shard_map/x1/ppermute | solution.py:428
  54.2 8.0 %collective-permute-done.10.rest_3_.rest_11_ = bf16[384,768]{1,0:T(8,128)(2,1)} collective-permute-done((bf16[384,768]{1,0:T(8,128)(2,1)S(1)}, bf16[384,768]{1,0:T(8,128)(2,1)}, u32[]{:S(2)}, u32[]{:S(2)}) %collective-permute-start.10) | collective-permute-done | bytes 589856 | tf_op jit(solution)/shard_map/d1/ppermute | solution.py:428
  62.2 2.0 %collective-permute-done.8.rest_2_.rest_10_.rest_18_ = bf16[2,384,768]{2,1,0:T(8,128)(2,1)} collective-permute-done((bf16[2,384,768]{2,1,0:T(8,128)(2,1)}, bf16[2,384,768]{2,1,0:T(8,128)(2,1)}, u32[]{:S(2)}, u32[]{:S(2)}) %collective-permute-start.8) | collective-permute-done | bytes 1179680 | tf_op jit(solution)/shard_map/y12/ppermute | solution.py:428
  65.2 3.2 %collective-permute-done.6.rest_1_.rest_9_ = bf16[384,768]{1,0:T(8,128)(2,1)} collective-permute-done((bf16[384,768]{1,0:T(8,128)(2,1)S(1)}, bf16[384,768]{1,0:T(8,128)(2,1)}, u32[]{:S(2)}, u32[]{:S(2)}) %collective-permute-start.6) | collective-permute-done | bytes 589856 | tf_op jit(solution)/shard_map/x1/ppermute | solution.py:428
  69.0 6.3 %project.3 = (bf16[3,384,768]{2,1,0:T(8,128)(2,1)}, bf16[3,768,384]{2,1,0:T(8,128)(2,1)}) custom-call(s32[3]{0:T(128)S(1)} %pad_add_fusion.at_ref, s32[1]{0:T(128)} %bitcast.3.plane_ref, bf16[1536,768]{1,0:T(8,128)(2,1)S(1)} %norm.1.n_ref, bf16[384,768]{1,0:T(8,128)(2,1)} %copy-done.3, bf16[384,768]{1,0:T(8,128)(2,1)} %copy-done.5, ...), custom_call_target="tpu_custom_call" | custom-call | flops 2717908992 | bytes 5898240 | tf_op jit(solution)/shard_map/project/pallas_call | solution.py:225
  75.4 8.3 %collective-permute-done.13.rest_3_.rest_19_ = bf16[384,768]{1,0:T(8,128)(2,1)} collective-permute-done((bf16[384,768]{1,0:T(8,128)(2,1)}, bf16[384,768]{1,0:T(8,128)(2,1)}, u32[]{:S(2)}, u32[]{:S(2)}) %collective-permute-start.13) | collective-permute-done | bytes 589856 | tf_op jit(solution)/shard_map/d2/ppermute | solution.py:428
  84.8 1.5 %collective-permute-start.19 = (bf16[384,768]{1,0:T(8,128)(2,1)S(1)}, bf16[384,768]{1,0:T(8,128)(2,1)}, u32[]{:S(2)}, u32[]{:S(2)}) collective-permute-start(bf16[384,768]{1,0:T(8,128)(2,1)S(1)} %collective-permute-done.9.rest_24_), channel_id=1, source_target_pairs={{0,1},{1,0},{2,3},{3,2},{4,5},{5,4},{6,7},{7,6},{8,9},{9,8},{10,11... | collective-permute-start | bytes 1769480 | tf_op jit(solution)/shard_map/x3/ppermute | solution.py:428
  86.7 6.3 %project.4 = (bf16[3,384,768]{2,1,0:T(8,128)(2,1)}, bf16[3,768,384]{2,1,0:T(8,128)(2,1)}) custom-call(s32[3]{0:T(128)S(1)} %pad_add_fusion.at_ref, s32[1]{0:T(128)} %bitcast.5.plane_ref, bf16[1536,768]{1,0:T(8,128)(2,1)S(1)} %norm.1.n_ref, bf16[2,384,768]{2,1,0:T(8,128)(2,1)} %pad_maximum_fusion.rest_0_.rest_8_.rest_16_, ...), custom_call_target="tpu_custom_call" | custom-call | flops 2717908992 | bytes 5898240 | tf_op jit(solution)/shard_map/project/pallas_call | solution.py:225
  93.1 6.3 %project.5 = (bf16[3,384,768]{2,1,0:T(8,128)(2,1)}, bf16[3,768,384]{2,1,0:T(8,128)(2,1)}) custom-call(s32[3]{0:T(128)S(1)} %pad_add_fusion.at_ref, s32[1]{0:T(128)} %bitcast.4.plane_ref, bf16[1536,768]{1,0:T(8,128)(2,1)S(1)} %norm.1.n_ref, bf16[2,384,768]{2,1,0:T(8,128)(2,1)} %pad_maximum_fusion.rest_0_.rest_8_.rest_16_, ...), custom_call_target="tpu_custom_call" | custom-call | flops 2717908992 | bytes 5898240 | tf_op jit(solution)/shard_map/project/pallas_call | solution.py:225
  99.4 0.6 collective-permute-done.20.rest_26_
  100.3 1.4 %collective-permute-done.21.rest_27_ = bf16[384,768]{1,0:T(8,128)(2,1)} collective-permute-done((bf16[384,768]{1,0:T(8,128)(2,1)}, bf16[384,768]{1,0:T(8,128)(2,1)}, u32[]{:S(2)}, u32[]{:S(2)}) %collective-permute-start.21) | collective-permute-done | bytes 589856 | tf_op jit(solution)/shard_map/d3/ppermute | solution.py:428
  103.0 1.1 collective-permute-done.25.rest_29_
  104.1 0.8 collective-permute-done.26.rest_30_
  104.9 0.8 collective-permute-done.27.rest_31_
  105.7 19.7 %finish.1 = bf16[768,1536]{1,0:T(8,128)(2,1)} custom-call(s32[3]{0:T(128)S(1)} %pad_add_fusion.at_ref, s32[4]{0:T(128)S(1)} %pad_add_fusion.1.planes_ref, s32[12]{0:T(128)S(1)} %copy-done.2, s32[1]{0:T(128)S(6)} %copy.8.live_ref, bf16[1536,768]{1,0:T(8,128)(2,1)S(1)} %norm.1.n_ref, bf16[768,1536]{1,0:T(8,128)(2,1)} %bitcast.13, ...), custom_call_target="tpu_custom_call" | custom-call | flops 10871635968 | bytes 9437184 | tf_op jit(solution)/shard_map/finish/pallas_call | solution.py:385
  (57 shorter events, 5.3 us)
Async XLA Ops:
  1.2 14.2 %copy-start.3 = (bf16[384,768]{1,0:T(8,128)(2,1)}, bf16[384,768]{1,0:T(8,128)(2,1)S(1)}, u32[]{:S(2)}) copy-start(bf16[384,768]{1,0:T(8,128)(2,1)S(1)} %pad_maximum_fusion.1.rest_0_) | copy-start | bytes 1769476
  1.2 7.7 %collective-permute-start.5 = (bf16[384,768]{1,0:T(8,128)(2,1)S(1)}, bf16[384,768]{1,0:T(8,128)(2,1)}, u32[]{:S(2)}, u32[]{:S(2)}) collective-permute-start(bf16[384,768]{1,0:T(8,128)(2,1)S(1)} %pad_maximum_fusion.1.rest_0_), channel_id=1, source_target_pairs={{0,2},{2,0},{4,6},{6,4},{8,10},{10,8},{12,14},{14,12},{16,18},{18,... | collective-permute-start | bytes 1769480 | tf_op jit(solution)/shard_map/core_u0/ppermute | solution.py:428
  1.7 30.3 %collective-permute-start.4 = (bf16[384,768]{1,0:T(8,128)(2,1)S(1)}, bf16[384,768]{1,0:T(8,128)(2,1)S(1)}, u32[]{:S(2)}, u32[]{:S(2)}) collective-permute-start(bf16[384,768]{1,0:T(8,128)(2,1)S(1)} %pad_maximum_fusion.1.rest_0_), channel_id=1, source_target_pairs={{0,16},{2,18},{4,20},{6,22},{8,24},{10,26},{12,28},{14,30},{16,0},... | collective-permute-start | bytes 1769480 | tf_op jit(solution)/shard_map/u2/ppermute | solution.py:428
  5.4 26.7 %collective-permute-start.3 = (bf16[384,768]{1,0:T(8,128)(2,1)S(1)}, bf16[384,768]{1,0:T(8,128)(2,1)S(1)}, u32[]{:S(2)}, u32[]{:S(2)}) collective-permute-start(bf16[384,768]{1,0:T(8,128)(2,1)S(1)} %pad_maximum_fusion.1.rest_0_), channel_id=1, source_target_pairs={{0,4},{2,6},{4,0},{6,2},{8,12},{10,14},{12,8},{14,10},{16,20},{18,... | collective-permute-start | bytes 1769480 | tf_op jit(solution)/shard_map/y0/ppermute | solution.py:428
  6.9 25.2 %collective-permute-start.2 = (bf16[384,768]{1,0:T(8,128)(2,1)S(1)}, bf16[384,768]{1,0:T(8,128)(2,1)S(1)}, u32[]{:S(2)}, u32[]{:S(2)}) collective-permute-start(bf16[384,768]{1,0:T(8,128)(2,1)S(1)} %pad_maximum_fusion.1.rest_0_), channel_id=1, source_target_pairs={{0,1},{1,0},{2,3},{3,2},{4,5},{5,4},{6,7},{7,6},{8,9},{9,8},{10,11... | collective-permute-start | bytes 1769480 | tf_op jit(solution)/shard_map/x0/ppermute | solution.py:428
  8.4 26.2 %collective-permute-start.1 = (bf16[384,768]{1,0:T(8,128)(2,1)S(1)}, bf16[384,768]{1,0:T(8,128)(2,1)S(1)}, u32[]{:S(2)}, u32[]{:S(2)}) collective-permute-start(bf16[384,768]{1,0:T(8,128)(2,1)S(1)} %pad_maximum_fusion.1.rest_0_), channel_id=1, source_target_pairs={{0,5},{1,4},{2,7},{3,6},{4,1},{5,0},{6,3},{7,2},{8,13},{9,12},{10,... | collective-permute-start | bytes 1769480 | tf_op jit(solution)/shard_map/d0/ppermute | solution.py:428
  8.8 26.0 %collective-permute-start = (bf16[384,768]{1,0:T(8,128)(2,1)S(1)}, bf16[384,768]{1,0:T(8,128)(2,1)S(1)}, u32[]{:S(2)}, u32[]{:S(2)}) collective-permute-start(bf16[384,768]{1,0:T(8,128)(2,1)S(1)} %pad_maximum_fusion.1.rest_0_), channel_id=1, source_target_pairs={{0,8},{2,10},{4,12},{6,14},{8,0},{10,2},{12,4},{14,6},{16,24},{18,... | collective-permute-start | bytes 1769480 | tf_op jit(solution)/shard_map/u1/ppermute | solution.py:428
  34.6 18.0 %copy-start.6 = (bf16[384,768]{1,0:T(8,128)(2,1)}, bf16[384,768]{1,0:T(8,128)(2,1)S(1)}, u32[]{:S(2)}) copy-start(bf16[384,768]{1,0:T(8,128)(2,1)S(1)} %collective-permute-done.1.rest_3_) | copy-start | bytes 1769476
  34.9 14.0 %collective-permute-start.9 = (bf16[384,768]{1,0:T(8,128)(2,1)S(1)}, bf16[384,768]{1,0:T(8,128)(2,1)S(1)}, u32[]{:S(2)}, u32[]{:S(2)}) collective-permute-start(bf16[384,768]{1,0:T(8,128)(2,1)S(1)} %collective-permute-done.4), channel_id=1, source_target_pairs={{0,8},{2,10},{4,12},{6,14},{8,0},{10,2},{12,4},{14,6},{16,24},{18,... | collective-permute-start | bytes 1769480 | tf_op jit(solution)/shard_map/u3/ppermute | solution.py:428
  37.3 26.9 %collective-permute-start.8 = (bf16[2,384,768]{2,1,0:T(8,128)(2,1)}, bf16[2,384,768]{2,1,0:T(8,128)(2,1)}, u32[]{:S(2)}, u32[]{:S(2)}) collective-permute-start(bf16[2,384,768]{2,1,0:T(8,128)(2,1)} %pad_maximum_fusion.rest_0_.rest_8_.rest_16_), channel_id=1, source_target_pairs={{0,4},{2,6},{4,0},{6,2},{8,12},{10,14},{12,8},{14,10},{16,20},{18,... | collective-permute-start | bytes 3538952 | tf_op jit(solution)/shard_map/y12/ppermute | solution.py:428
  38.8 13.8 %collective-permute-start.7 = (bf16[384,768]{1,0:T(8,128)(2,1)S(1)}, bf16[384,768]{1,0:T(8,128)(2,1)}, u32[]{:S(2)}, u32[]{:S(2)}) collective-permute-start(bf16[384,768]{1,0:T(8,128)(2,1)S(1)} %collective-permute-done.4), channel_id=1, source_target_pairs={{0,1},{1,0},{2,3},{3,2},{4,5},{5,4},{6,7},{7,6},{8,9},{9,8},{10,11... | collective-permute-start | bytes 1769480 | tf_op jit(solution)/shard_map/x2/ppermute | solution.py:428
  40.3 12.3 %collective-permute-start.11 = (bf16[384,768]{1,0:T(8,128)(2,1)S(1)}, bf16[384,768]{1,0:T(8,128)(2,1)S(1)}, u32[]{:S(2)}, u32[]{:S(2)}) collective-permute-start(bf16[384,768]{1,0:T(8,128)(2,1)S(1)} %collective-permute-done.2.rest_1_), channel_id=1, source_target_pairs={{0,2},{2,0},{4,6},{6,4},{8,10},{10,8},{12,14},{14,12},{16,18},{18,... | collective-permute-start | bytes 1769480 | tf_op jit(solution)/shard_map/core_x0/ppermute | solution.py:428
  40.3 13.9 %collective-permute-start.12 = (bf16[384,768]{1,0:T(8,128)(2,1)S(1)}, bf16[384,768]{1,0:T(8,128)(2,1)S(1)}, u32[]{:S(2)}, u32[]{:S(2)}) collective-permute-start(bf16[384,768]{1,0:T(8,128)(2,1)S(1)} %collective-permute-done.3.rest_2_), channel_id=1, source_target_pairs={{0,2},{2,0},{4,6},{6,4},{8,10},{10,8},{12,14},{14,12},{16,18},{18,... | collective-permute-start | bytes 1769480 | tf_op jit(solution)/shard_map/core_y0/ppermute | solution.py:428
  48.8 13.4 %collective-permute-start.10 = (bf16[384,768]{1,0:T(8,128)(2,1)S(1)}, bf16[384,768]{1,0:T(8,128)(2,1)}, u32[]{:S(2)}, u32[]{:S(2)}) collective-permute-start(bf16[384,768]{1,0:T(8,128)(2,1)S(1)} %collective-permute-done.1.rest_3_), channel_id=1, source_target_pairs={{0,8},{2,10},{4,12},{6,14},{8,0},{10,2},{12,4},{14,6},{16,24},{18,... | collective-permute-start | bytes 1769480 | tf_op jit(solution)/shard_map/d1/ppermute | solution.py:428
  52.6 12.1 %collective-permute-start.17 = (bf16[384,768]{1,0:T(8,128)(2,1)S(1)}, bf16[384,768]{1,0:T(8,128)(2,1)S(1)}, u32[]{:S(2)}, u32[]{:S(2)}) collective-permute-start(bf16[384,768]{1,0:T(8,128)(2,1)S(1)} %collective-permute-done.1.rest_3_), channel_id=1, source_target_pairs={{0,2},{2,0},{4,6},{6,4},{8,10},{10,8},{12,14},{14,12},{16,18},{18,... | collective-permute-start | bytes 1769480 | tf_op jit(solution)/shard_map/core_d0/ppermute | solution.py:428
  52.6 15.9 %copy-start.7 = (bf16[384,768]{1,0:T(8,128)(2,1)}, bf16[384,768]{1,0:T(8,128)(2,1)S(1)}, u32[]{:S(2)}) copy-start(bf16[384,768]{1,0:T(8,128)(2,1)S(1)} %collective-permute-done.11.rest_5_) | copy-start | bytes 1769476
  52.6 15.8 %collective-permute-start.6 = (bf16[384,768]{1,0:T(8,128)(2,1)S(1)}, bf16[384,768]{1,0:T(8,128)(2,1)}, u32[]{:S(2)}, u32[]{:S(2)}) collective-permute-start(bf16[384,768]{1,0:T(8,128)(2,1)S(1)} %collective-permute-done), channel_id=1, source_target_pairs={{0,1},{1,0},{2,3},{3,2},{4,5},{5,4},{6,7},{7,6},{8,9},{9,8},{10,11... | collective-permute-start | bytes 1769480 | tf_op jit(solution)/shard_map/x1/ppermute | solution.py:428
  54.2 14.8 %copy-start.8 = (bf16[384,768]{1,0:T(8,128)(2,1)}, bf16[384,768]{1,0:T(8,128)(2,1)S(1)}, u32[]{:S(2)}) copy-start(bf16[384,768]{1,0:T(8,128)(2,1)S(1)} %collective-permute-done.12.rest_6_) | copy-start | bytes 1769476
  64.2 19.5 %collective-permute-start.15 = (bf16[2,384,768]{2,1,0:T(8,128)(2,1)}, bf16[2,384,768]{2,1,0:T(8,128)(2,1)}, u32[]{:S(2)}, u32[]{:S(2)}) collective-permute-start(bf16[2,384,768]{2,1,0:T(8,128)(2,1)} %collective-permute-done.8.rest_2_.rest_10_.rest_18_), channel_id=1, source_target_pairs={{0,2},{2,0},{4,6},{6,4},{8,10},{10,8},{12,14},{14,12},{16,18},{18,... | collective-permute-start | bytes 3538952 | tf_op jit(solution)/shard_map/core_y12/ppermute | solution.py:428
  64.2 19.5 %collective-permute-start.16 = (bf16[2,384,768]{2,1,0:T(8,128)(2,1)}, bf16[2,384,768]{2,1,0:T(8,128)(2,1)}, u32[]{:S(2)}, u32[]{:S(2)}) collective-permute-start(bf16[2,384,768]{2,1,0:T(8,128)(2,1)} %pad_maximum_fusion.rest_0_.rest_8_.rest_16_), channel_id=1, source_target_pairs={{0,2},{2,0},{4,6},{6,4},{8,10},{10,8},{12,14},{14,12},{16,18},{18,... | collective-permute-start | bytes 3538952 | tf_op jit(solution)/shard_map/core_u12/ppermute | solution.py:428
  64.7 10.7 %collective-permute-start.18 = (bf16[384,768]{1,0:T(8,128)(2,1)S(1)}, bf16[384,768]{1,0:T(8,128)(2,1)S(1)}, u32[]{:S(2)}, u32[]{:S(2)}) collective-permute-start(bf16[384,768]{1,0:T(8,128)(2,1)S(1)} %collective-permute-done.9.rest_24_), channel_id=1, source_target_pairs={{0,2},{2,0},{4,6},{6,4},{8,10},{10,8},{12,14},{14,12},{16,18},{18,... | collective-permute-start | bytes 1769480 | tf_op jit(solution)/shard_map/core_u3/ppermute | solution.py:428
  64.8 10.6 %collective-permute-start.14 = (bf16[384,768]{1,0:T(8,128)(2,1)}, bf16[384,768]{1,0:T(8,128)(2,1)}, u32[]{:S(2)}, u32[]{:S(2)}) collective-permute-start(bf16[384,768]{1,0:T(8,128)(2,1)} %collective-permute-done.7.rest_1_.rest_17_), channel_id=1, source_target_pairs={{0,2},{2,0},{4,6},{6,4},{8,10},{10,8},{12,14},{14,12},{16,18},{18,... | collective-permute-start | bytes 1769480 | tf_op jit(solution)/shard_map/core_x2/ppermute | solution.py:428
  68.5 15.2 %collective-permute-start.13 = (bf16[384,768]{1,0:T(8,128)(2,1)}, bf16[384,768]{1,0:T(8,128)(2,1)}, u32[]{:S(2)}, u32[]{:S(2)}) collective-permute-start(bf16[384,768]{1,0:T(8,128)(2,1)} %collective-permute-done.7.rest_1_.rest_17_), channel_id=1, source_target_pairs={{0,4},{2,6},{4,0},{6,2},{8,12},{10,14},{12,8},{14,10},{16,20},{18,... | collective-permute-start | bytes 1769480 | tf_op jit(solution)/shard_map/d2/ppermute | solution.py:428
  83.7 2.6 %collective-permute-start.22 = (bf16[384,768]{1,0:T(8,128)(2,1)}, bf16[384,768]{1,0:T(8,128)(2,1)}, u32[]{:S(2)}, u32[]{:S(2)}) collective-permute-start(bf16[384,768]{1,0:T(8,128)(2,1)} %collective-permute-done.13.rest_3_.rest_19_), channel_id=1, source_target_pairs={{0,2},{2,0},{4,6},{6,4},{8,10},{10,8},{12,14},{14,12},{16,18},{18,... | collective-permute-start | bytes 1769480 | tf_op jit(solution)/shard_map/core_d2/ppermute | solution.py:428
  83.7 9.4 %collective-permute-start.23 = (bf16[384,768]{1,0:T(8,128)(2,1)}, bf16[384,768]{1,0:T(8,128)(2,1)}, u32[]{:S(2)}, u32[]{:S(2)}) collective-permute-start(bf16[384,768]{1,0:T(8,128)(2,1)} %collective-permute-done.6.rest_1_.rest_9_), channel_id=1, source_target_pairs={{0,2},{2,0},{4,6},{6,4},{8,10},{10,8},{12,14},{14,12},{16,18},{18,... | collective-permute-start | bytes 1769480 | tf_op jit(solution)/shard_map/core_x1/ppermute | solution.py:428
  84.2 8.9 %collective-permute-start.24 = (bf16[384,768]{1,0:T(8,128)(2,1)}, bf16[384,768]{1,0:T(8,128)(2,1)}, u32[]{:S(2)}, u32[]{:S(2)}) collective-permute-start(bf16[384,768]{1,0:T(8,128)(2,1)} %collective-permute-done.10.rest_3_.rest_11_), channel_id=1, source_target_pairs={{0,2},{2,0},{4,6},{6,4},{8,10},{10,8},{12,14},{14,12},{16,18},{18,... | collective-permute-start | bytes 1769480 | tf_op jit(solution)/shard_map/core_d1/ppermute | solution.py:428
  84.3 15.8 %collective-permute-start.20 = (bf16[384,768]{1,0:T(8,128)(2,1)S(1)}, bf16[384,768]{1,0:T(8,128)(2,1)}, u32[]{:S(2)}, u32[]{:S(2)}) collective-permute-start(bf16[384,768]{1,0:T(8,128)(2,1)S(1)} %collective-permute-done.9.rest_24_), channel_id=1, source_target_pairs={{0,4},{2,6},{4,0},{6,2},{8,12},{10,14},{12,8},{14,10},{16,20},{18,... | collective-permute-start | bytes 1769480 | tf_op jit(solution)/shard_map/y3/ppermute | solution.py:428
  84.8 15.5 %collective-permute-start.19 = (bf16[384,768]{1,0:T(8,128)(2,1)S(1)}, bf16[384,768]{1,0:T(8,128)(2,1)}, u32[]{:S(2)}, u32[]{:S(2)}) collective-permute-start(bf16[384,768]{1,0:T(8,128)(2,1)S(1)} %collective-permute-done.9.rest_24_), channel_id=1, source_target_pairs={{0,1},{1,0},{2,3},{3,2},{4,5},{5,4},{6,7},{7,6},{8,9},{9,8},{10,11... | collective-permute-start | bytes 1769480 | tf_op jit(solution)/shard_map/x3/ppermute | solution.py:428
  86.3 15.4 %collective-permute-start.21 = (bf16[384,768]{1,0:T(8,128)(2,1)}, bf16[384,768]{1,0:T(8,128)(2,1)}, u32[]{:S(2)}, u32[]{:S(2)}) collective-permute-start(bf16[384,768]{1,0:T(8,128)(2,1)} %collective-permute-done.13.rest_3_.rest_19_), channel_id=1, source_target_pairs={{0,8},{2,10},{4,12},{6,14},{8,0},{10,2},{12,4},{14,6},{16,24},{18,... | collective-permute-start | bytes 1769480 | tf_op jit(solution)/shard_map/d3/ppermute | solution.py:428
  101.7 2.3 %collective-permute-start.25 = (bf16[384,768]{1,0:T(8,128)(2,1)}, bf16[384,768]{1,0:T(8,128)(2,1)}, u32[]{:S(2)}, u32[]{:S(2)}) collective-permute-start(bf16[384,768]{1,0:T(8,128)(2,1)} %collective-permute-done.19.rest_25_), channel_id=1, source_target_pairs={{0,2},{2,0},{4,6},{6,4},{8,10},{10,8},{12,14},{14,12},{16,18},{18,... | collective-permute-start | bytes 1769480 | tf_op jit(solution)/shard_map/core_x3/ppermute | solution.py:428
  101.7 3.2 %collective-permute-start.26 = (bf16[384,768]{1,0:T(8,128)(2,1)}, bf16[384,768]{1,0:T(8,128)(2,1)}, u32[]{:S(2)}, u32[]{:S(2)}) collective-permute-start(bf16[384,768]{1,0:T(8,128)(2,1)} %collective-permute-done.20.rest_26_), channel_id=1, source_target_pairs={{0,2},{2,0},{4,6},{6,4},{8,10},{10,8},{12,14},{14,12},{16,18},{18,... | collective-permute-start | bytes 1769480 | tf_op jit(solution)/shard_map/core_y3/ppermute | solution.py:428
  102.2 3.5 %collective-permute-start.27 = (bf16[384,768]{1,0:T(8,128)(2,1)}, bf16[384,768]{1,0:T(8,128)(2,1)}, u32[]{:S(2)}, u32[]{:S(2)}) collective-permute-start(bf16[384,768]{1,0:T(8,128)(2,1)} %collective-permute-done.21.rest_27_), channel_id=1, source_target_pairs={{0,2},{2,0},{4,6},{6,4},{8,10},{10,8},{12,14},{14,12},{16,18},{18,... | collective-permute-start | bytes 1769480 | tf_op jit(solution)/shard_map/core_d3/ppermute | solution.py:428
  (7 other events, 56.0 us)
